TPU v7x, 256 devices: a whole 4x4x8 slice. The times are simulated.
256 devices in a mesh: dp: 8 (over z), ctx: 32 (over x, y, core).
Axes of the slice: x: 4, y: 4, z: 8, core: 2. Of those that a mesh axis runs over, the one named last changes fastest.
Arguments:
- queries: bfloat16 [8, 8192, 512], P('dp', 'ctx'), may hold values from -11 to 11
- key_rows: bfloat16 [8, 8192, 512], P('dp', 'ctx'), may hold values from -11 to 11
- value_rows: bfloat16 [8, 8192, 512], P('dp', 'ctx'), may hold values from -6 to 6
- segment_ids: int32 [8, 8192], P('dp', 'ctx'), may hold values from 0 to 3, never falling along the last dimension, each value on 1 to 4096 neighbouring positions
- w_out: bfloat16 [512, 512], replicated, may hold values from -0.25 to 0.25
- d_out: bfloat16 [8, 8192, 512], P('dp', 'ctx'), may hold values from -6 to 6
Outputs:
- layer_out: bfloat16 [8, 8192, 512], P('dp', 'ctx')
- d_queries: bfloat16 [8, 8192, 512], P('dp', 'ctx')
- d_key_rows: bfloat16 [8, 8192, 512], P('dp', 'ctx')
- d_value_rows: bfloat16 [8, 8192, 512], P('dp', 'ctx')
- d_w_out: bfloat16 [512, 512], P('ctx')
Inputs may be any that keep to these rules, and one draw needn't show every extreme that they name: `segment_ids`: never falls along a sequence; each of the 4 documents of a sequence holds 1 to 4096 tokens, one exactly 4096.
All inputs are finite; a program needn't handle non-finite values.
Results may differ from a plain program's by a relative error of at most 0.04.
Values may be sent and summed in bfloat16 or wider, within the bound.
No kernel may reach another device: no remote copies, remote signals or barrier semaphores. Data moves between devices by JAX's collectives and lax.ppermute only.
A program may use at most 192 MiB of HBM per device.

v0:
```python
import functools

import jax
import jax.numpy as jnp
import numpy as np
from jax import lax
from jax.experimental import pallas as pl
from jax.experimental.pallas import tpu as pltpu
from jax.sharding import PartitionSpec as P

HEAD_DIM = 64
BLOCK = 64
HALF = 32
LEVELS = 4
ROWS = 256
WIDTH = 512
PAIRS = 4
LANES = 128
DOCS = 4
NEGATIVE = -1e30
BLOCKED = -2e30
SCALE = HEAD_DIM**-0.5
PACK = 2 * WIDTH + LANES
COARSE = 240
OFFSET = {1: 0, 2: 128, 3: 192, 4: 224}
COUNT = {0: 256, 1: 128, 2: 64, 3: 32, 4: 16}
F32 = jnp.float32
BF16 = jnp.bfloat16


def level_tables():
    total = np.zeros((COARSE, ROWS), np.float32)
    mean = np.zeros((COARSE, ROWS), np.float32)
    last = np.zeros((COARSE, ROWS), np.float32)
    for level in range(1, LEVELS + 1):
        factor = 2**level
        for row in range(COUNT[level]):
            at = OFFSET[level] + row
            total[at, row * factor : (row + 1) * factor] = 1
            mean[at, row * factor : (row + 1) * factor] = 1 / factor
            last[at, (row + 1) * factor - 1] = 1
    return total, mean, last


def position_tables():
    query = np.zeros((128 + 128 + 64, LANES), np.float32)
    key = np.zeros((256 + 256 + 128, LANES), np.float32)
    for row in range(128):
        query[row, 8 + row // BLOCK] = 1
        query[128 + row, 8 + row // HALF] = 1
    for row in range(64):
        query[256 + row, 8 + row // HALF] = 1
    for row in range(256):
        for place in range(2):
            if row // BLOCK - place not in (0, 1, 2):
                key[row, 8 + place] = BLOCKED
        for place in range(4):
            there, here = row // HALF - 2, place
            near = abs(there // 2 - here // 2) <= 1 and abs(there - here) >= 2
            if not near:
                key[256 + row, 8 + place] = BLOCKED
    for row in range(128):
        for place in range(2):
            there = (-2, -1, 2, 3)[row // HALF]
            if abs(there - place) < 2:
                key[512 + row, 8 + place] = BLOCKED
    return query, key


def dot(a, b, a_dim=1, b_dim=0):
    return lax.dot_general(a, b, (((a_dim,), (b_dim,)), ((), ())), preferred_element_type=F32)


def split(x):
    high = x.astype(BF16)
    return high, (x - high.astype(F32)).astype(BF16)


def head_lanes(rows):
    lane = lax.broadcasted_iota(jnp.int32, (rows, LANES), 1)
    return lane < HEAD_DIM


def stacked(x):
    first = head_lanes(x.shape[0]).astype(F32).astype(BF16)
    return jnp.concatenate([x * first, x * (1 - first)], axis=0)


def unstacked(x, rows):
    return jnp.where(head_lanes(rows), x[:rows], x[rows:])


def coarsen_kernel(seg, k, v, total, mean, last, up, down, far3, far4, own1, doc0, qdoc):
    sub = lax.broadcasted_iota(jnp.int32, (LANES, ROWS), 0)
    marks = jnp.where(seg[...] == sub, 1.0, 0.0).T.astype(BF16)
    coarse_marks = dot(last[...], marks).astype(BF16)
    key_c = dot(mean[...], k[...]).astype(BF16)
    value_c = dot(total[...], v[...]).astype(BF16)

    def key_side(x):
        lane = lax.broadcasted_iota(jnp.int32, x.shape, 1)
        return jnp.where(lane < DOCS, (1.0 - x.astype(F32)) * BLOCKED, 0.0).astype(BF16)

    doc_0 = key_side(marks)
    doc_c = key_side(coarse_marks)
    qdoc[0:ROWS] = marks
    qdoc[ROWS : ROWS + COARSE] = coarse_marks
    doc0[...] = doc_0

    def put(ref, at, keys, values, docs):
        rows = keys.shape[0]
        ref[at : at + rows, 0:WIDTH] = keys
        ref[at : at + rows, WIDTH : 2 * WIDTH] = values
        ref[at : at + rows, 2 * WIDTH :] = docs

    def rows_of(level, start, stop):
        if level == 0:
            return k[start:stop], v[start:stop], doc_0[start:stop]
        at = OFFSET[level]
        return tuple(x[at + start : at + stop] for x in (key_c, value_c, doc_c))

    for level in range(3):
        put(up, BLOCK * level, *rows_of(level, COUNT[level] - BLOCK, COUNT[level]))
        put(down, BLOCK * level, *rows_of(level, 0, BLOCK))
    put(own1, 0, *rows_of(1, 0, COUNT[1]))
    put(far3, 0, *rows_of(3, 0, COUNT[3]))
    put(far4, 0, *rows_of(4, 0, COUNT[4]))


class Window:
    def __init__(self, level, start, rows, position=None):
        self.level, self.start, self.rows, self.position = level, start, rows, position


GROUPS = (
    Window(0, 0, 128, (0, 0)),
    Window(0, 128, 128, (0, 0)),
    Window(1, 0, 128, (128, 256)),
    Window(2, 0, 64, (256, 512)),
    Window(3, 0, 32),
    Window(4, 0, 16),
)
KEYS = (256, 256, 256, 128, 96, 96)
P_AT = (0, 256, 512, 768, 896, 960)
P_ROWS = 992
COARSE_AT = {0: 0, 1: 256, 2: 384, 3: 448, 4: 480}
ALL_ROWS = 496


def window_parts(index, k, v, doc0, own1, low, high, far3, far4, part):
    lanes = (slice(0, WIDTH), slice(WIDTH, 2 * WIDTH), slice(2 * WIDTH, PACK))[part]
    fine = (k, v, doc0)[part]

    def rim(ref, level):
        return ref[BLOCK * level : BLOCK * (level + 1), lanes]

    if index == 0:
        return [rim(low, 0), fine[0:192]]
    if index == 1:
        return [fine[64:256], rim(high, 0)]
    if index == 2:
        return [rim(low, 1), own1[:, lanes], rim(high, 1)]
    if index == 3:
        return [rim(low, 2), rim(high, 2)]
    return [ref[:, lanes] for ref in (far3 if index == 4 else far4)]


def forward_kernel(n3, n4, *refs):
    (q, k, v, doc0, qdoc, own1, low, high), refs = refs[:8], refs[8:]
    far3, refs = refs[:n3], refs[n3:]
    far4, refs = refs[:n4], refs[n4:]
    (w, d_out, total, mean, spread, pos_q, pos_k), refs = refs[:7], refs[7:]
    layer_out, d_w, p_out, g_out, d_side, q_out, kw_out, vw_out = refs
    sources = (k, v, doc0, own1, low, high, far3, far4)
    q_coarse = dot(mean[...], q[...]).astype(BF16)
    key_docs = []
    for index, group in enumerate(GROUPS):
        docs = jnp.concatenate(window_parts(index, *sources, 2), axis=0)
        if group.position is not None:
            at = group.position[1]
            docs = docs + pos_k[at : at + KEYS[index]]
        key_docs.append(docs)
    query_docs = []
    for group in GROUPS:
        at = COARSE_AT[group.level] + group.start
        docs = qdoc[at : at + group.rows]
        if group.position is not None:
            docs = docs + pos_q[group.position[0] : group.position[0] + group.rows]
        query_docs.append(jnp.concatenate([docs, docs], axis=0))
    for index in range(len(GROUPS)):
        at = sum(KEYS[:index])
        kw_out[at : at + KEYS[index]] = jnp.concatenate(window_parts(index, *sources, 0), axis=0)
        vw_out[at : at + KEYS[index]] = jnp.concatenate(window_parts(index, *sources, 1), axis=0)
    grad_att = dot(d_out[...], w[...], 1, 1)
    lane = lax.broadcasted_iota(jnp.int32, (LANES, LANES), 1) // HEAD_DIM
    sub = lax.broadcasted_iota(jnp.int32, (LANES, LANES), 0) // HEAD_DIM
    same_head = jnp.where(lane == sub, 1.0, 0.0).astype(BF16)
    result = jnp.zeros((ROWS, WIDTH), F32)
    for pair in range(PAIRS):
        cols = slice(pair * LANES, (pair + 1) * LANES)
        q_all = jnp.concatenate([q[:, cols], q_coarse[:, cols]], axis=0) * SCALE
        q_all = q_all.astype(BF16)
        q_out[:, cols] = q_all
        parts = []
        for index, group in enumerate(GROUPS):
            at = COARSE_AT[group.level] + group.start
            rows, key_at = group.rows, sum(KEYS[:index])
            queries = jnp.concatenate(
                [stacked(q_all[at : at + rows]), query_docs[index]], axis=1
            )
            keys = jnp.concatenate(
                [kw_out[key_at : key_at + KEYS[index], cols], key_docs[index]], axis=1
            )
            scores = dot(queries, keys, 1, 1)
            peak = jnp.maximum(jnp.max(scores, axis=1, keepdims=True), NEGATIVE)
            peak = peak.astype(BF16).astype(F32)
            p = jnp.exp(scores - peak).astype(BF16)
            p_out[pair, P_AT[index] : P_AT[index] + 2 * rows, 0 : KEYS[index]] = p
            ones = jnp.ones((KEYS[index], LANES), BF16)
            values = jnp.concatenate([vw_out[key_at : key_at + KEYS[index], cols], ones], axis=1)
            both = dot(p, values)
            both = jnp.where(
                jnp.concatenate([head_lanes(rows)] * 2, axis=1), both[:rows], both[rows:]
            )
            wide_peak = jnp.where(head_lanes(rows), peak[:rows], peak[rows:])
            parts.append((both[:, :LANES], both[:, LANES:], wide_peak))
        fine = [jnp.concatenate([a, b], axis=0) for a, b in zip(parts[0], parts[1])]
        levels = [tuple(fine)]
        for level in range(1, LEVELS + 1):
            packed = jnp.concatenate([x.astype(BF16) for x in parts[level + 1]], axis=1)
            at = OFFSET[level]
            wide = dot(spread[:, LANES * (level - 1) : LANES * (level - 1) + COUNT[level]], packed)
            levels.append(tuple(wide[:, LANES * i : LANES * (i + 1)] for i in range(3)))
        top = functools.reduce(jnp.maximum, [x[2] for x in levels])
        weights = [jnp.exp(x[2] - top) for x in levels]
        norm = functools.reduce(
            jnp.add, [wt * x[1] * float(2**i) for i, (wt, x) in enumerate(zip(weights, levels))]
        )
        numer = functools.reduce(jnp.add, [wt * x[0] for wt, x in zip(weights, levels)])
        inverse = 1.0 / norm
        attended = (numer * inverse).astype(BF16)
        result = result + dot(attended, w[cols, :])
        d_w[cols, :] = dot(attended, d_out[...], 0, 0)
        grad = grad_att[:, cols]
        high_part, low_part = split(grad * attended.astype(F32))
        delta = dot(high_part, same_head) + dot(low_part, same_head)
        for level in range(LEVELS + 1):
            share = weights[level] * inverse
            at, rows = COARSE_AT[level], COUNT[level]
            if level == 0:
                grad_c, delta_c = (share * grad), share * delta
            else:
                d_high, d_low = split(share * delta)
                packed = jnp.concatenate([(share * grad).astype(BF16), d_high, d_low], axis=1)
                summed = dot(total[OFFSET[level] : OFFSET[level] + rows], packed)
                grad_c = summed[:, :LANES]
                delta_c = summed[:, LANES : 2 * LANES] + summed[:, 2 * LANES :]
            g_out[at : at + rows, cols] = grad_c.astype(BF16)
            d_high, d_low = split(delta_c * -float(2**level))
            quarter = lax.broadcasted_iota(jnp.int32, (rows, LANES), 1) % HEAD_DIM < HALF
            d_side[at : at + rows, cols] = jnp.where(
                quarter, d_high.astype(F32), d_low.astype(F32)
            ).astype(BF16)
    layer_out[...] = result.astype(BF16)


def backward_kernel(n3, n4, *refs):
    (p_in, g_in, d_side, q_in, kw, vw, spread_mean, spread_total), refs = refs[:8], refs[8:]
    d_q, own_k, own_v, to_low, to_high = refs[:5]
    to3, to4 = refs[5 : 5 + n3], refs[5 + n3 :]
    for pair in range(PAIRS):
        cols = slice(pair * LANES, (pair + 1) * LANES)
        value_cols = slice(WIDTH + pair * LANES, WIDTH + (pair + 1) * LANES)
        grads_q, grads_k, grads_v = [], [], []
        for index, group in enumerate(GROUPS):
            at = COARSE_AT[group.level] + group.start
            rows, keys, key_at = group.rows, KEYS[index], sum(KEYS[:index])
            grad = stacked(g_in[at : at + rows, cols])
            side = stacked(d_side[at : at + rows, cols])
            lane = lax.broadcasted_iota(jnp.int32, (keys, LANES), 1)
            ones = jnp.where(lane % HALF == 0, 1.0, 0.0).astype(BF16)
            values = jnp.concatenate([vw[key_at : key_at + keys, cols], ones], axis=1)
            product = dot(jnp.concatenate([grad, side], axis=1), values, 1, 1)
            p = p_in[pair, P_AT[index] : P_AT[index] + 2 * rows, 0:keys]
            ds = (p.astype(F32) * product).astype(BF16)
            grad_q = dot(ds, kw[key_at : key_at + keys, cols])
            grads_q.append(unstacked(grad_q, rows) * SCALE)
            grads_k.append(dot(ds, stacked(q_in[at : at + rows, cols]), 0, 0))
            grads_v.append(dot(p, grad, 0, 0))
        coarse = jnp.concatenate([x.astype(BF16) for x in grads_q[2:]], axis=0)
        d_q[:, cols] = (
            jnp.concatenate(grads_q[:2], axis=0) + dot(spread_mean[...], coarse)
        ).astype(BF16)
        for grads, own, out_cols, table in (
            (grads_k, own_k, cols, spread_mean),
            (grads_v, own_v, value_cols, spread_total),
        ):
            a, b, c, d, e, f = grads
            middle = jnp.concatenate([a[64:128], a[128:256] + b[0:128], b[128:192]], axis=0)
            spread = dot(table[:, 0 : COUNT[1]], c[64:192].astype(BF16))
            own[:, cols] = middle + spread
            to_low[:, out_cols] = jnp.concatenate([a[:64], c[:64], d[:64]], axis=0).astype(BF16)
            to_high[:, out_cols] = jnp.concatenate([b[192:], c[192:], d[64:]], axis=0).astype(BF16)
            for at, ref in enumerate(to3):
                rows = 96 // n3
                ref[:, out_cols] = e[at * rows : (at + 1) * rows].astype(BF16)
            for at, ref in enumerate(to4):
                rows = 96 // n4
                ref[:, out_cols] = f[at * rows : (at + 1) * rows].astype(BF16)


def gather_kernel(n3, n4, *refs):
    (own_k, own_v, low, high, spread_mean, spread_total), refs = refs[:6], refs[6:]
    from3, from4, (d_k, d_v) = refs[:n3], refs[n3 : n3 + n4], refs[n3 + n4 :]
    for own, out, lanes, table in (
        (own_k, d_k, slice(0, WIDTH), spread_mean),
        (own_v, d_v, slice(WIDTH, 2 * WIDTH), spread_total),
    ):

        def rim(ref, level):
            return ref[BLOCK * level : BLOCK * (level + 1), lanes].astype(F32)

        def summed(parts):
            return functools.reduce(jnp.add, [ref[:, lanes].astype(F32) for ref in parts])

        coarse = jnp.concatenate(
            [
                rim(high, 1),
                rim(low, 1),
                rim(low, 2) + rim(high, 2),
                summed(from3),
                summed(from4),
            ],
            axis=0,
        ).astype(BF16)
        whole = own[...] + dot(table[...], coarse)
        out[0:64] = (whole[0:64] + rim(high, 0)).astype(BF16)
        out[64:192] = whole[64:192].astype(BF16)
        out[192:256] = (whole[192:256] + rim(low, 0)).astype(BF16)


def vmem(count):
    return [pl.BlockSpec(memory_space=pltpu.VMEM)] * count


def call(kernel, name, outs, args):
    return pl.pallas_call(
        kernel,
        name=name,
        out_shape=[jax.ShapeDtypeStruct(shape, dtype) for shape, dtype in outs],
        in_specs=vmem(len(args)),
        out_specs=vmem(len(outs)),
        compiler_params=pltpu.CompilerParams(vmem_limit_bytes=48 * 1024 * 1024),
    )(*args)


def moved(x, route, back=False):
    count = lax.axis_size("ctx")
    pairs = [(i, route(i) % count) for i in range(count)]
    if back:
        pairs = [(b, a) for a, b in pairs]
    return lax.ppermute(x, "ctx", pairs)


ROUTES_3 = (
    lambda i: i + 2,
    lambda i: i - 2,
    lambda i: i - 3 if i % 2 else i + 3,
)


def routes_4():
    def route(shift, swap):
        def go(i):
            pair, side = i // 2, i % 2
            if shift == 0:
                pair = pair + (-3 if pair % 2 else 3)
            else:
                pair = pair + shift
            return 2 * pair + (side ^ swap)

        return go

    return [(route(shift, swap), swap) for shift in (2, -2, 0) for swap in (0, 1)]


def body(queries, key_rows, value_rows, segment_ids, w_out, d_out):
    q, k, v, grad_out = queries[0], key_rows[0], value_rows[0], d_out[0]
    total, mean, last = level_tables()
    pos_q, pos_k = (jnp.asarray(x, BF16) for x in position_tables())
    spread_padded = np.zeros((ROWS, LEVELS * LANES), np.float32)
    for level in range(1, LEVELS + 1):
        at = LANES * (level - 1)
        spread_padded[:, at : at + COUNT[level]] = total[
            OFFSET[level] : OFFSET[level] + COUNT[level]
        ].T
    spread_padded = jnp.asarray(spread_padded, BF16)
    spread_mean = jnp.asarray(mean.T, BF16)
    spread_total = jnp.asarray(total.T, BF16)
    total, mean, last = (jnp.asarray(x, BF16) for x in (total, mean, last))
    up, down, far3, far4, own1, doc0, qdoc = call(
        coarsen_kernel,
        "coarsen",
        [
            ((192, PACK), BF16),
            ((192, PACK), BF16),
            ((32, PACK), BF16),
            ((16, PACK), BF16),
            ((128, PACK), BF16),
            ((ROWS, LANES), BF16),
            ((ALL_ROWS, LANES), BF16),
        ],
        [segment_ids, k, v, total, mean, last],
    )
    low = moved(up, lambda i: i + 1)
    high = moved(down, lambda i: i - 1)
    got3 = [moved(far3, route) for route in ROUTES_3]
    got4 = [moved(far4, route) for route, _ in routes_4()]
    n3, n4 = len(got3), len(got4)
    layer_out, d_w, p, g, d_side, q_all, kw, vw = call(
        functools.partial(forward_kernel, n3, n4),
        "forward",
        [
            ((ROWS, WIDTH), BF16),
            ((WIDTH, WIDTH), F32),
            ((PAIRS, P_ROWS, 256), BF16),
            ((ALL_ROWS, WIDTH), BF16),
            ((ALL_ROWS, WIDTH), BF16),
            ((ALL_ROWS, WIDTH), BF16),
            ((sum(KEYS), WIDTH), BF16),
            ((sum(KEYS), WIDTH), BF16),
        ],
        [q, k, v, doc0, qdoc, own1, low, high, *got3, *got4]
        + [w_out, grad_out, total, mean, spread_padded, pos_q, pos_k],
    )
    d_w = lax.psum_scatter(d_w, "ctx", scatter_dimension=0, tiled=True)
    d_w = lax.psum(d_w, "dp").astype(BF16)
    outs = call(
        functools.partial(backward_kernel, n3, n4),
        "backward",
        [
            ((ROWS, WIDTH), BF16),
            ((ROWS, WIDTH), F32),
            ((ROWS, WIDTH), F32),
            ((192, 2 * WIDTH), BF16),
            ((192, 2 * WIDTH), BF16),
        ]
        + [((32, 2 * WIDTH), BF16)] * n3
        + [((16, 2 * WIDTH), BF16)] * n4,
        [p, g, d_side, q_all, kw, vw, spread_mean, spread_total],
    )
    d_q, own_k, own_v, to_low, to_high = outs[:5]
    low_back = moved(to_low, lambda i: i - 1)
    high_back = moved(to_high, lambda i: i + 1)
    back3 = [moved(x, route, back=True) for x, route in zip(outs[5 : 5 + n3], ROUTES_3)]
    back4 = [moved(x, route, back=True) for x, (route, _) in zip(outs[5 + n3 :], routes_4())]
    d_k, d_v = call(
        functools.partial(gather_kernel, n3, n4),
        "combine",
        [((ROWS, WIDTH), BF16)] * 2,
        [own_k, own_v, low_back, high_back, spread_mean, spread_total, *back3, *back4],
    )
    return layer_out[None], d_q[None], d_k[None], d_v[None], d_w


def solution(mesh):
    tokens = P("dp", "ctx", None)
    return jax.shard_map(
        body,
        mesh=mesh,
        in_specs=(tokens, tokens, tokens, P("dp", "ctx"), P(), tokens),
        out_specs=(tokens, tokens, tokens, tokens, P("ctx", None)),
        check_vma=False,
    )
```

profile of v0, /device:TPU:32, one launch (start us, length us, event | category | flops | bytes accessed | tf_op | source)
XLA Modules:
  0.0 180.3 jit_solution(14714564008009185756)
XLA Ops:
  7.2 0.9 copy-done.1
  8.2 0.9 copy-done.3
  13.0 5.1 %collective-permute-start.1 = (bf16[192,1152]{1,0:T(8,128)(2,1)S(1)}, bf16[192,1152]{1,0:T(8,128)(2,1)S(1)}, u32[]{:S(2)}, u32[]{:S(2)}) collective-permute-start(bf16[192,1152]{1,0:T(8,128)(2,1)S(1)} %get-tuple-element.40), channel_id=1, source_target_pairs={{0,31},{1,0},{2,1},{3,2},{4,3},{5,4},{6,5},{7,6},{8,7},{9,8},{10,9... | collective-permute-start | bytes 1327112 | tf_op jit(solution)/shard_map/ppermute | solution.py:362
  18.1 5.6 %collective-permute-start.8 = (bf16[16,1152]{1,0:T(8,128)(2,1)S(1)}, bf16[16,1152]{1,0:T(8,128)(2,1)S(1)}, u32[]{:S(2)}, u32[]{:S(2)}) collective-permute-start(bf16[16,1152]{1,0:T(8,128)(2,1)S(1)} %get-tuple-element.42), channel_id=1, source_target_pairs={{0,29},{1,28},{2,31},{3,30},{4,1},{5,0},{6,3},{7,2},{8,5},{9,4},{1... | collective-permute-start | bytes 110600 | tf_op jit(solution)/shard_map/ppermute | solution.py:362
  23.7 1.6 collective-permute-done.10.refs_16_
  26.0 2.1 %collective-permute-start.6 = (bf16[16,1152]{1,0:T(8,128)(2,1)S(1)}, bf16[16,1152]{1,0:T(8,128)(2,1)S(1)}, u32[]{:S(2)}, u32[]{:S(2)}) collective-permute-start(bf16[16,1152]{1,0:T(8,128)(2,1)S(1)} %get-tuple-element.42), channel_id=1, source_target_pairs={{0,5},{1,4},{2,7},{3,6},{4,9},{5,8},{6,11},{7,10},{8,13},{9,12},{1... | collective-permute-start | bytes 110600 | tf_op jit(solution)/shard_map/ppermute | solution.py:362
  28.1 1.3 collective-permute-start.5
  29.4 1.4 collective-permute-done.7.refs_13_
  30.8 2.3 %collective-permute-done.6.refs_12_ = bf16[16,1152]{1,0:T(8,128)(2,1)S(1)} collective-permute-done((bf16[16,1152]{1,0:T(8,128)(2,1)S(1)}, bf16[16,1152]{1,0:T(8,128)(2,1)S(1)}, u32[]{:S(2)}, u32[]{:S(2)}) %collective-permute-start.6) | collective-permute-done | bytes 36896 | tf_op jit(solution)/shard_map/ppermute | solution.py:362
  33.1 2.6 %collective-permute-start.3 = (bf16[32,1152]{1,0:T(8,128)(2,1)S(1)}, bf16[32,1152]{1,0:T(8,128)(2,1)S(1)}, u32[]{:S(2)}, u32[]{:S(2)}) collective-permute-start(bf16[32,1152]{1,0:T(8,128)(2,1)S(1)} %get-tuple-element.41), channel_id=1, source_target_pairs={{0,30},{1,31},{2,0},{3,1},{4,2},{5,3},{6,4},{7,5},{8,6},{9,7},{10,... | collective-permute-start | bytes 221192 | tf_op jit(solution)/shard_map/ppermute | solution.py:362
  36.0 1.4 collective-permute-start.2
  38.0 5.7 %collective-permute-done.2.refs_8_ = bf16[32,1152]{1,0:T(8,128)(2,1)S(1)} collective-permute-done((bf16[32,1152]{1,0:T(8,128)(2,1)S(1)}, bf16[32,1152]{1,0:T(8,128)(2,1)S(1)}, u32[]{:S(2)}, u32[]{:S(2)}) %collective-permute-start.2) | collective-permute-done | bytes 73760 | tf_op jit(solution)/shard_map/ppermute | solution.py:362
  43.7 0.9 copy-done.2
  44.6 0.9 copy-done.4
  47.4 0.9 copy-done.12
  48.3 0.9 copy-done.13
  49.3 0.9 copy-done.14
  52.0 9.0 %forward.1 = (bf16[256,512]{1,0:T(8,128)(2,1)}, f32[512,512]{1,0:T(8,128)}, bf16[4,992,256]{2,1,0:T(8,128)(2,1)}, bf16[496,512]{1,0:T(8,128)(2,1)S(1)}, bf16[496...) custom-call(bf16[256,512]{1,0:T(8,128)(2,1)S(1)} %bitcast.12, ...), custom_call_target="tpu_custom_call" | custom-call | tf_op jit(solution)/shard_map/forward/pallas_call | solution.py:347
  62.0 1.2 copy-done
  63.3 9.2 %backward.1 = (bf16[256,512]{1,0:T(8,128)(2,1)}, f32[256,512]{1,0:T(8,128)S(1)}, f32[256,512]{1,0:T(8,128)S(1)}, bf16[192,1024]{1,0:T(8,128)(2,1)S(1)}, bf16[192...) custom-call(bf16[4,992,256]{2,1,0:T(8,128)(2,1)} %get-tuple-element., ...), custom_call_target="tpu_custom_call" | custom-call | tf_op jit(solution)/shard_map/backward/pallas_call | solution.py:347
  73.3 3.2 %collective-permute-start.17 = (bf16[16,1024]{1,0:T(8,128)(2,1)S(1)}, bf16[16,1024]{1,0:T(8,128)(2,1)S(1)}, u32[]{:S(2)}, u32[]{:S(2)}) collective-permute-start(bf16[16,1024]{1,0:T(8,128)(2,1)S(1)} %get-tuple-element.59), channel_id=1, source_target_pairs={{5,0},{4,1},{7,2},{6,3},{9,4},{8,5},{11,6},{10,7},{13,8},{12,9},{1... | collective-permute-start | bytes 98312 | tf_op jit(solution)/shard_map/ppermute | solution.py:362
  76.9 2.0 %collective-permute-done.16.refs_9_ = bf16[16,1024]{1,0:T(8,128)(2,1)S(1)} collective-permute-done((bf16[16,1024]{1,0:T(8,128)(2,1)S(1)}, bf16[16,1024]{1,0:T(8,128)(2,1)S(1)}, u32[]{:S(2)}, u32[]{:S(2)}) %collective-permute-start.16) | collective-permute-done | bytes 32800 | tf_op jit(solution)/shard_map/ppermute | solution.py:362
  78.9 1.5 collective-permute-start.19
  80.4 2.0 %collective-permute-start.20 = (bf16[16,1024]{1,0:T(8,128)(2,1)S(1)}, bf16[16,1024]{1,0:T(8,128)(2,1)S(1)}, u32[]{:S(2)}, u32[]{:S(2)}) collective-permute-start(bf16[16,1024]{1,0:T(8,128)(2,1)S(1)} %get-tuple-element.62), channel_id=1, source_target_pairs={{6,0},{7,1},{28,2},{29,3},{10,4},{11,5},{0,6},{1,7},{14,8},{15,9},... | collective-permute-start | bytes 98312 | tf_op jit(solution)/shard_map/ppermute | solution.py:362
  82.4 1.7 collective-permute-done.18.refs_11_
  84.1 1.9 %collective-permute-done.19.refs_12_ = bf16[16,1024]{1,0:T(8,128)(2,1)S(1)} collective-permute-done((bf16[16,1024]{1,0:T(8,128)(2,1)S(1)}, bf16[16,1024]{1,0:T(8,128)(2,1)S(1)}, u32[]{:S(2)}, u32[]{:S(2)}) %collective-permute-start.19) | collective-permute-done | bytes 32800 | tf_op jit(solution)/shard_map/ppermute | solution.py:362
  86.0 3.1 %collective-permute-start.13 = (bf16[32,1024]{1,0:T(8,128)(2,1)S(1)}, bf16[32,1024]{1,0:T(8,128)(2,1)S(1)}, u32[]{:S(2)}, u32[]{:S(2)}) collective-permute-start(bf16[32,1024]{1,0:T(8,128)(2,1)S(1)} %get-tuple-element.55), channel_id=1, source_target_pairs={{2,0},{3,1},{4,2},{5,3},{6,4},{7,5},{8,6},{9,7},{10,8},{11,9},{12,... | collective-permute-start | bytes 196616 | tf_op jit(solution)/shard_map/ppermute | solution.py:362
  89.9 1.1 collective-permute-done.13.refs_6_
  91.0 5.7 %collective-permute-done.14.refs_7_ = bf16[32,1024]{1,0:T(8,128)(2,1)S(1)} collective-permute-done((bf16[32,1024]{1,0:T(8,128)(2,1)S(1)}, bf16[32,1024]{1,0:T(8,128)(2,1)S(1)}, u32[]{:S(2)}, u32[]{:S(2)}) %collective-permute-start.14) | collective-permute-done | bytes 65568 | tf_op jit(solution)/shard_map/ppermute | solution.py:362
  96.7 1.1 combine.1
  97.8 46.1 %reduce-scatter.2.cloned.1.call-done = f32[16,512]{1,0:T(8,128)} async-done(((f32[512,512]{1,0:T(8,128)}), f32[16,512]{1,0:T(8,128)}) %reduce-scatter.2.cloned.1.call-update) | async-done | bytes 32784 | tf_op jit(solution)/shard_map/reduce_scatter | solution.py:436
  143.9 29.6 %psum.7 = bf16[16,512]{1,0:T(8,128)(2,1)} all-reduce(f32[16,512]{1,0:T(8,128)} %reduce-scatter.2.cloned.1.call-done), channel_id=1, replica_groups=mesh['dp'=8,'ctx'=32] {'dp'}, use_global_device_ids=true, to_apply=%region_1.0 | all-reduce | flops 8192 | bytes 49152 | tf_op jit(solution)/shard_map/psum | solution.py:437
  (58 shorter events, 12.1 us)
Async XLA Ops:
  7.2 136.7 %reduce-scatter.2.cloned.1.call-start = ((), (), s32[]{:S(2)}) async-start(), calls=%async_computation.1 | async-start | bytes 1081344 | tf_op jit(solution)/shard_map/reduce_scatter | solution.py:436
  7.2 1.0 copy-start.1
  8.2 0.9 copy-start.3
  12.5 31.2 %copy-start.5 = (bf16[512,512]{1,0:T(8,128)(2,1)S(1)}, bf16[512,512]{1,0:T(8,128)(2,1)}, u32[]{:S(2)}) copy-start(bf16[512,512]{1,0:T(8,128)(2,1)} %refs_17_.1) | copy-start | bytes 1572868
  12.9 30.7 %collective-permute-start = (bf16[192,1152]{1,0:T(8,128)(2,1)S(1)}, bf16[192,1152]{1,0:T(8,128)(2,1)S(1)}, u32[]{:S(2)}, u32[]{:S(2)}) collective-permute-start(bf16[192,1152]{1,0:T(8,128)(2,1)S(1)} %get-tuple-element.39), channel_id=1, source_target_pairs={{0,1},{1,2},{2,3},{3,4},{4,5},{5,6},{6,7},{7,8},{8,9},{9,10},{10,1... | collective-permute-start | bytes 1327112 | tf_op jit(solution)/shard_map/ppermute | solution.py:362
  13.0 30.6 %collective-permute-start.1 = (bf16[192,1152]{1,0:T(8,128)(2,1)S(1)}, bf16[192,1152]{1,0:T(8,128)(2,1)S(1)}, u32[]{:S(2)}, u32[]{:S(2)}) collective-permute-start(bf16[192,1152]{1,0:T(8,128)(2,1)S(1)} %get-tuple-element.40), channel_id=1, source_target_pairs={{0,31},{1,0},{2,1},{3,2},{4,3},{5,4},{6,5},{7,6},{8,7},{9,8},{10,9... | collective-permute-start | bytes 1327112 | tf_op jit(solution)/shard_map/ppermute | solution.py:362
  18.1 7.3 %collective-permute-start.10 = (bf16[16,1152]{1,0:T(8,128)(2,1)S(1)}, bf16[16,1152]{1,0:T(8,128)(2,1)S(1)}, u32[]{:S(2)}, u32[]{:S(2)}) collective-permute-start(bf16[16,1152]{1,0:T(8,128)(2,1)S(1)} %get-tuple-element.42), channel_id=1, source_target_pairs={{0,7},{1,6},{2,29},{3,28},{4,11},{5,10},{6,1},{7,0},{8,15},{9,14},... | collective-permute-start | bytes 110600 | tf_op jit(solution)/shard_map/ppermute | solution.py:362
  18.1 8.0 %collective-permute-start.9 = (bf16[16,1152]{1,0:T(8,128)(2,1)S(1)}, bf16[16,1152]{1,0:T(8,128)(2,1)S(1)}, u32[]{:S(2)}, u32[]{:S(2)}) collective-permute-start(bf16[16,1152]{1,0:T(8,128)(2,1)S(1)} %get-tuple-element.42), channel_id=1, source_target_pairs={{0,6},{1,7},{2,28},{3,29},{4,10},{5,11},{6,0},{7,1},{8,14},{9,15},... | collective-permute-start | bytes 110600 | tf_op jit(solution)/shard_map/ppermute | solution.py:362
  18.1 10.0 %collective-permute-start.8 = (bf16[16,1152]{1,0:T(8,128)(2,1)S(1)}, bf16[16,1152]{1,0:T(8,128)(2,1)S(1)}, u32[]{:S(2)}, u32[]{:S(2)}) collective-permute-start(bf16[16,1152]{1,0:T(8,128)(2,1)S(1)} %get-tuple-element.42), channel_id=1, source_target_pairs={{0,29},{1,28},{2,31},{3,30},{4,1},{5,0},{6,3},{7,2},{8,5},{9,4},{1... | collective-permute-start | bytes 110600 | tf_op jit(solution)/shard_map/ppermute | solution.py:362
  25.3 5.5 %collective-permute-start.7 = (bf16[16,1152]{1,0:T(8,128)(2,1)S(1)}, bf16[16,1152]{1,0:T(8,128)(2,1)S(1)}, u32[]{:S(2)}, u32[]{:S(2)}) collective-permute-start(bf16[16,1152]{1,0:T(8,128)(2,1)S(1)} %get-tuple-element.42), channel_id=1, source_target_pairs={{0,28},{1,29},{2,30},{3,31},{4,0},{5,1},{6,2},{7,3},{8,4},{9,5},{1... | collective-permute-start | bytes 110600 | tf_op jit(solution)/shard_map/ppermute | solution.py:362
  26.0 7.1 %collective-permute-start.6 = (bf16[16,1152]{1,0:T(8,128)(2,1)S(1)}, bf16[16,1152]{1,0:T(8,128)(2,1)S(1)}, u32[]{:S(2)}, u32[]{:S(2)}) collective-permute-start(bf16[16,1152]{1,0:T(8,128)(2,1)S(1)} %get-tuple-element.42), channel_id=1, source_target_pairs={{0,5},{1,4},{2,7},{3,6},{4,9},{5,8},{6,11},{7,10},{8,13},{9,12},{1... | collective-permute-start | bytes 110600 | tf_op jit(solution)/shard_map/ppermute | solution.py:362
  28.1 7.9 %collective-permute-start.5 = (bf16[16,1152]{1,0:T(8,128)(2,1)S(1)}, bf16[16,1152]{1,0:T(8,128)(2,1)S(1)}, u32[]{:S(2)}, u32[]{:S(2)}) collective-permute-start(bf16[16,1152]{1,0:T(8,128)(2,1)S(1)} %get-tuple-element.42), channel_id=1, source_target_pairs={{0,4},{1,5},{2,6},{3,7},{4,8},{5,9},{6,10},{7,11},{8,12},{9,13},{1... | collective-permute-start | bytes 110600 | tf_op jit(solution)/shard_map/ppermute | solution.py:362
  30.8 6.6 %collective-permute-start.4 = (bf16[32,1152]{1,0:T(8,128)(2,1)S(1)}, bf16[32,1152]{1,0:T(8,128)(2,1)S(1)}, u32[]{:S(2)}, u32[]{:S(2)}) collective-permute-start(bf16[32,1152]{1,0:T(8,128)(2,1)S(1)} %get-tuple-element.41), channel_id=1, source_target_pairs={{0,3},{1,30},{2,5},{3,0},{4,7},{5,2},{6,9},{7,4},{8,11},{9,6},{10,... | collective-permute-start | bytes 221192 | tf_op jit(solution)/shard_map/ppermute | solution.py:362
  33.1 4.9 %collective-permute-start.3 = (bf16[32,1152]{1,0:T(8,128)(2,1)S(1)}, bf16[32,1152]{1,0:T(8,128)(2,1)S(1)}, u32[]{:S(2)}, u32[]{:S(2)}) collective-permute-start(bf16[32,1152]{1,0:T(8,128)(2,1)S(1)} %get-tuple-element.41), channel_id=1, source_target_pairs={{0,30},{1,31},{2,0},{3,1},{4,2},{5,3},{6,4},{7,5},{8,6},{9,7},{10,... | collective-permute-start | bytes 221192 | tf_op jit(solution)/shard_map/ppermute | solution.py:362
  36.0 7.7 %collective-permute-start.2 = (bf16[32,1152]{1,0:T(8,128)(2,1)S(1)}, bf16[32,1152]{1,0:T(8,128)(2,1)S(1)}, u32[]{:S(2)}, u32[]{:S(2)}) collective-permute-start(bf16[32,1152]{1,0:T(8,128)(2,1)S(1)} %get-tuple-element.41), channel_id=1, source_target_pairs={{0,2},{1,3},{2,4},{3,5},{4,6},{5,7},{6,8},{7,9},{8,10},{9,11},{10,... | collective-permute-start | bytes 221192 | tf_op jit(solution)/shard_map/ppermute | solution.py:362
  43.7 1.0 copy-start.2
  44.6 0.9 copy-start.4
  47.4 0.9 copy-start.12
  48.3 0.9 copy-start.13
  61.1 1.0 copy-start.7
  62.0 1.2 copy-start
  72.4 24.2 %collective-permute-start.11 = (bf16[192,1024]{1,0:T(8,128)(2,1)S(1)}, bf16[192,1024]{1,0:T(8,128)(2,1)S(1)}, u32[]{:S(2)}, u32[]{:S(2)}) collective-permute-start(bf16[192,1024]{1,0:T(8,128)(2,1)S(1)} %get-tuple-element.53), channel_id=1, source_target_pairs={{0,31},{1,0},{2,1},{3,2},{4,3},{5,4},{6,5},{7,6},{8,7},{9,8},{10,9... | collective-permute-start | bytes 1179656 | tf_op jit(solution)/shard_map/ppermute | solution.py:362
  72.4 24.2 %collective-permute-start.12 = (bf16[192,1024]{1,0:T(8,128)(2,1)S(1)}, bf16[192,1024]{1,0:T(8,128)(2,1)S(1)}, u32[]{:S(2)}, u32[]{:S(2)}) collective-permute-start(bf16[192,1024]{1,0:T(8,128)(2,1)S(1)} %get-tuple-element.54), channel_id=1, source_target_pairs={{0,1},{1,2},{2,3},{3,4},{4,5},{5,6},{6,7},{7,8},{8,9},{9,10},{10,1... | collective-permute-start | bytes 1179656 | tf_op jit(solution)/shard_map/ppermute | solution.py:362
  73.0 5.9 %collective-permute-start.16 = (bf16[16,1024]{1,0:T(8,128)(2,1)S(1)}, bf16[16,1024]{1,0:T(8,128)(2,1)S(1)}, u32[]{:S(2)}, u32[]{:S(2)}) collective-permute-start(bf16[16,1024]{1,0:T(8,128)(2,1)S(1)} %get-tuple-element.58), channel_id=1, source_target_pairs={{4,0},{5,1},{6,2},{7,3},{8,4},{9,5},{10,6},{11,7},{12,8},{13,9},{1... | collective-permute-start | bytes 98312 | tf_op jit(solution)/shard_map/ppermute | solution.py:362
  73.3 7.0 %collective-permute-start.17 = (bf16[16,1024]{1,0:T(8,128)(2,1)S(1)}, bf16[16,1024]{1,0:T(8,128)(2,1)S(1)}, u32[]{:S(2)}, u32[]{:S(2)}) collective-permute-start(bf16[16,1024]{1,0:T(8,128)(2,1)S(1)} %get-tuple-element.59), channel_id=1, source_target_pairs={{5,0},{4,1},{7,2},{6,3},{9,4},{8,5},{11,6},{10,7},{13,8},{12,9},{1... | collective-permute-start | bytes 98312 | tf_op jit(solution)/shard_map/ppermute | solution.py:362
  76.5 7.5 %collective-permute-start.18 = (bf16[16,1024]{1,0:T(8,128)(2,1)S(1)}, bf16[16,1024]{1,0:T(8,128)(2,1)S(1)}, u32[]{:S(2)}, u32[]{:S(2)}) collective-permute-start(bf16[16,1024]{1,0:T(8,128)(2,1)S(1)} %get-tuple-element.60), channel_id=1, source_target_pairs={{28,0},{29,1},{30,2},{31,3},{0,4},{1,5},{2,6},{3,7},{4,8},{5,9},{6... | collective-permute-start | bytes 98312 | tf_op jit(solution)/shard_map/ppermute | solution.py:362
  78.9 7.1 %collective-permute-start.19 = (bf16[16,1024]{1,0:T(8,128)(2,1)S(1)}, bf16[16,1024]{1,0:T(8,128)(2,1)S(1)}, u32[]{:S(2)}, u32[]{:S(2)}) collective-permute-start(bf16[16,1024]{1,0:T(8,128)(2,1)S(1)} %get-tuple-element.61), channel_id=1, source_target_pairs={{29,0},{28,1},{31,2},{30,3},{1,4},{0,5},{3,6},{2,7},{5,8},{4,9},{7... | collective-permute-start | bytes 98312 | tf_op jit(solution)/shard_map/ppermute | solution.py:362
  80.4 8.7 %collective-permute-start.20 = (bf16[16,1024]{1,0:T(8,128)(2,1)S(1)}, bf16[16,1024]{1,0:T(8,128)(2,1)S(1)}, u32[]{:S(2)}, u32[]{:S(2)}) collective-permute-start(bf16[16,1024]{1,0:T(8,128)(2,1)S(1)} %get-tuple-element.62), channel_id=1, source_target_pairs={{6,0},{7,1},{28,2},{29,3},{10,4},{11,5},{0,6},{1,7},{14,8},{15,9},... | collective-permute-start | bytes 98312 | tf_op jit(solution)/shard_map/ppermute | solution.py:362
  84.1 5.0 %collective-permute-start.21 = (bf16[16,1024]{1,0:T(8,128)(2,1)S(1)}, bf16[16,1024]{1,0:T(8,128)(2,1)S(1)}, u32[]{:S(2)}, u32[]{:S(2)}) collective-permute-start(bf16[16,1024]{1,0:T(8,128)(2,1)S(1)} %get-tuple-element.63), channel_id=1, source_target_pairs={{7,0},{6,1},{29,2},{28,3},{11,4},{10,5},{1,6},{0,7},{15,8},{14,9},... | collective-permute-start | bytes 98312 | tf_op jit(solution)/shard_map/ppermute | solution.py:362
  86.0 5.0 %collective-permute-start.13 = (bf16[32,1024]{1,0:T(8,128)(2,1)S(1)}, bf16[32,1024]{1,0:T(8,128)(2,1)S(1)}, u32[]{:S(2)}, u32[]{:S(2)}) collective-permute-start(bf16[32,1024]{1,0:T(8,128)(2,1)S(1)} %get-tuple-element.55), channel_id=1, source_target_pairs={{2,0},{3,1},{4,2},{5,3},{6,4},{7,5},{8,6},{9,7},{10,8},{11,9},{12,... | collective-permute-start | bytes 196616 | tf_op jit(solution)/shard_map/ppermute | solution.py:362
  89.1 7.6 %collective-permute-start.14 = (bf16[32,1024]{1,0:T(8,128)(2,1)S(1)}, bf16[32,1024]{1,0:T(8,128)(2,1)S(1)}, u32[]{:S(2)}, u32[]{:S(2)}) collective-permute-start(bf16[32,1024]{1,0:T(8,128)(2,1)S(1)} %get-tuple-element.56), channel_id=1, source_target_pairs={{30,0},{31,1},{0,2},{1,3},{2,4},{3,5},{4,6},{5,7},{6,8},{7,9},{8,1... | collective-permute-start | bytes 196616 | tf_op jit(solution)/shard_map/ppermute | solution.py:362
  89.1 7.6 %collective-permute-start.15 = (bf16[32,1024]{1,0:T(8,128)(2,1)S(1)}, bf16[32,1024]{1,0:T(8,128)(2,1)S(1)}, u32[]{:S(2)}, u32[]{:S(2)}) collective-permute-start(bf16[32,1024]{1,0:T(8,128)(2,1)S(1)} %get-tuple-element.57), channel_id=1, source_target_pairs={{3,0},{30,1},{5,2},{0,3},{7,4},{2,5},{9,6},{4,7},{11,8},{6,9},{13,... | collective-permute-start | bytes 196616 | tf_op jit(solution)/shard_map/ppermute | solution.py:362
  (10 other events, 8.8 us)
Sparse Core Ops, SparseCore 0:
  61.2 82.6 reduce-scatter.1
where the time goes:
time: 183 us; the launch traced here: 180 us
  waiting for transfers between devices  70.3 us (38%)
  starting transfers between devices  30.8 us (17%)
  blocking collectives  29.6 us (16%)
  Pallas kernels  19.7 us (11%)
  local copies, waits for them, and re-layouts  15.8 us (9%)
  between operations  14.1 us (8%)
    reduce_scatter x1, waiting for transfers between devices, body(): d_w = lax.psum_scatter(d_w, 'ctx', scatter_dimension=0, tiled=True)  46.1 us
    ppermute x22, starting transfers between devices, moved(): return lax.ppermute(x, 'ctx', pairs)  30.7 us
    psum x1, blocking collectives, body(): d_w = lax.psum(d_w, 'dp').astype(BF16)  29.6 us
    ppermute x22, waiting for transfers between devices, moved(): return lax.ppermute(x, 'ctx', pairs)  24.2 us
    pallas_call x4, Pallas kernels, call(): pl.pallas_call(kernel, name=name, out_shape=[jax.ShapeDtypeStruct(shape,...  19.7 us
    unnamed x38, local copies, waits for them, and re-layouts  15.8 us
  transfers between devices with their start and end apart: 23, of which 12 were waited for; matrix products, arithmetic and copies ran while one was open for 0% of the time, Pallas kernels for 6%

commit v1 on v0

v1 whole, which is shorter than its diff:
```python
import functools

import jax
import jax.numpy as jnp
from jax import lax
from jax.experimental import pallas as pl
from jax.experimental.pallas import tpu as pltpu
from jax.sharding import PartitionSpec as P

HEAD_DIM = 64
BLOCK = 64
HALF = 32
LEVELS = 4
ROWS = 256
WIDTH = 512
PAIRS = 4
LANES = 128
DOCS = 4
NEGATIVE = -1e30
BLOCKED = -2e30
SCALE = HEAD_DIM**-0.5
PACK = 2 * WIDTH + LANES
COUNT = (256, 128, 64, 32, 16)
AT = (0, 256, 384, 448, 480)
ALL_ROWS = 496
F32 = jnp.float32
BF16 = jnp.bfloat16

GROUPS = (
    (0, 0, 128, 256),
    (0, 128, 128, 256),
    (1, 0, 128, 256),
    (2, 0, 64, 128),
    (3, 0, 32, 96),
    (4, 0, 16, 96),
)
NEAR = (0, 1, 2, 3)
FAR = (4, 5)
P_AT = {0: 0, 1: 256, 2: 512, 3: 768, 4: 0, 5: 64}
P_NEAR, P_FAR = 896, 96


def iota(shape, dim):
    return lax.broadcasted_iota(jnp.int32, shape, dim)


def gather_table(level, value=1.0):
    shape = (COUNT[level], ROWS)
    return jnp.where(iota(shape, 1) // 2**level == iota(shape, 0), value, 0.0).astype(BF16)


def spread_table(level, value=1.0):
    shape = (ROWS, COUNT[level])
    return jnp.where(iota(shape, 0) // 2**level == iota(shape, 1), value, 0.0).astype(BF16)


def last_table(level):
    shape = (COUNT[level], ROWS)
    last = iota(shape, 0) * 2**level + (2**level - 1)
    return jnp.where(iota(shape, 1) == last, 1.0, 0.0).astype(BF16)


def query_place(index):
    level, _, rows, _ = GROUPS[index]
    size = BLOCK if level == 0 else HALF
    shape = (rows, LANES)
    return jnp.where(iota(shape, 0) // size + 8 == iota(shape, 1), 1.0, 0.0).astype(BF16)


def key_place(index):
    level, _, _, keys = GROUPS[index]
    shape = (keys, LANES)
    row, place = iota(shape, 0), iota(shape, 1) - 8
    if level == 0:
        apart = row // BLOCK - place
        blocked = (apart < 0) | (apart > 2)
        places = 2
    elif level == 1:
        there, here = row // HALF, place + 2
        block_apart = jnp.abs(there // 2 - (place + 2) // 2)
        blocked = (block_apart > 1) | (jnp.abs(there - here) < 2)
        places = 4
    else:
        blocked = row // HALF == place + 1
        places = 2
    blocked = blocked & (place >= 0) & (place < places)
    return jnp.where(blocked, BLOCKED, 0.0).astype(BF16)


def dot(a, b, a_dim=1, b_dim=0):
    return lax.dot_general(a, b, (((a_dim,), (b_dim,)), ((), ())), preferred_element_type=F32)


def split(x):
    high = x.astype(BF16)
    return high, (x - high.astype(F32)).astype(BF16)


def head_lanes(rows, width=LANES):
    return iota((rows, width), 1) % LANES < HEAD_DIM


def stacked(x):
    first = head_lanes(x.shape[0]).astype(F32).astype(BF16)
    return jnp.concatenate([x * first, x * (1 - first)], axis=0)


def unstacked(x, rows):
    return jnp.where(head_lanes(rows, x.shape[1]), x[:rows], x[rows:])


def lanes_of(pair, part=0):
    return slice(part * WIDTH + pair * LANES, part * WIDTH + (pair + 1) * LANES)


DOC_LANES = slice(2 * WIDTH, PACK)


def near_window(index, own0, own1, low, high, lanes):
    def rim(ref, level):
        return ref[BLOCK * level : BLOCK * (level + 1), lanes]

    if index == 0:
        parts = [rim(low, 0), own0[0:192, lanes]]
    elif index == 1:
        parts = [own0[64:256, lanes], rim(high, 0)]
    elif index == 2:
        parts = [rim(low, 1), own1[:, lanes], rim(high, 1)]
    else:
        parts = [rim(low, 2), rim(high, 2)]
    return jnp.concatenate(parts, axis=0)


def far_window(refs, lanes):
    return jnp.concatenate([ref[:, lanes] for ref in refs], axis=0)


def fetch(sources, targets, sems):
    copies = [
        pltpu.make_async_copy(source, target, sems.at[i])
        for i, (source, target) in enumerate(zip(sources, targets))
    ]
    for copy in copies:
        copy.start()
    return copies


def coarsen_kernel(seg, k_hbm, v_hbm, up, down, far3, far4, own0, own1, qdoc, k, v, sems):
    copies = fetch((k_hbm, v_hbm), (k, v), sems)
    marks = jnp.where(seg[...] == iota((LANES, ROWS), 0), 1.0, 0.0).T.astype(BF16)

    def key_side(x):
        doc = iota(x.shape, 1) < DOCS
        return jnp.where(doc, (1.0 - x.astype(F32)) * BLOCKED, 0.0).astype(BF16)

    for copy in copies:
        copy.wait()
    levels = [(k[...], v[...], key_side(marks))]
    qdoc[0:ROWS] = marks
    for level in range(1, LEVELS + 1):
        marks_c = dot(last_table(level), marks).astype(BF16)
        qdoc[AT[level] : AT[level] + COUNT[level]] = marks_c
        keys = dot(gather_table(level, 0.5**level), levels[0][0]).astype(BF16)
        values = dot(gather_table(level), levels[0][1]).astype(BF16)
        levels.append((keys, values, key_side(marks_c)))

    def put(ref, at, level, start, stop):
        for part, lanes in zip(
            levels[level], (slice(0, WIDTH), slice(WIDTH, 2 * WIDTH), DOC_LANES)
        ):
            ref[at : at + stop - start, lanes] = part[start:stop]

    for level in range(3):
        put(up, BLOCK * level, level, COUNT[level] - BLOCK, COUNT[level])
        put(down, BLOCK * level, level, 0, BLOCK)
    put(far3, 0, 3, 0, COUNT[3])
    put(far4, 0, 4, 0, COUNT[4])
    put(own0, 0, 0, 0, COUNT[0])
    put(own1, 0, 1, 0, COUNT[1])


def prepare_kernel(q_hbm, d_hbm, w_hbm, q_out, grad_att, w, d_out, q, sems):
    copies = fetch((q_hbm, d_hbm, w_hbm), (q, d_out, w), sems)
    copies[0].wait()
    for level in range(LEVELS + 1):
        queries = q[...] if level == 0 else dot(gather_table(level, 0.5**level), q[...]).astype(BF16)
        q_out[AT[level] : AT[level] + COUNT[level]] = (queries * SCALE).astype(BF16)
    copies[1].wait()
    copies[2].wait()
    grad_att[...] = dot(d_out[...], w[...], 1, 1)


def attend(queries, query_docs, keys, key_docs, values):
    rows = queries.shape[0]
    scores = dot(
        jnp.concatenate([stacked(queries), query_docs], axis=1),
        jnp.concatenate([keys, key_docs], axis=1),
        1,
        1,
    )
    peak = jnp.maximum(jnp.max(scores, axis=1, keepdims=True), NEGATIVE)
    peak = peak.astype(BF16).astype(F32)
    p = jnp.exp(scores - peak).astype(BF16)
    ones = jnp.ones(values.shape, BF16)
    both = unstacked(dot(p, jnp.concatenate([values, ones], axis=1)), rows)
    wide_peak = jnp.where(head_lanes(rows), peak[:rows], peak[rows:])
    return p, jnp.concatenate([both, wide_peak], axis=1)


def docs_of(index, qdoc):
    level, start, rows, _ = GROUPS[index]
    docs = qdoc[AT[level] + start : AT[level] + start + rows]
    if index in NEAR:
        docs = docs + query_place(index)
    return jnp.concatenate([docs, docs], axis=0)


def near_kernel(q_all, qdoc, own0, own1, low, high, p_out, fine, coarse):
    for index in NEAR:
        level, start, rows, keys = GROUPS[index]
        at = AT[level] + start
        query_docs = docs_of(index, qdoc)
        key_docs = near_window(index, own0, own1, low, high, DOC_LANES) + key_place(index)
        for pair in range(PAIRS):
            window = [
                near_window(index, own0, own1, low, high, lanes_of(pair, part)) for part in (0, 1)
            ]
            p, stats = attend(
                q_all[at : at + rows, lanes_of(pair)], query_docs, window[0], key_docs, window[1]
            )
            p_out[pair, P_AT[index] : P_AT[index] + 2 * rows, 0:keys] = p
            if level == 0:
                fine[pair, at : at + rows] = stats
            else:
                coarse[pair, at - ROWS : at - ROWS + rows] = stats.astype(BF16)


def merge_kernel(n3, n4, q_all, qdoc, fine, coarse, grad_att, w, *refs):
    far = (refs[:n3], refs[n3 : n3 + n4])
    layer_out, attended_out, p_out, g_out, d_side = refs[n3 + n4 :]
    docs = [(docs_of(index, qdoc), far_window(ref, DOC_LANES)) for index, ref in zip(FAR, far)]
    shape = (LANES, LANES)
    same_head = jnp.where(iota(shape, 0) // HEAD_DIM == iota(shape, 1) // HEAD_DIM, 1.0, 0.0)
    same_head = same_head.astype(BF16)
    result = jnp.zeros((ROWS, WIDTH), F32)
    spreads = [None] + [spread_table(level) for level in range(1, LEVELS + 1)]
    gathers = [None] + [gather_table(level) for level in range(1, LEVELS + 1)]
    for pair in range(PAIRS):
        cols = lanes_of(pair)
        packed = [None, coarse[pair, 0:128], coarse[pair, 128:192]]
        for index, ref, (query_docs, key_docs) in zip(FAR, far, docs):
            level, _, rows, keys = GROUPS[index]
            p, stats = attend(
                q_all[AT[level] : AT[level] + rows, cols],
                query_docs,
                far_window(ref, lanes_of(pair)),
                key_docs,
                far_window(ref, lanes_of(pair, 1)),
            )
            p_out[pair, P_AT[index] : P_AT[index] + 2 * rows, 0:keys] = p
            packed.append(stats.astype(BF16))
        wide = [fine[pair]] + [
            dot(spreads[level], packed[level]) for level in range(1, LEVELS + 1)
        ]
        levels = [[x[:, LANES * i : LANES * (i + 1)] for i in range(3)] for x in wide]
        top = functools.reduce(jnp.maximum, [x[2] for x in levels])
        weights = [jnp.exp(x[2] - top) for x in levels]
        norm = functools.reduce(
            jnp.add, [wt * x[1] * float(2**i) for i, (wt, x) in enumerate(zip(weights, levels))]
        )
        numer = functools.reduce(jnp.add, [wt * x[0] for wt, x in zip(weights, levels)])
        inverse = 1.0 / norm
        attended = (numer * inverse).astype(BF16)
        attended_out[:, cols] = attended
        result = result + dot(attended, w[cols, :])
        grad = grad_att[:, cols]
        high_part, low_part = split(grad * attended.astype(F32))
        delta = dot(high_part, same_head) + dot(low_part, same_head)
        for level in range(LEVELS + 1):
            share = weights[level] * inverse
            at, rows = AT[level], COUNT[level]
            if level == 0:
                grad_c, delta_c = share * grad, share * delta
            else:
                d_high, d_low = split(share * delta)
                terms = jnp.concatenate([(share * grad).astype(BF16), d_high, d_low], axis=1)
                summed = dot(gathers[level], terms)
                grad_c = summed[:, :LANES]
                delta_c = summed[:, LANES : 2 * LANES] + summed[:, 2 * LANES :]
            g_out[at : at + rows, cols] = grad_c.astype(BF16)
            d_high, d_low = split(delta_c * -float(2**level))
            upper = iota((rows, LANES), 1) % HEAD_DIM < HALF
            d_side[at : at + rows, cols] = jnp.where(
                upper, d_high.astype(F32), d_low.astype(F32)
            ).astype(BF16)
    layer_out[...] = result.astype(BF16)


def attend_back(p, queries, grad, side, keys, values):
    rows = queries.shape[0]
    ones = jnp.where(iota(values.shape, 1) % HALF == 0, 1.0, 0.0).astype(BF16)
    grad = stacked(grad)
    product = dot(
        jnp.concatenate([grad, stacked(side)], axis=1),
        jnp.concatenate([values, ones], axis=1),
        1,
        1,
    )
    ds = (p.astype(F32) * product).astype(BF16)
    grad_q = unstacked(dot(ds, keys), rows) * SCALE
    return grad_q, dot(ds, stacked(queries), 0, 0), dot(p, grad, 0, 0)


def far_back_kernel(n3, n4, p_in, q_all, g_in, d_side, *refs):
    far = (refs[:n3], refs[n3 : n3 + n4])
    outs = refs[n3 + n4 :]
    d_q, to_far = outs[0], (outs[1 : 1 + n3], outs[1 + n3 :])
    for pair in range(PAIRS):
        cols = lanes_of(pair)
        for index, ref, to in zip(FAR, far, to_far):
            level, _, rows, keys = GROUPS[index]
            at = AT[level]
            grad_q, grad_k, grad_v = attend_back(
                p_in[pair, P_AT[index] : P_AT[index] + 2 * rows, 0:keys],
                q_all[at : at + rows, cols],
                g_in[at : at + rows, cols],
                d_side[at : at + rows, cols],
                far_window(ref, cols),
                far_window(ref, lanes_of(pair, 1)),
            )
            d_q[at - AT[3] : at - AT[3] + rows, cols] = grad_q.astype(BF16)
            size = keys // len(to)
            for i, out in enumerate(to):
                out[:, cols] = grad_k[i * size : (i + 1) * size].astype(BF16)
                out[:, lanes_of(pair, 1)] = grad_v[i * size : (i + 1) * size].astype(BF16)


def near_back_kernel(
    p_in, q_all, g_in, d_side, own0, own1, low, high, d_far, attended, d_out,
    d_q, own_k, own_v, to_low, to_high, d_w,
):
    spread = jnp.concatenate([spread_table(level, 0.5**level) for level in (1, 2, 3, 4)], axis=1)
    for pair in range(PAIRS):
        cols = lanes_of(pair)
        grads = []
        for index in NEAR:
            level, start, rows, keys = GROUPS[index]
            at = AT[level] + start
            grads.append(
                attend_back(
                    p_in[pair, P_AT[index] : P_AT[index] + 2 * rows, 0:keys],
                    q_all[at : at + rows, cols],
                    g_in[at : at + rows, cols],
                    d_side[at : at + rows, cols],
                    near_window(index, own0, own1, low, high, cols),
                    near_window(index, own0, own1, low, high, lanes_of(pair, 1)),
                )
            )
        coarse = [x[0].astype(BF16) for x in grads[2:]] + [d_far[:, cols]]
        whole = jnp.concatenate([x[0] for x in grads[:2]], axis=0)
        d_q[:, cols] = (whole + dot(spread, jnp.concatenate(coarse, axis=0))).astype(BF16)
        for part, own, value in ((0, own_k, 0.5), (1, own_v, 1.0)):
            a, b, c, d = (x[1 + part] for x in grads)
            lanes = lanes_of(pair, part)
            middle = jnp.concatenate([a[64:128], a[128:256] + b[0:128], b[128:192]], axis=0)
            own[:, cols] = middle + dot(spread_table(1, value), c[64:192].astype(BF16))
            to_low[:, lanes] = jnp.concatenate([a[:64], c[:64], d[:64]], axis=0).astype(BF16)
            to_high[:, lanes] = jnp.concatenate([b[192:], c[192:], d[64:]], axis=0).astype(BF16)
        d_w[cols, :] = dot(attended[:, cols], d_out[...], 0, 0).astype(BF16)


def combine_kernel(n3, n4, own_k, own_v, low, high, *refs):
    from3, from4, (d_k, d_v) = refs[:n3], refs[n3 : n3 + n4], refs[n3 + n4 :]
    for part, own, out in ((0, own_k, d_k), (1, own_v, d_v)):
        lanes = slice(part * WIDTH, (part + 1) * WIDTH)
        table = jnp.concatenate(
            [spread_table(level, 1.0 if part else 0.5**level) for level in (1, 2, 3, 4)], axis=1
        )

        def rim(ref, level):
            return ref[BLOCK * level : BLOCK * (level + 1), lanes].astype(F32)

        def summed(parts):
            return functools.reduce(jnp.add, [ref[:, lanes].astype(F32) for ref in parts])

        coarse = jnp.concatenate(
            [
                rim(high, 1),
                rim(low, 1),
                rim(low, 2) + rim(high, 2),
                summed(from3),
                summed(from4),
            ],
            axis=0,
        ).astype(BF16)
        whole = own[...] + dot(table, coarse)
        out[0:64] = (whole[0:64] + rim(high, 0)).astype(BF16)
        out[64:192] = whole[64:192].astype(BF16)
        out[192:256] = (whole[192:256] + rim(low, 0)).astype(BF16)


def call(kernel, name, outs, args, scratch=(), in_hbm=0):
    vmem, hbm = pl.BlockSpec(memory_space=pltpu.VMEM), pl.BlockSpec(memory_space=pl.ANY)
    return pl.pallas_call(
        kernel,
        name=name,
        out_shape=[jax.ShapeDtypeStruct(shape, dtype) for shape, dtype in outs],
        in_specs=[vmem] * (len(args) - in_hbm) + [hbm] * in_hbm,
        out_specs=[vmem] * len(outs),
        scratch_shapes=scratch,
        compiler_params=pltpu.CompilerParams(vmem_limit_bytes=48 * 1024 * 1024),
    )(*args)


def moved(x, route, back=False):
    count = lax.axis_size("ctx")
    pairs = [(i, route(i) % count) for i in range(count)]
    if back:
        pairs = [(b, a) for a, b in pairs]
    return lax.ppermute(x, "ctx", pairs)


ROUTES_3 = (
    lambda i: i + 2,
    lambda i: i - 2,
    lambda i: i - 3 if i % 2 else i + 3,
)


def route_4(shift, swap):
    def route(i):
        pair, side = i // 2, i % 2
        pair = pair + shift if shift else pair + (-3 if pair % 2 else 3)
        return 2 * pair + (side ^ swap)

    return route


ROUTES_4 = tuple(route_4(shift, swap) for shift in (2, -2, 0) for swap in (0, 1))


def body(queries, key_rows, value_rows, segment_ids, w_out, d_out):
    q, k, v, grad_out = queries[0], key_rows[0], value_rows[0], d_out[0]
    tokens, dma = (ROWS, WIDTH), pltpu.SemaphoreType.DMA
    up, down, far3, far4, own0, own1, qdoc = call(
        coarsen_kernel,
        "coarsen",
        [((192, PACK), BF16), ((192, PACK), BF16), ((32, PACK), BF16), ((16, PACK), BF16)]
        + [((ROWS, PACK), BF16), ((128, PACK), BF16), ((ALL_ROWS, LANES), BF16)],
        [segment_ids, k, v],
        [pltpu.VMEM(tokens, BF16), pltpu.VMEM(tokens, BF16), dma((2,))],
        in_hbm=2,
    )
    low = moved(up, lambda i: i + 1)
    high = moved(down, lambda i: i - 1)
    got = [moved(far3, route) for route in ROUTES_3] + [moved(far4, route) for route in ROUTES_4]
    n3, n4 = len(ROUTES_3), len(ROUTES_4)
    q_all, grad_att, w, grad_rows = call(
        prepare_kernel,
        "prepare",
        [((ALL_ROWS, WIDTH), BF16), (tokens, F32), ((WIDTH, WIDTH), BF16), (tokens, BF16)],
        [q, grad_out, w_out],
        [pltpu.VMEM(tokens, BF16), dma((3,))],
        in_hbm=3,
    )
    near = (own0, own1, low, high)
    p_near, fine, coarse = call(
        near_kernel,
        "near",
        [
            ((PAIRS, P_NEAR, 256), BF16),
            ((PAIRS, ROWS, 3 * LANES), F32),
            ((PAIRS, 192, 3 * LANES), BF16),
        ],
        [q_all, qdoc, *near],
    )
    layer_out, attended, p_far, g, d_side = call(
        functools.partial(merge_kernel, n3, n4),
        "merge",
        [(tokens, BF16), (tokens, BF16), ((PAIRS, P_FAR, LANES), BF16)]
        + [((ALL_ROWS, WIDTH), BF16)] * 2,
        [q_all, qdoc, fine, coarse, grad_att, w, *got],
    )
    d_far, *to_far = call(
        functools.partial(far_back_kernel, n3, n4),
        "far_back",
        [((48, WIDTH), BF16)]
        + [((32, 2 * WIDTH), BF16)] * n3
        + [((16, 2 * WIDTH), BF16)] * n4,
        [p_far, q_all, g, d_side, *got],
    )
    back = [moved(x, route, back=True) for x, route in zip(to_far, ROUTES_3 + ROUTES_4)]
    d_q, own_k, own_v, to_low, to_high, d_w = call(
        near_back_kernel,
        "near_back",
        [(tokens, BF16), (tokens, F32), (tokens, F32)]
        + [((192, 2 * WIDTH), BF16)] * 2
        + [((WIDTH, WIDTH), BF16)],
        [p_near, q_all, g, d_side, *near, d_far, attended, grad_rows],
    )
    low_back = moved(to_low, lambda i: i - 1)
    high_back = moved(to_high, lambda i: i + 1)
    count, dp_count = lax.axis_size("ctx"), lax.axis_size("dp")
    parts = d_w.reshape(count, WIDTH // count, WIDTH)
    parts = lax.all_to_all(parts, "ctx", 0, 0, tiled=True)
    mine = jnp.sum(parts.astype(F32), axis=0)
    copies = jnp.broadcast_to(mine[None], (dp_count,) + mine.shape)
    d_w = jnp.sum(lax.all_to_all(copies, "dp", 0, 0, tiled=True), axis=0).astype(BF16)
    d_k, d_v = call(
        functools.partial(combine_kernel, n3, n4),
        "combine",
        [(tokens, BF16)] * 2,
        [own_k, own_v, low_back, high_back, *back],
    )
    return layer_out[None], d_q[None], d_k[None], d_v[None], d_w


def solution(mesh):
    tokens = P("dp", "ctx", None)
    return jax.shard_map(
        body,
        mesh=mesh,
        in_specs=(tokens, tokens, tokens, P("dp", "ctx"), P(), tokens),
        out_specs=(tokens, tokens, tokens, tokens, P("ctx", None)),
        check_vma=False,
    )
```

time: 183 us -> 104 us (0.57)
  the two profiles are of different devices: /device:TPU:32 before, /device:TPU:1 now
where the time goes in v1:
time: 104 us
  starting transfers between devices  46.1 us (44%)
  blocking collectives  21.1 us (20%)
  Pallas kernels  19.3 us (19%)
  waiting for transfers between devices  9.77 us (9%)
  local copies, waits for them, and re-layouts  6.24 us (6%)
    ppermute x22, starting transfers between devices, moved(): return lax.ppermute(x, 'ctx', pairs)  38.5 us
    all_to_all x1, blocking collectives, body(): parts = lax.all_to_all(parts, 'ctx', 0, 0, tiled=True)  21.1 us
    pallas_call x7, Pallas kernels, call(): pl.pallas_call(kernel, name=name, out_shape=[jax.ShapeDtypeStruct(shape,...  19.3 us
    ppermute x22, waiting for transfers between devices, moved(): return lax.ppermute(x, 'ctx', pairs)  9.77 us
    all_to_all x1, starting transfers between devices, body(): lax.all_to_all(copies, 'dp', 0, 0, tiled=True)  7.66 us
    unnamed x12, local copies, waits for them, and re-layouts  5.51 us
  transfers between devices with their start and end apart: 23, of which 6 were waited for; matrix products, arithmetic and copies ran while one was open for 0% of the time, Pallas kernels for 4%

profile of v1, /device:TPU:1, one launch (start us, length us, event | category | flops | bytes accessed | tf_op | source)
XLA Modules:
  0.0 103.9 jit_solution(15519362111031169384)
XLA Ops:
  0.6 0.9 copy-done.1
  1.6 0.9 copy-done.2
  3.9 2.8 %collective-permute-start = (bf16[192,1152]{1,0:T(8,128)(2,1)S(1)}, bf16[192,1152]{1,0:T(8,128)(2,1)S(1)}, u32[]{:S(2)}, u32[]{:S(2)}) collective-permute-start(bf16[192,1152]{1,0:T(8,128)(2,1)S(1)} %get-tuple-element.46), channel_id=1, source_target_pairs={{0,1},{1,2},{2,3},{3,4},{4,5},{5,6},{6,7},{7,8},{8,9},{9,10},{10,1... | collective-permute-start | bytes 1327112 | tf_op jit(solution)/shard_map/ppermute | solution.py:420
  7.3 2.5 %collective-permute-start.10 = (bf16[16,1152]{1,0:T(8,128)(2,1)S(1)}, bf16[16,1152]{1,0:T(8,128)(2,1)S(1)}, u32[]{:S(2)}, u32[]{:S(2)}) collective-permute-start(bf16[16,1152]{1,0:T(8,128)(2,1)S(1)} %get-tuple-element.53), channel_id=1, source_target_pairs={{0,7},{1,6},{2,29},{3,28},{4,11},{5,10},{6,1},{7,0},{8,15},{9,14},... | collective-permute-start | bytes 110600 | tf_op jit(solution)/shard_map/ppermute | solution.py:420
  9.9 5.0 %collective-permute-start.9 = (bf16[16,1152]{1,0:T(8,128)(2,1)S(1)}, bf16[16,1152]{1,0:T(8,128)(2,1)S(1)}, u32[]{:S(2)}, u32[]{:S(2)}) collective-permute-start(bf16[16,1152]{1,0:T(8,128)(2,1)S(1)} %get-tuple-element.53), channel_id=1, source_target_pairs={{0,6},{1,7},{2,28},{3,29},{4,10},{5,11},{6,0},{7,1},{8,14},{9,15},... | collective-permute-start | bytes 110600 | tf_op jit(solution)/shard_map/ppermute | solution.py:420
  15.6 1.9 %collective-permute-start.7 = (bf16[16,1152]{1,0:T(8,128)(2,1)S(1)}, bf16[16,1152]{1,0:T(8,128)(2,1)S(1)}, u32[]{:S(2)}, u32[]{:S(2)}) collective-permute-start(bf16[16,1152]{1,0:T(8,128)(2,1)S(1)} %get-tuple-element.53), channel_id=1, source_target_pairs={{0,28},{1,29},{2,30},{3,31},{4,0},{5,1},{6,2},{7,3},{8,4},{9,5},{1... | collective-permute-start | bytes 110600 | tf_op jit(solution)/shard_map/ppermute | solution.py:420
  17.5 1.7 %collective-permute-done.9.refs_7_ = bf16[16,1152]{1,0:T(8,128)(2,1)S(1)} collective-permute-done((bf16[16,1152]{1,0:T(8,128)(2,1)S(1)}, bf16[16,1152]{1,0:T(8,128)(2,1)S(1)}, u32[]{:S(2)}, u32[]{:S(2)}) %collective-permute-start.9) | collective-permute-done | bytes 36896 | tf_op jit(solution)/shard_map/ppermute | solution.py:420
  20.0 2.5 %collective-permute-start.3 = (bf16[32,1152]{1,0:T(8,128)(2,1)S(1)}, bf16[32,1152]{1,0:T(8,128)(2,1)S(1)}, u32[]{:S(2)}, u32[]{:S(2)}) collective-permute-start(bf16[32,1152]{1,0:T(8,128)(2,1)S(1)} %get-tuple-element.52), channel_id=1, source_target_pairs={{0,30},{1,31},{2,0},{3,1},{4,2},{5,3},{6,4},{7,5},{8,6},{9,7},{10,... | collective-permute-start | bytes 221192 | tf_op jit(solution)/shard_map/ppermute | solution.py:420
  22.5 2.2 %collective-permute-start.6 = (bf16[16,1152]{1,0:T(8,128)(2,1)S(1)}, bf16[16,1152]{1,0:T(8,128)(2,1)S(1)}, u32[]{:S(2)}, u32[]{:S(2)}) collective-permute-start(bf16[16,1152]{1,0:T(8,128)(2,1)S(1)} %get-tuple-element.53), channel_id=1, source_target_pairs={{0,5},{1,4},{2,7},{3,6},{4,9},{5,8},{6,11},{7,10},{8,13},{9,12},{1... | collective-permute-start | bytes 110600 | tf_op jit(solution)/shard_map/ppermute | solution.py:420
  24.7 1.2 %collective-permute-start.5 = (bf16[16,1152]{1,0:T(8,128)(2,1)S(1)}, bf16[16,1152]{1,0:T(8,128)(2,1)S(1)}, u32[]{:S(2)}, u32[]{:S(2)}) collective-permute-start(bf16[16,1152]{1,0:T(8,128)(2,1)S(1)} %get-tuple-element.53), channel_id=1, source_target_pairs={{0,4},{1,5},{2,6},{3,7},{4,8},{5,9},{6,10},{7,11},{8,12},{9,13},{1... | collective-permute-start | bytes 110600 | tf_op jit(solution)/shard_map/ppermute | solution.py:420
  25.9 1.0 %copy-done = bf16[512,512]{1,0:T(8,128)(2,1)S(1)} copy-done((bf16[512,512]{1,0:T(8,128)(2,1)S(1)}, bf16[512,512]{1,0:T(8,128)(2,1)}, u32[]{:S(2)}) %copy-start) | copy-done | bytes 524312
  26.9 0.9 copy-done.3
  27.9 0.9 copy-done.4
  29.5 2.8 %near.1 = (bf16[4,896,256]{2,1,0:T(8,128)(2,1)}, f32[4,256,384]{2,1,0:T(8,128)S(1)}, bf16[4,192,384]{2,1,0:T(8,128)(2,1)S(1)}) custom-call(bf16[496,512]{1,0:T(8,128)(2,1)S(1)} %get-tuple-element.42.q_all, bf16[496,128]{1,0:T(8,128)(2,1)S(1)} %get-tuple-element.43.qdoc, bf16[256,1152]{1,0:T(8,128)(2,1)S(1)} %get-tuple-element.44.own0, ...), custom_call_target="tpu_custom_call" | custom-call | tf_op jit(solution)/shard_map/near/pallas_call | solution.py:404
  32.4 5.5 %merge.1 = (bf16[256,512]{1,0:T(8,128)(2,1)}, bf16[256,512]{1,0:T(8,128)(2,1)S(1)}, bf16[4,96,128]{2,1,0:T(8,128)(2,1)S(1)}, bf16[496,512]{1,0:T(8,128)(2,1)S(1)}, bf16[496,512]{1,0:T(8,128)(2,1)S(1)}) custom-call(bf16[496,512]{1,0:T(8,128)(2,1)S(1)} %get-tuple-element.42.q_all, bf16[496,128]{1,0:T(8,128)(2,1)S(1)} %get-tuple-element.43.qdoc, ...), custom_call_target="tpu_custom_call" | custom-call | tf_op jit(solution)/shard_map/merge/pallas_call | solution.py:404
  37.9 1.1 %far_back.1 = (bf16[48,512]{1,0:T(8,128)(2,1)S(1)}, bf16[32,1024]{1,0:T(8,128)(2,1)S(1)}, bf16[32,1024]{1,0:T(8,128)(2,1)S(1)}, bf16[32,1024]{1,0:T(8,128)(2,1)S...) custom-call(bf16[4,96,128]{2,1,0:T(8,128)(2,1)S(1)} %get-tuple-eleme, ...), custom_call_target="tpu_custom_call" | custom-call | tf_op jit(solution)/shard_map/far_back/pallas_call | solution.py:404
  39.0 7.3 %near_back.1 = (bf16[256,512]{1,0:T(8,128)(2,1)}, f32[256,512]{1,0:T(8,128)S(1)}, f32[256,512]{1,0:T(8,128)S(1)}, bf16[192,1024]{1,0:T(8,128)(2,1)S(1)}, bf16[19...) custom-call(bf16[4,896,256]{2,1,0:T(8,128)(2,1)} %get-tuple-element.55.p_in, ...), custom_call_target="tpu_custom_call" | custom-call | tf_op jit(solution)/shard_map/near_back/pallas_call | solution.py:404
  46.3 21.1 %all_to_all.10 = bf16[32,16,512]{2,1,0:T(8,128)(2,1)S(1)} all-to-all(bf16[32,16,512]{2,1,0:T(8,128)(2,1)S(1)} %bitcast.9), channel_id=1, replica_groups=mesh['dp'=8,'ctx'=32] {'ctx'}, dimensions={0} | all-to-all | bytes 1048576 | tf_op jit(solution)/shard_map/all_to_all | solution.py:505
  68.2 7.7 %all-to-all-start.1 = ((f32[8,16,512]{2,1,0:T(8,128)}), f32[8,16,512]{2,1,0:T(8,128)S(1)}, u32[]{:S(2)}, u32[]{:S(2)}) async-start(f32[8,16,512]{2,1,0:T(8,128)} %broadcast_in_dim.22), calls=%async_computation.1 | async-start | bytes 524288 | tf_op jit(solution)/shard_map/all_to_all | solution.py:508
  76.0 1.7 %collective-permute-start.12 = (bf16[192,1024]{1,0:T(8,128)(2,1)S(1)}, bf16[192,1024]{1,0:T(8,128)(2,1)S(1)}, u32[]{:S(2)}, u32[]{:S(2)}) collective-permute-start(bf16[192,1024]{1,0:T(8,128)(2,1)S(1)} %get-tuple-element.66), channel_id=1, source_target_pairs={{0,1},{1,2},{2,3},{3,4},{4,5},{5,6},{6,7},{7,8},{8,9},{9,10},{10,1... | collective-permute-start | bytes 1179656 | tf_op jit(solution)/shard_map/ppermute | solution.py:420
  77.6 1.5 %collective-permute-start.16 = (bf16[16,1024]{1,0:T(8,128)(2,1)S(1)}, bf16[16,1024]{1,0:T(8,128)(2,1)S(1)}, u32[]{:S(2)}, u32[]{:S(2)}) collective-permute-start(bf16[16,1024]{1,0:T(8,128)(2,1)S(1)} %get-tuple-element.70), channel_id=1, source_target_pairs={{4,0},{5,1},{6,2},{7,3},{8,4},{9,5},{10,6},{11,7},{12,8},{13,9},{1... | collective-permute-start | bytes 98312 | tf_op jit(solution)/shard_map/ppermute | solution.py:420
  79.2 1.5 %collective-permute-start.17 = (bf16[16,1024]{1,0:T(8,128)(2,1)S(1)}, bf16[16,1024]{1,0:T(8,128)(2,1)S(1)}, u32[]{:S(2)}, u32[]{:S(2)}) collective-permute-start(bf16[16,1024]{1,0:T(8,128)(2,1)S(1)} %get-tuple-element.71), channel_id=1, source_target_pairs={{5,0},{4,1},{7,2},{6,3},{9,4},{8,5},{11,6},{10,7},{13,8},{12,9},{1... | collective-permute-start | bytes 98312 | tf_op jit(solution)/shard_map/ppermute | solution.py:420
  80.6 1.4 %collective-permute-start.18 = (bf16[16,1024]{1,0:T(8,128)(2,1)S(1)}, bf16[16,1024]{1,0:T(8,128)(2,1)S(1)}, u32[]{:S(2)}, u32[]{:S(2)}) collective-permute-start(bf16[16,1024]{1,0:T(8,128)(2,1)S(1)} %get-tuple-element.72), channel_id=1, source_target_pairs={{28,0},{29,1},{30,2},{31,3},{0,4},{1,5},{2,6},{3,7},{4,8},{5,9},{6... | collective-permute-start | bytes 98312 | tf_op jit(solution)/shard_map/ppermute | solution.py:420
  82.1 3.4 %collective-permute-done.16.refs_3_ = bf16[16,1024]{1,0:T(8,128)(2,1)S(1)} collective-permute-done((bf16[16,1024]{1,0:T(8,128)(2,1)S(1)}, bf16[16,1024]{1,0:T(8,128)(2,1)S(1)}, u32[]{:S(2)}, u32[]{:S(2)}) %collective-permute-start.16) | collective-permute-done | bytes 32800 | tf_op jit(solution)/shard_map/ppermute | solution.py:420
  85.5 2.7 %collective-permute-start.19 = (bf16[16,1024]{1,0:T(8,128)(2,1)S(1)}, bf16[16,1024]{1,0:T(8,128)(2,1)S(1)}, u32[]{:S(2)}, u32[]{:S(2)}) collective-permute-start(bf16[16,1024]{1,0:T(8,128)(2,1)S(1)} %get-tuple-element.73), channel_id=1, source_target_pairs={{29,0},{28,1},{31,2},{30,3},{1,4},{0,5},{3,6},{2,7},{5,8},{4,9},{7... | collective-permute-start | bytes 98312 | tf_op jit(solution)/shard_map/ppermute | solution.py:420
  88.2 3.1 %collective-permute-start.21 = (bf16[16,1024]{1,0:T(8,128)(2,1)S(1)}, bf16[16,1024]{1,0:T(8,128)(2,1)S(1)}, u32[]{:S(2)}, u32[]{:S(2)}) collective-permute-start(bf16[16,1024]{1,0:T(8,128)(2,1)S(1)} %get-tuple-element.75), channel_id=1, source_target_pairs={{7,0},{6,1},{29,2},{28,3},{11,4},{10,5},{1,6},{0,7},{15,8},{14,9},... | collective-permute-start | bytes 98312 | tf_op jit(solution)/shard_map/ppermute | solution.py:420
  91.3 1.2 %collective-permute-done.19.refs_6_ = bf16[16,1024]{1,0:T(8,128)(2,1)S(1)} collective-permute-done((bf16[16,1024]{1,0:T(8,128)(2,1)S(1)}, bf16[16,1024]{1,0:T(8,128)(2,1)S(1)}, u32[]{:S(2)}, u32[]{:S(2)}) %collective-permute-start.19) | collective-permute-done | bytes 32800 | tf_op jit(solution)/shard_map/ppermute | solution.py:420
  92.5 1.5 %collective-permute-start.13 = (bf16[32,1024]{1,0:T(8,128)(2,1)S(1)}, bf16[32,1024]{1,0:T(8,128)(2,1)S(1)}, u32[]{:S(2)}, u32[]{:S(2)}) collective-permute-start(bf16[32,1024]{1,0:T(8,128)(2,1)S(1)} %get-tuple-element.67), channel_id=1, source_target_pairs={{2,0},{3,1},{4,2},{5,3},{6,4},{7,5},{8,6},{9,7},{10,8},{11,9},{12,... | collective-permute-start | bytes 196616 | tf_op jit(solution)/shard_map/ppermute | solution.py:420
  94.0 5.5 %collective-permute-start.15 = (bf16[32,1024]{1,0:T(8,128)(2,1)S(1)}, bf16[32,1024]{1,0:T(8,128)(2,1)S(1)}, u32[]{:S(2)}, u32[]{:S(2)}) collective-permute-start(bf16[32,1024]{1,0:T(8,128)(2,1)S(1)} %get-tuple-element.69), channel_id=1, source_target_pairs={{3,0},{30,1},{5,2},{0,3},{7,4},{2,5},{9,6},{4,7},{11,8},{6,9},{13,... | collective-permute-start | bytes 196616 | tf_op jit(solution)/shard_map/ppermute | solution.py:420
  99.5 0.9 collective-permute-done.14.refs_1_
  100.5 1.7 %collective-permute-done.15.refs_2_ = bf16[32,1024]{1,0:T(8,128)(2,1)S(1)} collective-permute-done((bf16[32,1024]{1,0:T(8,128)(2,1)S(1)}, bf16[32,1024]{1,0:T(8,128)(2,1)S(1)}, u32[]{:S(2)}, u32[]{:S(2)}) %collective-permute-start.15) | collective-permute-done | bytes 65568 | tf_op jit(solution)/shard_map/ppermute | solution.py:420
  102.2 1.1 %combine.1 = (bf16[256,512]{1,0:T(8,128)(2,1)}, bf16[256,512]{1,0:T(8,128)(2,1)}) custom-call(f32[256,512]{1,0:T(8,128)S(1)} %get-tuple-element.63.own_k, f32[256,512]{1,0:T(8,128)S(1)} %get-tuple-element.64.own_v, bf16[192,1024]{1,0:T(8,128)(2,1)S(1)} %collective-permute-done.11.low, bf16[192,1024]{1,0:T(8,128)(2,1)S(1)} %collective-permute-done.12.high, ...), custom_call_target="tpu_custom_call" | custom-call | tf_op jit(solution)/shard_map/combine/pallas_call | solution.py:404
  (37 shorter events, 5.9 us)
Async XLA Ops:
  0.6 1.0 copy-start.1
  1.6 0.9 copy-start.2
  2.5 0.7 copy-start.5
  3.9 18.6 %collective-permute-start = (bf16[192,1152]{1,0:T(8,128)(2,1)S(1)}, bf16[192,1152]{1,0:T(8,128)(2,1)S(1)}, u32[]{:S(2)}, u32[]{:S(2)}) collective-permute-start(bf16[192,1152]{1,0:T(8,128)(2,1)S(1)} %get-tuple-element.46), channel_id=1, source_target_pairs={{0,1},{1,2},{2,3},{3,4},{4,5},{5,6},{6,7},{7,8},{8,9},{9,10},{10,1... | collective-permute-start | bytes 1327112 | tf_op jit(solution)/shard_map/ppermute | solution.py:420
  6.7 18.0 %collective-permute-start.1 = (bf16[192,1152]{1,0:T(8,128)(2,1)S(1)}, bf16[192,1152]{1,0:T(8,128)(2,1)S(1)}, u32[]{:S(2)}, u32[]{:S(2)}) collective-permute-start(bf16[192,1152]{1,0:T(8,128)(2,1)S(1)} %get-tuple-element.47), channel_id=1, source_target_pairs={{0,31},{1,0},{2,1},{3,2},{4,3},{5,4},{6,5},{7,6},{8,7},{9,8},{10,9... | collective-permute-start | bytes 1327112 | tf_op jit(solution)/shard_map/ppermute | solution.py:420
  7.3 8.3 %collective-permute-start.10 = (bf16[16,1152]{1,0:T(8,128)(2,1)S(1)}, bf16[16,1152]{1,0:T(8,128)(2,1)S(1)}, u32[]{:S(2)}, u32[]{:S(2)}) collective-permute-start(bf16[16,1152]{1,0:T(8,128)(2,1)S(1)} %get-tuple-element.53), channel_id=1, source_target_pairs={{0,7},{1,6},{2,29},{3,28},{4,11},{5,10},{6,1},{7,0},{8,15},{9,14},... | collective-permute-start | bytes 110600 | tf_op jit(solution)/shard_map/ppermute | solution.py:420
  9.9 9.3 %collective-permute-start.9 = (bf16[16,1152]{1,0:T(8,128)(2,1)S(1)}, bf16[16,1152]{1,0:T(8,128)(2,1)S(1)}, u32[]{:S(2)}, u32[]{:S(2)}) collective-permute-start(bf16[16,1152]{1,0:T(8,128)(2,1)S(1)} %get-tuple-element.53), channel_id=1, source_target_pairs={{0,6},{1,7},{2,28},{3,29},{4,10},{5,11},{6,0},{7,1},{8,14},{9,15},... | collective-permute-start | bytes 110600 | tf_op jit(solution)/shard_map/ppermute | solution.py:420
  14.9 5.1 %collective-permute-start.8 = (bf16[16,1152]{1,0:T(8,128)(2,1)S(1)}, bf16[16,1152]{1,0:T(8,128)(2,1)S(1)}, u32[]{:S(2)}, u32[]{:S(2)}) collective-permute-start(bf16[16,1152]{1,0:T(8,128)(2,1)S(1)} %get-tuple-element.53), channel_id=1, source_target_pairs={{0,29},{1,28},{2,31},{3,30},{4,1},{5,0},{6,3},{7,2},{8,5},{9,4},{1... | collective-permute-start | bytes 110600 | tf_op jit(solution)/shard_map/ppermute | solution.py:420
  15.6 6.9 %collective-permute-start.7 = (bf16[16,1152]{1,0:T(8,128)(2,1)S(1)}, bf16[16,1152]{1,0:T(8,128)(2,1)S(1)}, u32[]{:S(2)}, u32[]{:S(2)}) collective-permute-start(bf16[16,1152]{1,0:T(8,128)(2,1)S(1)} %get-tuple-element.53), channel_id=1, source_target_pairs={{0,28},{1,29},{2,30},{3,31},{4,0},{5,1},{6,2},{7,3},{8,4},{9,5},{1... | collective-permute-start | bytes 110600 | tf_op jit(solution)/shard_map/ppermute | solution.py:420
  19.2 13.2 %collective-permute-start.4 = (bf16[32,1152]{1,0:T(8,128)(2,1)S(1)}, bf16[32,1152]{1,0:T(8,128)(2,1)S(1)}, u32[]{:S(2)}, u32[]{:S(2)}) collective-permute-start(bf16[32,1152]{1,0:T(8,128)(2,1)S(1)} %get-tuple-element.52), channel_id=1, source_target_pairs={{0,3},{1,30},{2,5},{3,0},{4,7},{5,2},{6,9},{7,4},{8,11},{9,6},{10,... | collective-permute-start | bytes 221192 | tf_op jit(solution)/shard_map/ppermute | solution.py:420
  20.0 12.4 %collective-permute-start.3 = (bf16[32,1152]{1,0:T(8,128)(2,1)S(1)}, bf16[32,1152]{1,0:T(8,128)(2,1)S(1)}, u32[]{:S(2)}, u32[]{:S(2)}) collective-permute-start(bf16[32,1152]{1,0:T(8,128)(2,1)S(1)} %get-tuple-element.52), channel_id=1, source_target_pairs={{0,30},{1,31},{2,0},{3,1},{4,2},{5,3},{6,4},{7,5},{8,6},{9,7},{10,... | collective-permute-start | bytes 221192 | tf_op jit(solution)/shard_map/ppermute | solution.py:420
  22.5 9.9 %collective-permute-start.2 = (bf16[32,1152]{1,0:T(8,128)(2,1)S(1)}, bf16[32,1152]{1,0:T(8,128)(2,1)S(1)}, u32[]{:S(2)}, u32[]{:S(2)}) collective-permute-start(bf16[32,1152]{1,0:T(8,128)(2,1)S(1)} %get-tuple-element.52), channel_id=1, source_target_pairs={{0,2},{1,3},{2,4},{3,5},{4,6},{5,7},{6,8},{7,9},{8,10},{9,11},{10,... | collective-permute-start | bytes 221192 | tf_op jit(solution)/shard_map/ppermute | solution.py:420
  22.5 9.9 %collective-permute-start.6 = (bf16[16,1152]{1,0:T(8,128)(2,1)S(1)}, bf16[16,1152]{1,0:T(8,128)(2,1)S(1)}, u32[]{:S(2)}, u32[]{:S(2)}) collective-permute-start(bf16[16,1152]{1,0:T(8,128)(2,1)S(1)} %get-tuple-element.53), channel_id=1, source_target_pairs={{0,5},{1,4},{2,7},{3,6},{4,9},{5,8},{6,11},{7,10},{8,13},{9,12},{1... | collective-permute-start | bytes 110600 | tf_op jit(solution)/shard_map/ppermute | solution.py:420
  24.7 7.7 %collective-permute-start.5 = (bf16[16,1152]{1,0:T(8,128)(2,1)S(1)}, bf16[16,1152]{1,0:T(8,128)(2,1)S(1)}, u32[]{:S(2)}, u32[]{:S(2)}) collective-permute-start(bf16[16,1152]{1,0:T(8,128)(2,1)S(1)} %get-tuple-element.53), channel_id=1, source_target_pairs={{0,4},{1,5},{2,6},{3,7},{4,8},{5,9},{6,10},{7,11},{8,12},{9,13},{1... | collective-permute-start | bytes 110600 | tf_op jit(solution)/shard_map/ppermute | solution.py:420
  25.9 1.0 %copy-start = (bf16[512,512]{1,0:T(8,128)(2,1)S(1)}, bf16[512,512]{1,0:T(8,128)(2,1)}, u32[]{:S(2)}) copy-start(bf16[512,512]{1,0:T(8,128)(2,1)} %w_hbm.1) | copy-start | bytes 1572868
  26.9 0.9 copy-start.3
  27.9 0.9 copy-start.4
  68.2 35.1 %all-to-all-start.1 = ((f32[8,16,512]{2,1,0:T(8,128)}), f32[8,16,512]{2,1,0:T(8,128)S(1)}, u32[]{:S(2)}, u32[]{:S(2)}) async-start(f32[8,16,512]{2,1,0:T(8,128)} %broadcast_in_dim.22), calls=%async_computation.1 | async-start | bytes 524288 | tf_op jit(solution)/shard_map/all_to_all | solution.py:508
  75.9 26.3 %collective-permute-start.11 = (bf16[192,1024]{1,0:T(8,128)(2,1)S(1)}, bf16[192,1024]{1,0:T(8,128)(2,1)S(1)}, u32[]{:S(2)}, u32[]{:S(2)}) collective-permute-start(bf16[192,1024]{1,0:T(8,128)(2,1)S(1)} %get-tuple-element.65), channel_id=1, source_target_pairs={{0,31},{1,0},{2,1},{3,2},{4,3},{5,4},{6,5},{7,6},{8,7},{9,8},{10,9... | collective-permute-start | bytes 1179656 | tf_op jit(solution)/shard_map/ppermute | solution.py:420
  76.0 26.2 %collective-permute-start.12 = (bf16[192,1024]{1,0:T(8,128)(2,1)S(1)}, bf16[192,1024]{1,0:T(8,128)(2,1)S(1)}, u32[]{:S(2)}, u32[]{:S(2)}) collective-permute-start(bf16[192,1024]{1,0:T(8,128)(2,1)S(1)} %get-tuple-element.66), channel_id=1, source_target_pairs={{0,1},{1,2},{2,3},{3,4},{4,5},{5,6},{6,7},{7,8},{8,9},{9,10},{10,1... | collective-permute-start | bytes 1179656 | tf_op jit(solution)/shard_map/ppermute | solution.py:420
  77.6 7.9 %collective-permute-start.16 = (bf16[16,1024]{1,0:T(8,128)(2,1)S(1)}, bf16[16,1024]{1,0:T(8,128)(2,1)S(1)}, u32[]{:S(2)}, u32[]{:S(2)}) collective-permute-start(bf16[16,1024]{1,0:T(8,128)(2,1)S(1)} %get-tuple-element.70), channel_id=1, source_target_pairs={{4,0},{5,1},{6,2},{7,3},{8,4},{9,5},{10,6},{11,7},{12,8},{13,9},{1... | collective-permute-start | bytes 98312 | tf_op jit(solution)/shard_map/ppermute | solution.py:420
  79.2 9.0 %collective-permute-start.17 = (bf16[16,1024]{1,0:T(8,128)(2,1)S(1)}, bf16[16,1024]{1,0:T(8,128)(2,1)S(1)}, u32[]{:S(2)}, u32[]{:S(2)}) collective-permute-start(bf16[16,1024]{1,0:T(8,128)(2,1)S(1)} %get-tuple-element.71), channel_id=1, source_target_pairs={{5,0},{4,1},{7,2},{6,3},{9,4},{8,5},{11,6},{10,7},{13,8},{12,9},{1... | collective-permute-start | bytes 98312 | tf_op jit(solution)/shard_map/ppermute | solution.py:420
  80.6 7.6 %collective-permute-start.18 = (bf16[16,1024]{1,0:T(8,128)(2,1)S(1)}, bf16[16,1024]{1,0:T(8,128)(2,1)S(1)}, u32[]{:S(2)}, u32[]{:S(2)}) collective-permute-start(bf16[16,1024]{1,0:T(8,128)(2,1)S(1)} %get-tuple-element.72), channel_id=1, source_target_pairs={{28,0},{29,1},{30,2},{31,3},{0,4},{1,5},{2,6},{3,7},{4,8},{5,9},{6... | collective-permute-start | bytes 98312 | tf_op jit(solution)/shard_map/ppermute | solution.py:420
  85.5 7.0 %collective-permute-start.19 = (bf16[16,1024]{1,0:T(8,128)(2,1)S(1)}, bf16[16,1024]{1,0:T(8,128)(2,1)S(1)}, u32[]{:S(2)}, u32[]{:S(2)}) collective-permute-start(bf16[16,1024]{1,0:T(8,128)(2,1)S(1)} %get-tuple-element.73), channel_id=1, source_target_pairs={{29,0},{28,1},{31,2},{30,3},{1,4},{0,5},{3,6},{2,7},{5,8},{4,9},{7... | collective-permute-start | bytes 98312 | tf_op jit(solution)/shard_map/ppermute | solution.py:420
  88.2 5.8 %collective-permute-start.20 = (bf16[16,1024]{1,0:T(8,128)(2,1)S(1)}, bf16[16,1024]{1,0:T(8,128)(2,1)S(1)}, u32[]{:S(2)}, u32[]{:S(2)}) collective-permute-start(bf16[16,1024]{1,0:T(8,128)(2,1)S(1)} %get-tuple-element.74), channel_id=1, source_target_pairs={{6,0},{7,1},{28,2},{29,3},{10,4},{11,5},{0,6},{1,7},{14,8},{15,9},... | collective-permute-start | bytes 98312 | tf_op jit(solution)/shard_map/ppermute | solution.py:420
  88.2 5.8 %collective-permute-start.21 = (bf16[16,1024]{1,0:T(8,128)(2,1)S(1)}, bf16[16,1024]{1,0:T(8,128)(2,1)S(1)}, u32[]{:S(2)}, u32[]{:S(2)}) collective-permute-start(bf16[16,1024]{1,0:T(8,128)(2,1)S(1)} %get-tuple-element.75), channel_id=1, source_target_pairs={{7,0},{6,1},{29,2},{28,3},{11,4},{10,5},{1,6},{0,7},{15,8},{14,9},... | collective-permute-start | bytes 98312 | tf_op jit(solution)/shard_map/ppermute | solution.py:420
  92.5 7.0 %collective-permute-start.13 = (bf16[32,1024]{1,0:T(8,128)(2,1)S(1)}, bf16[32,1024]{1,0:T(8,128)(2,1)S(1)}, u32[]{:S(2)}, u32[]{:S(2)}) collective-permute-start(bf16[32,1024]{1,0:T(8,128)(2,1)S(1)} %get-tuple-element.67), channel_id=1, source_target_pairs={{2,0},{3,1},{4,2},{5,3},{6,4},{7,5},{8,6},{9,7},{10,8},{11,9},{12,... | collective-permute-start | bytes 196616 | tf_op jit(solution)/shard_map/ppermute | solution.py:420
  94.0 6.4 %collective-permute-start.14 = (bf16[32,1024]{1,0:T(8,128)(2,1)S(1)}, bf16[32,1024]{1,0:T(8,128)(2,1)S(1)}, u32[]{:S(2)}, u32[]{:S(2)}) collective-permute-start(bf16[32,1024]{1,0:T(8,128)(2,1)S(1)} %get-tuple-element.68), channel_id=1, source_target_pairs={{30,0},{31,1},{0,2},{1,3},{2,4},{3,5},{4,6},{5,7},{6,8},{7,9},{8,1... | collective-permute-start | bytes 196616 | tf_op jit(solution)/shard_map/ppermute | solution.py:420
  94.0 8.1 %collective-permute-start.15 = (bf16[32,1024]{1,0:T(8,128)(2,1)S(1)}, bf16[32,1024]{1,0:T(8,128)(2,1)S(1)}, u32[]{:S(2)}, u32[]{:S(2)}) collective-permute-start(bf16[32,1024]{1,0:T(8,128)(2,1)S(1)} %get-tuple-element.69), channel_id=1, source_target_pairs={{3,0},{30,1},{5,2},{0,3},{7,4},{2,5},{9,6},{4,7},{11,8},{6,9},{13,... | collective-permute-start | bytes 196616 | tf_op jit(solution)/shard_map/ppermute | solution.py:420

commit v2 on v1

--- a/solution.py
+++ b/solution.py
@@ -25,6 +25,7 @@
 ALL_ROWS = 496
 F32 = jnp.float32
 BF16 = jnp.bfloat16
+VMEM_MIB = 20
 
 GROUPS = (
     (0, 0, 128, 256),
@@ -145,16 +146,19 @@
     return copies
 
 
-def coarsen_kernel(seg, k_hbm, v_hbm, up, down, far3, far4, own0, own1, qdoc, k, v, sems):
-    copies = fetch((k_hbm, v_hbm), (k, v), sems)
+def coarsen_kernel(
+    seg_hbm, k_hbm, v_hbm, up, down, far3, far4, own0, own1, qdoc, seg, k, v, sems
+):
+    copies = fetch((seg_hbm, k_hbm, v_hbm), (seg, k, v), sems)
+    copies[0].wait()
     marks = jnp.where(seg[...] == iota((LANES, ROWS), 0), 1.0, 0.0).T.astype(BF16)
 
     def key_side(x):
         doc = iota(x.shape, 1) < DOCS
         return jnp.where(doc, (1.0 - x.astype(F32)) * BLOCKED, 0.0).astype(BF16)
 
-    for copy in copies:
-        copy.wait()
+    copies[1].wait()
+    copies[2].wait()
     levels = [(k[...], v[...], key_side(marks))]
     qdoc[0:ROWS] = marks
     for level in range(1, LEVELS + 1):
@@ -179,8 +183,12 @@
     put(own1, 0, 1, 0, COUNT[1])
 
 
-def prepare_kernel(q_hbm, d_hbm, w_hbm, q_out, grad_att, w, d_out, q, sems):
+def prepare_kernel(
+    far3_in, far4_in, q_hbm, d_hbm, w_hbm, far3, far4, q_out, grad_att, w, d_out, q, sems
+):
     copies = fetch((q_hbm, d_hbm, w_hbm), (q, d_out, w), sems)
+    far3[...] = far3_in[...]
+    far4[...] = far4_in[...]
     copies[0].wait()
     for level in range(LEVELS + 1):
         queries = q[...] if level == 0 else dot(gather_table(level, 0.5**level), q[...]).astype(BF16)
@@ -235,14 +243,26 @@
                 coarse[pair, at - ROWS : at - ROWS + rows] = stats.astype(BF16)
 
 
-def merge_kernel(n3, n4, q_all, qdoc, fine, coarse, grad_att, w, *refs):
-    far = (refs[:n3], refs[n3 : n3 + n4])
-    layer_out, attended_out, p_out, g_out, d_side = refs[n3 + n4 :]
+def far_refs(refs):
+    below, above, four_a, four_b, four_c, partner = refs
+    return (
+        (below, above, partner.at[0:32]),
+        (four_a, four_b, four_c, partner.at[32:80]),
+    )
+
+
+def block_at(block):
+    x, y, core = block // 8, block // 2 % 4, block % 2
+    return 16 * (16 * core + 4 * y + x)
+
+
+def merge_kernel(q_all, qdoc, fine, coarse, grad_att, d_out, *refs):
+    far = far_refs(refs[:6])
+    attended_out, d_w, p_out, g_out, d_side = refs[6:]
     docs = [(docs_of(index, qdoc), far_window(ref, DOC_LANES)) for index, ref in zip(FAR, far)]
     shape = (LANES, LANES)
     same_head = jnp.where(iota(shape, 0) // HEAD_DIM == iota(shape, 1) // HEAD_DIM, 1.0, 0.0)
     same_head = same_head.astype(BF16)
-    result = jnp.zeros((ROWS, WIDTH), F32)
     spreads = [None] + [spread_table(level) for level in range(1, LEVELS + 1)]
     gathers = [None] + [gather_table(level) for level in range(1, LEVELS + 1)]
     for pair in range(PAIRS):
@@ -271,8 +291,11 @@
         numer = functools.reduce(jnp.add, [wt * x[0] for wt, x in zip(weights, levels)])
         inverse = 1.0 / norm
         attended = (numer * inverse).astype(BF16)
+        grad_w = dot(attended, d_out[...], 0, 0)
+        for block in range(8):
+            at = block_at(8 * pair + block)
+            d_w[at : at + 16] = grad_w[16 * block : 16 * (block + 1)]
         attended_out[:, cols] = attended
-        result = result + dot(attended, w[cols, :])
         grad = grad_att[:, cols]
         high_part, low_part = split(grad * attended.astype(F32))
         delta = dot(high_part, same_head) + dot(low_part, same_head)
@@ -293,7 +316,6 @@
             d_side[at : at + rows, cols] = jnp.where(
                 upper, d_high.astype(F32), d_low.astype(F32)
             ).astype(BF16)
-    layer_out[...] = result.astype(BF16)
 
 
 def attend_back(p, queries, grad, side, keys, values):
@@ -311,10 +333,13 @@
     return grad_q, dot(ds, stacked(queries), 0, 0), dot(p, grad, 0, 0)
 
 
-def far_back_kernel(n3, n4, p_in, q_all, g_in, d_side, *refs):
-    far = (refs[:n3], refs[n3 : n3 + n4])
-    outs = refs[n3 + n4 :]
-    d_q, to_far = outs[0], (outs[1 : 1 + n3], outs[1 + n3 :])
+def far_back_kernel(p_in, q_all, g_in, d_side, *refs):
+    far = far_refs(refs[:6])
+    d_q, to_3, to_4, to_partner = refs[6:]
+    to_far = (
+        (to_3.at[0], to_3.at[1], to_partner.at[0:32]),
+        (to_4.at[0], to_4.at[1], to_4.at[2], to_partner.at[32:80]),
+    )
     for pair in range(PAIRS):
         cols = lanes_of(pair)
         for index, ref, to in zip(FAR, far, to_far):
@@ -329,18 +354,20 @@
                 far_window(ref, lanes_of(pair, 1)),
             )
             d_q[at - AT[3] : at - AT[3] + rows, cols] = grad_q.astype(BF16)
-            size = keys // len(to)
-            for i, out in enumerate(to):
-                out[:, cols] = grad_k[i * size : (i + 1) * size].astype(BF16)
-                out[:, lanes_of(pair, 1)] = grad_v[i * size : (i + 1) * size].astype(BF16)
-
-
-def near_back_kernel(
-    p_in, q_all, g_in, d_side, own0, own1, low, high, d_far, attended, d_out,
-    d_q, own_k, own_v, to_low, to_high, d_w,
-):
+            start = 0
+            for out in to:
+                stop = start + out.shape[0]
+                out[:, cols] = grad_k[start:stop].astype(BF16)
+                out[:, lanes_of(pair, 1)] = grad_v[start:stop].astype(BF16)
+                start = stop
+
+
+NEAR_PARTS = ((0,), (1, 2), (3,))
+
+
+def near_back(pairs, p_in, q_all, g_in, d_side, own0, own1, low, high, d_far):
     spread = jnp.concatenate([spread_table(level, 0.5**level) for level in (1, 2, 3, 4)], axis=1)
-    for pair in range(PAIRS):
+    for pair in pairs:
         cols = lanes_of(pair)
         grads = []
         for index in NEAR:
@@ -358,20 +385,74 @@
             )
         coarse = [x[0].astype(BF16) for x in grads[2:]] + [d_far[:, cols]]
         whole = jnp.concatenate([x[0] for x in grads[:2]], axis=0)
-        d_q[:, cols] = (whole + dot(spread, jnp.concatenate(coarse, axis=0))).astype(BF16)
-        for part, own, value in ((0, own_k, 0.5), (1, own_v, 1.0)):
+        d_q = (whole + dot(spread, jnp.concatenate(coarse, axis=0))).astype(BF16)
+        own, to_low, to_high = [], [], []
+        for part, value in ((0, 0.5), (1, 1.0)):
             a, b, c, d = (x[1 + part] for x in grads)
-            lanes = lanes_of(pair, part)
             middle = jnp.concatenate([a[64:128], a[128:256] + b[0:128], b[128:192]], axis=0)
-            own[:, cols] = middle + dot(spread_table(1, value), c[64:192].astype(BF16))
-            to_low[:, lanes] = jnp.concatenate([a[:64], c[:64], d[:64]], axis=0).astype(BF16)
-            to_high[:, lanes] = jnp.concatenate([b[192:], c[192:], d[64:]], axis=0).astype(BF16)
-        d_w[cols, :] = dot(attended[:, cols], d_out[...], 0, 0).astype(BF16)
-
-
-def combine_kernel(n3, n4, own_k, own_v, low, high, *refs):
-    from3, from4, (d_k, d_v) = refs[:n3], refs[n3 : n3 + n4], refs[n3 + n4 :]
-    for part, own, out in ((0, own_k, d_k), (1, own_v, d_v)):
+            own.append(middle + dot(spread_table(1, value), c[64:192].astype(BF16)))
+            to_low.append(jnp.concatenate([a[:64], c[:64], d[:64]], axis=0).astype(BF16))
+            to_high.append(jnp.concatenate([b[192:], c[192:], d[64:]], axis=0).astype(BF16))
+        yield pair, d_q, own, to_low, to_high
+
+
+def near_back_first_kernel(pairs, attended, w, *refs):
+    inputs, outs = refs[:9], refs[9:]
+    layer_out = None
+    if attended is not None:
+        layer_out, result, sem = outs[-3:]
+        result[...] = dot(attended[...], w[...]).astype(BF16)
+        copy = pltpu.make_async_copy(result, layer_out, sem)
+        copy.start()
+    d_q, own_k, own_v, to_low, to_high = outs[:5]
+    for pair, dq, own, low, high in near_back(pairs, *inputs):
+        at = slice((pair - pairs[0]) * LANES, (pair - pairs[0] + 1) * LANES)
+        d_q[:, at], own_k[:, at], own_v[:, at] = dq, own[0], own[1]
+        for part in range(2):
+            to_low[part, :, at], to_high[part, :, at] = low[part], high[part]
+    if attended is not None:
+        copy.wait()
+
+
+def near_back_a_kernel(attended, w, *refs):
+    near_back_first_kernel(NEAR_PARTS[0], attended, w, *refs)
+
+
+def near_back_b_kernel(*refs):
+    near_back_first_kernel(NEAR_PARTS[1], None, None, *refs[:9], *refs[-5:])
+
+
+def near_back_c_kernel(*refs):
+    inputs, earlier = refs[:9], (refs[9:12], refs[12:15])
+    d_q_hbm, own_k, own_v, to_low, to_high, d_q, sems = refs[-7:]
+    for pairs, (dq, low, high) in zip(NEAR_PARTS, earlier):
+        cols = slice(pairs[0] * LANES, (pairs[-1] + 1) * LANES)
+        d_q[:, cols] = dq[...]
+        for part in range(2):
+            lanes = slice(part * WIDTH + cols.start, part * WIDTH + cols.stop)
+            to_low[:, lanes], to_high[:, lanes] = low[part], high[part]
+    last = NEAR_PARTS[2][0] * LANES
+    before = pltpu.make_async_copy(d_q.at[:, 0:last], d_q_hbm.at[:, 0:last], sems.at[0])
+    before.start()
+    for pair, dq, own, low, high in near_back(NEAR_PARTS[2], *inputs):
+        d_q[:, lanes_of(pair)] = dq
+        own_k[...], own_v[...] = own[0], own[1]
+        after = pltpu.make_async_copy(
+            d_q.at[:, lanes_of(pair)], d_q_hbm.at[:, lanes_of(pair)], sems.at[1]
+        )
+        after.start()
+        for part in range(2):
+            to_low[:, lanes_of(pair, part)] = low[part]
+            to_high[:, lanes_of(pair, part)] = high[part]
+    before.wait()
+    after.wait()
+
+
+def combine_kernel(*refs):
+    own, (low, high), from3, from4 = (refs[0:3], refs[3:6]), refs[6:8], refs[8:10], refs[10:13]
+    d_k_hbm, d_v_hbm, d_k, d_v, sems = refs[13:]
+    copies = []
+    for part, out, out_hbm in ((0, d_k, d_k_hbm), (1, d_v, d_v_hbm)):
         lanes = slice(part * WIDTH, (part + 1) * WIDTH)
         table = jnp.concatenate(
             [spread_table(level, 1.0 if part else 0.5**level) for level in (1, 2, 3, 4)], axis=1
@@ -393,76 +474,99 @@
             ],
             axis=0,
         ).astype(BF16)
-        whole = own[...] + dot(table, coarse)
+        whole = jnp.concatenate([x[...] for x in own[part]], axis=1) + dot(table, coarse)
         out[0:64] = (whole[0:64] + rim(high, 0)).astype(BF16)
         out[64:192] = whole[64:192].astype(BF16)
         out[192:256] = (whole[192:256] + rim(low, 0)).astype(BF16)
-
-
-def call(kernel, name, outs, args, scratch=(), in_hbm=0):
+        copies.append(pltpu.make_async_copy(out, out_hbm, sems.at[part]))
+        copies[-1].start()
+    for copy in copies:
+        copy.wait()
+
+
+def call(
+    kernel, name, outs, args, scratch=(), in_hbm=0, microseconds=1.0, to_hbm=()
+):
     vmem, hbm = pl.BlockSpec(memory_space=pltpu.VMEM), pl.BlockSpec(memory_space=pl.ANY)
     return pl.pallas_call(
         kernel,
         name=name,
         out_shape=[jax.ShapeDtypeStruct(shape, dtype) for shape, dtype in outs],
         in_specs=[vmem] * (len(args) - in_hbm) + [hbm] * in_hbm,
-        out_specs=[vmem] * len(outs),
+        out_specs=[hbm if i in to_hbm else vmem for i in range(len(outs))],
         scratch_shapes=scratch,
-        compiler_params=pltpu.CompilerParams(vmem_limit_bytes=48 * 1024 * 1024),
+        cost_estimate=pl.CostEstimate(
+            flops=int(microseconds * 1e9), bytes_accessed=1 << 20, transcendentals=0
+        ),
+        compiler_params=pltpu.CompilerParams(vmem_limit_bytes=VMEM_MIB * 1024 * 1024),
     )(*args)
 
 
-def moved(x, route, back=False):
+def moved(x, route):
     count = lax.axis_size("ctx")
-    pairs = [(i, route(i) % count) for i in range(count)]
-    if back:
-        pairs = [(b, a) for a, b in pairs]
-    return lax.ppermute(x, "ctx", pairs)
-
-
-ROUTES_3 = (
-    lambda i: i + 2,
-    lambda i: i - 2,
-    lambda i: i - 3 if i % 2 else i + 3,
-)
-
-
-def route_4(shift, swap):
-    def route(i):
-        pair, side = i // 2, i % 2
-        pair = pair + shift if shift else pair + (-3 if pair % 2 else 3)
-        return 2 * pair + (side ^ swap)
-
-    return route
-
-
-ROUTES_4 = tuple(route_4(shift, swap) for shift in (2, -2, 0) for swap in (0, 1))
+    return lax.ppermute(x, "ctx", [(i, route(i) % count) for i in range(count)])
+
+
+def partner(i):
+    return i ^ 1
+
+
+def third(i):
+    return i - 6 if i // 2 % 2 else i + 6
+
+
+ROUTES_3 = (lambda i: i + 2, lambda i: i - 2)
+ROUTES_4 = (lambda i: i + 4, lambda i: i - 4, third)
+BACK_3 = (lambda i: i - 2, lambda i: i + 2)
+BACK_4 = (lambda i: i - 4, lambda i: i + 4, third)
+
+
+def scattered(y, low, bits, after=None):
+    side, count = lax.axis_index("ctx") >> low & (1 << bits) - 1, 1 << bits
+    rows = y.shape[0] // count
+
+    def part(index):
+        return lax.dynamic_slice_in_dim(y, index * rows, rows)
+
+    result = part(side)
+    if after is not None:
+        result, _ = lax.optimization_barrier((result, after))
+    for step in range(1, count):
+        message = part(side ^ step).astype(BF16)
+        result = result + moved(message, lambda i, step=step: i ^ step << low).astype(F32)
+    return result
 
 
 def body(queries, key_rows, value_rows, segment_ids, w_out, d_out):
     q, k, v, grad_out = queries[0], key_rows[0], value_rows[0], d_out[0]
     tokens, dma = (ROWS, WIDTH), pltpu.SemaphoreType.DMA
+    even = lax.axis_index("ctx") % 2 == 0
     up, down, far3, far4, own0, own1, qdoc = call(
         coarsen_kernel,
         "coarsen",
         [((192, PACK), BF16), ((192, PACK), BF16), ((32, PACK), BF16), ((16, PACK), BF16)]
         + [((ROWS, PACK), BF16), ((128, PACK), BF16), ((ALL_ROWS, LANES), BF16)],
         [segment_ids, k, v],
-        [pltpu.VMEM(tokens, BF16), pltpu.VMEM(tokens, BF16), dma((2,))],
-        in_hbm=2,
+        [pltpu.VMEM((1, ROWS), jnp.int32)] + [pltpu.VMEM(tokens, BF16)] * 2 + [dma((3,))],
+        in_hbm=3,
+    )
+    far3, far4, q_all, grad_att, w, grad_rows = call(
+        prepare_kernel,
+        "prepare",
+        [((32, PACK), BF16), ((16, PACK), BF16)]
+        + [((ALL_ROWS, WIDTH), BF16), (tokens, F32), ((WIDTH, WIDTH), BF16), (tokens, BF16)],
+        [far3, far4, q, grad_out, w_out],
+        [pltpu.VMEM(tokens, BF16), dma((3,))],
+        in_hbm=3,
     )
     low = moved(up, lambda i: i + 1)
     high = moved(down, lambda i: i - 1)
-    got = [moved(far3, route) for route in ROUTES_3] + [moved(far4, route) for route in ROUTES_4]
-    n3, n4 = len(ROUTES_3), len(ROUTES_4)
-    q_all, grad_att, w, grad_rows = call(
-        prepare_kernel,
-        "prepare",
-        [((ALL_ROWS, WIDTH), BF16), (tokens, F32), ((WIDTH, WIDTH), BF16), (tokens, BF16)],
-        [q, grad_out, w_out],
-        [pltpu.VMEM(tokens, BF16), dma((3,))],
-        in_hbm=3,
-    )
+    got3 = [moved(far3, route) for route in ROUTES_3]
+    got4 = [moved(far4, route) for route in ROUTES_4]
+    low, high, *got3 = lax.optimization_barrier((low, high, *got3))
+    passed = jnp.concatenate([jnp.where(even, got3[0], got3[1]), *got4], axis=0)
+    low, high, passed = lax.optimization_barrier((low, high, passed))
+    far = (*got3, *got4, moved(passed, partner))
     near = (own0, own1, low, high)
     p_near, fine, coarse = call(
         near_kernel,
@@ -473,44 +577,83 @@
             ((PAIRS, 192, 3 * LANES), BF16),
         ],
         [q_all, qdoc, *near],
-    )
-    layer_out, attended, p_far, g, d_side = call(
-        functools.partial(merge_kernel, n3, n4),
+        microseconds=50,
+    )
+    attended, d_w, p_far, g, d_side = call(
+        merge_kernel,
         "merge",
-        [(tokens, BF16), (tokens, BF16), ((PAIRS, P_FAR, LANES), BF16)]
+        [(tokens, BF16), ((WIDTH, WIDTH), F32), ((PAIRS, P_FAR, LANES), BF16)]
         + [((ALL_ROWS, WIDTH), BF16)] * 2,
-        [q_all, qdoc, fine, coarse, grad_att, w, *got],
-    )
-    d_far, *to_far = call(
-        functools.partial(far_back_kernel, n3, n4),
+        [q_all, qdoc, fine, coarse, grad_att, grad_rows, *far],
+        microseconds=6,
+    )
+    d_far, to_3, to_4, to_partner = call(
+        far_back_kernel,
         "far_back",
-        [((48, WIDTH), BF16)]
-        + [((32, 2 * WIDTH), BF16)] * n3
-        + [((16, 2 * WIDTH), BF16)] * n4,
-        [p_far, q_all, g, d_side, *got],
-    )
-    back = [moved(x, route, back=True) for x, route in zip(to_far, ROUTES_3 + ROUTES_4)]
-    d_q, own_k, own_v, to_low, to_high, d_w = call(
-        near_back_kernel,
-        "near_back",
-        [(tokens, BF16), (tokens, F32), (tokens, F32)]
-        + [((192, 2 * WIDTH), BF16)] * 2
-        + [((WIDTH, WIDTH), BF16)],
-        [p_near, q_all, g, d_side, *near, d_far, attended, grad_rows],
-    )
+        [((48, WIDTH), BF16), ((2, 32, 2 * WIDTH), BF16)]
+        + [((3, 16, 2 * WIDTH), BF16), ((80, 2 * WIDTH), BF16)],
+        [p_far, q_all, g, d_side, *far],
+    )
+    d_w = scattered(d_w, 0, 1)
+    from_partner = moved(to_partner, partner).astype(F32)
+    swapped3, swapped4 = from_partner[:32], from_partner[32:].reshape(3, 16, 2 * WIDTH)
+    mine = jnp.stack([jnp.where(even, swapped3, 0), jnp.where(even, 0, swapped3)])
+    to_3 = (to_3.astype(F32) + mine).astype(BF16)
+    to_4 = (to_4.astype(F32) + swapped4).astype(BF16)
+
+    def part_outs(part):
+        width = len(NEAR_PARTS[part]) * LANES
+        return [((ROWS, width), BF16), ((ROWS, width), F32), ((ROWS, width), F32)] + [
+            ((2, 192, width), BF16)
+        ] * 2
+
+    args = [p_near, q_all, g, d_side, *near, d_far]
+    *part_a, layer_out = call(
+        near_back_a_kernel,
+        "near_back_a",
+        part_outs(0) + [(tokens, BF16)],
+        [attended, w, *args],
+        [pltpu.VMEM(tokens, BF16), dma(())],
+        microseconds=3,
+        to_hbm=(5,),
+    )
+    part_b = call(
+        near_back_b_kernel,
+        "near_back_b",
+        part_outs(1),
+        [*args, part_a[0], to_3, d_w],
+        in_hbm=3,
+        microseconds=4,
+    )
+    back = [moved(to_3[i], route) for i, route in enumerate(BACK_3)]
+    d_w = scattered(d_w, 1, 2, after=part_b[0])
+    to_4, _ = lax.optimization_barrier((to_4, part_b[0]))
+    d_q, own_k, own_v, to_low, to_high = call(
+        near_back_c_kernel,
+        "near_back_c",
+        [(tokens, BF16), ((ROWS, LANES), F32), ((ROWS, LANES), F32)]
+        + [((192, 2 * WIDTH), BF16)] * 2,
+        [*args, part_a[0], *part_a[3:], part_b[0], *part_b[3:], to_4, d_w, *back],
+        [pltpu.VMEM(tokens, BF16), dma((2,))],
+        in_hbm=4,
+        microseconds=2,
+        to_hbm=(0,),
+    )
+    back += [moved(to_4[i], route) for i, route in enumerate(BACK_4)]
+    d_w = scattered(d_w, 3, 2, after=to_low)
     low_back = moved(to_low, lambda i: i - 1)
     high_back = moved(to_high, lambda i: i + 1)
-    count, dp_count = lax.axis_size("ctx"), lax.axis_size("dp")
-    parts = d_w.reshape(count, WIDTH // count, WIDTH)
-    parts = lax.all_to_all(parts, "ctx", 0, 0, tiled=True)
-    mine = jnp.sum(parts.astype(F32), axis=0)
-    copies = jnp.broadcast_to(mine[None], (dp_count,) + mine.shape)
-    d_w = jnp.sum(lax.all_to_all(copies, "dp", 0, 0, tiled=True), axis=0).astype(BF16)
+    dp_count = lax.axis_size("dp")
+    copies = jnp.broadcast_to(d_w.astype(BF16)[None], (dp_count,) + d_w.shape)
+    copies = lax.all_to_all(copies, "dp", 0, 0, tiled=True)
+    d_w = jnp.sum(copies.astype(F32), axis=0).astype(BF16)
     d_k, d_v = call(
-        functools.partial(combine_kernel, n3, n4),
+        combine_kernel,
         "combine",
         [(tokens, BF16)] * 2,
-        [own_k, own_v, low_back, high_back, *back],
+        [part_a[1], part_b[1], own_k, part_a[2], part_b[2], own_v, low_back, high_back, *back],
+        [pltpu.VMEM(tokens, BF16)] * 2 + [dma((2,))],
+        to_hbm=(0, 1),
     )
     return layer_out[None], d_q[None], d_k[None], d_v[None], d_w
 

time: 104 us -> 93.5 us (0.90)
  the two profiles are of different devices: /device:TPU:1 before, /device:TPU:32 now
where the time goes in v2:
time: 93.5 us; the launch traced here: 92.5 us
  starting transfers between devices  41.7 us (45%)
  Pallas kernels  17.7 us (19%)
  waiting for transfers between devices  16.4 us (18%)
  local copies, waits for them, and re-layouts  14.6 us (16%)
  between operations  1.18 us (1%)
    ppermute x23, starting transfers between devices, moved(): return lax.ppermute(x, 'ctx', [(i, route(i) % count) for i in range(count)])  33.2 us
    pallas_call x9, Pallas kernels, call(): pl.pallas_call(kernel, name=name, out_shape=[jax.ShapeDtypeStruct(shape,...  17.7 us
    unnamed x52, local copies, waits for them, and re-layouts  13.8 us
    ppermute x23, waiting for transfers between devices, moved(): return lax.ppermute(x, 'ctx', [(i, route(i) % count) for i in range(count)])  13.4 us
    all_to_all x1, starting transfers between devices, body(): copies = lax.all_to_all(copies, 'dp', 0, 0, tiled=True)  8.57 us
    all_to_all x1, waiting for transfers between devices, body(): copies = lax.all_to_all(copies, 'dp', 0, 0, tiled=True)  3.02 us
  transfers between devices with their start and end apart: 24, of which 10 were waited for; matrix products, arithmetic and copies ran while one was open for 2% of the time, Pallas kernels for 11%

profile of v2, /device:TPU:32, one launch (start us, length us, event | category | flops | bytes accessed | tf_op | source)
XLA Modules:
  0.0 92.5 jit_solution(15540040407100758663)
XLA Ops:
  0.6 0.9 %copy-done.1 = bf16[1,256,512]{2,1,0:T(8,128)(2,1)S(1)} copy-done((bf16[1,256,512]{2,1,0:T(8,128)(2,1)S(1)}, bf16[1,256,512]{2,1,0:T(8,128)(2,1)}, u32[]{:S(2)}) %copy-start.1) | copy-done | bytes 262168
  1.6 0.9 %copy-done.2 = bf16[1,256,512]{2,1,0:T(8,128)(2,1)S(1)} copy-done((bf16[1,256,512]{2,1,0:T(8,128)(2,1)S(1)}, bf16[1,256,512]{2,1,0:T(8,128)(2,1)}, u32[]{:S(2)}) %copy-start.2) | copy-done | bytes 262168
  4.6 5.1 %collective-permute-start.1 = (bf16[192,1152]{1,0:T(8,128)(2,1)S(1)}, bf16[192,1152]{1,0:T(8,128)(2,1)S(1)}, u32[]{:S(2)}, u32[]{:S(2)}) collective-permute-start(bf16[192,1152]{1,0:T(8,128)(2,1)S(1)} %get-tuple-element.65), channel_id=1, source_target_pairs={{0,31},{1,0},{2,1},{3,2},{4,3},{5,4},{6,5},{7,6},{8,7},{9,8},{10,9... | collective-permute-start | bytes 1327112 | tf_op jit(solution)/shard_map/ppermute | solution.py:507
  12.7 5.3 %collective-permute-start.3 = (bf16[32,1152]{1,0:T(8,128)(2,1)S(1)}, bf16[32,1152]{1,0:T(8,128)(2,1)S(1)}, u32[]{:S(2)}, u32[]{:S(2)}) collective-permute-start(bf16[32,1152]{1,0:T(8,128)(2,1)S(1)} %get-tuple-element.66), channel_id=1, source_target_pairs={{0,30},{1,31},{2,0},{3,1},{4,2},{5,3},{6,4},{7,5},{8,6},{9,7},{10,... | collective-permute-start | bytes 221192 | tf_op jit(solution)/shard_map/ppermute | solution.py:507
  18.1 2.4 %collective-permute-done.2.refs_0_ = bf16[32,1152]{1,0:T(8,128)(2,1)S(1)} collective-permute-done((bf16[32,1152]{1,0:T(8,128)(2,1)S(1)}, bf16[32,1152]{1,0:T(8,128)(2,1)S(1)}, u32[]{:S(2)}, u32[]{:S(2)}) %collective-permute-start.2) | collective-permute-done | bytes 73760 | tf_op jit(solution)/shard_map/ppermute | solution.py:507
  20.5 3.3 %collective-permute-start.5 = (bf16[16,1152]{1,0:T(8,128)(2,1)S(1)}, bf16[16,1152]{1,0:T(8,128)(2,1)S(1)}, u32[]{:S(2)}, u32[]{:S(2)}) collective-permute-start(bf16[16,1152]{1,0:T(8,128)(2,1)S(1)} %get-tuple-element.71), channel_id=1, source_target_pairs={{0,28},{1,29},{2,30},{3,31},{4,0},{5,1},{6,2},{7,3},{8,4},{9,5},{1... | collective-permute-start | bytes 110600 | tf_op jit(solution)/shard_map/ppermute | solution.py:507
  23.8 1.9 %collective-permute-done.4.refs_2_ = bf16[16,1152]{1,0:T(8,128)(2,1)S(1)} collective-permute-done((bf16[16,1152]{1,0:T(8,128)(2,1)S(1)}, bf16[16,1152]{1,0:T(8,128)(2,1)S(1)}, u32[]{:S(2)}, u32[]{:S(2)}) %collective-permute-start.4) | collective-permute-done | bytes 36896 | tf_op jit(solution)/shard_map/ppermute | solution.py:507
  26.0 2.8 %collective-permute-done.6.refs_4_ = bf16[16,1152]{1,0:T(8,128)(2,1)S(1)} collective-permute-done((bf16[16,1152]{1,0:T(8,128)(2,1)S(1)}, bf16[16,1152]{1,0:T(8,128)(2,1)S(1)}, u32[]{:S(2)}, u32[]{:S(2)}) %collective-permute-start.6) | collective-permute-done | bytes 36896 | tf_op jit(solution)/shard_map/ppermute | solution.py:507
  30.1 1.7 %near.1 = (bf16[4,896,256]{2,1,0:T(8,128)(2,1)S(1)}, f32[4,256,384]{2,1,0:T(8,128)S(1)}, bf16[4,192,384]{2,1,0:T(8,128)(2,1)S(1)}) custom-call(bf16[496,512]{1,0:T(8,128)(2,1)S(1)} %get-tuple-element.60.q_all.refs_1_, bf16[496,128]{1,0:T(8,128)(2,1)S(1)} %copy-done.25, bf16[256,1152]{1,0:T(8,128)(2,1)S(1)} %get-tuple-element.62.own0.refs_4_, ...), custom_call_target="tpu_custom_call" | custom-call | flops 49999998976 | bytes 1048576 | tf_op jit(solution)/shard_map/near/pallas_call | solution.py:491
  31.8 5.5 %merge.1 = (bf16[256,512]{1,0:T(8,128)(2,1)S(1)}, f32[512,512]{1,0:T(8,128)S(1)}, bf16[4,96,128]{2,1,0:T(8,128)(2,1)S(1)}, bf16[496,512]{1,0:T(8,128)(2,1)S(1)}, bf16[496,512]{1,0:T(8,128)(2,1)S(1)}) custom-call(bf16[496,512]{1,0:T(8,128)(2,1)S(1)} %get-tuple-element.60.q_all.refs_1_, bf16[496,128]{1,0:T(8,128)(2,1)S(1)} %copy-done.25, ...), custom_call_target="tpu_custom_call" | custom-call | flops 6000000000 | bytes 1048576 | tf_op jit(solution)/shard_map/merge/pallas_call | solution.py:491
  38.0 1.1 %far_back.1 = (bf16[48,512]{1,0:T(8,128)(2,1)S(1)}, bf16[2,32,1024]{2,1,0:T(8,128)(2,1)S(1)}, bf16[3,16,1024]{2,1,0:T(8,128)(2,1)S(1)}, bf16[80,1024]{1,0:T(8,128)(2,1)S(1)}) custom-call(bf16[4,96,128]{2,1,0:T(8,128)(2,1)S(1)} %get-tuple-element.84.p_in, bf16[496,512]{1,0:T(8,128)(2,1)S(1)} %get-tuple-element.60.q_all.refs_1_, ...), custom_call_target="tpu_custom_call" | custom-call | flops 1000000000 | bytes 1048576 | tf_op jit(solution)/shard_map/far_back/pallas_call | solution.py:491
  39.2 2.0 %near_back_a.1 = (bf16[256,128]{1,0:T(8,128)(2,1)S(1)}, f32[256,128]{1,0:T(8,128)S(1)}, f32[256,128]{1,0:T(8,128)S(1)}, bf16[2,192,128]{2,1,0:T(8,128)(2,1)S(1)}...) custom-call(bf16[256,512]{1,0:T(8,128)(2,1)S(1)} %get-tuple-element.79.attended, ...), custom_call_target="tpu_custom_call" | custom-call | flops 3000000000 | bytes 1048576 | tf_op jit(solution)/shard_map/near_back_a/pallas_call | solution.py:491
  41.9 2.5 %collective-permute-start.13 = (bf16[32,1024]{1,0:T(8,128)(2,1)S(1)}, bf16[32,1024]{1,0:T(8,128)(2,1)S(1)}, u32[]{:S(2)}, u32[]{:S(2)}) collective-permute-start(bf16[32,1024]{1,0:T(8,128)(2,1)S(1)} %get-tuple-element.120), channel_id=1, source_target_pairs={{0,30},{1,31},{2,0},{3,1},{4,2},{5,3},{6,4},{7,5},{8,6},{9,7},{10,... | collective-permute-start | bytes 196616 | tf_op jit(solution)/shard_map/ppermute | solution.py:507
  44.5 2.7 %near_back_b.1 = (bf16[256,256]{1,0:T(8,128)(2,1)S(1)}, f32[256,256]{1,0:T(8,128)S(1)}, f32[256,256]{1,0:T(8,128)S(1)}, bf16[2,192,256]{2,1,0:T(8,128)(2,1)S(1)}, bf16[2,192,256]{2,1,0:T(8,128)(2,1)S(1)}) custom-call(bf16[4,896,256]{2,1,0:T(8,128)(2,1)S(1)} %get-tuple-element.81.refs_0_, bf16[496,512]{1,0:T(8,128)(2,1)S(1)} %get-tuple-element.60.q_all.refs_1_, ...), custom_call_target="tpu_custom_call" | custom-call | flops 4000000000 | bytes 1048576 | tf_op jit(solution)/shard_map/near_back_b/pallas_call | solution.py:491
  47.4 3.2 %collective-permute-start.11 = (bf16[64,512]{1,0:T(8,128)(2,1)S(1)}, bf16[64,512]{1,0:T(8,128)(2,1)S(1)}, u32[]{:S(2)}, u32[]{:S(2)}) collective-permute-start(bf16[64,512]{1,0:T(8,128)(2,1)S(1)} %get-tuple-element.113), channel_id=1, source_target_pairs={{0,4},{1,5},{2,6},{3,7},{4,0},{5,1},{6,2},{7,3},{8,12},{9,13},{10,... | collective-permute-start | bytes 196616 | tf_op jit(solution)/shard_map/ppermute | solution.py:507
  50.6 1.5 %collective-permute-start.12 = (bf16[64,512]{1,0:T(8,128)(2,1)S(1)}, bf16[64,512]{1,0:T(8,128)(2,1)S(1)}, u32[]{:S(2)}, u32[]{:S(2)}) collective-permute-start(bf16[64,512]{1,0:T(8,128)(2,1)S(1)} %get-tuple-element.112), channel_id=1, source_target_pairs={{0,6},{1,7},{2,4},{3,5},{4,2},{5,3},{6,0},{7,1},{8,14},{9,15},{10,... | collective-permute-start | bytes 196616 | tf_op jit(solution)/shard_map/ppermute | solution.py:507
  52.3 1.6 %collective-permute-done.11 = bf16[64,512]{1,0:T(8,128)(2,1)S(1)} collective-permute-done((bf16[64,512]{1,0:T(8,128)(2,1)S(1)}, bf16[64,512]{1,0:T(8,128)(2,1)S(1)}, u32[]{:S(2)}, u32[]{:S(2)}) %collective-permute-start.11) | collective-permute-done | bytes 65568 | tf_op jit(solution)/shard_map/ppermute | solution.py:507
  53.9 2.2 %collective-permute-done.12 = bf16[64,512]{1,0:T(8,128)(2,1)S(1)} collective-permute-done((bf16[64,512]{1,0:T(8,128)(2,1)S(1)}, bf16[64,512]{1,0:T(8,128)(2,1)S(1)}, u32[]{:S(2)}, u32[]{:S(2)}) %collective-permute-start.12) | collective-permute-done | bytes 65568 | tf_op jit(solution)/shard_map/ppermute | solution.py:507
  56.5 5.4 %collective-permute-start.21 = (bf16[16,512]{1,0:T(8,128)(2,1)S(1)}, bf16[16,512]{1,0:T(8,128)(2,1)S(1)}, u32[]{:S(2)}, u32[]{:S(2)}) collective-permute-start(bf16[16,512]{1,0:T(8,128)(2,1)S(1)} %get-tuple-element.118), channel_id=1, source_target_pairs={{0,16},{1,17},{2,18},{3,19},{4,20},{5,21},{6,22},{7,23},{8,24},{9,... | collective-permute-start | bytes 49160 | tf_op jit(solution)/shard_map/ppermute | solution.py:507
  61.9 2.1 %near_back_c.1 = (bf16[256,512]{1,0:T(8,128)(2,1)}, f32[256,128]{1,0:T(8,128)S(1)}, f32[256,128]{1,0:T(8,128)S(1)}, bf16[192,1024]{1,0:T(8,128)(2,1)S(1)}, bf16[192,1024]{1,0:T(8,128)(2,1)S(1)}) custom-call(bf16[4,896,256]{2,1,0:T(8,128)(2,1)S(1)} %get-tuple-element.81.refs_0_, bf16[496,512]{1,0:T(8,128)(2,1)S(1)} %get-tuple-element.60.q_all.refs_1_, ...), custom_call_target="tpu_custom_call" | custom-call | flops 2000000000 | bytes 1048576 | tf_op jit(solution)/shard_map/near_back_c/pallas_call | solution.py:491
  65.3 0.9 %collective-permute-start.15 = (bf16[192,1024]{1,0:T(8,128)(2,1)S(1)}, bf16[192,1024]{1,0:T(8,128)(2,1)S(1)}, u32[]{:S(2)}, u32[]{:S(2)}) collective-permute-start(bf16[192,1024]{1,0:T(8,128)(2,1)S(1)} %get-tuple-element.106), channel_id=1, source_target_pairs={{0,31},{1,0},{2,1},{3,2},{4,3},{5,4},{6,5},{7,6},{8,7},{9,8},{10,9... | collective-permute-start | bytes 1179656 | tf_op jit(solution)/shard_map/ppermute | solution.py:507
  67.5 8.6 %all-to-all-start = ((bf16[8,16,512]{2,1,0:T(8,128)(2,1)}), bf16[8,16,512]{2,1,0:T(8,128)(2,1)S(1)}, u32[]{:S(2)}, u32[]{:S(2)}) async-start(bf16[8,16,512]{2,1,0:T(8,128)(2,1)} %broadcast_in_dim.29), calls=%async_computation | async-start | bytes 262144 | tf_op jit(solution)/shard_map/all_to_all | solution.py:648
  76.1 2.1 %collective-permute-start.17 = (bf16[16,1024]{1,0:T(8,128)(2,1)S(1)}, bf16[16,1024]{1,0:T(8,128)(2,1)S(1)}, u32[]{:S(2)}, u32[]{:S(2)}) collective-permute-start(bf16[16,1024]{1,0:T(8,128)(2,1)S(1)} %get-tuple-element.123), channel_id=1, source_target_pairs={{0,28},{1,29},{2,30},{3,31},{4,0},{5,1},{6,2},{7,3},{8,4},{9,5},{1... | collective-permute-start | bytes 98312 | tf_op jit(solution)/shard_map/ppermute | solution.py:507
  78.2 1.5 %collective-permute-start.18 = (bf16[16,1024]{1,0:T(8,128)(2,1)S(1)}, bf16[16,1024]{1,0:T(8,128)(2,1)S(1)}, u32[]{:S(2)}, u32[]{:S(2)}) collective-permute-start(bf16[16,1024]{1,0:T(8,128)(2,1)S(1)} %get-tuple-element.122), channel_id=1, source_target_pairs={{0,4},{1,5},{2,6},{3,7},{4,8},{5,9},{6,10},{7,11},{8,12},{9,13},{1... | collective-permute-start | bytes 98312 | tf_op jit(solution)/shard_map/ppermute | solution.py:507
  79.7 1.0 %collective-permute-start.19 = (bf16[16,1024]{1,0:T(8,128)(2,1)S(1)}, bf16[16,1024]{1,0:T(8,128)(2,1)S(1)}, u32[]{:S(2)}, u32[]{:S(2)}) collective-permute-start(bf16[16,1024]{1,0:T(8,128)(2,1)S(1)} %get-tuple-element.121), channel_id=1, source_target_pairs={{0,6},{1,7},{2,28},{3,29},{4,10},{5,11},{6,0},{7,1},{8,14},{9,15},... | collective-permute-start | bytes 98312 | tf_op jit(solution)/shard_map/ppermute | solution.py:507
  80.6 3.0 %all-to-all-done = bf16[8,16,512]{2,1,0:T(8,128)(2,1)S(1)} async-done(((bf16[8,16,512]{2,1,0:T(8,128)(2,1)}), bf16[8,16,512]{2,1,0:T(8,128)(2,1)S(1)}, u32[]{:S(2)}, u32[]{:S(2)}) %all-to-all-start) | async-done | bytes 131104 | tf_op jit(solution)/shard_map/all_to_all | solution.py:648
  84.3 1.4 %collective-permute-done.18.refs_11_ = bf16[16,1024]{1,0:T(8,128)(2,1)S(1)} collective-permute-done((bf16[16,1024]{1,0:T(8,128)(2,1)S(1)}, bf16[16,1024]{1,0:T(8,128)(2,1)S(1)}, u32[]{:S(2)}, u32[]{:S(2)}) %collective-permute-start.18) | collective-permute-done | bytes 32800 | tf_op jit(solution)/shard_map/ppermute | solution.py:507
  86.6 0.9 copy-done.9
  87.5 0.9 %copy-done.11 = f32[256,256]{1,0:T(8,128)S(1)} copy-done((f32[256,256]{1,0:T(8,128)S(1)}, f32[256,256]{1,0:T(8,128)}, u32[]{:S(2)}) %copy-start.11) | copy-done | bytes 262168
  88.5 0.9 %copy-done.13 = f32[256,256]{1,0:T(8,128)S(1)} copy-done((f32[256,256]{1,0:T(8,128)S(1)}, f32[256,256]{1,0:T(8,128)}, u32[]{:S(2)}) %copy-start.13) | copy-done | bytes 262168
  89.4 0.9 copy-done.19
  91.2 1.1 %combine.1 = (bf16[256,512]{1,0:T(8,128)(2,1)}, bf16[256,512]{1,0:T(8,128)(2,1)}) custom-call(f32[256,128]{1,0:T(8,128)S(1)} %copy-done.19, f32[256,256]{1,0:T(8,128)S(1)} %copy-done.11, f32[256,128]{1,0:T(8,128)S(1)} %copy-done.7, f32[256,128]{1,0:T(8,128)S(1)} %copy-done.21, f32[256,256]{1,0:T(8,128)S(1)} %copy-done.13, f32[256,128]{1,0:T(8,128)S(1)} %copy-done.9, ...), custom_call_target="tpu_custom_call" | custom-call | flops 1000000000 | bytes 1048576 | tf_op jit(solution)/shard_map/combine/pallas_call | solution.py:491
  (96 shorter events, 13.9 us)
Async XLA Ops:
  3.2 6.4 %copy-start = (bf16[512,512]{1,0:T(8,128)(2,1)S(1)}, bf16[512,512]{1,0:T(8,128)(2,1)}, u32[]{:S(2)}) copy-start(bf16[512,512]{1,0:T(8,128)(2,1)} %w_hbm.1) | copy-start | bytes 1572868
  3.2 6.4 %copy-start.3 = (bf16[1,256,512]{2,1,0:T(8,128)(2,1)S(1)}, bf16[1,256,512]{2,1,0:T(8,128)(2,1)}, u32[]{:S(2)}) copy-start(bf16[1,256,512]{2,1,0:T(8,128)(2,1)} %param.6) | copy-start | bytes 786436
  3.2 6.4 %copy-start.4 = (bf16[1,256,512]{2,1,0:T(8,128)(2,1)S(1)}, bf16[1,256,512]{2,1,0:T(8,128)(2,1)}, u32[]{:S(2)}) copy-start(bf16[1,256,512]{2,1,0:T(8,128)(2,1)} %param.11) | copy-start | bytes 786436
  4.6 19.1 %collective-permute-start = (bf16[192,1152]{1,0:T(8,128)(2,1)S(1)}, bf16[192,1152]{1,0:T(8,128)(2,1)S(1)}, u32[]{:S(2)}, u32[]{:S(2)}) collective-permute-start(bf16[192,1152]{1,0:T(8,128)(2,1)S(1)} %get-tuple-element.64), channel_id=1, source_target_pairs={{0,1},{1,2},{2,3},{3,4},{4,5},{5,6},{6,7},{7,8},{8,9},{9,10},{10,1... | collective-permute-start | bytes 1327112 | tf_op jit(solution)/shard_map/ppermute | solution.py:507
  4.6 19.1 %collective-permute-start.1 = (bf16[192,1152]{1,0:T(8,128)(2,1)S(1)}, bf16[192,1152]{1,0:T(8,128)(2,1)S(1)}, u32[]{:S(2)}, u32[]{:S(2)}) collective-permute-start(bf16[192,1152]{1,0:T(8,128)(2,1)S(1)} %get-tuple-element.65), channel_id=1, source_target_pairs={{0,31},{1,0},{2,1},{3,2},{4,3},{5,4},{6,5},{7,6},{8,7},{9,8},{10,9... | collective-permute-start | bytes 1327112 | tf_op jit(solution)/shard_map/ppermute | solution.py:507
  12.7 7.7 %collective-permute-start.2 = (bf16[32,1152]{1,0:T(8,128)(2,1)S(1)}, bf16[32,1152]{1,0:T(8,128)(2,1)S(1)}, u32[]{:S(2)}, u32[]{:S(2)}) collective-permute-start(bf16[32,1152]{1,0:T(8,128)(2,1)S(1)} %get-tuple-element.66), channel_id=1, source_target_pairs={{0,2},{1,3},{2,4},{3,5},{4,6},{5,7},{6,8},{7,9},{8,10},{9,11},{10,... | collective-permute-start | bytes 221192 | tf_op jit(solution)/shard_map/ppermute | solution.py:507
  12.7 11.0 %collective-permute-start.3 = (bf16[32,1152]{1,0:T(8,128)(2,1)S(1)}, bf16[32,1152]{1,0:T(8,128)(2,1)S(1)}, u32[]{:S(2)}, u32[]{:S(2)}) collective-permute-start(bf16[32,1152]{1,0:T(8,128)(2,1)S(1)} %get-tuple-element.66), channel_id=1, source_target_pairs={{0,30},{1,31},{2,0},{3,1},{4,2},{5,3},{6,4},{7,5},{8,6},{9,7},{10,... | collective-permute-start | bytes 221192 | tf_op jit(solution)/shard_map/ppermute | solution.py:507
  18.1 7.6 %collective-permute-start.4 = (bf16[16,1152]{1,0:T(8,128)(2,1)S(1)}, bf16[16,1152]{1,0:T(8,128)(2,1)S(1)}, u32[]{:S(2)}, u32[]{:S(2)}) collective-permute-start(bf16[16,1152]{1,0:T(8,128)(2,1)S(1)} %get-tuple-element.71), channel_id=1, source_target_pairs={{0,4},{1,5},{2,6},{3,7},{4,8},{5,9},{6,10},{7,11},{8,12},{9,13},{1... | collective-permute-start | bytes 110600 | tf_op jit(solution)/shard_map/ppermute | solution.py:507
  20.5 5.6 %collective-permute-start.5 = (bf16[16,1152]{1,0:T(8,128)(2,1)S(1)}, bf16[16,1152]{1,0:T(8,128)(2,1)S(1)}, u32[]{:S(2)}, u32[]{:S(2)}) collective-permute-start(bf16[16,1152]{1,0:T(8,128)(2,1)S(1)} %get-tuple-element.71), channel_id=1, source_target_pairs={{0,28},{1,29},{2,30},{3,31},{4,0},{5,1},{6,2},{7,3},{8,4},{9,5},{1... | collective-permute-start | bytes 110600 | tf_op jit(solution)/shard_map/ppermute | solution.py:507
  23.7 5.2 %collective-permute-start.6 = (bf16[16,1152]{1,0:T(8,128)(2,1)S(1)}, bf16[16,1152]{1,0:T(8,128)(2,1)S(1)}, u32[]{:S(2)}, u32[]{:S(2)}) collective-permute-start(bf16[16,1152]{1,0:T(8,128)(2,1)S(1)} %get-tuple-element.71), channel_id=1, source_target_pairs={{0,6},{1,7},{2,28},{3,29},{4,10},{5,11},{6,0},{7,1},{8,14},{9,15},... | collective-permute-start | bytes 110600 | tf_op jit(solution)/shard_map/ppermute | solution.py:507
  28.9 2.9 %collective-permute-start.7 = (bf16[80,1152]{1,0:T(8,128)(2,1)S(1)}, bf16[80,1152]{1,0:T(8,128)(2,1)S(1)}, u32[]{:S(2)}, u32[]{:S(2)}) collective-permute-start(bf16[80,1152]{1,0:T(8,128)(2,1)S(1)} %pad_maximum_fusion), channel_id=1, source_target_pairs={{0,1},{1,0},{2,3},{3,2},{4,5},{5,4},{6,7},{7,6},{8,9},{9,8},{10,11... | collective-permute-start | bytes 552968 | tf_op jit(solution)/shard_map/ppermute | solution.py:507
  30.1 1.7 %copy-start.17 = (f32[256,512]{1,0:T(8,128)S(1)}, f32[256,512]{1,0:T(8,128)}, u32[]{:S(2)}) copy-start(f32[256,512]{1,0:T(8,128)} %copy-done.16) | copy-start | bytes 1572868
  30.1 1.7 %copy-start.23 = (bf16[256,512]{1,0:T(8,128)(2,1)S(1)}, bf16[256,512]{1,0:T(8,128)(2,1)}, u32[]{:S(2)}) copy-start(bf16[256,512]{1,0:T(8,128)(2,1)} %copy-done.22) | copy-start | bytes 786436
  37.4 7.0 %collective-permute-start.9 = (bf16[256,512]{1,0:T(8,128)(2,1)S(1)}, bf16[256,512]{1,0:T(8,128)(2,1)S(1)}, u32[]{:S(2)}, u32[]{:S(2)}) collective-permute-start(bf16[256,512]{1,0:T(8,128)(2,1)S(1)} %dynamic-slice_convert_fusion), channel_id=1, source_target_pairs={{0,1},{1,0},{2,3},{3,2},{4,5},{5,4},{6,7},{7,6},{8,9},{9,8},{10,11... | collective-permute-start | bytes 786440 | tf_op jit(solution)/shard_map/ppermute | solution.py:507
  39.1 2.1 %collective-permute-start.8 = (bf16[80,1024]{1,0:T(8,128)(2,1)S(1)}, bf16[80,1024]{1,0:T(8,128)(2,1)S(1)}, u32[]{:S(2)}, u32[]{:S(2)}) collective-permute-start(bf16[80,1024]{1,0:T(8,128)(2,1)S(1)} %get-tuple-element.91), channel_id=1, source_target_pairs={{0,1},{1,0},{2,3},{3,2},{4,5},{5,4},{6,7},{7,6},{8,9},{9,8},{10,11... | collective-permute-start | bytes 491528 | tf_op jit(solution)/shard_map/ppermute | solution.py:507
  41.2 3.3 %copy-start.20 = (f32[256,128]{1,0:T(8,128)}, f32[256,128]{1,0:T(8,128)S(1)}, u32[]{:S(2)}) copy-start(f32[256,128]{1,0:T(8,128)S(1)} %get-tuple-element.103.refs_3_) | copy-start | bytes 393220
  41.9 20.0 %collective-permute-start.13 = (bf16[32,1024]{1,0:T(8,128)(2,1)S(1)}, bf16[32,1024]{1,0:T(8,128)(2,1)S(1)}, u32[]{:S(2)}, u32[]{:S(2)}) collective-permute-start(bf16[32,1024]{1,0:T(8,128)(2,1)S(1)} %get-tuple-element.120), channel_id=1, source_target_pairs={{0,30},{1,31},{2,0},{3,1},{4,2},{5,3},{6,4},{7,5},{8,6},{9,7},{10,... | collective-permute-start | bytes 196616 | tf_op jit(solution)/shard_map/ppermute | solution.py:507
  44.4 17.5 %collective-permute-start.14 = (bf16[32,1024]{1,0:T(8,128)(2,1)S(1)}, bf16[32,1024]{1,0:T(8,128)(2,1)S(1)}, u32[]{:S(2)}, u32[]{:S(2)}) collective-permute-start(bf16[32,1024]{1,0:T(8,128)(2,1)S(1)} %get-tuple-element.119), channel_id=1, source_target_pairs={{0,2},{1,3},{2,4},{3,5},{4,6},{5,7},{6,8},{7,9},{8,10},{9,11},{10,... | collective-permute-start | bytes 196616 | tf_op jit(solution)/shard_map/ppermute | solution.py:507
  47.2 14.6 %copy-start.12 = (f32[256,256]{1,0:T(8,128)}, f32[256,256]{1,0:T(8,128)S(1)}, u32[]{:S(2)}) copy-start(f32[256,256]{1,0:T(8,128)S(1)} %get-tuple-element.104.refs_4_) | copy-start | bytes 786436
  47.2 16.8 %copy-start.10 = (f32[256,256]{1,0:T(8,128)}, f32[256,256]{1,0:T(8,128)S(1)}, u32[]{:S(2)}) copy-start(f32[256,256]{1,0:T(8,128)S(1)} %get-tuple-element.101.refs_1_) | copy-start | bytes 786436
  47.3 5.0 %collective-permute-start.10 = (bf16[64,512]{1,0:T(8,128)(2,1)S(1)}, bf16[64,512]{1,0:T(8,128)(2,1)S(1)}, u32[]{:S(2)}, u32[]{:S(2)}) collective-permute-start(bf16[64,512]{1,0:T(8,128)(2,1)S(1)} %get-tuple-element.111), channel_id=1, source_target_pairs={{0,2},{1,3},{2,0},{3,1},{4,6},{5,7},{6,4},{7,5},{8,10},{9,11},{10,... | collective-permute-start | bytes 196616 | tf_op jit(solution)/shard_map/ppermute | solution.py:507
  47.4 6.5 %collective-permute-start.11 = (bf16[64,512]{1,0:T(8,128)(2,1)S(1)}, bf16[64,512]{1,0:T(8,128)(2,1)S(1)}, u32[]{:S(2)}, u32[]{:S(2)}) collective-permute-start(bf16[64,512]{1,0:T(8,128)(2,1)S(1)} %get-tuple-element.113), channel_id=1, source_target_pairs={{0,4},{1,5},{2,6},{3,7},{4,0},{5,1},{6,2},{7,3},{8,12},{9,13},{10,... | collective-permute-start | bytes 196616 | tf_op jit(solution)/shard_map/ppermute | solution.py:507
  50.6 5.5 %collective-permute-start.12 = (bf16[64,512]{1,0:T(8,128)(2,1)S(1)}, bf16[64,512]{1,0:T(8,128)(2,1)S(1)}, u32[]{:S(2)}, u32[]{:S(2)}) collective-permute-start(bf16[64,512]{1,0:T(8,128)(2,1)S(1)} %get-tuple-element.112), channel_id=1, source_target_pairs={{0,6},{1,7},{2,4},{3,5},{4,2},{5,3},{6,0},{7,1},{8,14},{9,15},{10,... | collective-permute-start | bytes 196616 | tf_op jit(solution)/shard_map/ppermute | solution.py:507
  56.1 10.2 %collective-permute-start.20 = (bf16[16,512]{1,0:T(8,128)(2,1)S(1)}, bf16[16,512]{1,0:T(8,128)(2,1)S(1)}, u32[]{:S(2)}, u32[]{:S(2)}) collective-permute-start(bf16[16,512]{1,0:T(8,128)(2,1)S(1)} %get-tuple-element.116), channel_id=1, source_target_pairs={{0,8},{1,9},{2,10},{3,11},{4,12},{5,13},{6,14},{7,15},{8,0},{9,1},... | collective-permute-start | bytes 49160 | tf_op jit(solution)/shard_map/ppermute | solution.py:507
  56.5 9.8 %collective-permute-start.21 = (bf16[16,512]{1,0:T(8,128)(2,1)S(1)}, bf16[16,512]{1,0:T(8,128)(2,1)S(1)}, u32[]{:S(2)}, u32[]{:S(2)}) collective-permute-start(bf16[16,512]{1,0:T(8,128)(2,1)S(1)} %get-tuple-element.118), channel_id=1, source_target_pairs={{0,16},{1,17},{2,18},{3,19},{4,20},{5,21},{6,22},{7,23},{8,24},{9,... | collective-permute-start | bytes 49160 | tf_op jit(solution)/shard_map/ppermute | solution.py:507
  61.9 4.9 %collective-permute-start.22 = (bf16[16,512]{1,0:T(8,128)(2,1)S(1)}, bf16[16,512]{1,0:T(8,128)(2,1)S(1)}, u32[]{:S(2)}, u32[]{:S(2)}) collective-permute-start(bf16[16,512]{1,0:T(8,128)(2,1)S(1)} %get-tuple-element.117), channel_id=1, source_target_pairs={{0,24},{1,25},{2,26},{3,27},{4,28},{5,29},{6,30},{7,31},{8,16},{9,... | collective-permute-start | bytes 49160 | tf_op jit(solution)/shard_map/ppermute | solution.py:507
  65.3 20.4 %collective-permute-start.15 = (bf16[192,1024]{1,0:T(8,128)(2,1)S(1)}, bf16[192,1024]{1,0:T(8,128)(2,1)S(1)}, u32[]{:S(2)}, u32[]{:S(2)}) collective-permute-start(bf16[192,1024]{1,0:T(8,128)(2,1)S(1)} %get-tuple-element.106), channel_id=1, source_target_pairs={{0,31},{1,0},{2,1},{3,2},{4,3},{5,4},{6,5},{7,6},{8,7},{9,8},{10,9... | collective-permute-start | bytes 1179656 | tf_op jit(solution)/shard_map/ppermute | solution.py:507
  66.3 19.4 %collective-permute-start.16 = (bf16[192,1024]{1,0:T(8,128)(2,1)S(1)}, bf16[192,1024]{1,0:T(8,128)(2,1)S(1)}, u32[]{:S(2)}, u32[]{:S(2)}) collective-permute-start(bf16[192,1024]{1,0:T(8,128)(2,1)S(1)} %get-tuple-element.107), channel_id=1, source_target_pairs={{0,1},{1,2},{2,3},{3,4},{4,5},{5,6},{6,7},{7,8},{8,9},{9,10},{10,1... | collective-permute-start | bytes 1179656 | tf_op jit(solution)/shard_map/ppermute | solution.py:507
  67.5 16.2 %all-to-all-start = ((bf16[8,16,512]{2,1,0:T(8,128)(2,1)}), bf16[8,16,512]{2,1,0:T(8,128)(2,1)S(1)}, u32[]{:S(2)}, u32[]{:S(2)}) async-start(bf16[8,16,512]{2,1,0:T(8,128)(2,1)} %broadcast_in_dim.29), calls=%async_computation | async-start | bytes 262144 | tf_op jit(solution)/shard_map/all_to_all | solution.py:648
  76.1 8.2 %collective-permute-start.17 = (bf16[16,1024]{1,0:T(8,128)(2,1)S(1)}, bf16[16,1024]{1,0:T(8,128)(2,1)S(1)}, u32[]{:S(2)}, u32[]{:S(2)}) collective-permute-start(bf16[16,1024]{1,0:T(8,128)(2,1)S(1)} %get-tuple-element.123), channel_id=1, source_target_pairs={{0,28},{1,29},{2,30},{3,31},{4,0},{5,1},{6,2},{7,3},{8,4},{9,5},{1... | collective-permute-start | bytes 98312 | tf_op jit(solution)/shard_map/ppermute | solution.py:507
  78.2 7.5 %collective-permute-start.18 = (bf16[16,1024]{1,0:T(8,128)(2,1)S(1)}, bf16[16,1024]{1,0:T(8,128)(2,1)S(1)}, u32[]{:S(2)}, u32[]{:S(2)}) collective-permute-start(bf16[16,1024]{1,0:T(8,128)(2,1)S(1)} %get-tuple-element.122), channel_id=1, source_target_pairs={{0,4},{1,5},{2,6},{3,7},{4,8},{5,9},{6,10},{7,11},{8,12},{9,13},{1... | collective-permute-start | bytes 98312 | tf_op jit(solution)/shard_map/ppermute | solution.py:507
  79.7 6.0 %collective-permute-start.19 = (bf16[16,1024]{1,0:T(8,128)(2,1)S(1)}, bf16[16,1024]{1,0:T(8,128)(2,1)S(1)}, u32[]{:S(2)}, u32[]{:S(2)}) collective-permute-start(bf16[16,1024]{1,0:T(8,128)(2,1)S(1)} %get-tuple-element.121), channel_id=1, source_target_pairs={{0,6},{1,7},{2,28},{3,29},{4,10},{5,11},{6,0},{7,1},{8,14},{9,15},... | collective-permute-start | bytes 98312 | tf_op jit(solution)/shard_map/ppermute | solution.py:507
  (18 other events, 15.2 us)

commit v3 on v2

--- a/solution.py
+++ b/solution.py
@@ -258,7 +258,7 @@
 
 def merge_kernel(q_all, qdoc, fine, coarse, grad_att, d_out, *refs):
     far = far_refs(refs[:6])
-    attended_out, d_w, p_out, g_out, d_side = refs[6:]
+    attended_out, keep, give, p_out, g_out, d_side, d_w = refs[6:]
     docs = [(docs_of(index, qdoc), far_window(ref, DOC_LANES)) for index, ref in zip(FAR, far)]
     shape = (LANES, LANES)
     same_head = jnp.where(iota(shape, 0) // HEAD_DIM == iota(shape, 1) // HEAD_DIM, 1.0, 0.0)
@@ -316,6 +316,9 @@
             d_side[at : at + rows, cols] = jnp.where(
                 upper, d_high.astype(F32), d_low.astype(F32)
             ).astype(BF16)
+    core = lax.axis_index("ctx") % 2
+    keep[...] = d_w[pl.ds(pl.multiple_of(core * 256, 256), 256)]
+    give[...] = d_w[pl.ds(pl.multiple_of((1 - core) * 256, 256), 256)].astype(BF16)
 
 
 def attend_back(p, queries, grad, side, keys, values):
@@ -448,6 +451,50 @@
     after.wait()
 
 
+def pass_on_kernel(below, above, four_a, four_b, four_c, out):
+    even = lax.axis_index("ctx") % 2 == 0
+    out[0:32] = jnp.where(even, below[...], above[...])
+    for i, ref in enumerate((four_a, four_b, four_c)):
+        out[32 + 16 * i : 48 + 16 * i] = ref[...]
+
+
+def far_sum_kernel(to_3, to_4, swapped, *outs):
+    even = lax.axis_index("ctx") % 2 == 0
+    third = swapped[0:32].astype(F32)
+    outs[0][...] = (to_3[0].astype(F32) + jnp.where(even, third, 0.0)).astype(BF16)
+    outs[1][...] = (to_3[1].astype(F32) + jnp.where(even, 0.0, third)).astype(BF16)
+    for i in range(3):
+        part = swapped[32 + 16 * i : 48 + 16 * i].astype(F32)
+        outs[2 + i][...] = (to_4[i].astype(F32) + part).astype(BF16)
+
+
+def scatter_kernel(low, bits, count, keep, *refs):
+    got, outs = refs[:count], refs[-(1 << bits) - 1 : -1]
+    total = refs[-1]
+    total[...] = functools.reduce(jnp.add, [x[...].astype(F32) for x in got], keep[...])
+    side = (lax.axis_index("ctx") // (1 << low)) % (1 << bits)
+    rows = total.shape[0] >> bits
+    for step, out in enumerate(outs):
+        flipped = side if step == 0 else side + step - 2 * sum(
+            (side // (1 << bit) % 2) * (1 << bit) for bit in range(bits) if step >> bit & 1
+        )
+        part = total[pl.ds(pl.multiple_of(flipped * rows, rows), rows)]
+        out[...] = part if step == 0 else part.astype(BF16)
+
+
+def copies_kernel(keep, *refs):
+    total = functools.reduce(jnp.add, [x[...].astype(F32) for x in refs[:3]], keep[...])
+    for i in range(refs[-1].shape[0]):
+        refs[-1][i] = total.astype(BF16)
+
+
+def last_sum_kernel(parts, out):
+    total = parts[0].astype(F32)
+    for i in range(1, parts.shape[0]):
+        total = total + parts[i].astype(F32)
+    out[...] = total.astype(BF16)
+
+
 def combine_kernel(*refs):
     own, (low, high), from3, from4 = (refs[0:3], refs[3:6]), refs[6:8], refs[8:10], refs[10:13]
     d_k_hbm, d_v_hbm, d_k, d_v, sems = refs[13:]
@@ -521,26 +568,15 @@
 BACK_4 = (lambda i: i - 4, lambda i: i + 4, third)
 
 
-def scattered(y, low, bits, after=None):
-    side, count = lax.axis_index("ctx") >> low & (1 << bits) - 1, 1 << bits
-    rows = y.shape[0] // count
-
-    def part(index):
-        return lax.dynamic_slice_in_dim(y, index * rows, rows)
-
-    result = part(side)
-    if after is not None:
-        result, _ = lax.optimization_barrier((result, after))
-    for step in range(1, count):
-        message = part(side ^ step).astype(BF16)
-        result = result + moved(message, lambda i, step=step: i ^ step << low).astype(F32)
-    return result
+def messages(parts, low):
+    return [
+        moved(part, lambda i, step=step: i ^ step << low) for step, part in enumerate(parts, 1)
+    ]
 
 
 def body(queries, key_rows, value_rows, segment_ids, w_out, d_out):
     q, k, v, grad_out = queries[0], key_rows[0], value_rows[0], d_out[0]
     tokens, dma = (ROWS, WIDTH), pltpu.SemaphoreType.DMA
-    even = lax.axis_index("ctx") % 2 == 0
     up, down, far3, far4, own0, own1, qdoc = call(
         coarsen_kernel,
         "coarsen",
@@ -564,8 +600,7 @@
     got3 = [moved(far3, route) for route in ROUTES_3]
     got4 = [moved(far4, route) for route in ROUTES_4]
     low, high, *got3 = lax.optimization_barrier((low, high, *got3))
-    passed = jnp.concatenate([jnp.where(even, got3[0], got3[1]), *got4], axis=0)
-    low, high, passed = lax.optimization_barrier((low, high, passed))
+    passed = call(pass_on_kernel, "pass_on", [((80, PACK), BF16)], [*got3, *got4])[0]
     far = (*got3, *got4, moved(passed, partner))
     near = (own0, own1, low, high)
     p_near, fine, coarse = call(
@@ -579,14 +614,17 @@
         [q_all, qdoc, *near],
         microseconds=50,
     )
-    attended, d_w, p_far, g, d_side = call(
+    attended, keep, give, p_far, g, d_side = call(
         merge_kernel,
         "merge",
-        [(tokens, BF16), ((WIDTH, WIDTH), F32), ((PAIRS, P_FAR, LANES), BF16)]
+        [(tokens, BF16), ((256, WIDTH), F32), ((256, WIDTH), BF16)]
+        + [((PAIRS, P_FAR, LANES), BF16)]
         + [((ALL_ROWS, WIDTH), BF16)] * 2,
         [q_all, qdoc, fine, coarse, grad_att, grad_rows, *far],
+        [pltpu.VMEM((WIDTH, WIDTH), F32)],
         microseconds=6,
     )
+    got_w = moved(give, partner)
     d_far, to_3, to_4, to_partner = call(
         far_back_kernel,
         "far_back",
@@ -594,12 +632,7 @@
         + [((3, 16, 2 * WIDTH), BF16), ((80, 2 * WIDTH), BF16)],
         [p_far, q_all, g, d_side, *far],
     )
-    d_w = scattered(d_w, 0, 1)
-    from_partner = moved(to_partner, partner).astype(F32)
-    swapped3, swapped4 = from_partner[:32], from_partner[32:].reshape(3, 16, 2 * WIDTH)
-    mine = jnp.stack([jnp.where(even, swapped3, 0), jnp.where(even, 0, swapped3)])
-    to_3 = (to_3.astype(F32) + mine).astype(BF16)
-    to_4 = (to_4.astype(F32) + swapped4).astype(BF16)
+    swapped = moved(to_partner, partner)
 
     def part_outs(part):
         width = len(NEAR_PARTS[part]) * LANES
@@ -617,41 +650,68 @@
         microseconds=3,
         to_hbm=(5,),
     )
+    far_sums = call(
+        far_sum_kernel,
+        "far_sum",
+        [((32, 2 * WIDTH), BF16)] * 2 + [((16, 2 * WIDTH), BF16)] * 3,
+        [to_3, to_4, swapped],
+    )
+    keep, *parts = call(
+        functools.partial(scatter_kernel, 1, 2, 1),
+        "scatter_y",
+        [((64, WIDTH), F32)] + [((64, WIDTH), BF16)] * 3,
+        [keep, got_w],
+        [pltpu.VMEM((256, WIDTH), F32)],
+    )
+    got_w = messages(parts, 1)
+    back = [moved(x, route) for x, route in zip(far_sums[:2], BACK_3)]
     part_b = call(
         near_back_b_kernel,
         "near_back_b",
         part_outs(1),
-        [*args, part_a[0], to_3, d_w],
+        [*args, part_a[0], far_sums[0], keep],
         in_hbm=3,
         microseconds=4,
     )
-    back = [moved(to_3[i], route) for i, route in enumerate(BACK_3)]
-    d_w = scattered(d_w, 1, 2, after=part_b[0])
-    to_4, _ = lax.optimization_barrier((to_4, part_b[0]))
+    keep, *parts = call(
+        functools.partial(scatter_kernel, 3, 2, 3),
+        "scatter_x",
+        [((16, WIDTH), F32)] + [((16, WIDTH), BF16)] * 3,
+        [keep, *got_w, part_b[0]],
+        [pltpu.VMEM((64, WIDTH), F32)],
+        in_hbm=1,
+    )
+    got_w = messages(parts, 3)
+    to_4, _ = lax.optimization_barrier((far_sums[2:], part_b[0]))
+    back_4 = [moved(x, route) for x, route in zip(to_4, BACK_4)]
     d_q, own_k, own_v, to_low, to_high = call(
         near_back_c_kernel,
         "near_back_c",
         [(tokens, BF16), ((ROWS, LANES), F32), ((ROWS, LANES), F32)]
         + [((192, 2 * WIDTH), BF16)] * 2,
-        [*args, part_a[0], *part_a[3:], part_b[0], *part_b[3:], to_4, d_w, *back],
+        [*args, part_a[0], *part_a[3:], part_b[0], *part_b[3:], to_4[0], keep, *back],
         [pltpu.VMEM(tokens, BF16), dma((2,))],
         in_hbm=4,
         microseconds=2,
         to_hbm=(0,),
     )
-    back += [moved(to_4[i], route) for i, route in enumerate(BACK_4)]
-    d_w = scattered(d_w, 3, 2, after=to_low)
     low_back = moved(to_low, lambda i: i - 1)
     high_back = moved(to_high, lambda i: i + 1)
-    dp_count = lax.axis_size("dp")
-    copies = jnp.broadcast_to(d_w.astype(BF16)[None], (dp_count,) + d_w.shape)
+    copies = call(
+        copies_kernel,
+        "copies",
+        [((lax.axis_size("dp"), 16, WIDTH), BF16)],
+        [keep, *got_w, to_low],
+        in_hbm=1,
+    )[0]
     copies = lax.all_to_all(copies, "dp", 0, 0, tiled=True)
-    d_w = jnp.sum(copies.astype(F32), axis=0).astype(BF16)
+    d_w = call(last_sum_kernel, "last_sum", [((16, WIDTH), BF16)], [copies])[0]
     d_k, d_v = call(
         combine_kernel,
         "combine",
         [(tokens, BF16)] * 2,
-        [part_a[1], part_b[1], own_k, part_a[2], part_b[2], own_v, low_back, high_back, *back],
+        [part_a[1], part_b[1], own_k, part_a[2], part_b[2], own_v, low_back, high_back]
+        + [*back, *back_4],
         [pltpu.VMEM(tokens, BF16)] * 2 + [dma((2,))],
         to_hbm=(0, 1),
     )

time: 93.5 us -> 84.1 us (0.90)
  local copies, waits for them, and re-layouts: 14.6 us -> 2.58 us
  starting transfers between devices: 41.7 us -> 46.1 us
  Pallas kernels: 17.7 us -> 19.4 us
  waiting for transfers between devices: 16.4 us -> 14.8 us
    unnamed x52 -> x12, local copies, waits for them, and re-layouts: 13.8 us -> 2.58 us
    ppermute x23, starting transfers between devices: 33.2 us -> 37.5 us  [moved(): return lax.ppermute(x, 'ctx', [(i, route(i) % count) for i in range(count)])]
    ppermute x23, waiting for transfers between devices: 13.4 us -> 11 us  [moved(): return lax.ppermute(x, 'ctx', [(i, route(i) % count) for i in range(count)])]
    pallas_call x9 -> x15, Pallas kernels: 17.7 us -> 19.4 us  [call(): pl.pallas_call(kernel, name=name, out_shape=[jax.ShapeDtypeStruct(shape,...]
  transfers between devices with their start and end apart: 24 -> 24, of which waited for: 10 -> 5; matrix products, arithmetic and copies ran while one was open for 2% -> 0% of each run, Pallas kernels for 11% -> 13%
where the time goes in v3:
time: 84.1 us; the launch traced here: 83.9 us
  starting transfers between devices  46.1 us (55%)
  Pallas kernels  19.4 us (23%)
  waiting for transfers between devices  14.8 us (18%)
  local copies, waits for them, and re-layouts  2.58 us (3%)
  between operations  1.01 us (1%)
    ppermute x23, starting transfers between devices, moved(): return lax.ppermute(x, 'ctx', [(i, route(i) % count) for i in range(count)])  37.5 us
    pallas_call x15, Pallas kernels, call(): pl.pallas_call(kernel, name=name, out_shape=[jax.ShapeDtypeStruct(shape,...  19.4 us
    ppermute x23, waiting for transfers between devices, moved(): return lax.ppermute(x, 'ctx', [(i, route(i) % count) for i in range(count)])  11 us
    all_to_all x1, starting transfers between devices, body(): copies = lax.all_to_all(copies, 'dp', 0, 0, tiled=True)  8.58 us
    all_to_all x1, waiting for transfers between devices, body(): copies = lax.all_to_all(copies, 'dp', 0, 0, tiled=True)  3.77 us
    unnamed x12, local copies, waits for them, and re-layouts  2.58 us
  transfers between devices with their start and end apart: 24, of which 5 were waited for; matrix products, arithmetic and copies ran while one was open for 0% of the time, Pallas kernels for 13%

profile of v3, /device:TPU:32, one launch (start us, length us, event | category | flops | bytes accessed | tf_op | source)
XLA Modules:
  0.0 83.9 jit_solution(6629180459882130731)
XLA Ops:
  0.6 0.9 %copy-done.1 = bf16[1,256,512]{2,1,0:T(8,128)(2,1)S(1)} copy-done((bf16[1,256,512]{2,1,0:T(8,128)(2,1)S(1)}, bf16[1,256,512]{2,1,0:T(8,128)(2,1)}, u32[]{:S(2)}) %copy-start.1) | copy-done | bytes 262168
  1.6 0.9 %copy-done.2 = bf16[1,256,512]{2,1,0:T(8,128)(2,1)S(1)} copy-done((bf16[1,256,512]{2,1,0:T(8,128)(2,1)S(1)}, bf16[1,256,512]{2,1,0:T(8,128)(2,1)}, u32[]{:S(2)}) %copy-start.2) | copy-done | bytes 262168
  2.5 0.7 copy-done.5
  3.2 0.7 coarsen.1
  4.0 5.1 %collective-permute-start.1 = (bf16[192,1152]{1,0:T(8,128)(2,1)S(1)}, bf16[192,1152]{1,0:T(8,128)(2,1)S(1)}, u32[]{:S(2)}, u32[]{:S(2)}) collective-permute-start(bf16[192,1152]{1,0:T(8,128)(2,1)S(1)} %get-tuple-element.76), channel_id=1, source_target_pairs={{0,31},{1,0},{2,1},{3,2},{4,3},{5,4},{6,5},{7,6},{8,7},{9,8},{10,9... | collective-permute-start | bytes 1327112 | tf_op jit(solution)/shard_map/ppermute | solution.py:554
  9.1 0.7 prepare.1
  9.8 2.0 %collective-permute-start.3 = (bf16[32,1152]{1,0:T(8,128)(2,1)S(1)}, bf16[32,1152]{1,0:T(8,128)(2,1)S(1)}, u32[]{:S(2)}, u32[]{:S(2)}) collective-permute-start(bf16[32,1152]{1,0:T(8,128)(2,1)S(1)} %get-tuple-element.77), channel_id=1, source_target_pairs={{0,30},{1,31},{2,0},{3,1},{4,2},{5,3},{6,4},{7,5},{8,6},{9,7},{10,... | collective-permute-start | bytes 221192 | tf_op jit(solution)/shard_map/ppermute | solution.py:554
  11.9 1.8 %collective-permute-start.6 = (bf16[16,1152]{1,0:T(8,128)(2,1)S(1)}, bf16[16,1152]{1,0:T(8,128)(2,1)S(1)}, u32[]{:S(2)}, u32[]{:S(2)}) collective-permute-start(bf16[16,1152]{1,0:T(8,128)(2,1)S(1)} %get-tuple-element.86), channel_id=1, source_target_pairs={{0,6},{1,7},{2,28},{3,29},{4,10},{5,11},{6,0},{7,1},{8,14},{9,15},... | collective-permute-start | bytes 110600 | tf_op jit(solution)/shard_map/ppermute | solution.py:554
  13.7 3.1 %collective-permute-done.3.above.refs_1_ = bf16[32,1152]{1,0:T(8,128)(2,1)S(1)} collective-permute-done((bf16[32,1152]{1,0:T(8,128)(2,1)S(1)}, bf16[32,1152]{1,0:T(8,128)(2,1)S(1)}, u32[]{:S(2)}, u32[]{:S(2)}) %collective-permute-start.3) | collective-permute-done | bytes 73760 | tf_op jit(solution)/shard_map/ppermute | solution.py:554
  16.9 3.4 %collective-permute-start.5 = (bf16[16,1152]{1,0:T(8,128)(2,1)S(1)}, bf16[16,1152]{1,0:T(8,128)(2,1)S(1)}, u32[]{:S(2)}, u32[]{:S(2)}) collective-permute-start(bf16[16,1152]{1,0:T(8,128)(2,1)S(1)} %get-tuple-element.86), channel_id=1, source_target_pairs={{0,28},{1,29},{2,30},{3,31},{4,0},{5,1},{6,2},{7,3},{8,4},{9,5},{1... | collective-permute-start | bytes 110600 | tf_op jit(solution)/shard_map/ppermute | solution.py:554
  20.4 1.9 %collective-permute-done.5.four_b.refs_3_ = bf16[16,1152]{1,0:T(8,128)(2,1)S(1)} collective-permute-done((bf16[16,1152]{1,0:T(8,128)(2,1)S(1)}, bf16[16,1152]{1,0:T(8,128)(2,1)S(1)}, u32[]{:S(2)}, u32[]{:S(2)}) %collective-permute-start.5) | collective-permute-done | bytes 36896 | tf_op jit(solution)/shard_map/ppermute | solution.py:554
  22.3 5.5 %collective-permute-done.4.four_a.refs_2_ = bf16[16,1152]{1,0:T(8,128)(2,1)S(1)} collective-permute-done((bf16[16,1152]{1,0:T(8,128)(2,1)S(1)}, bf16[16,1152]{1,0:T(8,128)(2,1)S(1)}, u32[]{:S(2)}, u32[]{:S(2)}) %collective-permute-start.4) | collective-permute-done | bytes 36896 | tf_op jit(solution)/shard_map/ppermute | solution.py:554
  28.2 1.7 %near.1 = (bf16[4,896,256]{2,1,0:T(8,128)(2,1)S(1)}, f32[4,256,384]{2,1,0:T(8,128)S(1)}, bf16[4,192,384]{2,1,0:T(8,128)(2,1)S(1)}) custom-call(bf16[496,512]{1,0:T(8,128)(2,1)S(1)} %get-tuple-element.71.q_all.refs_1_, bf16[496,128]{1,0:T(8,128)(2,1)S(1)} %get-tuple-element.72.qdoc, bf16[256,1152]{1,0:T(8,128)(2,1)S(1)} %get-tuple-element.73.own0.refs_4_, ...), custom_call_target="tpu_custom_call" | custom-call | flops 49999998976 | bytes 1048576 | tf_op jit(solution)/shard_map/near/pallas_call | solution.py:538
  29.9 5.7 %merge.1 = (bf16[256,512]{1,0:T(8,128)(2,1)S(1)}, f32[256,512]{1,0:T(8,128)S(1)}, bf16[256,512]{1,0:T(8,128)(2,1)S(1)}, bf16[4,96,128]{2,1,0:T(8,128)(2,1)S(1)},...) custom-call(bf16[496,512]{1,0:T(8,128)(2,1)S(1)} %get-tuple-element.71.q_all.refs_1_, ...), custom_call_target="tpu_custom_call" | custom-call | flops 6000000000 | bytes 1048576 | tf_op jit(solution)/shard_map/merge/pallas_call | solution.py:538
  35.6 1.1 %far_back.1 = (bf16[48,512]{1,0:T(8,128)(2,1)S(1)}, bf16[2,32,1024]{2,1,0:T(8,128)(2,1)S(1)}, bf16[3,16,1024]{2,1,0:T(8,128)(2,1)S(1)}, bf16[80,1024]{1,0:T(8,128)(2,1)S(1)}) custom-call(bf16[4,96,128]{2,1,0:T(8,128)(2,1)S(1)} %get-tuple-element.92.p_in, bf16[496,512]{1,0:T(8,128)(2,1)S(1)} %get-tuple-element.71.q_all.refs_1_, ...), custom_call_target="tpu_custom_call" | custom-call | flops 1000000000 | bytes 1048576 | tf_op jit(solution)/shard_map/far_back/pallas_call | solution.py:538
  36.7 0.6 collective-permute-start.8
  37.4 2.0 %near_back_a.1 = (bf16[256,128]{1,0:T(8,128)(2,1)S(1)}, f32[256,128]{1,0:T(8,128)S(1)}, f32[256,128]{1,0:T(8,128)S(1)}, bf16[2,192,128]{2,1,0:T(8,128)(2,1)S(1)}...) custom-call(bf16[256,512]{1,0:T(8,128)(2,1)S(1)} %get-tuple-element.87.attended, ...), custom_call_target="tpu_custom_call" | custom-call | flops 3000000000 | bytes 1048576 | tf_op jit(solution)/shard_map/near_back_a/pallas_call | solution.py:538
  39.5 3.4 %collective-permute-start.14 = (bf16[32,1024]{1,0:T(8,128)(2,1)S(1)}, bf16[32,1024]{1,0:T(8,128)(2,1)S(1)}, u32[]{:S(2)}, u32[]{:S(2)}) collective-permute-start(bf16[32,1024]{1,0:T(8,128)(2,1)S(1)} %get-tuple-element.116), channel_id=1, source_target_pairs={{0,2},{1,3},{2,4},{3,5},{4,6},{5,7},{6,8},{7,9},{8,10},{9,11},{10,... | collective-permute-start | bytes 196616 | tf_op jit(solution)/shard_map/ppermute | solution.py:554
  42.9 2.0 %collective-permute-start.13 = (bf16[32,1024]{1,0:T(8,128)(2,1)S(1)}, bf16[32,1024]{1,0:T(8,128)(2,1)S(1)}, u32[]{:S(2)}, u32[]{:S(2)}) collective-permute-start(bf16[32,1024]{1,0:T(8,128)(2,1)S(1)} %get-tuple-element.101.refs_10_), channel_id=1, source_target_pairs={{0,30},{1,31},{2,0},{3,1},{4,2},{5,3},{6,4},{7,5},{8,6},{9,7},{10,... | collective-permute-start | bytes 196616 | tf_op jit(solution)/shard_map/ppermute | solution.py:554
  45.3 4.5 %collective-permute-start.12 = (bf16[64,512]{1,0:T(8,128)(2,1)S(1)}, bf16[64,512]{1,0:T(8,128)(2,1)S(1)}, u32[]{:S(2)}, u32[]{:S(2)}) collective-permute-start(bf16[64,512]{1,0:T(8,128)(2,1)S(1)} %get-tuple-element.114), channel_id=1, source_target_pairs={{0,6},{1,7},{2,4},{3,5},{4,2},{5,3},{6,0},{7,1},{8,14},{9,15},{10,... | collective-permute-start | bytes 196616 | tf_op jit(solution)/shard_map/ppermute | solution.py:554
  49.8 2.7 %near_back_b.1 = (bf16[256,256]{1,0:T(8,128)(2,1)S(1)}, f32[256,256]{1,0:T(8,128)S(1)}, f32[256,256]{1,0:T(8,128)S(1)}, bf16[2,192,256]{2,1,0:T(8,128)(2,1)S(1)}, bf16[2,192,256]{2,1,0:T(8,128)(2,1)S(1)}) custom-call(bf16[4,896,256]{2,1,0:T(8,128)(2,1)S(1)} %get-tuple-element.89.refs_0_, bf16[496,512]{1,0:T(8,128)(2,1)S(1)} %get-tuple-element.71.q_all.refs_1_, ...), custom_call_target="tpu_custom_call" | custom-call | flops 4000000000 | bytes 1048576 | tf_op jit(solution)/shard_map/near_back_b/pallas_call | solution.py:538
  52.7 1.5 %collective-permute-start.21 = (bf16[16,512]{1,0:T(8,128)(2,1)S(1)}, bf16[16,512]{1,0:T(8,128)(2,1)S(1)}, u32[]{:S(2)}, u32[]{:S(2)}) collective-permute-start(bf16[16,512]{1,0:T(8,128)(2,1)S(1)} %get-tuple-element.131), channel_id=1, source_target_pairs={{0,16},{1,17},{2,18},{3,19},{4,20},{5,21},{6,22},{7,23},{8,24},{9,... | collective-permute-start | bytes 49160 | tf_op jit(solution)/shard_map/ppermute | solution.py:554
  54.2 3.2 %collective-permute-start.22 = (bf16[16,512]{1,0:T(8,128)(2,1)S(1)}, bf16[16,512]{1,0:T(8,128)(2,1)S(1)}, u32[]{:S(2)}, u32[]{:S(2)}) collective-permute-start(bf16[16,512]{1,0:T(8,128)(2,1)S(1)} %get-tuple-element.132), channel_id=1, source_target_pairs={{0,24},{1,25},{2,26},{3,27},{4,28},{5,29},{6,30},{7,31},{8,16},{9,... | collective-permute-start | bytes 49160 | tf_op jit(solution)/shard_map/ppermute | solution.py:554
  57.4 2.1 %near_back_c.1 = (bf16[256,512]{1,0:T(8,128)(2,1)}, f32[256,128]{1,0:T(8,128)S(1)}, f32[256,128]{1,0:T(8,128)S(1)}, bf16[192,1024]{1,0:T(8,128)(2,1)S(1)}, bf16[192,1024]{1,0:T(8,128)(2,1)S(1)}) custom-call(bf16[4,896,256]{2,1,0:T(8,128)(2,1)S(1)} %get-tuple-element.89.refs_0_, bf16[496,512]{1,0:T(8,128)(2,1)S(1)} %get-tuple-element.71.q_all.refs_1_, ...), custom_call_target="tpu_custom_call" | custom-call | flops 2000000000 | bytes 1048576 | tf_op jit(solution)/shard_map/near_back_c/pallas_call | solution.py:538
  59.6 5.1 %collective-permute-start.15 = (bf16[192,1024]{1,0:T(8,128)(2,1)S(1)}, bf16[192,1024]{1,0:T(8,128)(2,1)S(1)}, u32[]{:S(2)}, u32[]{:S(2)}) collective-permute-start(bf16[192,1024]{1,0:T(8,128)(2,1)S(1)} %get-tuple-element.124.refs_3_), channel_id=1, source_target_pairs={{0,31},{1,0},{2,1},{3,2},{4,3},{5,4},{6,5},{7,6},{8,7},{9,8},{10,9... | collective-permute-start | bytes 1179656 | tf_op jit(solution)/shard_map/ppermute | solution.py:554
  64.7 0.7 copies.1
  65.3 8.6 %all-to-all-start = ((bf16[8,16,512]{2,1,0:T(8,128)(2,1)}), bf16[8,16,512]{2,1,0:T(8,128)(2,1)S(1)}, u32[]{:S(2)}, u32[]{:S(2)}) async-start(bf16[8,16,512]{2,1,0:T(8,128)(2,1)} %copies.1), calls=%async_computation | async-start | bytes 262144 | tf_op jit(solution)/shard_map/all_to_all | solution.py:707
  73.9 3.5 %collective-permute-start.18 = (bf16[16,1024]{1,0:T(8,128)(2,1)S(1)}, bf16[16,1024]{1,0:T(8,128)(2,1)S(1)}, u32[]{:S(2)}, u32[]{:S(2)}) collective-permute-start(bf16[16,1024]{1,0:T(8,128)(2,1)S(1)} %get-tuple-element.126), channel_id=1, source_target_pairs={{0,4},{1,5},{2,6},{3,7},{4,8},{5,9},{6,10},{7,11},{8,12},{9,13},{1... | collective-permute-start | bytes 98312 | tf_op jit(solution)/shard_map/ppermute | solution.py:554
  77.8 3.8 %all-to-all-done.parts = bf16[8,16,512]{2,1,0:T(8,128)(2,1)S(1)} async-done(((bf16[8,16,512]{2,1,0:T(8,128)(2,1)}), bf16[8,16,512]{2,1,0:T(8,128)(2,1)S(1)}, u32[]{:S(2)}, u32[]{:S(2)}) %all-to-all-start) | async-done | bytes 131104 | tf_op jit(solution)/shard_map/all_to_all | solution.py:707
  81.5 0.6 last_sum.1
  82.2 0.4 collective-permute-done.19.refs_12_
  82.6 1.1 %combine.1 = (bf16[256,512]{1,0:T(8,128)(2,1)}, bf16[256,512]{1,0:T(8,128)(2,1)}) custom-call(f32[256,128]{1,0:T(8,128)S(1)} %get-tuple-element.118.refs_0_, f32[256,256]{1,0:T(8,128)S(1)} %get-tuple-element.119.refs_1_, f32[256,128]{1,0:T(8,128)S(1)} %get-tuple-element.120.refs_2_, f32[256,128]{1,0:T(8,128)S(1)} %get-tuple-element.121.refs_3_, ...), custom_call_target="tpu_custom_call" | custom-call | flops 1000000000 | bytes 1048576 | tf_op jit(solution)/shard_map/combine/pallas_call | solution.py:538
  (43 shorter events, 1.8 us)
Async XLA Ops:
  0.6 1.0 %copy-start.1 = (bf16[1,256,512]{2,1,0:T(8,128)(2,1)S(1)}, bf16[1,256,512]{2,1,0:T(8,128)(2,1)}, u32[]{:S(2)}) copy-start(bf16[1,256,512]{2,1,0:T(8,128)(2,1)} %param.7) | copy-start | bytes 786436
  1.6 0.9 %copy-start.2 = (bf16[1,256,512]{2,1,0:T(8,128)(2,1)S(1)}, bf16[1,256,512]{2,1,0:T(8,128)(2,1)}, u32[]{:S(2)}) copy-start(bf16[1,256,512]{2,1,0:T(8,128)(2,1)} %param.8) | copy-start | bytes 786436
  2.5 0.7 copy-start.5
  3.2 5.9 %copy-start = (bf16[512,512]{1,0:T(8,128)(2,1)S(1)}, bf16[512,512]{1,0:T(8,128)(2,1)}, u32[]{:S(2)}) copy-start(bf16[512,512]{1,0:T(8,128)(2,1)} %w_hbm.1) | copy-start | bytes 1572868
  3.2 5.9 %copy-start.3 = (bf16[1,256,512]{2,1,0:T(8,128)(2,1)S(1)}, bf16[1,256,512]{2,1,0:T(8,128)(2,1)}, u32[]{:S(2)}) copy-start(bf16[1,256,512]{2,1,0:T(8,128)(2,1)} %param.6) | copy-start | bytes 786436
  3.2 5.9 %copy-start.4 = (bf16[1,256,512]{2,1,0:T(8,128)(2,1)S(1)}, bf16[1,256,512]{2,1,0:T(8,128)(2,1)}, u32[]{:S(2)}) copy-start(bf16[1,256,512]{2,1,0:T(8,128)(2,1)} %param.11) | copy-start | bytes 786436
  3.9 16.5 %collective-permute-start = (bf16[192,1152]{1,0:T(8,128)(2,1)S(1)}, bf16[192,1152]{1,0:T(8,128)(2,1)S(1)}, u32[]{:S(2)}, u32[]{:S(2)}) collective-permute-start(bf16[192,1152]{1,0:T(8,128)(2,1)S(1)} %get-tuple-element.75), channel_id=1, source_target_pairs={{0,1},{1,2},{2,3},{3,4},{4,5},{5,6},{6,7},{7,8},{8,9},{9,10},{10,1... | collective-permute-start | bytes 1327112 | tf_op jit(solution)/shard_map/ppermute | solution.py:554
  4.0 16.4 %collective-permute-start.1 = (bf16[192,1152]{1,0:T(8,128)(2,1)S(1)}, bf16[192,1152]{1,0:T(8,128)(2,1)S(1)}, u32[]{:S(2)}, u32[]{:S(2)}) collective-permute-start(bf16[192,1152]{1,0:T(8,128)(2,1)S(1)} %get-tuple-element.76), channel_id=1, source_target_pairs={{0,31},{1,0},{2,1},{3,2},{4,3},{5,4},{6,5},{7,6},{8,7},{9,8},{10,9... | collective-permute-start | bytes 1327112 | tf_op jit(solution)/shard_map/ppermute | solution.py:554
  9.8 7.0 %collective-permute-start.3 = (bf16[32,1152]{1,0:T(8,128)(2,1)S(1)}, bf16[32,1152]{1,0:T(8,128)(2,1)S(1)}, u32[]{:S(2)}, u32[]{:S(2)}) collective-permute-start(bf16[32,1152]{1,0:T(8,128)(2,1)S(1)} %get-tuple-element.77), channel_id=1, source_target_pairs={{0,30},{1,31},{2,0},{3,1},{4,2},{5,3},{6,4},{7,5},{8,6},{9,7},{10,... | collective-permute-start | bytes 221192 | tf_op jit(solution)/shard_map/ppermute | solution.py:554
  11.8 8.5 %collective-permute-start.2 = (bf16[32,1152]{1,0:T(8,128)(2,1)S(1)}, bf16[32,1152]{1,0:T(8,128)(2,1)S(1)}, u32[]{:S(2)}, u32[]{:S(2)}) collective-permute-start(bf16[32,1152]{1,0:T(8,128)(2,1)S(1)} %get-tuple-element.77), channel_id=1, source_target_pairs={{0,2},{1,3},{2,4},{3,5},{4,6},{5,7},{6,8},{7,9},{8,10},{9,11},{10,... | collective-permute-start | bytes 221192 | tf_op jit(solution)/shard_map/ppermute | solution.py:554
  11.9 8.5 %collective-permute-start.6 = (bf16[16,1152]{1,0:T(8,128)(2,1)S(1)}, bf16[16,1152]{1,0:T(8,128)(2,1)S(1)}, u32[]{:S(2)}, u32[]{:S(2)}) collective-permute-start(bf16[16,1152]{1,0:T(8,128)(2,1)S(1)} %get-tuple-element.86), channel_id=1, source_target_pairs={{0,6},{1,7},{2,28},{3,29},{4,10},{5,11},{6,0},{7,1},{8,14},{9,15},... | collective-permute-start | bytes 110600 | tf_op jit(solution)/shard_map/ppermute | solution.py:554
  16.9 5.5 %collective-permute-start.5 = (bf16[16,1152]{1,0:T(8,128)(2,1)S(1)}, bf16[16,1152]{1,0:T(8,128)(2,1)S(1)}, u32[]{:S(2)}, u32[]{:S(2)}) collective-permute-start(bf16[16,1152]{1,0:T(8,128)(2,1)S(1)} %get-tuple-element.86), channel_id=1, source_target_pairs={{0,28},{1,29},{2,30},{3,31},{4,0},{5,1},{6,2},{7,3},{8,4},{9,5},{1... | collective-permute-start | bytes 110600 | tf_op jit(solution)/shard_map/ppermute | solution.py:554
  20.3 7.6 %collective-permute-start.4 = (bf16[16,1152]{1,0:T(8,128)(2,1)S(1)}, bf16[16,1152]{1,0:T(8,128)(2,1)S(1)}, u32[]{:S(2)}, u32[]{:S(2)}) collective-permute-start(bf16[16,1152]{1,0:T(8,128)(2,1)S(1)} %get-tuple-element.86), channel_id=1, source_target_pairs={{0,4},{1,5},{2,6},{3,7},{4,8},{5,9},{6,10},{7,11},{8,12},{9,13},{1... | collective-permute-start | bytes 110600 | tf_op jit(solution)/shard_map/ppermute | solution.py:554
  27.9 2.0 %collective-permute-start.7 = (bf16[80,1152]{1,0:T(8,128)(2,1)S(1)}, bf16[80,1152]{1,0:T(8,128)(2,1)S(1)}, u32[]{:S(2)}, u32[]{:S(2)}) collective-permute-start(bf16[80,1152]{1,0:T(8,128)(2,1)S(1)} %pass_on.1), channel_id=1, source_target_pairs={{0,1},{1,0},{2,3},{3,2},{4,5},{5,4},{6,7},{7,6},{8,9},{9,8},{10,11... | collective-permute-start | bytes 552968 | tf_op jit(solution)/shard_map/ppermute | solution.py:554
  36.7 2.7 %collective-permute-start.8 = (bf16[80,1024]{1,0:T(8,128)(2,1)S(1)}, bf16[80,1024]{1,0:T(8,128)(2,1)S(1)}, u32[]{:S(2)}, u32[]{:S(2)}) collective-permute-start(bf16[80,1024]{1,0:T(8,128)(2,1)S(1)} %get-tuple-element.100), channel_id=1, source_target_pairs={{0,1},{1,0},{2,3},{3,2},{4,5},{5,4},{6,7},{7,6},{8,9},{9,8},{10,11... | collective-permute-start | bytes 491528 | tf_op jit(solution)/shard_map/ppermute | solution.py:554
  37.3 7.6 %collective-permute-start.9 = (bf16[256,512]{1,0:T(8,128)(2,1)S(1)}, bf16[256,512]{1,0:T(8,128)(2,1)S(1)}, u32[]{:S(2)}, u32[]{:S(2)}) collective-permute-start(bf16[256,512]{1,0:T(8,128)(2,1)S(1)} %get-tuple-element.103), channel_id=1, source_target_pairs={{0,1},{1,0},{2,3},{3,2},{4,5},{5,4},{6,7},{7,6},{8,9},{9,8},{10,11... | collective-permute-start | bytes 786440 | tf_op jit(solution)/shard_map/ppermute | solution.py:554
  39.5 17.9 %collective-permute-start.14 = (bf16[32,1024]{1,0:T(8,128)(2,1)S(1)}, bf16[32,1024]{1,0:T(8,128)(2,1)S(1)}, u32[]{:S(2)}, u32[]{:S(2)}) collective-permute-start(bf16[32,1024]{1,0:T(8,128)(2,1)S(1)} %get-tuple-element.116), channel_id=1, source_target_pairs={{0,2},{1,3},{2,4},{3,5},{4,6},{5,7},{6,8},{7,9},{8,10},{9,11},{10,... | collective-permute-start | bytes 196616 | tf_op jit(solution)/shard_map/ppermute | solution.py:554
  42.9 14.5 %collective-permute-start.13 = (bf16[32,1024]{1,0:T(8,128)(2,1)S(1)}, bf16[32,1024]{1,0:T(8,128)(2,1)S(1)}, u32[]{:S(2)}, u32[]{:S(2)}) collective-permute-start(bf16[32,1024]{1,0:T(8,128)(2,1)S(1)} %get-tuple-element.101.refs_10_), channel_id=1, source_target_pairs={{0,30},{1,31},{2,0},{3,1},{4,2},{5,3},{6,4},{7,5},{8,6},{9,7},{10,... | collective-permute-start | bytes 196616 | tf_op jit(solution)/shard_map/ppermute | solution.py:554
  45.0 7.5 %collective-permute-start.10 = (bf16[64,512]{1,0:T(8,128)(2,1)S(1)}, bf16[64,512]{1,0:T(8,128)(2,1)S(1)}, u32[]{:S(2)}, u32[]{:S(2)}) collective-permute-start(bf16[64,512]{1,0:T(8,128)(2,1)S(1)} %get-tuple-element.112), channel_id=1, source_target_pairs={{0,2},{1,3},{2,0},{3,1},{4,6},{5,7},{6,4},{7,5},{8,10},{9,11},{10,... | collective-permute-start | bytes 196616 | tf_op jit(solution)/shard_map/ppermute | solution.py:554
  45.1 7.4 %collective-permute-start.11 = (bf16[64,512]{1,0:T(8,128)(2,1)S(1)}, bf16[64,512]{1,0:T(8,128)(2,1)S(1)}, u32[]{:S(2)}, u32[]{:S(2)}) collective-permute-start(bf16[64,512]{1,0:T(8,128)(2,1)S(1)} %get-tuple-element.113), channel_id=1, source_target_pairs={{0,4},{1,5},{2,6},{3,7},{4,0},{5,1},{6,2},{7,3},{8,12},{9,13},{10,... | collective-permute-start | bytes 196616 | tf_op jit(solution)/shard_map/ppermute | solution.py:554
  45.3 7.2 %collective-permute-start.12 = (bf16[64,512]{1,0:T(8,128)(2,1)S(1)}, bf16[64,512]{1,0:T(8,128)(2,1)S(1)}, u32[]{:S(2)}, u32[]{:S(2)}) collective-permute-start(bf16[64,512]{1,0:T(8,128)(2,1)S(1)} %get-tuple-element.114), channel_id=1, source_target_pairs={{0,6},{1,7},{2,4},{3,5},{4,2},{5,3},{6,0},{7,1},{8,14},{9,15},{10,... | collective-permute-start | bytes 196616 | tf_op jit(solution)/shard_map/ppermute | solution.py:554
  52.6 12.1 %collective-permute-start.20 = (bf16[16,512]{1,0:T(8,128)(2,1)S(1)}, bf16[16,512]{1,0:T(8,128)(2,1)S(1)}, u32[]{:S(2)}, u32[]{:S(2)}) collective-permute-start(bf16[16,512]{1,0:T(8,128)(2,1)S(1)} %get-tuple-element.130), channel_id=1, source_target_pairs={{0,8},{1,9},{2,10},{3,11},{4,12},{5,13},{6,14},{7,15},{8,0},{9,1},... | collective-permute-start | bytes 49160 | tf_op jit(solution)/shard_map/ppermute | solution.py:554
  52.7 12.0 %collective-permute-start.21 = (bf16[16,512]{1,0:T(8,128)(2,1)S(1)}, bf16[16,512]{1,0:T(8,128)(2,1)S(1)}, u32[]{:S(2)}, u32[]{:S(2)}) collective-permute-start(bf16[16,512]{1,0:T(8,128)(2,1)S(1)} %get-tuple-element.131), channel_id=1, source_target_pairs={{0,16},{1,17},{2,18},{3,19},{4,20},{5,21},{6,22},{7,23},{8,24},{9,... | collective-permute-start | bytes 49160 | tf_op jit(solution)/shard_map/ppermute | solution.py:554
  54.2 10.5 %collective-permute-start.22 = (bf16[16,512]{1,0:T(8,128)(2,1)S(1)}, bf16[16,512]{1,0:T(8,128)(2,1)S(1)}, u32[]{:S(2)}, u32[]{:S(2)}) collective-permute-start(bf16[16,512]{1,0:T(8,128)(2,1)S(1)} %get-tuple-element.132), channel_id=1, source_target_pairs={{0,24},{1,25},{2,26},{3,27},{4,28},{5,29},{6,30},{7,31},{8,16},{9,... | collective-permute-start | bytes 49160 | tf_op jit(solution)/shard_map/ppermute | solution.py:554
  59.5 23.1 %collective-permute-start.16 = (bf16[192,1024]{1,0:T(8,128)(2,1)S(1)}, bf16[192,1024]{1,0:T(8,128)(2,1)S(1)}, u32[]{:S(2)}, u32[]{:S(2)}) collective-permute-start(bf16[192,1024]{1,0:T(8,128)(2,1)S(1)} %get-tuple-element.125), channel_id=1, source_target_pairs={{0,1},{1,2},{2,3},{3,4},{4,5},{5,6},{6,7},{7,8},{8,9},{9,10},{10,1... | collective-permute-start | bytes 1179656 | tf_op jit(solution)/shard_map/ppermute | solution.py:554
  59.6 23.0 %collective-permute-start.15 = (bf16[192,1024]{1,0:T(8,128)(2,1)S(1)}, bf16[192,1024]{1,0:T(8,128)(2,1)S(1)}, u32[]{:S(2)}, u32[]{:S(2)}) collective-permute-start(bf16[192,1024]{1,0:T(8,128)(2,1)S(1)} %get-tuple-element.124.refs_3_), channel_id=1, source_target_pairs={{0,31},{1,0},{2,1},{3,2},{4,3},{5,4},{6,5},{7,6},{8,7},{9,8},{10,9... | collective-permute-start | bytes 1179656 | tf_op jit(solution)/shard_map/ppermute | solution.py:554
  65.3 16.2 %all-to-all-start = ((bf16[8,16,512]{2,1,0:T(8,128)(2,1)}), bf16[8,16,512]{2,1,0:T(8,128)(2,1)S(1)}, u32[]{:S(2)}, u32[]{:S(2)}) async-start(bf16[8,16,512]{2,1,0:T(8,128)(2,1)} %copies.1), calls=%async_computation | async-start | bytes 262144 | tf_op jit(solution)/shard_map/all_to_all | solution.py:707
  73.9 8.7 %collective-permute-start.17 = (bf16[16,1024]{1,0:T(8,128)(2,1)S(1)}, bf16[16,1024]{1,0:T(8,128)(2,1)S(1)}, u32[]{:S(2)}, u32[]{:S(2)}) collective-permute-start(bf16[16,1024]{1,0:T(8,128)(2,1)S(1)} %get-tuple-element.111.refs_15_), channel_id=1, source_target_pairs={{0,28},{1,29},{2,30},{3,31},{4,0},{5,1},{6,2},{7,3},{8,4},{9,5},{1... | collective-permute-start | bytes 98312 | tf_op jit(solution)/shard_map/ppermute | solution.py:554
  73.9 8.2 %collective-permute-start.18 = (bf16[16,1024]{1,0:T(8,128)(2,1)S(1)}, bf16[16,1024]{1,0:T(8,128)(2,1)S(1)}, u32[]{:S(2)}, u32[]{:S(2)}) collective-permute-start(bf16[16,1024]{1,0:T(8,128)(2,1)S(1)} %get-tuple-element.126), channel_id=1, source_target_pairs={{0,4},{1,5},{2,6},{3,7},{4,8},{5,9},{6,10},{7,11},{8,12},{9,13},{1... | collective-permute-start | bytes 98312 | tf_op jit(solution)/shard_map/ppermute | solution.py:554
  77.4 5.1 %collective-permute-start.19 = (bf16[16,1024]{1,0:T(8,128)(2,1)S(1)}, bf16[16,1024]{1,0:T(8,128)(2,1)S(1)}, u32[]{:S(2)}, u32[]{:S(2)}) collective-permute-start(bf16[16,1024]{1,0:T(8,128)(2,1)S(1)} %get-tuple-element.127), channel_id=1, source_target_pairs={{0,6},{1,7},{2,28},{3,29},{4,10},{5,11},{6,0},{7,1},{8,14},{9,15},... | collective-permute-start | bytes 98312 | tf_op jit(solution)/shard_map/ppermute | solution.py:554

commit v4 on v2

--- a/solution.py
+++ b/solution.py
@@ -147,7 +147,7 @@
 
 
 def coarsen_kernel(
-    seg_hbm, k_hbm, v_hbm, up, down, far3, far4, own0, own1, qdoc, seg, k, v, sems
+    seg_hbm, k_hbm, v_hbm, up, down, far, own0, own1, qdoc, seg, k, v, sems
 ):
     copies = fetch((seg_hbm, k_hbm, v_hbm), (seg, k, v), sems)
     copies[0].wait()
@@ -177,18 +177,26 @@
     for level in range(3):
         put(up, BLOCK * level, level, COUNT[level] - BLOCK, COUNT[level])
         put(down, BLOCK * level, level, 0, BLOCK)
-    put(far3, 0, 3, 0, COUNT[3])
-    put(far4, 0, 4, 0, COUNT[4])
+    put(far, 0, 3, 0, COUNT[3])
+    put(far, COUNT[3], 4, 0, COUNT[4])
     put(own0, 0, 0, 0, COUNT[0])
     put(own1, 0, 1, 0, COUNT[1])
 
 
+def core_index():
+    return lax.axis_index("ctx") % 2
+
+
 def prepare_kernel(
-    far3_in, far4_in, q_hbm, d_hbm, w_hbm, far3, far4, q_out, grad_att, w, d_out, q, sems
+    far, far_partner, q_hbm, d_hbm, w_hbm, far3, far4, third, q_out, grad_att, w, d_out, q, sems
 ):
     copies = fetch((q_hbm, d_hbm, w_hbm), (q, d_out, w), sems)
-    far3[...] = far3_in[...]
-    far4[...] = far4_in[...]
+    even = core_index() == 0
+    for out, start, rows in ((far3, 0, 32), (far4, 32, 16)):
+        own, other = far[start : start + rows], far_partner[start : start + rows]
+        out[0:rows] = jnp.where(even, own, other)
+        out[rows : 2 * rows] = jnp.where(even, other, own)
+    third[...] = far[32:48]
     copies[0].wait()
     for level in range(LEVELS + 1):
         queries = q[...] if level == 0 else dot(gather_table(level, 0.5**level), q[...]).astype(BF16)
@@ -244,10 +252,10 @@
 
 
 def far_refs(refs):
-    below, above, four_a, four_b, four_c, partner = refs
+    own3, got4, third, passed = refs
     return (
-        (below, above, partner.at[0:32]),
-        (four_a, four_b, four_c, partner.at[32:80]),
+        (own3, passed.at[0:64]),
+        (got4, passed.at[64:96], third, passed.at[96:112]),
     )
 
 
@@ -257,8 +265,8 @@
 
 
 def merge_kernel(q_all, qdoc, fine, coarse, grad_att, d_out, *refs):
-    far = far_refs(refs[:6])
-    attended_out, d_w, p_out, g_out, d_side = refs[6:]
+    far = far_refs(refs[:4])
+    attended_out, keep, give, p_out, g_out, d_side, d_w = refs[4:]
     docs = [(docs_of(index, qdoc), far_window(ref, DOC_LANES)) for index, ref in zip(FAR, far)]
     shape = (LANES, LANES)
     same_head = jnp.where(iota(shape, 0) // HEAD_DIM == iota(shape, 1) // HEAD_DIM, 1.0, 0.0)
@@ -316,6 +324,9 @@
             d_side[at : at + rows, cols] = jnp.where(
                 upper, d_high.astype(F32), d_low.astype(F32)
             ).astype(BF16)
+    core = core_index()
+    keep[...] = d_w[pl.ds(pl.multiple_of(core * 256, 256), 256)]
+    give[...] = d_w[pl.ds(pl.multiple_of((1 - core) * 256, 256), 256)].astype(BF16)
 
 
 def attend_back(p, queries, grad, side, keys, values):
@@ -334,11 +345,11 @@
 
 
 def far_back_kernel(p_in, q_all, g_in, d_side, *refs):
-    far = far_refs(refs[:6])
-    d_q, to_3, to_4, to_partner = refs[6:]
+    far = far_refs(refs[:4])
+    d_q, to_3, to_4, to_third, to_partner = refs[4:]
     to_far = (
-        (to_3.at[0], to_3.at[1], to_partner.at[0:32]),
-        (to_4.at[0], to_4.at[1], to_4.at[2], to_partner.at[32:80]),
+        (to_3, to_partner.at[0:64]),
+        (to_4, to_partner.at[64:96], to_third, to_partner.at[96:112]),
     )
     for pair in range(PAIRS):
         cols = lanes_of(pair)
@@ -415,7 +426,7 @@
 
 
 def near_back_a_kernel(attended, w, *refs):
-    near_back_first_kernel(NEAR_PARTS[0], attended, w, *refs)
+    near_back_first_kernel(NEAR_PARTS[0], attended, w, *refs[:9], *refs[-8:])
 
 
 def near_back_b_kernel(*refs):
@@ -448,9 +459,62 @@
     after.wait()
 
 
+def pass_on_kernel(got3, got4, third, own3, out):
+    out[0:64] = got3[...]
+    out[64:96] = got4[...]
+    out[96:112] = third[...]
+    own3[...] = jnp.where(core_index() == 0, got3[0:32], got3[32:64])
+
+
+def far_sum_kernel(to_3, to_4, to_third, swapped, sum3, sum4, sum_third):
+    even = core_index() == 0
+    own3 = to_3[...].astype(F32)
+    sum3[0:32] = (swapped[0:32].astype(F32) + jnp.where(even, own3, 0.0)).astype(BF16)
+    sum3[32:64] = (swapped[32:64].astype(F32) + jnp.where(even, 0.0, own3)).astype(BF16)
+    sum4[...] = (swapped[64:96].astype(F32) + to_4[...].astype(F32)).astype(BF16)
+    sum_third[...] = (swapped[96:112].astype(F32) + to_third[...].astype(F32)).astype(BF16)
+
+
+def core_rows(ref, core, rows):
+    return ref[pl.ds(pl.multiple_of(core * rows, rows), rows)]
+
+
+def far_split_kernel(back3, back4, give):
+    other = 1 - core_index()
+    give[0:32] = core_rows(back3, other, 32)
+    give[32:48] = core_rows(back4, other, 16)
+
+
+def halve_kernel(divisor, keep, got, *refs):
+    keep_out, give_out, total = refs[-3:]
+    total[...] = keep[...] + got[...].astype(F32)
+    side = lax.axis_index("ctx") // divisor % 2
+    half = total.shape[0] // 2
+    keep_out[...] = total[pl.ds(pl.multiple_of(side * half, half), half)]
+    give_out[...] = total[pl.ds(pl.multiple_of((1 - side) * half, half), half)].astype(BF16)
+
+
+def copies_kernel(keep, got, *refs):
+    total = keep[...] + got[...].astype(F32)
+    for i in range(refs[-1].shape[0]):
+        refs[-1][i] = total.astype(BF16)
+
+
+def last_sum_kernel(parts, out):
+    total = parts[0].astype(F32)
+    for i in range(1, parts.shape[0]):
+        total = total + parts[i].astype(F32)
+    out[...] = total.astype(BF16)
+
+
 def combine_kernel(*refs):
-    own, (low, high), from3, from4 = (refs[0:3], refs[3:6]), refs[6:8], refs[8:10], refs[10:13]
-    d_k_hbm, d_v_hbm, d_k, d_v, sems = refs[13:]
+    own, (low, high) = (refs[0:3], refs[3:6]), refs[6:8]
+    back3, back4, third, swapped = refs[8:12]
+    d_k_hbm, d_v_hbm, d_k, d_v, sems = refs[12:]
+    core = core_index()
+    far3 = core_rows(back3, core, 32).astype(F32) + swapped[0:32].astype(F32)
+    far4 = core_rows(back4, core, 16).astype(F32) + swapped[32:48].astype(F32)
+    far4 = far4 + third[...].astype(F32)
     copies = []
     for part, out, out_hbm in ((0, d_k, d_k_hbm), (1, d_v, d_v_hbm)):
         lanes = slice(part * WIDTH, (part + 1) * WIDTH)
@@ -461,16 +525,13 @@
         def rim(ref, level):
             return ref[BLOCK * level : BLOCK * (level + 1), lanes].astype(F32)
 
-        def summed(parts):
-            return functools.reduce(jnp.add, [ref[:, lanes].astype(F32) for ref in parts])
-
         coarse = jnp.concatenate(
             [
                 rim(high, 1),
                 rim(low, 1),
                 rim(low, 2) + rim(high, 2),
-                summed(from3),
-                summed(from4),
+                far3[:, lanes],
+                far4[:, lanes],
             ],
             axis=0,
         ).astype(BF16)
@@ -515,58 +576,57 @@
     return i - 6 if i // 2 % 2 else i + 6
 
 
-ROUTES_3 = (lambda i: i + 2, lambda i: i - 2)
-ROUTES_4 = (lambda i: i + 4, lambda i: i - 4, third)
-BACK_3 = (lambda i: i - 2, lambda i: i + 2)
-BACK_4 = (lambda i: i - 4, lambda i: i + 4, third)
-
-
-def scattered(y, low, bits, after=None):
-    side, count = lax.axis_index("ctx") >> low & (1 << bits) - 1, 1 << bits
-    rows = y.shape[0] // count
-
-    def part(index):
-        return lax.dynamic_slice_in_dim(y, index * rows, rows)
-
-    result = part(side)
-    if after is not None:
-        result, _ = lax.optimization_barrier((result, after))
-    for step in range(1, count):
-        message = part(side ^ step).astype(BF16)
-        result = result + moved(message, lambda i, step=step: i ^ step << low).astype(F32)
-    return result
+def route_3(i):
+    return i - 2 if i % 2 else i + 2
+
+
+def route_4(i):
+    return i - 4 if i % 2 else i + 4
+
+
+def back_3(i):
+    return i + 2 if i % 2 else i - 2
+
+
+def back_4(i):
+    return i + 4 if i % 2 else i - 4
 
 
 def body(queries, key_rows, value_rows, segment_ids, w_out, d_out):
     q, k, v, grad_out = queries[0], key_rows[0], value_rows[0], d_out[0]
     tokens, dma = (ROWS, WIDTH), pltpu.SemaphoreType.DMA
-    even = lax.axis_index("ctx") % 2 == 0
-    up, down, far3, far4, own0, own1, qdoc = call(
+    up, down, far, own0, own1, qdoc = call(
         coarsen_kernel,
         "coarsen",
-        [((192, PACK), BF16), ((192, PACK), BF16), ((32, PACK), BF16), ((16, PACK), BF16)]
+        [((192, PACK), BF16), ((192, PACK), BF16), ((48, PACK), BF16)]
         + [((ROWS, PACK), BF16), ((128, PACK), BF16), ((ALL_ROWS, LANES), BF16)],
         [segment_ids, k, v],
         [pltpu.VMEM((1, ROWS), jnp.int32)] + [pltpu.VMEM(tokens, BF16)] * 2 + [dma((3,))],
         in_hbm=3,
     )
-    far3, far4, q_all, grad_att, w, grad_rows = call(
+    far_partner = moved(far, partner)
+    far3, far4, third_rows, q_all, grad_att, w, grad_rows = call(
         prepare_kernel,
         "prepare",
-        [((32, PACK), BF16), ((16, PACK), BF16)]
+        [((64, PACK), BF16), ((32, PACK), BF16), ((16, PACK), BF16)]
         + [((ALL_ROWS, WIDTH), BF16), (tokens, F32), ((WIDTH, WIDTH), BF16), (tokens, BF16)],
-        [far3, far4, q, grad_out, w_out],
+        [far, far_partner, q, grad_out, w_out],
         [pltpu.VMEM(tokens, BF16), dma((3,))],
         in_hbm=3,
     )
     low = moved(up, lambda i: i + 1)
     high = moved(down, lambda i: i - 1)
-    got3 = [moved(far3, route) for route in ROUTES_3]
-    got4 = [moved(far4, route) for route in ROUTES_4]
-    low, high, *got3 = lax.optimization_barrier((low, high, *got3))
-    passed = jnp.concatenate([jnp.where(even, got3[0], got3[1]), *got4], axis=0)
-    low, high, passed = lax.optimization_barrier((low, high, passed))
-    far = (*got3, *got4, moved(passed, partner))
+    got3 = moved(far3, route_3)
+    got4 = moved(far4, route_4)
+    got_third = moved(third_rows, third)
+    low, high, got3 = lax.optimization_barrier((low, high, got3))
+    own3, passed = call(
+        pass_on_kernel,
+        "pass_on",
+        [((32, PACK), BF16), ((112, PACK), BF16)],
+        [got3, got4, got_third],
+    )
+    far = (own3, got4, got_third, moved(passed, partner))
     near = (own0, own1, low, high)
     p_near, fine, coarse = call(
         near_kernel,
@@ -579,27 +639,39 @@
         [q_all, qdoc, *near],
         microseconds=50,
     )
-    attended, d_w, p_far, g, d_side = call(
+    attended, keep, give, p_far, g, d_side = call(
         merge_kernel,
         "merge",
-        [(tokens, BF16), ((WIDTH, WIDTH), F32), ((PAIRS, P_FAR, LANES), BF16)]
+        [(tokens, BF16), ((256, WIDTH), F32), ((256, WIDTH), BF16)]
+        + [((PAIRS, P_FAR, LANES), BF16)]
         + [((ALL_ROWS, WIDTH), BF16)] * 2,
         [q_all, qdoc, fine, coarse, grad_att, grad_rows, *far],
+        [pltpu.VMEM((WIDTH, WIDTH), F32)],
         microseconds=6,
     )
-    d_far, to_3, to_4, to_partner = call(
+    got_w = moved(give, partner)
+    d_far, *to_far, to_partner = call(
         far_back_kernel,
         "far_back",
-        [((48, WIDTH), BF16), ((2, 32, 2 * WIDTH), BF16)]
-        + [((3, 16, 2 * WIDTH), BF16), ((80, 2 * WIDTH), BF16)],
+        [((48, WIDTH), BF16), ((32, 2 * WIDTH), BF16), ((32, 2 * WIDTH), BF16)]
+        + [((16, 2 * WIDTH), BF16), ((112, 2 * WIDTH), BF16)],
         [p_far, q_all, g, d_side, *far],
     )
-    d_w = scattered(d_w, 0, 1)
-    from_partner = moved(to_partner, partner).astype(F32)
-    swapped3, swapped4 = from_partner[:32], from_partner[32:].reshape(3, 16, 2 * WIDTH)
-    mine = jnp.stack([jnp.where(even, swapped3, 0), jnp.where(even, 0, swapped3)])
-    to_3 = (to_3.astype(F32) + mine).astype(BF16)
-    to_4 = (to_4.astype(F32) + swapped4).astype(BF16)
+    swapped = moved(to_partner, partner)
+
+    def halved(keep, got, divisor, route, after):
+        rows = keep.shape[0] // 2
+        keep, give = call(
+            functools.partial(halve_kernel, divisor),
+            "halve_" + str(rows),
+            [((rows, WIDTH), F32), ((rows, WIDTH), BF16)],
+            [keep, got, after],
+            [pltpu.VMEM((2 * rows, WIDTH), F32)],
+            in_hbm=1,
+        )
+        return keep, moved(give, route)
+
+    keep, got_w = halved(keep, got_w, 4, lambda i: i ^ 6, d_far)
 
     def part_outs(part):
         width = len(NEAR_PARTS[part]) * LANES
@@ -612,46 +684,61 @@
         near_back_a_kernel,
         "near_back_a",
         part_outs(0) + [(tokens, BF16)],
-        [attended, w, *args],
+        [attended, w, *args, keep],
         [pltpu.VMEM(tokens, BF16), dma(())],
+        in_hbm=1,
         microseconds=3,
         to_hbm=(5,),
     )
+    sum3, sum4, sum_third = call(
+        far_sum_kernel,
+        "far_sum",
+        [((64, 2 * WIDTH), BF16), ((32, 2 * WIDTH), BF16), ((16, 2 * WIDTH), BF16)],
+        [*to_far, swapped],
+    )
+    back3 = moved(sum3, back_3)
+    back4 = moved(sum4, back_4)
+    back_third = moved(sum_third, third)
+    keep, got_w = halved(keep, got_w, 2, lambda i: i ^ 2, part_a[0])
     part_b = call(
         near_back_b_kernel,
         "near_back_b",
         part_outs(1),
-        [*args, part_a[0], to_3, d_w],
+        [*args, part_a[0], sum3, keep],
         in_hbm=3,
         microseconds=4,
     )
-    back = [moved(to_3[i], route) for i, route in enumerate(BACK_3)]
-    d_w = scattered(d_w, 1, 2, after=part_b[0])
-    to_4, _ = lax.optimization_barrier((to_4, part_b[0]))
+    keep, got_w = halved(keep, got_w, 16, lambda i: i ^ 24, part_b[0])
     d_q, own_k, own_v, to_low, to_high = call(
         near_back_c_kernel,
         "near_back_c",
         [(tokens, BF16), ((ROWS, LANES), F32), ((ROWS, LANES), F32)]
         + [((192, 2 * WIDTH), BF16)] * 2,
-        [*args, part_a[0], *part_a[3:], part_b[0], *part_b[3:], to_4, d_w, *back],
+        [*args, part_a[0], *part_a[3:], part_b[0], *part_b[3:], keep],
         [pltpu.VMEM(tokens, BF16), dma((2,))],
-        in_hbm=4,
+        in_hbm=1,
         microseconds=2,
         to_hbm=(0,),
     )
-    back += [moved(to_4[i], route) for i, route in enumerate(BACK_4)]
-    d_w = scattered(d_w, 3, 2, after=to_low)
     low_back = moved(to_low, lambda i: i - 1)
     high_back = moved(to_high, lambda i: i + 1)
-    dp_count = lax.axis_size("dp")
-    copies = jnp.broadcast_to(d_w.astype(BF16)[None], (dp_count,) + d_w.shape)
+    give = call(far_split_kernel, "far_split", [((48, 2 * WIDTH), BF16)], [back3, back4])[0]
+    swapped = moved(give, partner)
+    keep, got_w = halved(keep, got_w, 8, lambda i: i ^ 8, to_low)
+    copies = call(
+        copies_kernel,
+        "copies",
+        [((lax.axis_size("dp"), 16, WIDTH), BF16)],
+        [keep, got_w],
+    )[0]
     copies = lax.all_to_all(copies, "dp", 0, 0, tiled=True)
-    d_w = jnp.sum(copies.astype(F32), axis=0).astype(BF16)
+    d_w = call(last_sum_kernel, "last_sum", [((16, WIDTH), BF16)], [copies])[0]
     d_k, d_v = call(
         combine_kernel,
         "combine",
         [(tokens, BF16)] * 2,
-        [part_a[1], part_b[1], own_k, part_a[2], part_b[2], own_v, low_back, high_back, *back],
+        [part_a[1], part_b[1], own_k, part_a[2], part_b[2], own_v, low_back, high_back]
+        + [back3, back4, back_third, swapped],
         [pltpu.VMEM(tokens, BF16)] * 2 + [dma((2,))],
         to_hbm=(0, 1),
     )

time: 93.5 us -> 78.3 us (0.84)
  starting transfers between devices: 41.7 us -> 25.4 us
  waiting for transfers between devices: 16.4 us -> 29.4 us
  local copies, waits for them, and re-layouts: 14.6 us -> 2.58 us
  Pallas kernels: 17.7 us -> 19.4 us
    ppermute x23 -> x19, starting transfers between devices: 33.2 us -> 16.9 us  [moved(): return lax.ppermute(x, 'ctx', [(i, route(i) % count) for i in range(count)])]
    ppermute x23 -> x19, waiting for transfers between devices: 13.4 us -> 29.4 us  [moved(): return lax.ppermute(x, 'ctx', [(i, route(i) % count) for i in range(count)])]
    unnamed x52 -> x12, local copies, waits for them, and re-layouts: 13.8 us -> 2.58 us
    all_to_all x1, waiting for transfers between devices: 3.02 us -> 0.01 us  [body(): copies = lax.all_to_all(copies, 'dp', 0, 0, tiled=True)]
    pallas_call x9 -> x18, Pallas kernels: 17.7 us -> 19.4 us  [call(): pl.pallas_call(kernel, name=name, out_shape=[jax.ShapeDtypeStruct(shape,...]
  transfers between devices with their start and end apart: 24 -> 20, of which waited for: 10 -> 11; matrix products, arithmetic and copies ran while one was open for 2% -> 0% of each run, Pallas kernels for 11% -> 14%
where the time goes in v4:
time: 78.3 us; the launch traced here: 77.9 us
  waiting for transfers between devices  29.4 us (38%)
  starting transfers between devices  25.4 us (32%)
  Pallas kernels  19.4 us (25%)
  local copies, waits for them, and re-layouts  2.58 us (3%)
  between operations  0.98 us (1%)
    ppermute x19, waiting for transfers between devices, moved(): return lax.ppermute(x, 'ctx', [(i, route(i) % count) for i in range(count)])  29.4 us
    pallas_call x18, Pallas kernels, call(): pl.pallas_call(kernel, name=name, out_shape=[jax.ShapeDtypeStruct(shape,...  19.4 us
    ppermute x19, starting transfers between devices, moved(): return lax.ppermute(x, 'ctx', [(i, route(i) % count) for i in range(count)])  16.9 us
    all_to_all x1, starting transfers between devices, body(): copies = lax.all_to_all(copies, 'dp', 0, 0, tiled=True)  8.57 us
    unnamed x12, local copies, waits for them, and re-layouts  2.58 us
  transfers between devices with their start and end apart: 20, of which 11 were waited for; matrix products, arithmetic and copies ran while one was open for 0% of the time, Pallas kernels for 14%

profile of v4, /device:TPU:32, one launch (start us, length us, event | category | flops | bytes accessed | tf_op | source)
XLA Modules:
  0.0 77.9 jit_solution(4448281357537916146)
XLA Ops:
  0.6 0.9 %copy-done.1 = bf16[1,256,512]{2,1,0:T(8,128)(2,1)S(1)} copy-done((bf16[1,256,512]{2,1,0:T(8,128)(2,1)S(1)}, bf16[1,256,512]{2,1,0:T(8,128)(2,1)}, u32[]{:S(2)}) %copy-start.1) | copy-done | bytes 262168
  1.6 0.9 %copy-done.2 = bf16[1,256,512]{2,1,0:T(8,128)(2,1)S(1)} copy-done((bf16[1,256,512]{2,1,0:T(8,128)(2,1)S(1)}, bf16[1,256,512]{2,1,0:T(8,128)(2,1)}, u32[]{:S(2)}) %copy-start.2) | copy-done | bytes 262168
  2.5 0.7 copy-done.5
  3.2 0.7 coarsen.1
  4.0 5.1 %collective-permute-start.2 = (bf16[192,1152]{1,0:T(8,128)(2,1)S(1)}, bf16[192,1152]{1,0:T(8,128)(2,1)S(1)}, u32[]{:S(2)}, u32[]{:S(2)}) collective-permute-start(bf16[192,1152]{1,0:T(8,128)(2,1)S(1)} %get-tuple-element.72), channel_id=1, source_target_pairs={{0,31},{1,0},{2,1},{3,2},{4,3},{5,4},{6,5},{7,6},{8,7},{9,8},{10,9... | collective-permute-start | bytes 1327112 | tf_op jit(solution)/shard_map/ppermute | solution.py:568
  9.1 1.3 %collective-permute-done.far_partner = bf16[48,1152]{1,0:T(8,128)(2,1)S(1)} collective-permute-done((bf16[48,1152]{1,0:T(8,128)(2,1)S(1)}, bf16[48,1152]{1,0:T(8,128)(2,1)S(1)}, u32[]{:S(2)}, u32[]{:S(2)}) %collective-permute-start) | collective-permute-done | bytes 110624 | tf_op jit(solution)/shard_map/ppermute | solution.py:568
  10.4 0.8 prepare.1
  11.3 1.1 %collective-permute-start.4 = (bf16[32,1152]{1,0:T(8,128)(2,1)S(1)}, bf16[32,1152]{1,0:T(8,128)(2,1)S(1)}, u32[]{:S(2)}, u32[]{:S(2)}) collective-permute-start(bf16[32,1152]{1,0:T(8,128)(2,1)S(1)} %get-tuple-element.81), channel_id=1, source_target_pairs={{0,4},{1,29},{2,6},{3,31},{4,8},{5,1},{6,10},{7,3},{8,12},{9,5},{1... | collective-permute-start | bytes 221192 | tf_op jit(solution)/shard_map/ppermute | solution.py:568
  12.4 2.3 %collective-permute-start.5 = (bf16[16,1152]{1,0:T(8,128)(2,1)S(1)}, bf16[16,1152]{1,0:T(8,128)(2,1)S(1)}, u32[]{:S(2)}, u32[]{:S(2)}) collective-permute-start(bf16[16,1152]{1,0:T(8,128)(2,1)S(1)} %get-tuple-element.82), channel_id=1, source_target_pairs={{0,6},{1,7},{2,28},{3,29},{4,10},{5,11},{6,0},{7,1},{8,14},{9,15},... | collective-permute-start | bytes 110600 | tf_op jit(solution)/shard_map/ppermute | solution.py:568
  14.7 5.9 %collective-permute-done.3.got3 = bf16[64,1152]{1,0:T(8,128)(2,1)S(1)} collective-permute-done((bf16[64,1152]{1,0:T(8,128)(2,1)S(1)}, bf16[64,1152]{1,0:T(8,128)(2,1)S(1)}, u32[]{:S(2)}, u32[]{:S(2)}) %collective-permute-start.3) | collective-permute-done | bytes 147488 | tf_op jit(solution)/shard_map/ppermute | solution.py:568
  21.3 1.7 %near.1 = (bf16[4,896,256]{2,1,0:T(8,128)(2,1)S(1)}, f32[4,256,384]{2,1,0:T(8,128)S(1)}, bf16[4,192,384]{2,1,0:T(8,128)(2,1)S(1)}) custom-call(bf16[496,512]{1,0:T(8,128)(2,1)S(1)} %get-tuple-element.67.q_all.refs_1_, bf16[496,128]{1,0:T(8,128)(2,1)S(1)} %get-tuple-element.68.qdoc, bf16[256,1152]{1,0:T(8,128)(2,1)S(1)} %get-tuple-element.69.own0.refs_4_, ...), custom_call_target="tpu_custom_call" | custom-call | flops 49999998976 | bytes 1048576 | tf_op jit(solution)/shard_map/near/pallas_call | solution.py:552
  23.0 5.6 %merge.1 = (bf16[256,512]{1,0:T(8,128)(2,1)S(1)}, f32[256,512]{1,0:T(8,128)S(1)}, bf16[256,512]{1,0:T(8,128)(2,1)S(1)}, bf16[4,96,128]{2,1,0:T(8,128)(2,1)S(1)},...) custom-call(bf16[496,512]{1,0:T(8,128)(2,1)S(1)} %get-tuple-element.67.q_all.refs_1_, ...), custom_call_target="tpu_custom_call" | custom-call | flops 6000000000 | bytes 1048576 | tf_op jit(solution)/shard_map/merge/pallas_call | solution.py:552
  28.6 1.1 %far_back.1 = (bf16[48,512]{1,0:T(8,128)(2,1)S(1)}, bf16[32,1024]{1,0:T(8,128)(2,1)S(1)}, bf16[32,1024]{1,0:T(8,128)(2,1)S(1)}, bf16[16,1024]{1,0:T(8,128)(2,1)S(1)}, bf16[112,1024]{1,0:T(8,128)(2,1)S(1)}) custom-call(bf16[4,96,128]{2,1,0:T(8,128)(2,1)S(1)} %get-tuple-element.90.p_in, bf16[496,512]{1,0:T(8,128)(2,1)S(1)} %get-tuple-element.67.q_all.refs_1_, ...), custom_call_target="tpu_custom_call" | custom-call | flops 1000000000 | bytes 1048576 | tf_op jit(solution)/shard_map/far_back/pallas_call | solution.py:552
  29.7 0.7 collective-permute-start.8
  30.5 1.0 %collective-permute-done.8.swapped = bf16[112,1024]{1,0:T(8,128)(2,1)S(1)} collective-permute-done((bf16[112,1024]{1,0:T(8,128)(2,1)S(1)}, bf16[112,1024]{1,0:T(8,128)(2,1)S(1)}, u32[]{:S(2)}, u32[]{:S(2)}) %collective-permute-start.8) | collective-permute-done | bytes 229408 | tf_op jit(solution)/shard_map/ppermute | solution.py:568
  32.0 1.3 %collective-permute-start.9 = (bf16[128,512]{1,0:T(8,128)(2,1)S(1)}, bf16[128,512]{1,0:T(8,128)(2,1)S(1)}, u32[]{:S(2)}, u32[]{:S(2)}) collective-permute-start(bf16[128,512]{1,0:T(8,128)(2,1)S(1)} %get-tuple-element.104), channel_id=1, source_target_pairs={{0,6},{1,7},{2,4},{3,5},{4,2},{5,3},{6,0},{7,1},{8,14},{9,15},{10,... | collective-permute-start | bytes 393224 | tf_op jit(solution)/shard_map/ppermute | solution.py:568
  33.3 2.0 %near_back_a.1 = (bf16[256,128]{1,0:T(8,128)(2,1)S(1)}, f32[256,128]{1,0:T(8,128)S(1)}, f32[256,128]{1,0:T(8,128)S(1)}, bf16[2,192,128]{2,1,0:T(8,128)(2,1)S(1)}...) custom-call(bf16[256,512]{1,0:T(8,128)(2,1)S(1)} %get-tuple-element.85.attended, ...), custom_call_target="tpu_custom_call" | custom-call | flops 3000000000 | bytes 1048576 | tf_op jit(solution)/shard_map/near_back_a/pallas_call | solution.py:552
  35.3 3.7 %collective-permute-done.9.got = bf16[128,512]{1,0:T(8,128)(2,1)S(1)} collective-permute-done((bf16[128,512]{1,0:T(8,128)(2,1)S(1)}, bf16[128,512]{1,0:T(8,128)(2,1)S(1)}, u32[]{:S(2)}, u32[]{:S(2)}) %collective-permute-start.9) | collective-permute-done | bytes 131104 | tf_op jit(solution)/shard_map/ppermute | solution.py:568
  39.2 2.7 %near_back_b.1 = (bf16[256,256]{1,0:T(8,128)(2,1)S(1)}, f32[256,256]{1,0:T(8,128)S(1)}, f32[256,256]{1,0:T(8,128)S(1)}, bf16[2,192,256]{2,1,0:T(8,128)(2,1)S(1)}, bf16[2,192,256]{2,1,0:T(8,128)(2,1)S(1)}) custom-call(bf16[4,896,256]{2,1,0:T(8,128)(2,1)S(1)} %get-tuple-element.87.refs_0_, bf16[496,512]{1,0:T(8,128)(2,1)S(1)} %get-tuple-element.67.q_all.refs_1_, ...), custom_call_target="tpu_custom_call" | custom-call | flops 4000000000 | bytes 1048576 | tf_op jit(solution)/shard_map/near_back_b/pallas_call | solution.py:552
  41.9 1.5 %collective-permute-done.10.got = bf16[64,512]{1,0:T(8,128)(2,1)S(1)} collective-permute-done((bf16[64,512]{1,0:T(8,128)(2,1)S(1)}, bf16[64,512]{1,0:T(8,128)(2,1)S(1)}, u32[]{:S(2)}, u32[]{:S(2)}) %collective-permute-start.10) | collective-permute-done | bytes 65568 | tf_op jit(solution)/shard_map/ppermute | solution.py:568
  43.5 1.3 %collective-permute-start.17 = (bf16[32,512]{1,0:T(8,128)(2,1)S(1)}, bf16[32,512]{1,0:T(8,128)(2,1)S(1)}, u32[]{:S(2)}, u32[]{:S(2)}) collective-permute-start(bf16[32,512]{1,0:T(8,128)(2,1)S(1)} %get-tuple-element.124), channel_id=1, source_target_pairs={{0,24},{1,25},{2,26},{3,27},{4,28},{5,29},{6,30},{7,31},{8,16},{9,... | collective-permute-start | bytes 98312 | tf_op jit(solution)/shard_map/ppermute | solution.py:568
  44.8 2.1 %near_back_c.1 = (bf16[256,512]{1,0:T(8,128)(2,1)}, f32[256,128]{1,0:T(8,128)S(1)}, f32[256,128]{1,0:T(8,128)S(1)}, bf16[192,1024]{1,0:T(8,128)(2,1)S(1)}, bf16[192,1024]{1,0:T(8,128)(2,1)S(1)}) custom-call(bf16[4,896,256]{2,1,0:T(8,128)(2,1)S(1)} %get-tuple-element.87.refs_0_, bf16[496,512]{1,0:T(8,128)(2,1)S(1)} %get-tuple-element.67.q_all.refs_1_, ...), custom_call_target="tpu_custom_call" | custom-call | flops 2000000000 | bytes 1048576 | tf_op jit(solution)/shard_map/near_back_c/pallas_call | solution.py:552
  47.0 1.7 %collective-permute-done.17.got = bf16[32,512]{1,0:T(8,128)(2,1)S(1)} collective-permute-done((bf16[32,512]{1,0:T(8,128)(2,1)S(1)}, bf16[32,512]{1,0:T(8,128)(2,1)S(1)}, u32[]{:S(2)}, u32[]{:S(2)}) %collective-permute-start.17) | collective-permute-done | bytes 32800 | tf_op jit(solution)/shard_map/ppermute | solution.py:568
  48.8 0.5 collective-permute-start.11
  49.4 3.1 %collective-permute-done.18.got = bf16[16,512]{1,0:T(8,128)(2,1)S(1)} collective-permute-done((bf16[16,512]{1,0:T(8,128)(2,1)S(1)}, bf16[16,512]{1,0:T(8,128)(2,1)S(1)}, u32[]{:S(2)}, u32[]{:S(2)}) %collective-permute-start.18) | collective-permute-done | bytes 16416 | tf_op jit(solution)/shard_map/ppermute | solution.py:568
  52.6 0.7 copies.1
  53.2 8.6 %all-to-all-start = ((bf16[8,16,512]{2,1,0:T(8,128)(2,1)}), bf16[8,16,512]{2,1,0:T(8,128)(2,1)S(1)}, u32[]{:S(2)}, u32[]{:S(2)}) async-start(bf16[8,16,512]{2,1,0:T(8,128)(2,1)} %copies.1), calls=%async_computation | async-start | bytes 262144 | tf_op jit(solution)/shard_map/all_to_all | solution.py:734
  61.8 3.7 %collective-permute-start.13 = (bf16[64,1024]{1,0:T(8,128)(2,1)S(1)}, bf16[64,1024]{1,0:T(8,128)(2,1)S(1)}, u32[]{:S(2)}, u32[]{:S(2)}) collective-permute-start(bf16[64,1024]{1,0:T(8,128)(2,1)S(1)} %get-tuple-element.103.refs_10_), channel_id=1, source_target_pairs={{0,30},{1,3},{2,0},{3,5},{4,2},{5,7},{6,4},{7,9},{8,6},{9,11},{10,... | collective-permute-start | bytes 393224 | tf_op jit(solution)/shard_map/ppermute | solution.py:568
  65.5 5.8 %collective-permute-done.14.back4.refs_9_ = bf16[32,1024]{1,0:T(8,128)(2,1)S(1)} collective-permute-done((bf16[32,1024]{1,0:T(8,128)(2,1)S(1)}, bf16[32,1024]{1,0:T(8,128)(2,1)S(1)}, u32[]{:S(2)}, u32[]{:S(2)}) %collective-permute-start.14) | collective-permute-done | bytes 65568 | tf_op jit(solution)/shard_map/ppermute | solution.py:568
  71.5 0.6 last_sum.1
  72.1 4.5 %collective-permute-done.15.refs_10_ = bf16[16,1024]{1,0:T(8,128)(2,1)S(1)} collective-permute-done((bf16[16,1024]{1,0:T(8,128)(2,1)S(1)}, bf16[16,1024]{1,0:T(8,128)(2,1)S(1)}, u32[]{:S(2)}, u32[]{:S(2)}) %collective-permute-start.15) | collective-permute-done | bytes 32800 | tf_op jit(solution)/shard_map/ppermute | solution.py:568
  76.6 1.1 %combine.1 = (bf16[256,512]{1,0:T(8,128)(2,1)}, bf16[256,512]{1,0:T(8,128)(2,1)}) custom-call(f32[256,128]{1,0:T(8,128)S(1)} %get-tuple-element.112.refs_0_, f32[256,256]{1,0:T(8,128)S(1)} %get-tuple-element.113.refs_1_, f32[256,128]{1,0:T(8,128)S(1)} %get-tuple-element.114.refs_2_, f32[256,128]{1,0:T(8,128)S(1)} %get-tuple-element.115.refs_3_, ...), custom_call_target="tpu_custom_call" | custom-call | flops 1000000000 | bytes 1048576 | tf_op jit(solution)/shard_map/combine/pallas_call | solution.py:552
  (38 shorter events, 2.1 us)
Async XLA Ops:
  0.6 1.0 %copy-start.1 = (bf16[1,256,512]{2,1,0:T(8,128)(2,1)S(1)}, bf16[1,256,512]{2,1,0:T(8,128)(2,1)}, u32[]{:S(2)}) copy-start(bf16[1,256,512]{2,1,0:T(8,128)(2,1)} %param.7) | copy-start | bytes 786436
  1.6 0.9 %copy-start.2 = (bf16[1,256,512]{2,1,0:T(8,128)(2,1)S(1)}, bf16[1,256,512]{2,1,0:T(8,128)(2,1)}, u32[]{:S(2)}) copy-start(bf16[1,256,512]{2,1,0:T(8,128)(2,1)} %param.8) | copy-start | bytes 786436
  2.5 0.7 copy-start.5
  3.2 7.2 %copy-start = (bf16[512,512]{1,0:T(8,128)(2,1)S(1)}, bf16[512,512]{1,0:T(8,128)(2,1)}, u32[]{:S(2)}) copy-start(bf16[512,512]{1,0:T(8,128)(2,1)} %w_hbm.1) | copy-start | bytes 1572868
  3.2 7.2 %copy-start.3 = (bf16[1,256,512]{2,1,0:T(8,128)(2,1)S(1)}, bf16[1,256,512]{2,1,0:T(8,128)(2,1)}, u32[]{:S(2)}) copy-start(bf16[1,256,512]{2,1,0:T(8,128)(2,1)} %param.6) | copy-start | bytes 786436
  3.2 7.2 %copy-start.4 = (bf16[1,256,512]{2,1,0:T(8,128)(2,1)S(1)}, bf16[1,256,512]{2,1,0:T(8,128)(2,1)}, u32[]{:S(2)}) copy-start(bf16[1,256,512]{2,1,0:T(8,128)(2,1)} %param.11) | copy-start | bytes 786436
  3.9 16.6 %collective-permute-start.1 = (bf16[192,1152]{1,0:T(8,128)(2,1)S(1)}, bf16[192,1152]{1,0:T(8,128)(2,1)S(1)}, u32[]{:S(2)}, u32[]{:S(2)}) collective-permute-start(bf16[192,1152]{1,0:T(8,128)(2,1)S(1)} %get-tuple-element.71), channel_id=1, source_target_pairs={{0,1},{1,2},{2,3},{3,4},{4,5},{5,6},{6,7},{7,8},{8,9},{9,10},{10,1... | collective-permute-start | bytes 1327112 | tf_op jit(solution)/shard_map/ppermute | solution.py:568
  4.0 16.5 %collective-permute-start.2 = (bf16[192,1152]{1,0:T(8,128)(2,1)S(1)}, bf16[192,1152]{1,0:T(8,128)(2,1)S(1)}, u32[]{:S(2)}, u32[]{:S(2)}) collective-permute-start(bf16[192,1152]{1,0:T(8,128)(2,1)S(1)} %get-tuple-element.72), channel_id=1, source_target_pairs={{0,31},{1,0},{2,1},{3,2},{4,3},{5,4},{6,5},{7,6},{8,7},{9,8},{10,9... | collective-permute-start | bytes 1327112 | tf_op jit(solution)/shard_map/ppermute | solution.py:568
  9.1 1.3 %collective-permute-start = (bf16[48,1152]{1,0:T(8,128)(2,1)S(1)}, bf16[48,1152]{1,0:T(8,128)(2,1)S(1)}, u32[]{:S(2)}, u32[]{:S(2)}) collective-permute-start(bf16[48,1152]{1,0:T(8,128)(2,1)S(1)} %get-tuple-element.66.far), channel_id=1, source_target_pairs={{0,1},{1,0},{2,3},{3,2},{4,5},{5,4},{6,7},{7,6},{8,9},{9,8},{10,11... | collective-permute-start | bytes 331784 | tf_op jit(solution)/shard_map/ppermute | solution.py:568
  11.2 9.4 %collective-permute-start.3 = (bf16[64,1152]{1,0:T(8,128)(2,1)S(1)}, bf16[64,1152]{1,0:T(8,128)(2,1)S(1)}, u32[]{:S(2)}, u32[]{:S(2)}) collective-permute-start(bf16[64,1152]{1,0:T(8,128)(2,1)S(1)} %get-tuple-element.73), channel_id=1, source_target_pairs={{0,2},{1,31},{2,4},{3,1},{4,6},{5,3},{6,8},{7,5},{8,10},{9,7},{10,... | collective-permute-start | bytes 442376 | tf_op jit(solution)/shard_map/ppermute | solution.py:568
  11.3 9.8 %collective-permute-start.4 = (bf16[32,1152]{1,0:T(8,128)(2,1)S(1)}, bf16[32,1152]{1,0:T(8,128)(2,1)S(1)}, u32[]{:S(2)}, u32[]{:S(2)}) collective-permute-start(bf16[32,1152]{1,0:T(8,128)(2,1)S(1)} %get-tuple-element.81), channel_id=1, source_target_pairs={{0,4},{1,29},{2,6},{3,31},{4,8},{5,1},{6,10},{7,3},{8,12},{9,5},{1... | collective-permute-start | bytes 221192 | tf_op jit(solution)/shard_map/ppermute | solution.py:568
  12.4 8.6 %collective-permute-start.5 = (bf16[16,1152]{1,0:T(8,128)(2,1)S(1)}, bf16[16,1152]{1,0:T(8,128)(2,1)S(1)}, u32[]{:S(2)}, u32[]{:S(2)}) collective-permute-start(bf16[16,1152]{1,0:T(8,128)(2,1)S(1)} %get-tuple-element.82), channel_id=1, source_target_pairs={{0,6},{1,7},{2,28},{3,29},{4,10},{5,11},{6,0},{7,1},{8,14},{9,15},... | collective-permute-start | bytes 110600 | tf_op jit(solution)/shard_map/ppermute | solution.py:568
  21.1 1.9 %collective-permute-start.6 = (bf16[112,1152]{1,0:T(8,128)(2,1)S(1)}, bf16[112,1152]{1,0:T(8,128)(2,1)S(1)}, u32[]{:S(2)}, u32[]{:S(2)}) collective-permute-start(bf16[112,1152]{1,0:T(8,128)(2,1)S(1)} %get-tuple-element.84), channel_id=1, source_target_pairs={{0,1},{1,0},{2,3},{3,2},{4,5},{5,4},{6,7},{7,6},{8,9},{9,8},{10,11... | collective-permute-start | bytes 774152 | tf_op jit(solution)/shard_map/ppermute | solution.py:568
  29.7 1.8 %collective-permute-start.8 = (bf16[112,1024]{1,0:T(8,128)(2,1)S(1)}, bf16[112,1024]{1,0:T(8,128)(2,1)S(1)}, u32[]{:S(2)}, u32[]{:S(2)}) collective-permute-start(bf16[112,1024]{1,0:T(8,128)(2,1)S(1)} %get-tuple-element.102), channel_id=1, source_target_pairs={{0,1},{1,0},{2,3},{3,2},{4,5},{5,4},{6,7},{7,6},{8,9},{9,8},{10,11... | collective-permute-start | bytes 688136 | tf_op jit(solution)/shard_map/ppermute | solution.py:568
  30.4 1.5 %collective-permute-start.7 = (bf16[256,512]{1,0:T(8,128)(2,1)S(1)}, bf16[256,512]{1,0:T(8,128)(2,1)S(1)}, u32[]{:S(2)}, u32[]{:S(2)}) collective-permute-start(bf16[256,512]{1,0:T(8,128)(2,1)S(1)} %get-tuple-element.93), channel_id=1, source_target_pairs={{0,1},{1,0},{2,3},{3,2},{4,5},{5,4},{6,7},{7,6},{8,9},{9,8},{10,11... | collective-permute-start | bytes 786440 | tf_op jit(solution)/shard_map/ppermute | solution.py:568
  32.0 7.0 %collective-permute-start.9 = (bf16[128,512]{1,0:T(8,128)(2,1)S(1)}, bf16[128,512]{1,0:T(8,128)(2,1)S(1)}, u32[]{:S(2)}, u32[]{:S(2)}) collective-permute-start(bf16[128,512]{1,0:T(8,128)(2,1)S(1)} %get-tuple-element.104), channel_id=1, source_target_pairs={{0,6},{1,7},{2,4},{3,5},{4,2},{5,3},{6,0},{7,1},{8,14},{9,15},{10,... | collective-permute-start | bytes 393224 | tf_op jit(solution)/shard_map/ppermute | solution.py:568
  39.1 4.4 %collective-permute-start.10 = (bf16[64,512]{1,0:T(8,128)(2,1)S(1)}, bf16[64,512]{1,0:T(8,128)(2,1)S(1)}, u32[]{:S(2)}, u32[]{:S(2)}) collective-permute-start(bf16[64,512]{1,0:T(8,128)(2,1)S(1)} %get-tuple-element.109), channel_id=1, source_target_pairs={{0,2},{1,3},{2,0},{3,1},{4,6},{5,7},{6,4},{7,5},{8,10},{9,11},{10,... | collective-permute-start | bytes 196616 | tf_op jit(solution)/shard_map/ppermute | solution.py:568
  43.5 5.2 %collective-permute-start.17 = (bf16[32,512]{1,0:T(8,128)(2,1)S(1)}, bf16[32,512]{1,0:T(8,128)(2,1)S(1)}, u32[]{:S(2)}, u32[]{:S(2)}) collective-permute-start(bf16[32,512]{1,0:T(8,128)(2,1)S(1)} %get-tuple-element.124), channel_id=1, source_target_pairs={{0,24},{1,25},{2,26},{3,27},{4,28},{5,29},{6,30},{7,31},{8,16},{9,... | collective-permute-start | bytes 98312 | tf_op jit(solution)/shard_map/ppermute | solution.py:568
  48.7 3.8 %collective-permute-start.18 = (bf16[16,512]{1,0:T(8,128)(2,1)S(1)}, bf16[16,512]{1,0:T(8,128)(2,1)S(1)}, u32[]{:S(2)}, u32[]{:S(2)}) collective-permute-start(bf16[16,512]{1,0:T(8,128)(2,1)S(1)} %get-tuple-element.126), channel_id=1, source_target_pairs={{0,8},{1,9},{2,10},{3,11},{4,12},{5,13},{6,14},{7,15},{8,0},{9,1},... | collective-permute-start | bytes 49160 | tf_op jit(solution)/shard_map/ppermute | solution.py:568
  48.8 27.7 %collective-permute-start.11 = (bf16[192,1024]{1,0:T(8,128)(2,1)S(1)}, bf16[192,1024]{1,0:T(8,128)(2,1)S(1)}, u32[]{:S(2)}, u32[]{:S(2)}) collective-permute-start(bf16[192,1024]{1,0:T(8,128)(2,1)S(1)} %get-tuple-element.118.refs_0_), channel_id=1, source_target_pairs={{0,31},{1,0},{2,1},{3,2},{4,3},{5,4},{6,5},{7,6},{8,7},{9,8},{10,9... | collective-permute-start | bytes 1179656 | tf_op jit(solution)/shard_map/ppermute | solution.py:568
  49.4 27.2 %collective-permute-start.12 = (bf16[192,1024]{1,0:T(8,128)(2,1)S(1)}, bf16[192,1024]{1,0:T(8,128)(2,1)S(1)}, u32[]{:S(2)}, u32[]{:S(2)}) collective-permute-start(bf16[192,1024]{1,0:T(8,128)(2,1)S(1)} %get-tuple-element.119), channel_id=1, source_target_pairs={{0,1},{1,2},{2,3},{3,4},{4,5},{5,6},{6,7},{7,8},{8,9},{9,10},{10,1... | collective-permute-start | bytes 1179656 | tf_op jit(solution)/shard_map/ppermute | solution.py:568
  53.2 18.2 %all-to-all-start = ((bf16[8,16,512]{2,1,0:T(8,128)(2,1)}), bf16[8,16,512]{2,1,0:T(8,128)(2,1)S(1)}, u32[]{:S(2)}, u32[]{:S(2)}) async-start(bf16[8,16,512]{2,1,0:T(8,128)(2,1)} %copies.1), calls=%async_computation | async-start | bytes 262144 | tf_op jit(solution)/shard_map/all_to_all | solution.py:734
  61.8 9.4 %collective-permute-start.13 = (bf16[64,1024]{1,0:T(8,128)(2,1)S(1)}, bf16[64,1024]{1,0:T(8,128)(2,1)S(1)}, u32[]{:S(2)}, u32[]{:S(2)}) collective-permute-start(bf16[64,1024]{1,0:T(8,128)(2,1)S(1)} %get-tuple-element.103.refs_10_), channel_id=1, source_target_pairs={{0,30},{1,3},{2,0},{3,5},{4,2},{5,7},{6,4},{7,9},{8,6},{9,11},{10,... | collective-permute-start | bytes 393224 | tf_op jit(solution)/shard_map/ppermute | solution.py:568
  65.5 5.8 %collective-permute-start.14 = (bf16[32,1024]{1,0:T(8,128)(2,1)S(1)}, bf16[32,1024]{1,0:T(8,128)(2,1)S(1)}, u32[]{:S(2)}, u32[]{:S(2)}) collective-permute-start(bf16[32,1024]{1,0:T(8,128)(2,1)S(1)} %get-tuple-element.120), channel_id=1, source_target_pairs={{0,28},{1,5},{2,30},{3,7},{4,0},{5,9},{6,2},{7,11},{8,4},{9,13},{1... | collective-permute-start | bytes 196616 | tf_op jit(solution)/shard_map/ppermute | solution.py:568
  71.3 5.3 %collective-permute-start.16 = (bf16[48,1024]{1,0:T(8,128)(2,1)S(1)}, bf16[48,1024]{1,0:T(8,128)(2,1)S(1)}, u32[]{:S(2)}, u32[]{:S(2)}) collective-permute-start(bf16[48,1024]{1,0:T(8,128)(2,1)S(1)} %far_split.1), channel_id=1, source_target_pairs={{0,1},{1,0},{2,3},{3,2},{4,5},{5,4},{6,7},{7,6},{8,9},{9,8},{10,11... | collective-permute-start | bytes 294920 | tf_op jit(solution)/shard_map/ppermute | solution.py:568
  71.4 5.2 %collective-permute-start.15 = (bf16[16,1024]{1,0:T(8,128)(2,1)S(1)}, bf16[16,1024]{1,0:T(8,128)(2,1)S(1)}, u32[]{:S(2)}, u32[]{:S(2)}) collective-permute-start(bf16[16,1024]{1,0:T(8,128)(2,1)S(1)} %get-tuple-element.121), channel_id=1, source_target_pairs={{0,6},{1,7},{2,28},{3,29},{4,10},{5,11},{6,0},{7,1},{8,14},{9,15},... | collective-permute-start | bytes 98312 | tf_op jit(solution)/shard_map/ppermute | solution.py:568

commit v5 on v4

--- a/solution.py
+++ b/solution.py
@@ -147,7 +147,7 @@
 
 
 def coarsen_kernel(
-    seg_hbm, k_hbm, v_hbm, up, down, far, own0, own1, qdoc, seg, k, v, sems
+    seg_hbm, k_hbm, v_hbm, up, down, far, third, own0, own1, qdoc, seg, k, v, sems
 ):
     copies = fetch((seg_hbm, k_hbm, v_hbm), (seg, k, v), sems)
     copies[0].wait()
@@ -179,6 +179,7 @@
         put(down, BLOCK * level, level, 0, BLOCK)
     put(far, 0, 3, 0, COUNT[3])
     put(far, COUNT[3], 4, 0, COUNT[4])
+    put(third, 0, 4, 0, COUNT[4])
     put(own0, 0, 0, 0, COUNT[0])
     put(own1, 0, 1, 0, COUNT[1])
 
@@ -187,16 +188,16 @@
     return lax.axis_index("ctx") % 2
 
 
-def prepare_kernel(
-    far, far_partner, q_hbm, d_hbm, w_hbm, far3, far4, third, q_out, grad_att, w, d_out, q, sems
-):
-    copies = fetch((q_hbm, d_hbm, w_hbm), (q, d_out, w), sems)
+def pair_kernel(far, far_partner, far3, far4):
     even = core_index() == 0
     for out, start, rows in ((far3, 0, 32), (far4, 32, 16)):
         own, other = far[start : start + rows], far_partner[start : start + rows]
         out[0:rows] = jnp.where(even, own, other)
         out[rows : 2 * rows] = jnp.where(even, other, own)
-    third[...] = far[32:48]
+
+
+def prepare_kernel(q_hbm, d_hbm, w_hbm, q_out, grad_att, w, d_out, q, sems):
+    copies = fetch((q_hbm, d_hbm, w_hbm), (q, d_out, w), sems)
     copies[0].wait()
     for level in range(LEVELS + 1):
         queries = q[...] if level == 0 else dot(gather_table(level, 0.5**level), q[...]).astype(BF16)
@@ -346,7 +347,7 @@
 
 def far_back_kernel(p_in, q_all, g_in, d_side, *refs):
     far = far_refs(refs[:4])
-    d_q, to_3, to_4, to_third, to_partner = refs[4:]
+    d_q, to_3, to_4, to_third, to_partner = refs[-5:]
     to_far = (
         (to_3, to_partner.at[0:64]),
         (to_4, to_partner.at[64:96], to_third, to_partner.at[96:112]),
@@ -595,22 +596,24 @@
 def body(queries, key_rows, value_rows, segment_ids, w_out, d_out):
     q, k, v, grad_out = queries[0], key_rows[0], value_rows[0], d_out[0]
     tokens, dma = (ROWS, WIDTH), pltpu.SemaphoreType.DMA
-    up, down, far, own0, own1, qdoc = call(
+    up, down, far, third_rows, own0, own1, qdoc = call(
         coarsen_kernel,
         "coarsen",
-        [((192, PACK), BF16), ((192, PACK), BF16), ((48, PACK), BF16)]
+        [((192, PACK), BF16), ((192, PACK), BF16), ((48, PACK), BF16), ((16, PACK), BF16)]
         + [((ROWS, PACK), BF16), ((128, PACK), BF16), ((ALL_ROWS, LANES), BF16)],
         [segment_ids, k, v],
         [pltpu.VMEM((1, ROWS), jnp.int32)] + [pltpu.VMEM(tokens, BF16)] * 2 + [dma((3,))],
         in_hbm=3,
     )
     far_partner = moved(far, partner)
-    far3, far4, third_rows, q_all, grad_att, w, grad_rows = call(
+    far3, far4 = call(
+        pair_kernel, "pair", [((64, PACK), BF16), ((32, PACK), BF16)], [far, far_partner]
+    )
+    q_all, grad_att, w, grad_rows = call(
         prepare_kernel,
         "prepare",
-        [((64, PACK), BF16), ((32, PACK), BF16), ((16, PACK), BF16)]
-        + [((ALL_ROWS, WIDTH), BF16), (tokens, F32), ((WIDTH, WIDTH), BF16), (tokens, BF16)],
-        [far, far_partner, q, grad_out, w_out],
+        [((ALL_ROWS, WIDTH), BF16), (tokens, F32), ((WIDTH, WIDTH), BF16), (tokens, BF16)],
+        [q, grad_out, w_out],
         [pltpu.VMEM(tokens, BF16), dma((3,))],
         in_hbm=3,
     )
@@ -650,28 +653,30 @@
         microseconds=6,
     )
     got_w = moved(give, partner)
+
+    def halved(keep, got, divisor, route, *after):
+        rows = keep.shape[0] // 2
+        keep, give = call(
+            functools.partial(halve_kernel, divisor),
+            "halve_" + str(rows),
+            [((rows, WIDTH), F32), ((rows, WIDTH), BF16)],
+            [keep, got, *after],
+            [pltpu.VMEM((2 * rows, WIDTH), F32)],
+            in_hbm=len(after),
+        )
+        return keep, moved(give, route)
+
+    keep, got_w = halved(keep, got_w, 4, lambda i: i ^ 6)
     d_far, *to_far, to_partner = call(
         far_back_kernel,
         "far_back",
         [((48, WIDTH), BF16), ((32, 2 * WIDTH), BF16), ((32, 2 * WIDTH), BF16)]
         + [((16, 2 * WIDTH), BF16), ((112, 2 * WIDTH), BF16)],
-        [p_far, q_all, g, d_side, *far],
+        [p_far, q_all, g, d_side, *far, keep],
+        in_hbm=1,
     )
     swapped = moved(to_partner, partner)
 
-    def halved(keep, got, divisor, route, after):
-        rows = keep.shape[0] // 2
-        keep, give = call(
-            functools.partial(halve_kernel, divisor),
-            "halve_" + str(rows),
-            [((rows, WIDTH), F32), ((rows, WIDTH), BF16)],
-            [keep, got, after],
-            [pltpu.VMEM((2 * rows, WIDTH), F32)],
-            in_hbm=1,
-        )
-        return keep, moved(give, route)
-
-    keep, got_w = halved(keep, got_w, 4, lambda i: i ^ 6, d_far)
 
     def part_outs(part):
         width = len(NEAR_PARTS[part]) * LANES
@@ -680,6 +685,16 @@
         ] * 2
 
     args = [p_near, q_all, g, d_side, *near, d_far]
+    sum3, sum4, sum_third = call(
+        far_sum_kernel,
+        "far_sum",
+        [((64, 2 * WIDTH), BF16), ((32, 2 * WIDTH), BF16), ((16, 2 * WIDTH), BF16)],
+        [*to_far, swapped],
+    )
+    back3 = moved(sum3, back_3)
+    back4 = moved(sum4, back_4)
+    back_third = moved(sum_third, third)
+    keep, got_w = halved(keep, got_w, 2, lambda i: i ^ 2, sum3)
     *part_a, layer_out = call(
         near_back_a_kernel,
         "near_back_a",
@@ -690,46 +705,38 @@
         microseconds=3,
         to_hbm=(5,),
     )
-    sum3, sum4, sum_third = call(
-        far_sum_kernel,
-        "far_sum",
-        [((64, 2 * WIDTH), BF16), ((32, 2 * WIDTH), BF16), ((16, 2 * WIDTH), BF16)],
-        [*to_far, swapped],
-    )
-    back3 = moved(sum3, back_3)
-    back4 = moved(sum4, back_4)
-    back_third = moved(sum_third, third)
-    keep, got_w = halved(keep, got_w, 2, lambda i: i ^ 2, part_a[0])
+    keep, got_w = halved(keep, got_w, 16, lambda i: i ^ 24, part_a[0])
     part_b = call(
         near_back_b_kernel,
         "near_back_b",
         part_outs(1),
-        [*args, part_a[0], sum3, keep],
-        in_hbm=3,
+        [*args, part_a[0], keep],
+        in_hbm=2,
         microseconds=4,
     )
-    keep, got_w = halved(keep, got_w, 16, lambda i: i ^ 24, part_b[0])
+    keep, got_w = halved(keep, got_w, 8, lambda i: i ^ 8, part_b[0])
+    give = call(far_split_kernel, "far_split", [((48, 2 * WIDTH), BF16)], [back3, back4])[0]
+    swapped = moved(give, partner)
     d_q, own_k, own_v, to_low, to_high = call(
         near_back_c_kernel,
         "near_back_c",
         [(tokens, BF16), ((ROWS, LANES), F32), ((ROWS, LANES), F32)]
         + [((192, 2 * WIDTH), BF16)] * 2,
-        [*args, part_a[0], *part_a[3:], part_b[0], *part_b[3:], keep],
+        [*args, part_a[0], *part_a[3:], part_b[0], *part_b[3:]]
+        + [keep, give, back_third],
         [pltpu.VMEM(tokens, BF16), dma((2,))],
-        in_hbm=1,
+        in_hbm=3,
         microseconds=2,
         to_hbm=(0,),
     )
     low_back = moved(to_low, lambda i: i - 1)
     high_back = moved(to_high, lambda i: i + 1)
-    give = call(far_split_kernel, "far_split", [((48, 2 * WIDTH), BF16)], [back3, back4])[0]
-    swapped = moved(give, partner)
-    keep, got_w = halved(keep, got_w, 8, lambda i: i ^ 8, to_low)
     copies = call(
         copies_kernel,
         "copies",
         [((lax.axis_size("dp"), 16, WIDTH), BF16)],
-        [keep, got_w],
+        [keep, got_w, to_low],
+        in_hbm=1,
     )[0]
     copies = lax.all_to_all(copies, "dp", 0, 0, tiled=True)
     d_w = call(last_sum_kernel, "last_sum", [((16, WIDTH), BF16)], [copies])[0]

time: 78.3 us -> 76.4 us (0.976)
  waiting for transfers between devices: 29.4 us -> 20.4 us
  starting transfers between devices: 25.4 us -> 32.1 us
    ppermute x19, waiting for transfers between devices: 29.4 us -> 12.8 us  [moved(): return lax.ppermute(x, 'ctx', [(i, route(i) % count) for i in range(count)])]
    all_to_all x1, waiting for transfers between devices: 0.01 us -> 7.62 us  [body(): copies = lax.all_to_all(copies, 'dp', 0, 0, tiled=True)]
    ppermute x19, starting transfers between devices: 16.9 us -> 23.6 us  [moved(): return lax.ppermute(x, 'ctx', [(i, route(i) % count) for i in range(count)])]
    pallas_call x18 -> x19, Pallas kernels: 19.4 us -> 19.4 us  [call(): pl.pallas_call(kernel, name=name, out_shape=[jax.ShapeDtypeStruct(shape,...]
  transfers between devices with their start and end apart: 20 -> 20, of which waited for: 11 -> 9; matrix products, arithmetic and copies ran while one was open for 0% -> 0% of each run, Pallas kernels for 14% -> 14%
where the time goes in v5:
time: 76.4 us; the launch traced here: 75.6 us
  starting transfers between devices  32.1 us (42%)
  waiting for transfers between devices  20.4 us (27%)
  Pallas kernels  19.4 us (25%)
  local copies, waits for them, and re-layouts  2.58 us (3%)
  between operations  1.01 us (1%)
    ppermute x19, starting transfers between devices, moved(): return lax.ppermute(x, 'ctx', [(i, route(i) % count) for i in range(count)])  23.6 us
    pallas_call x19, Pallas kernels, call(): pl.pallas_call(kernel, name=name, out_shape=[jax.ShapeDtypeStruct(shape,...  19.4 us
    ppermute x19, waiting for transfers between devices, moved(): return lax.ppermute(x, 'ctx', [(i, route(i) % count) for i in range(count)])  12.8 us
    all_to_all x1, starting transfers between devices, body(): copies = lax.all_to_all(copies, 'dp', 0, 0, tiled=True)  8.57 us
    all_to_all x1, waiting for transfers between devices, body(): copies = lax.all_to_all(copies, 'dp', 0, 0, tiled=True)  7.62 us
    unnamed x12, local copies, waits for them, and re-layouts  2.58 us
  transfers between devices with their start and end apart: 20, of which 9 were waited for; matrix products, arithmetic and copies ran while one was open for 0% of the time, Pallas kernels for 14%

profile of v5, /device:TPU:32, one launch (start us, length us, event | category | flops | bytes accessed | tf_op | source)
XLA Modules:
  0.0 75.6 jit_solution(10208910072321185423)
XLA Ops:
  0.6 0.9 %copy-done.1 = bf16[1,256,512]{2,1,0:T(8,128)(2,1)S(1)} copy-done((bf16[1,256,512]{2,1,0:T(8,128)(2,1)S(1)}, bf16[1,256,512]{2,1,0:T(8,128)(2,1)}, u32[]{:S(2)}) %copy-start.1) | copy-done | bytes 262168
  1.6 0.9 %copy-done.2 = bf16[1,256,512]{2,1,0:T(8,128)(2,1)S(1)} copy-done((bf16[1,256,512]{2,1,0:T(8,128)(2,1)S(1)}, bf16[1,256,512]{2,1,0:T(8,128)(2,1)}, u32[]{:S(2)}) %copy-start.2) | copy-done | bytes 262168
  2.5 0.7 copy-done.5
  3.2 0.7 coarsen.1
  4.0 5.1 %collective-permute-start.1 = (bf16[192,1152]{1,0:T(8,128)(2,1)S(1)}, bf16[192,1152]{1,0:T(8,128)(2,1)S(1)}, u32[]{:S(2)}, u32[]{:S(2)}) collective-permute-start(bf16[192,1152]{1,0:T(8,128)(2,1)S(1)} %get-tuple-element.71), channel_id=1, source_target_pairs={{0,31},{1,0},{2,1},{3,2},{4,3},{5,4},{6,5},{7,6},{8,7},{9,8},{10,9... | collective-permute-start | bytes 1327112 | tf_op jit(solution)/shard_map/ppermute | solution.py:569
  9.1 1.3 %collective-permute-done.2.far_partner = bf16[48,1152]{1,0:T(8,128)(2,1)S(1)} collective-permute-done((bf16[48,1152]{1,0:T(8,128)(2,1)S(1)}, bf16[48,1152]{1,0:T(8,128)(2,1)S(1)}, u32[]{:S(2)}, u32[]{:S(2)}) %collective-permute-start.2) | collective-permute-done | bytes 110624 | tf_op jit(solution)/shard_map/ppermute | solution.py:569
  10.5 2.9 %collective-permute-start.5 = (bf16[16,1152]{1,0:T(8,128)(2,1)S(1)}, bf16[16,1152]{1,0:T(8,128)(2,1)S(1)}, u32[]{:S(2)}, u32[]{:S(2)}) collective-permute-start(bf16[16,1152]{1,0:T(8,128)(2,1)S(1)} %get-tuple-element.82), channel_id=1, source_target_pairs={{0,6},{1,7},{2,28},{3,29},{4,10},{5,11},{6,0},{7,1},{8,14},{9,15},... | collective-permute-start | bytes 110600 | tf_op jit(solution)/shard_map/ppermute | solution.py:569
  13.5 0.7 prepare.1
  14.2 4.8 %collective-permute-done.3.got3 = bf16[64,1152]{1,0:T(8,128)(2,1)S(1)} collective-permute-done((bf16[64,1152]{1,0:T(8,128)(2,1)S(1)}, bf16[64,1152]{1,0:T(8,128)(2,1)S(1)}, u32[]{:S(2)}, u32[]{:S(2)}) %collective-permute-start.3) | collective-permute-done | bytes 147488 | tf_op jit(solution)/shard_map/ppermute | solution.py:569
  19.0 2.4 %collective-permute-done.4.got4.refs_1_ = bf16[32,1152]{1,0:T(8,128)(2,1)S(1)} collective-permute-done((bf16[32,1152]{1,0:T(8,128)(2,1)S(1)}, bf16[32,1152]{1,0:T(8,128)(2,1)S(1)}, u32[]{:S(2)}, u32[]{:S(2)}) %collective-permute-start.4) | collective-permute-done | bytes 73760 | tf_op jit(solution)/shard_map/ppermute | solution.py:569
  21.6 1.7 %near.1 = (bf16[4,896,256]{2,1,0:T(8,128)(2,1)S(1)}, f32[4,256,384]{2,1,0:T(8,128)S(1)}, bf16[4,192,384]{2,1,0:T(8,128)(2,1)S(1)}) custom-call(bf16[496,512]{1,0:T(8,128)(2,1)S(1)} %get-tuple-element.66.q_all.refs_1_, bf16[496,128]{1,0:T(8,128)(2,1)S(1)} %get-tuple-element.67.qdoc, bf16[256,1152]{1,0:T(8,128)(2,1)S(1)} %get-tuple-element.68.own0.refs_4_, ...), custom_call_target="tpu_custom_call" | custom-call | flops 49999998976 | bytes 1048576 | tf_op jit(solution)/shard_map/near/pallas_call | solution.py:553
  23.2 5.6 %merge.1 = (bf16[256,512]{1,0:T(8,128)(2,1)S(1)}, f32[256,512]{1,0:T(8,128)S(1)}, bf16[256,512]{1,0:T(8,128)(2,1)S(1)}, bf16[4,96,128]{2,1,0:T(8,128)(2,1)S(1)},...) custom-call(bf16[496,512]{1,0:T(8,128)(2,1)S(1)} %get-tuple-element.66.q_all.refs_1_, ...), custom_call_target="tpu_custom_call" | custom-call | flops 6000000000 | bytes 1048576 | tf_op jit(solution)/shard_map/merge/pallas_call | solution.py:553
  28.9 0.8 collective-permute-start.7
  29.6 1.2 %collective-permute-done.7.got = bf16[256,512]{1,0:T(8,128)(2,1)S(1)} collective-permute-done((bf16[256,512]{1,0:T(8,128)(2,1)S(1)}, bf16[256,512]{1,0:T(8,128)(2,1)S(1)}, u32[]{:S(2)}, u32[]{:S(2)}) %collective-permute-start.7) | collective-permute-done | bytes 262176 | tf_op jit(solution)/shard_map/ppermute | solution.py:569
  30.9 1.1 %far_back.1 = (bf16[48,512]{1,0:T(8,128)(2,1)S(1)}, bf16[32,1024]{1,0:T(8,128)(2,1)S(1)}, bf16[32,1024]{1,0:T(8,128)(2,1)S(1)}, bf16[16,1024]{1,0:T(8,128)(2,1)S(1)}, bf16[112,1024]{1,0:T(8,128)(2,1)S(1)}) custom-call(bf16[4,96,128]{2,1,0:T(8,128)(2,1)S(1)} %get-tuple-element.90.p_in, bf16[496,512]{1,0:T(8,128)(2,1)S(1)} %get-tuple-element.66.q_all.refs_1_, ...), custom_call_target="tpu_custom_call" | custom-call | flops 1000000000 | bytes 1048576 | tf_op jit(solution)/shard_map/far_back/pallas_call | solution.py:553
  32.5 0.8 %collective-permute-start.8 = (bf16[128,512]{1,0:T(8,128)(2,1)S(1)}, bf16[128,512]{1,0:T(8,128)(2,1)S(1)}, u32[]{:S(2)}, u32[]{:S(2)}) collective-permute-start(bf16[128,512]{1,0:T(8,128)(2,1)S(1)} %get-tuple-element.95), channel_id=1, source_target_pairs={{0,6},{1,7},{2,4},{3,5},{4,2},{5,3},{6,0},{7,1},{8,14},{9,15},{10,... | collective-permute-start | bytes 393224 | tf_op jit(solution)/shard_map/ppermute | solution.py:569
  33.7 2.2 %collective-permute-start.14 = (bf16[16,1024]{1,0:T(8,128)(2,1)S(1)}, bf16[16,1024]{1,0:T(8,128)(2,1)S(1)}, u32[]{:S(2)}, u32[]{:S(2)}) collective-permute-start(bf16[16,1024]{1,0:T(8,128)(2,1)S(1)} %get-tuple-element.114), channel_id=1, source_target_pairs={{0,6},{1,7},{2,28},{3,29},{4,10},{5,11},{6,0},{7,1},{8,14},{9,15},... | collective-permute-start | bytes 98312 | tf_op jit(solution)/shard_map/ppermute | solution.py:569
  35.9 2.4 %collective-permute-start.13 = (bf16[32,1024]{1,0:T(8,128)(2,1)S(1)}, bf16[32,1024]{1,0:T(8,128)(2,1)S(1)}, u32[]{:S(2)}, u32[]{:S(2)}) collective-permute-start(bf16[32,1024]{1,0:T(8,128)(2,1)S(1)} %get-tuple-element.113), channel_id=1, source_target_pairs={{0,28},{1,5},{2,30},{3,7},{4,0},{5,9},{6,2},{7,11},{8,4},{9,13},{1... | collective-permute-start | bytes 196616 | tf_op jit(solution)/shard_map/ppermute | solution.py:569
  38.3 0.8 %collective-permute-start.12 = (bf16[64,1024]{1,0:T(8,128)(2,1)S(1)}, bf16[64,1024]{1,0:T(8,128)(2,1)S(1)}, u32[]{:S(2)}, u32[]{:S(2)}) collective-permute-start(bf16[64,1024]{1,0:T(8,128)(2,1)S(1)} %get-tuple-element.100.refs_0_), channel_id=1, source_target_pairs={{0,30},{1,3},{2,0},{3,5},{4,2},{5,7},{6,4},{7,9},{8,6},{9,11},{10,... | collective-permute-start | bytes 393224 | tf_op jit(solution)/shard_map/ppermute | solution.py:569
  39.6 0.9 %collective-permute-start.10 = (bf16[64,512]{1,0:T(8,128)(2,1)S(1)}, bf16[64,512]{1,0:T(8,128)(2,1)S(1)}, u32[]{:S(2)}, u32[]{:S(2)}) collective-permute-start(bf16[64,512]{1,0:T(8,128)(2,1)S(1)} %get-tuple-element.106), channel_id=1, source_target_pairs={{0,2},{1,3},{2,0},{3,1},{4,6},{5,7},{6,4},{7,5},{8,10},{9,11},{10,... | collective-permute-start | bytes 196616 | tf_op jit(solution)/shard_map/ppermute | solution.py:569
  40.5 2.0 %near_back_a.1 = (bf16[256,128]{1,0:T(8,128)(2,1)S(1)}, f32[256,128]{1,0:T(8,128)S(1)}, f32[256,128]{1,0:T(8,128)S(1)}, bf16[2,192,128]{2,1,0:T(8,128)(2,1)S(1)}...) custom-call(bf16[256,512]{1,0:T(8,128)(2,1)S(1)} %get-tuple-element.85.attended, ...), custom_call_target="tpu_custom_call" | custom-call | flops 3000000000 | bytes 1048576 | tf_op jit(solution)/shard_map/near_back_a/pallas_call | solution.py:553
  42.5 1.6 %collective-permute-done.10.got = bf16[64,512]{1,0:T(8,128)(2,1)S(1)} collective-permute-done((bf16[64,512]{1,0:T(8,128)(2,1)S(1)}, bf16[64,512]{1,0:T(8,128)(2,1)S(1)}, u32[]{:S(2)}, u32[]{:S(2)}) %collective-permute-start.10) | collective-permute-done | bytes 65568 | tf_op jit(solution)/shard_map/ppermute | solution.py:569
  44.1 1.7 %collective-permute-start.11 = (bf16[32,512]{1,0:T(8,128)(2,1)S(1)}, bf16[32,512]{1,0:T(8,128)(2,1)S(1)}, u32[]{:S(2)}, u32[]{:S(2)}) collective-permute-start(bf16[32,512]{1,0:T(8,128)(2,1)S(1)} %get-tuple-element.111), channel_id=1, source_target_pairs={{0,24},{1,25},{2,26},{3,27},{4,28},{5,29},{6,30},{7,31},{8,16},{9,... | collective-permute-start | bytes 98312 | tf_op jit(solution)/shard_map/ppermute | solution.py:569
  45.8 2.7 %near_back_b.1 = (bf16[256,256]{1,0:T(8,128)(2,1)S(1)}, f32[256,256]{1,0:T(8,128)S(1)}, f32[256,256]{1,0:T(8,128)S(1)}, bf16[2,192,256]{2,1,0:T(8,128)(2,1)S(1)}, bf16[2,192,256]{2,1,0:T(8,128)(2,1)S(1)}) custom-call(bf16[4,896,256]{2,1,0:T(8,128)(2,1)S(1)} %get-tuple-element.87.refs_0_, bf16[496,512]{1,0:T(8,128)(2,1)S(1)} %get-tuple-element.66.q_all.refs_1_, ...), custom_call_target="tpu_custom_call" | custom-call | flops 4000000000 | bytes 1048576 | tf_op jit(solution)/shard_map/near_back_b/pallas_call | solution.py:553
  48.5 0.8 %collective-permute-done.11.got = bf16[32,512]{1,0:T(8,128)(2,1)S(1)} collective-permute-done((bf16[32,512]{1,0:T(8,128)(2,1)S(1)}, bf16[32,512]{1,0:T(8,128)(2,1)S(1)}, u32[]{:S(2)}, u32[]{:S(2)}) %collective-permute-start.11) | collective-permute-done | bytes 32800 | tf_op jit(solution)/shard_map/ppermute | solution.py:569
  49.5 2.1 %near_back_c.1 = (bf16[256,512]{1,0:T(8,128)(2,1)}, f32[256,128]{1,0:T(8,128)S(1)}, f32[256,128]{1,0:T(8,128)S(1)}, bf16[192,1024]{1,0:T(8,128)(2,1)S(1)}, bf16[192,1024]{1,0:T(8,128)(2,1)S(1)}) custom-call(bf16[4,896,256]{2,1,0:T(8,128)(2,1)S(1)} %get-tuple-element.87.refs_0_, bf16[496,512]{1,0:T(8,128)(2,1)S(1)} %get-tuple-element.66.q_all.refs_1_, ...), custom_call_target="tpu_custom_call" | custom-call | flops 2000000000 | bytes 1048576 | tf_op jit(solution)/shard_map/near_back_c/pallas_call | solution.py:553
  51.7 5.1 %collective-permute-start.15 = (bf16[192,1024]{1,0:T(8,128)(2,1)S(1)}, bf16[192,1024]{1,0:T(8,128)(2,1)S(1)}, u32[]{:S(2)}, u32[]{:S(2)}) collective-permute-start(bf16[192,1024]{1,0:T(8,128)(2,1)S(1)} %get-tuple-element.122.refs_0_), channel_id=1, source_target_pairs={{0,31},{1,0},{2,1},{3,2},{4,3},{5,4},{6,5},{7,6},{8,7},{9,8},{10,9... | collective-permute-start | bytes 1179656 | tf_op jit(solution)/shard_map/ppermute | solution.py:569
  56.8 0.7 copies.1
  57.4 8.6 %all-to-all-start = ((bf16[8,16,512]{2,1,0:T(8,128)(2,1)}), bf16[8,16,512]{2,1,0:T(8,128)(2,1)S(1)}, u32[]{:S(2)}, u32[]{:S(2)}) async-start(bf16[8,16,512]{2,1,0:T(8,128)(2,1)} %copies.1), calls=%async_computation | async-start | bytes 262144 | tf_op jit(solution)/shard_map/all_to_all | solution.py:741
  66.0 7.6 %all-to-all-done.parts = bf16[8,16,512]{2,1,0:T(8,128)(2,1)S(1)} async-done(((bf16[8,16,512]{2,1,0:T(8,128)(2,1)}), bf16[8,16,512]{2,1,0:T(8,128)(2,1)S(1)}, u32[]{:S(2)}, u32[]{:S(2)}) %all-to-all-start) | async-done | bytes 131104 | tf_op jit(solution)/shard_map/all_to_all | solution.py:741
  73.6 0.6 last_sum.1
  74.3 1.1 %combine.1 = (bf16[256,512]{1,0:T(8,128)(2,1)}, bf16[256,512]{1,0:T(8,128)(2,1)}) custom-call(f32[256,128]{1,0:T(8,128)S(1)} %get-tuple-element.116.refs_0_, f32[256,256]{1,0:T(8,128)S(1)} %get-tuple-element.117.refs_1_, f32[256,128]{1,0:T(8,128)S(1)} %get-tuple-element.118.refs_2_, f32[256,128]{1,0:T(8,128)S(1)} %get-tuple-element.119.refs_3_, ...), custom_call_target="tpu_custom_call" | custom-call | flops 1000000000 | bytes 1048576 | tf_op jit(solution)/shard_map/combine/pallas_call | solution.py:553
  (39 shorter events, 2.0 us)
Async XLA Ops:
  0.6 1.0 %copy-start.1 = (bf16[1,256,512]{2,1,0:T(8,128)(2,1)S(1)}, bf16[1,256,512]{2,1,0:T(8,128)(2,1)}, u32[]{:S(2)}) copy-start(bf16[1,256,512]{2,1,0:T(8,128)(2,1)} %param.7) | copy-start | bytes 786436
  1.6 0.9 %copy-start.2 = (bf16[1,256,512]{2,1,0:T(8,128)(2,1)S(1)}, bf16[1,256,512]{2,1,0:T(8,128)(2,1)}, u32[]{:S(2)}) copy-start(bf16[1,256,512]{2,1,0:T(8,128)(2,1)} %param.8) | copy-start | bytes 786436
  2.5 0.7 copy-start.5
  3.9 15.0 %collective-permute-start = (bf16[192,1152]{1,0:T(8,128)(2,1)S(1)}, bf16[192,1152]{1,0:T(8,128)(2,1)S(1)}, u32[]{:S(2)}, u32[]{:S(2)}) collective-permute-start(bf16[192,1152]{1,0:T(8,128)(2,1)S(1)} %get-tuple-element.70), channel_id=1, source_target_pairs={{0,1},{1,2},{2,3},{3,4},{4,5},{5,6},{6,7},{7,8},{8,9},{9,10},{10,1... | collective-permute-start | bytes 1327112 | tf_op jit(solution)/shard_map/ppermute | solution.py:569
  4.0 15.0 %collective-permute-start.1 = (bf16[192,1152]{1,0:T(8,128)(2,1)S(1)}, bf16[192,1152]{1,0:T(8,128)(2,1)S(1)}, u32[]{:S(2)}, u32[]{:S(2)}) collective-permute-start(bf16[192,1152]{1,0:T(8,128)(2,1)S(1)} %get-tuple-element.71), channel_id=1, source_target_pairs={{0,31},{1,0},{2,1},{3,2},{4,3},{5,4},{6,5},{7,6},{8,7},{9,8},{10,9... | collective-permute-start | bytes 1327112 | tf_op jit(solution)/shard_map/ppermute | solution.py:569
  9.1 4.4 %copy-start = (bf16[512,512]{1,0:T(8,128)(2,1)S(1)}, bf16[512,512]{1,0:T(8,128)(2,1)}, u32[]{:S(2)}) copy-start(bf16[512,512]{1,0:T(8,128)(2,1)} %w_hbm.1) | copy-start | bytes 1572868
  9.1 4.4 %copy-start.3 = (bf16[1,256,512]{2,1,0:T(8,128)(2,1)S(1)}, bf16[1,256,512]{2,1,0:T(8,128)(2,1)}, u32[]{:S(2)}) copy-start(bf16[1,256,512]{2,1,0:T(8,128)(2,1)} %param.6) | copy-start | bytes 786436
  9.1 4.4 %copy-start.4 = (bf16[1,256,512]{2,1,0:T(8,128)(2,1)S(1)}, bf16[1,256,512]{2,1,0:T(8,128)(2,1)}, u32[]{:S(2)}) copy-start(bf16[1,256,512]{2,1,0:T(8,128)(2,1)} %param.11) | copy-start | bytes 786436
  9.1 1.3 %collective-permute-start.2 = (bf16[48,1152]{1,0:T(8,128)(2,1)S(1)}, bf16[48,1152]{1,0:T(8,128)(2,1)S(1)}, u32[]{:S(2)}, u32[]{:S(2)}) collective-permute-start(bf16[48,1152]{1,0:T(8,128)(2,1)S(1)} %get-tuple-element.72.far), channel_id=1, source_target_pairs={{0,1},{1,0},{2,3},{3,2},{4,5},{5,4},{6,7},{7,6},{8,9},{9,8},{10,11... | collective-permute-start | bytes 331784 | tf_op jit(solution)/shard_map/ppermute | solution.py:569
  10.4 8.5 %collective-permute-start.3 = (bf16[64,1152]{1,0:T(8,128)(2,1)S(1)}, bf16[64,1152]{1,0:T(8,128)(2,1)S(1)}, u32[]{:S(2)}, u32[]{:S(2)}) collective-permute-start(bf16[64,1152]{1,0:T(8,128)(2,1)S(1)} %get-tuple-element.73), channel_id=1, source_target_pairs={{0,2},{1,31},{2,4},{3,1},{4,6},{5,3},{6,8},{7,5},{8,10},{9,7},{10,... | collective-permute-start | bytes 442376 | tf_op jit(solution)/shard_map/ppermute | solution.py:569
  10.5 8.5 %collective-permute-start.5 = (bf16[16,1152]{1,0:T(8,128)(2,1)S(1)}, bf16[16,1152]{1,0:T(8,128)(2,1)S(1)}, u32[]{:S(2)}, u32[]{:S(2)}) collective-permute-start(bf16[16,1152]{1,0:T(8,128)(2,1)S(1)} %get-tuple-element.82), channel_id=1, source_target_pairs={{0,6},{1,7},{2,28},{3,29},{4,10},{5,11},{6,0},{7,1},{8,14},{9,15},... | collective-permute-start | bytes 110600 | tf_op jit(solution)/shard_map/ppermute | solution.py:569
  13.5 8.0 %collective-permute-start.4 = (bf16[32,1152]{1,0:T(8,128)(2,1)S(1)}, bf16[32,1152]{1,0:T(8,128)(2,1)S(1)}, u32[]{:S(2)}, u32[]{:S(2)}) collective-permute-start(bf16[32,1152]{1,0:T(8,128)(2,1)S(1)} %get-tuple-element.81), channel_id=1, source_target_pairs={{0,4},{1,29},{2,6},{3,31},{4,8},{5,1},{6,10},{7,3},{8,12},{9,5},{1... | collective-permute-start | bytes 221192 | tf_op jit(solution)/shard_map/ppermute | solution.py:569
  21.5 1.8 %collective-permute-start.6 = (bf16[112,1152]{1,0:T(8,128)(2,1)S(1)}, bf16[112,1152]{1,0:T(8,128)(2,1)S(1)}, u32[]{:S(2)}, u32[]{:S(2)}) collective-permute-start(bf16[112,1152]{1,0:T(8,128)(2,1)S(1)} %get-tuple-element.84), channel_id=1, source_target_pairs={{0,1},{1,0},{2,3},{3,2},{4,5},{5,4},{6,7},{7,6},{8,9},{9,8},{10,11... | collective-permute-start | bytes 774152 | tf_op jit(solution)/shard_map/ppermute | solution.py:569
  28.9 1.9 %collective-permute-start.7 = (bf16[256,512]{1,0:T(8,128)(2,1)S(1)}, bf16[256,512]{1,0:T(8,128)(2,1)S(1)}, u32[]{:S(2)}, u32[]{:S(2)}) collective-permute-start(bf16[256,512]{1,0:T(8,128)(2,1)S(1)} %get-tuple-element.92), channel_id=1, source_target_pairs={{0,1},{1,0},{2,3},{3,2},{4,5},{5,4},{6,7},{7,6},{8,9},{9,8},{10,11... | collective-permute-start | bytes 786440 | tf_op jit(solution)/shard_map/ppermute | solution.py:569
  32.0 1.6 %collective-permute-start.9 = (bf16[112,1024]{1,0:T(8,128)(2,1)S(1)}, bf16[112,1024]{1,0:T(8,128)(2,1)S(1)}, u32[]{:S(2)}, u32[]{:S(2)}) collective-permute-start(bf16[112,1024]{1,0:T(8,128)(2,1)S(1)} %get-tuple-element.99), channel_id=1, source_target_pairs={{0,1},{1,0},{2,3},{3,2},{4,5},{5,4},{6,7},{7,6},{8,9},{9,8},{10,11... | collective-permute-start | bytes 688136 | tf_op jit(solution)/shard_map/ppermute | solution.py:569
  32.5 7.1 %collective-permute-start.8 = (bf16[128,512]{1,0:T(8,128)(2,1)S(1)}, bf16[128,512]{1,0:T(8,128)(2,1)S(1)}, u32[]{:S(2)}, u32[]{:S(2)}) collective-permute-start(bf16[128,512]{1,0:T(8,128)(2,1)S(1)} %get-tuple-element.95), channel_id=1, source_target_pairs={{0,6},{1,7},{2,4},{3,5},{4,2},{5,3},{6,0},{7,1},{8,14},{9,15},{10,... | collective-permute-start | bytes 393224 | tf_op jit(solution)/shard_map/ppermute | solution.py:569
  33.7 15.8 %collective-permute-start.14 = (bf16[16,1024]{1,0:T(8,128)(2,1)S(1)}, bf16[16,1024]{1,0:T(8,128)(2,1)S(1)}, u32[]{:S(2)}, u32[]{:S(2)}) collective-permute-start(bf16[16,1024]{1,0:T(8,128)(2,1)S(1)} %get-tuple-element.114), channel_id=1, source_target_pairs={{0,6},{1,7},{2,28},{3,29},{4,10},{5,11},{6,0},{7,1},{8,14},{9,15},... | collective-permute-start | bytes 98312 | tf_op jit(solution)/shard_map/ppermute | solution.py:569
  35.9 13.6 %collective-permute-start.13 = (bf16[32,1024]{1,0:T(8,128)(2,1)S(1)}, bf16[32,1024]{1,0:T(8,128)(2,1)S(1)}, u32[]{:S(2)}, u32[]{:S(2)}) collective-permute-start(bf16[32,1024]{1,0:T(8,128)(2,1)S(1)} %get-tuple-element.113), channel_id=1, source_target_pairs={{0,28},{1,5},{2,30},{3,7},{4,0},{5,9},{6,2},{7,11},{8,4},{9,13},{1... | collective-permute-start | bytes 196616 | tf_op jit(solution)/shard_map/ppermute | solution.py:569
  38.3 11.2 %collective-permute-start.12 = (bf16[64,1024]{1,0:T(8,128)(2,1)S(1)}, bf16[64,1024]{1,0:T(8,128)(2,1)S(1)}, u32[]{:S(2)}, u32[]{:S(2)}) collective-permute-start(bf16[64,1024]{1,0:T(8,128)(2,1)S(1)} %get-tuple-element.100.refs_0_), channel_id=1, source_target_pairs={{0,30},{1,3},{2,0},{3,5},{4,2},{5,7},{6,4},{7,9},{8,6},{9,11},{10,... | collective-permute-start | bytes 393224 | tf_op jit(solution)/shard_map/ppermute | solution.py:569
  39.6 4.4 %collective-permute-start.10 = (bf16[64,512]{1,0:T(8,128)(2,1)S(1)}, bf16[64,512]{1,0:T(8,128)(2,1)S(1)}, u32[]{:S(2)}, u32[]{:S(2)}) collective-permute-start(bf16[64,512]{1,0:T(8,128)(2,1)S(1)} %get-tuple-element.106), channel_id=1, source_target_pairs={{0,2},{1,3},{2,0},{3,1},{4,6},{5,7},{6,4},{7,5},{8,10},{9,11},{10,... | collective-permute-start | bytes 196616 | tf_op jit(solution)/shard_map/ppermute | solution.py:569
  44.1 5.2 %collective-permute-start.11 = (bf16[32,512]{1,0:T(8,128)(2,1)S(1)}, bf16[32,512]{1,0:T(8,128)(2,1)S(1)}, u32[]{:S(2)}, u32[]{:S(2)}) collective-permute-start(bf16[32,512]{1,0:T(8,128)(2,1)S(1)} %get-tuple-element.111), channel_id=1, source_target_pairs={{0,24},{1,25},{2,26},{3,27},{4,28},{5,29},{6,30},{7,31},{8,16},{9,... | collective-permute-start | bytes 98312 | tf_op jit(solution)/shard_map/ppermute | solution.py:569
  49.3 7.5 %collective-permute-start.18 = (bf16[16,512]{1,0:T(8,128)(2,1)S(1)}, bf16[16,512]{1,0:T(8,128)(2,1)S(1)}, u32[]{:S(2)}, u32[]{:S(2)}) collective-permute-start(bf16[16,512]{1,0:T(8,128)(2,1)S(1)} %get-tuple-element.126), channel_id=1, source_target_pairs={{0,8},{1,9},{2,10},{3,11},{4,12},{5,13},{6,14},{7,15},{8,0},{9,1},... | collective-permute-start | bytes 49160 | tf_op jit(solution)/shard_map/ppermute | solution.py:569
  51.6 22.6 %collective-permute-start.16 = (bf16[192,1024]{1,0:T(8,128)(2,1)S(1)}, bf16[192,1024]{1,0:T(8,128)(2,1)S(1)}, u32[]{:S(2)}, u32[]{:S(2)}) collective-permute-start(bf16[192,1024]{1,0:T(8,128)(2,1)S(1)} %get-tuple-element.123), channel_id=1, source_target_pairs={{0,1},{1,2},{2,3},{3,4},{4,5},{5,6},{6,7},{7,8},{8,9},{9,10},{10,1... | collective-permute-start | bytes 1179656 | tf_op jit(solution)/shard_map/ppermute | solution.py:569
  51.7 22.6 %collective-permute-start.15 = (bf16[192,1024]{1,0:T(8,128)(2,1)S(1)}, bf16[192,1024]{1,0:T(8,128)(2,1)S(1)}, u32[]{:S(2)}, u32[]{:S(2)}) collective-permute-start(bf16[192,1024]{1,0:T(8,128)(2,1)S(1)} %get-tuple-element.122.refs_0_), channel_id=1, source_target_pairs={{0,31},{1,0},{2,1},{3,2},{4,3},{5,4},{6,5},{7,6},{8,7},{9,8},{10,9... | collective-permute-start | bytes 1179656 | tf_op jit(solution)/shard_map/ppermute | solution.py:569
  57.4 16.2 %all-to-all-start = ((bf16[8,16,512]{2,1,0:T(8,128)(2,1)}), bf16[8,16,512]{2,1,0:T(8,128)(2,1)S(1)}, u32[]{:S(2)}, u32[]{:S(2)}) async-start(bf16[8,16,512]{2,1,0:T(8,128)(2,1)} %copies.1), calls=%async_computation | async-start | bytes 262144 | tf_op jit(solution)/shard_map/all_to_all | solution.py:741
  66.0 8.3 %collective-permute-start.17 = (bf16[48,1024]{1,0:T(8,128)(2,1)S(1)}, bf16[48,1024]{1,0:T(8,128)(2,1)S(1)}, u32[]{:S(2)}, u32[]{:S(2)}) collective-permute-start(bf16[48,1024]{1,0:T(8,128)(2,1)S(1)} %far_split.1.refs_16_), channel_id=1, source_target_pairs={{0,1},{1,0},{2,3},{3,2},{4,5},{5,4},{6,7},{7,6},{8,9},{9,8},{10,11... | collective-permute-start | bytes 294920 | tf_op jit(solution)/shard_map/ppermute | solution.py:569

commit v6 on v5

--- a/solution.py
+++ b/solution.py
@@ -345,13 +345,15 @@
     return grad_q, dot(ds, stacked(queries), 0, 0), dot(p, grad, 0, 0)
 
 
-def far_back_kernel(p_in, q_all, g_in, d_side, *refs):
-    far = far_refs(refs[:4])
-    d_q, to_3, to_4, to_third, to_partner = refs[-5:]
-    to_far = (
-        (to_3, to_partner.at[0:64]),
-        (to_4, to_partner.at[64:96], to_third, to_partner.at[96:112]),
-    )
+PARTNER_ROWS = 112
+MESSAGE_ROWS = 256 + 2 * PARTNER_ROWS
+
+
+def far_back_kernel(p_in, q_all, g_in, d_side, own3, got4, third, passed, give, *refs):
+    far = far_refs((own3, got4, third, passed))
+    d_q, to_3, to_4, to_third, message = refs
+    message[0:256] = give[...]
+    to_far = ((to_3, (0, 64)), (to_4, (64, 96), to_third, (96, 112)))
     for pair in range(PAIRS):
         cols = lanes_of(pair)
         for index, ref, to in zip(FAR, far, to_far):
@@ -368,13 +370,19 @@
             d_q[at - AT[3] : at - AT[3] + rows, cols] = grad_q.astype(BF16)
             start = 0
             for out in to:
-                stop = start + out.shape[0]
-                out[:, cols] = grad_k[start:stop].astype(BF16)
-                out[:, lanes_of(pair, 1)] = grad_v[start:stop].astype(BF16)
+                partners = isinstance(out, tuple)
+                stop = start + (out[1] - out[0] if partners else out.shape[0])
+                for part, grad in enumerate((grad_k, grad_v)):
+                    rows = grad[start:stop].astype(BF16)
+                    if partners:
+                        first = 256 + part * PARTNER_ROWS
+                        message[first + out[0] : first + out[1], cols] = rows
+                    else:
+                        out[:, lanes_of(pair, part)] = rows
                 start = stop
 
 
-NEAR_PARTS = ((0,), (1, 2), (3,))
+NEAR_PARTS = ((0,), (1,), (2,), (3,))
 
 
 def near_back(pairs, p_in, q_all, g_in, d_side, own0, own1, low, high, d_far):
@@ -427,15 +435,15 @@
 
 
 def near_back_a_kernel(attended, w, *refs):
-    near_back_first_kernel(NEAR_PARTS[0], attended, w, *refs[:9], *refs[-8:])
-
-
-def near_back_b_kernel(*refs):
-    near_back_first_kernel(NEAR_PARTS[1], None, None, *refs[:9], *refs[-5:])
-
-
-def near_back_c_kernel(*refs):
-    inputs, earlier = refs[:9], (refs[9:12], refs[12:15])
+    near_back_first_kernel(NEAR_PARTS[0], attended, w, *refs)
+
+
+def near_back_more_kernel(pairs, *refs):
+    near_back_first_kernel(pairs, None, None, *refs[:9], *refs[-5:])
+
+
+def near_back_last_kernel(*refs):
+    inputs, earlier = refs[:9], [refs[at : at + 3] for at in (9, 12, 15)]
     d_q_hbm, own_k, own_v, to_low, to_high, d_q, sems = refs[-7:]
     for pairs, (dq, low, high) in zip(NEAR_PARTS, earlier):
         cols = slice(pairs[0] * LANES, (pairs[-1] + 1) * LANES)
@@ -443,10 +451,10 @@
         for part in range(2):
             lanes = slice(part * WIDTH + cols.start, part * WIDTH + cols.stop)
             to_low[:, lanes], to_high[:, lanes] = low[part], high[part]
-    last = NEAR_PARTS[2][0] * LANES
+    last = NEAR_PARTS[-1][0] * LANES
     before = pltpu.make_async_copy(d_q.at[:, 0:last], d_q_hbm.at[:, 0:last], sems.at[0])
     before.start()
-    for pair, dq, own, low, high in near_back(NEAR_PARTS[2], *inputs):
+    for pair, dq, own, low, high in near_back(NEAR_PARTS[-1], *inputs):
         d_q[:, lanes_of(pair)] = dq
         own_k[...], own_v[...] = own[0], own[1]
         after = pltpu.make_async_copy(
@@ -467,13 +475,30 @@
     own3[...] = jnp.where(core_index() == 0, got3[0:32], got3[32:64])
 
 
-def far_sum_kernel(to_3, to_4, to_third, swapped, sum3, sum4, sum_third):
+def partner_sum_kernel(to_3, to_4, to_third, keep, message, *refs):
+    sum3, sum4, sum_third, keep_out, give_out, total = refs[-6:]
     even = core_index() == 0
-    own3 = to_3[...].astype(F32)
-    sum3[0:32] = (swapped[0:32].astype(F32) + jnp.where(even, own3, 0.0)).astype(BF16)
-    sum3[32:64] = (swapped[32:64].astype(F32) + jnp.where(even, 0.0, own3)).astype(BF16)
-    sum4[...] = (swapped[64:96].astype(F32) + to_4[...].astype(F32)).astype(BF16)
-    sum_third[...] = (swapped[96:112].astype(F32) + to_third[...].astype(F32)).astype(BF16)
+    for part in range(2):
+        lanes = slice(part * WIDTH, (part + 1) * WIDTH)
+        at = 256 + part * PARTNER_ROWS
+        own3 = to_3[:, lanes].astype(F32)
+
+        def came(start, stop):
+            return message[at + start : at + stop].astype(F32)
+
+        sum3[0:32, lanes] = (came(0, 32) + jnp.where(even, own3, 0.0)).astype(BF16)
+        sum3[32:64, lanes] = (came(32, 64) + jnp.where(even, 0.0, own3)).astype(BF16)
+        sum4[:, lanes] = (came(64, 96) + to_4[:, lanes].astype(F32)).astype(BF16)
+        sum_third[:, lanes] = (came(96, 112) + to_third[:, lanes].astype(F32)).astype(BF16)
+    total[...] = keep[...] + message[0:256].astype(F32)
+    halve(total, 4, keep_out, give_out)
+
+
+def halve(total, divisor, keep, give):
+    side = lax.axis_index("ctx") // divisor % 2
+    half = total.shape[0] // 2
+    keep[...] = total[pl.ds(pl.multiple_of(side * half, half), half)]
+    give[...] = total[pl.ds(pl.multiple_of((1 - side) * half, half), half)].astype(BF16)
 
 
 def core_rows(ref, core, rows):
@@ -489,10 +514,7 @@
 def halve_kernel(divisor, keep, got, *refs):
     keep_out, give_out, total = refs[-3:]
     total[...] = keep[...] + got[...].astype(F32)
-    side = lax.axis_index("ctx") // divisor % 2
-    half = total.shape[0] // 2
-    keep_out[...] = total[pl.ds(pl.multiple_of(side * half, half), half)]
-    give_out[...] = total[pl.ds(pl.multiple_of((1 - side) * half, half), half)].astype(BF16)
+    halve(total, divisor, keep_out, give_out)
 
 
 def copies_kernel(keep, got, *refs):
@@ -501,7 +523,7 @@
         refs[-1][i] = total.astype(BF16)
 
 
-def last_sum_kernel(parts, out):
+def last_sum_kernel(parts, _, out):
     total = parts[0].astype(F32)
     for i in range(1, parts.shape[0]):
         total = total + parts[i].astype(F32)
@@ -509,9 +531,10 @@
 
 
 def combine_kernel(*refs):
-    own, (low, high) = (refs[0:3], refs[3:6]), refs[6:8]
-    back3, back4, third, swapped = refs[8:12]
-    d_k_hbm, d_v_hbm, d_k, d_v, sems = refs[12:]
+    own, (low, high) = (refs[0:4], refs[4:8]), refs[8:10]
+    back3, back4, third, swapped = refs[10:14]
+    d_k_hbm, d_v_hbm, finished, d_k, d_v, sems = refs[14:]
+    finished[...] = jnp.zeros(finished.shape, F32)
     core = core_index()
     far3 = core_rows(back3, core, 32).astype(F32) + swapped[0:32].astype(F32)
     far4 = core_rows(back4, core, 16).astype(F32) + swapped[32:48].astype(F32)
@@ -652,8 +675,6 @@
         [pltpu.VMEM((WIDTH, WIDTH), F32)],
         microseconds=6,
     )
-    got_w = moved(give, partner)
-
     def halved(keep, got, divisor, route, *after):
         rows = keep.shape[0] // 2
         keep, give = call(
@@ -666,17 +687,14 @@
         )
         return keep, moved(give, route)
 
-    keep, got_w = halved(keep, got_w, 4, lambda i: i ^ 6)
-    d_far, *to_far, to_partner = call(
+    d_far, *to_far, message = call(
         far_back_kernel,
         "far_back",
         [((48, WIDTH), BF16), ((32, 2 * WIDTH), BF16), ((32, 2 * WIDTH), BF16)]
-        + [((16, 2 * WIDTH), BF16), ((112, 2 * WIDTH), BF16)],
-        [p_far, q_all, g, d_side, *far, keep],
-        in_hbm=1,
-    )
-    swapped = moved(to_partner, partner)
-
+        + [((16, 2 * WIDTH), BF16), ((MESSAGE_ROWS, WIDTH), BF16)],
+        [p_far, q_all, g, d_side, *far, give],
+    )
+    message = moved(message, partner)
 
     def part_outs(part):
         width = len(NEAR_PARTS[part]) * LANES
@@ -685,70 +703,82 @@
         ] * 2
 
     args = [p_near, q_all, g, d_side, *near, d_far]
-    sum3, sum4, sum_third = call(
-        far_sum_kernel,
-        "far_sum",
-        [((64, 2 * WIDTH), BF16), ((32, 2 * WIDTH), BF16), ((16, 2 * WIDTH), BF16)],
-        [*to_far, swapped],
-    )
-    back3 = moved(sum3, back_3)
-    back4 = moved(sum4, back_4)
-    back_third = moved(sum_third, third)
-    keep, got_w = halved(keep, got_w, 2, lambda i: i ^ 2, sum3)
     *part_a, layer_out = call(
         near_back_a_kernel,
         "near_back_a",
         part_outs(0) + [(tokens, BF16)],
-        [attended, w, *args, keep],
+        [attended, w, *args],
         [pltpu.VMEM(tokens, BF16), dma(())],
-        in_hbm=1,
         microseconds=3,
         to_hbm=(5,),
     )
-    keep, got_w = halved(keep, got_w, 16, lambda i: i ^ 24, part_a[0])
+    sum3, sum4, sum_third, keep, give = call(
+        partner_sum_kernel,
+        "partner_sum",
+        [((64, 2 * WIDTH), BF16), ((32, 2 * WIDTH), BF16), ((16, 2 * WIDTH), BF16)]
+        + [((128, WIDTH), F32), ((128, WIDTH), BF16)],
+        [*to_far, keep, message, part_a[0]],
+        [pltpu.VMEM((256, WIDTH), F32)],
+        in_hbm=1,
+    )
+    got_w = moved(give, lambda i: i ^ 6)
+    back3 = moved(sum3, back_3)
+    back4 = moved(sum4, back_4)
+    keep, got_w = halved(keep, got_w, 2, lambda i: i ^ 2)
     part_b = call(
-        near_back_b_kernel,
+        functools.partial(near_back_more_kernel, NEAR_PARTS[1]),
         "near_back_b",
         part_outs(1),
         [*args, part_a[0], keep],
         in_hbm=2,
-        microseconds=4,
-    )
-    keep, got_w = halved(keep, got_w, 8, lambda i: i ^ 8, part_b[0])
+        microseconds=3,
+    )
+    keep, got_w = halved(keep, got_w, 16, lambda i: i ^ 24, part_b[0])
+    part_c = call(
+        functools.partial(near_back_more_kernel, NEAR_PARTS[2]),
+        "near_back_c",
+        part_outs(2),
+        [*args, part_b[0], keep],
+        in_hbm=2,
+        microseconds=3,
+    )
+    keep, got_w = halved(keep, got_w, 8, lambda i: i ^ 8, part_c[0])
     give = call(far_split_kernel, "far_split", [((48, 2 * WIDTH), BF16)], [back3, back4])[0]
     swapped = moved(give, partner)
     d_q, own_k, own_v, to_low, to_high = call(
-        near_back_c_kernel,
-        "near_back_c",
+        near_back_last_kernel,
+        "near_back_d",
         [(tokens, BF16), ((ROWS, LANES), F32), ((ROWS, LANES), F32)]
         + [((192, 2 * WIDTH), BF16)] * 2,
-        [*args, part_a[0], *part_a[3:], part_b[0], *part_b[3:]]
-        + [keep, give, back_third],
+        [*args, *(x for part in (part_a, part_b, part_c) for x in (part[0], *part[3:]))]
+        + [keep, give],
         [pltpu.VMEM(tokens, BF16), dma((2,))],
-        in_hbm=3,
-        microseconds=2,
+        in_hbm=2,
+        microseconds=3,
         to_hbm=(0,),
     )
+    to_low, to_high, got_w = lax.optimization_barrier((to_low, to_high, got_w))
     low_back = moved(to_low, lambda i: i - 1)
     high_back = moved(to_high, lambda i: i + 1)
     copies = call(
         copies_kernel,
         "copies",
         [((lax.axis_size("dp"), 16, WIDTH), BF16)],
-        [keep, got_w, to_low],
-        in_hbm=1,
+        [keep, got_w],
     )[0]
+    sum_third, copies = lax.optimization_barrier((sum_third, copies))
     copies = lax.all_to_all(copies, "dp", 0, 0, tiled=True)
-    d_w = call(last_sum_kernel, "last_sum", [((16, WIDTH), BF16)], [copies])[0]
-    d_k, d_v = call(
+    back_third = moved(sum_third, third)
+    d_k, d_v, finished = call(
         combine_kernel,
         "combine",
-        [(tokens, BF16)] * 2,
-        [part_a[1], part_b[1], own_k, part_a[2], part_b[2], own_v, low_back, high_back]
-        + [back3, back4, back_third, swapped],
+        [(tokens, BF16)] * 2 + [((8, LANES), F32)],
+        [part_a[1], part_b[1], part_c[1], own_k, part_a[2], part_b[2], part_c[2], own_v]
+        + [low_back, high_back, back3, back4, back_third, swapped],
         [pltpu.VMEM(tokens, BF16)] * 2 + [dma((2,))],
         to_hbm=(0, 1),
     )
+    d_w = call(last_sum_kernel, "last_sum", [((16, WIDTH), BF16)], [copies, finished], in_hbm=1)[0]
     return layer_out[None], d_q[None], d_k[None], d_v[None], d_w
 
 

time: 76.4 us -> 75 us (0.982)
  starting transfers between devices: 32.1 us -> 27 us
  waiting for transfers between devices: 20.4 us -> 24 us
    ppermute x19 -> x18, waiting for transfers between devices: 12.8 us -> 22.5 us  [moved(): return lax.ppermute(x, 'ctx', [(i, route(i) % count) for i in range(count)])]
    all_to_all x1, waiting for transfers between devices: 7.62 us -> 1.52 us  [body(): copies = lax.all_to_all(copies, 'dp', 0, 0, tiled=True)]
    ppermute x19 -> x18, starting transfers between devices: 23.6 us -> 18.4 us  [moved(): return lax.ppermute(x, 'ctx', [(i, route(i) % count) for i in range(count)])]
  transfers between devices with their start and end apart: 20 -> 19, of which waited for: 9 -> 9; matrix products, arithmetic and copies ran while one was open for 0% -> 0% of each run, Pallas kernels for 14% -> 15%
where the time goes in v6:
time: 75 us; the launch traced here: 74.2 us
  starting transfers between devices  27 us (36%)
  waiting for transfers between devices  24 us (32%)
  Pallas kernels  19.7 us (26%)
  local copies, waits for them, and re-layouts  2.58 us (3%)
  between operations  0.86 us (1%)
    ppermute x18, waiting for transfers between devices, moved(): return lax.ppermute(x, 'ctx', [(i, route(i) % count) for i in range(count)])  22.5 us
    pallas_call x19, Pallas kernels, call(): pl.pallas_call(kernel, name=name, out_shape=[jax.ShapeDtypeStruct(shape,...  19.7 us
    ppermute x18, starting transfers between devices, moved(): return lax.ppermute(x, 'ctx', [(i, route(i) % count) for i in range(count)])  18.4 us
    all_to_all x1, starting transfers between devices, body(): copies = lax.all_to_all(copies, 'dp', 0, 0, tiled=True)  8.57 us
    unnamed x12, local copies, waits for them, and re-layouts  2.58 us
    all_to_all x1, waiting for transfers between devices, body(): copies = lax.all_to_all(copies, 'dp', 0, 0, tiled=True)  1.52 us
  transfers between devices with their start and end apart: 19, of which 9 were waited for; matrix products, arithmetic and copies ran while one was open for 0% of the time, Pallas kernels for 15%

profile of v6, /device:TPU:32, one launch (start us, length us, event | category | flops | bytes accessed | tf_op | source)
XLA Modules:
  0.0 74.2 jit_solution(17614299181290683711)
XLA Ops:
  0.6 0.9 %copy-done.1 = bf16[1,256,512]{2,1,0:T(8,128)(2,1)S(1)} copy-done((bf16[1,256,512]{2,1,0:T(8,128)(2,1)S(1)}, bf16[1,256,512]{2,1,0:T(8,128)(2,1)}, u32[]{:S(2)}) %copy-start.1) | copy-done | bytes 262168
  1.6 0.9 %copy-done.2 = bf16[1,256,512]{2,1,0:T(8,128)(2,1)S(1)} copy-done((bf16[1,256,512]{2,1,0:T(8,128)(2,1)S(1)}, bf16[1,256,512]{2,1,0:T(8,128)(2,1)}, u32[]{:S(2)}) %copy-start.2) | copy-done | bytes 262168
  2.5 0.7 copy-done.5
  3.2 0.7 coarsen.1
  4.0 5.1 %collective-permute-start.1 = (bf16[192,1152]{1,0:T(8,128)(2,1)S(1)}, bf16[192,1152]{1,0:T(8,128)(2,1)S(1)}, u32[]{:S(2)}, u32[]{:S(2)}) collective-permute-start(bf16[192,1152]{1,0:T(8,128)(2,1)S(1)} %get-tuple-element.82), channel_id=1, source_target_pairs={{0,31},{1,0},{2,1},{3,2},{4,3},{5,4},{6,5},{7,6},{8,7},{9,8},{10,9... | collective-permute-start | bytes 1327112 | tf_op jit(solution)/shard_map/ppermute | solution.py:592
  9.1 1.3 %collective-permute-done.2.far_partner = bf16[48,1152]{1,0:T(8,128)(2,1)S(1)} collective-permute-done((bf16[48,1152]{1,0:T(8,128)(2,1)S(1)}, bf16[48,1152]{1,0:T(8,128)(2,1)S(1)}, u32[]{:S(2)}, u32[]{:S(2)}) %collective-permute-start.2) | collective-permute-done | bytes 110624 | tf_op jit(solution)/shard_map/ppermute | solution.py:592
  10.5 2.9 %collective-permute-start.5 = (bf16[16,1152]{1,0:T(8,128)(2,1)S(1)}, bf16[16,1152]{1,0:T(8,128)(2,1)S(1)}, u32[]{:S(2)}, u32[]{:S(2)}) collective-permute-start(bf16[16,1152]{1,0:T(8,128)(2,1)S(1)} %get-tuple-element.93), channel_id=1, source_target_pairs={{0,6},{1,7},{2,28},{3,29},{4,10},{5,11},{6,0},{7,1},{8,14},{9,15},... | collective-permute-start | bytes 110600 | tf_op jit(solution)/shard_map/ppermute | solution.py:592
  13.5 0.7 prepare.1
  14.2 4.8 %collective-permute-done.3.got3 = bf16[64,1152]{1,0:T(8,128)(2,1)S(1)} collective-permute-done((bf16[64,1152]{1,0:T(8,128)(2,1)S(1)}, bf16[64,1152]{1,0:T(8,128)(2,1)S(1)}, u32[]{:S(2)}, u32[]{:S(2)}) %collective-permute-start.3) | collective-permute-done | bytes 147488 | tf_op jit(solution)/shard_map/ppermute | solution.py:592
  19.0 2.4 %collective-permute-done.4.got4.refs_1_ = bf16[32,1152]{1,0:T(8,128)(2,1)S(1)} collective-permute-done((bf16[32,1152]{1,0:T(8,128)(2,1)S(1)}, bf16[32,1152]{1,0:T(8,128)(2,1)S(1)}, u32[]{:S(2)}, u32[]{:S(2)}) %collective-permute-start.4) | collective-permute-done | bytes 73760 | tf_op jit(solution)/shard_map/ppermute | solution.py:592
  21.6 1.7 %near.1 = (bf16[4,896,256]{2,1,0:T(8,128)(2,1)S(1)}, f32[4,256,384]{2,1,0:T(8,128)S(1)}, bf16[4,192,384]{2,1,0:T(8,128)(2,1)S(1)}) custom-call(bf16[496,512]{1,0:T(8,128)(2,1)S(1)} %get-tuple-element.77.q_all.refs_1_, bf16[496,128]{1,0:T(8,128)(2,1)S(1)} %get-tuple-element.78.qdoc, bf16[256,1152]{1,0:T(8,128)(2,1)S(1)} %get-tuple-element.79.own0.refs_4_, ...), custom_call_target="tpu_custom_call" | custom-call | flops 49999998976 | bytes 1048576 | tf_op jit(solution)/shard_map/near/pallas_call | solution.py:576
  23.3 5.6 %merge.1 = (bf16[256,512]{1,0:T(8,128)(2,1)S(1)}, f32[256,512]{1,0:T(8,128)S(1)}, bf16[256,512]{1,0:T(8,128)(2,1)S(1)}, bf16[4,96,128]{2,1,0:T(8,128)(2,1)S(1)},...) custom-call(bf16[496,512]{1,0:T(8,128)(2,1)S(1)} %get-tuple-element.77.q_all.refs_1_, ...), custom_call_target="tpu_custom_call" | custom-call | flops 6000000000 | bytes 1048576 | tf_op jit(solution)/shard_map/merge/pallas_call | solution.py:576
  28.9 1.1 %far_back.1 = (bf16[48,512]{1,0:T(8,128)(2,1)S(1)}, bf16[32,1024]{1,0:T(8,128)(2,1)S(1)}, bf16[32,1024]{1,0:T(8,128)(2,1)S(1)}, bf16[16,1024]{1,0:T(8,128)(2,1)S(1)}, bf16[480,512]{1,0:T(8,128)(2,1)S(1)}) custom-call(bf16[4,96,128]{2,1,0:T(8,128)(2,1)S(1)} %get-tuple-element.101.p_in, bf16[496,512]{1,0:T(8,128)(2,1)S(1)} %get-tuple-element.77.q_all.refs_1_, ...), custom_call_target="tpu_custom_call" | custom-call | flops 1000000000 | bytes 1048576 | tf_op jit(solution)/shard_map/far_back/pallas_call | solution.py:576
  30.0 0.8 %collective-permute-start.7 = (bf16[480,512]{1,0:T(8,128)(2,1)S(1)}, bf16[480,512]{1,0:T(8,128)(2,1)S(1)}, u32[]{:S(2)}, u32[]{:S(2)}) collective-permute-start(bf16[480,512]{1,0:T(8,128)(2,1)S(1)} %get-tuple-element.112), channel_id=1, source_target_pairs={{0,1},{1,0},{2,3},{3,2},{4,5},{5,4},{6,7},{7,6},{8,9},{9,8},{10,11... | collective-permute-start | bytes 1474568 | tf_op jit(solution)/shard_map/ppermute | solution.py:592
  30.8 2.0 %near_back_a.1 = (bf16[256,128]{1,0:T(8,128)(2,1)S(1)}, f32[256,128]{1,0:T(8,128)S(1)}, f32[256,128]{1,0:T(8,128)S(1)}, bf16[2,192,128]{2,1,0:T(8,128)(2,1)S(1)}...) custom-call(bf16[256,512]{1,0:T(8,128)(2,1)S(1)} %get-tuple-element.96.attended, ...), custom_call_target="tpu_custom_call" | custom-call | flops 3000000000 | bytes 1048576 | tf_op jit(solution)/shard_map/near_back_a/pallas_call | solution.py:576
  33.0 0.9 %collective-permute-start.8 = (bf16[128,512]{1,0:T(8,128)(2,1)S(1)}, bf16[128,512]{1,0:T(8,128)(2,1)S(1)}, u32[]{:S(2)}, u32[]{:S(2)}) collective-permute-start(bf16[128,512]{1,0:T(8,128)(2,1)S(1)} %get-tuple-element.114), channel_id=1, source_target_pairs={{0,6},{1,7},{2,4},{3,5},{4,2},{5,3},{6,0},{7,1},{8,14},{9,15},{10,... | collective-permute-start | bytes 393224 | tf_op jit(solution)/shard_map/ppermute | solution.py:592
  33.9 0.8 %collective-permute-start.12 = (bf16[32,1024]{1,0:T(8,128)(2,1)S(1)}, bf16[32,1024]{1,0:T(8,128)(2,1)S(1)}, u32[]{:S(2)}, u32[]{:S(2)}) collective-permute-start(bf16[32,1024]{1,0:T(8,128)(2,1)S(1)} %get-tuple-element.127), channel_id=1, source_target_pairs={{0,28},{1,5},{2,30},{3,7},{4,0},{5,9},{6,2},{7,11},{8,4},{9,13},{1... | collective-permute-start | bytes 196616 | tf_op jit(solution)/shard_map/ppermute | solution.py:592
  34.7 2.8 %collective-permute-start.11 = (bf16[64,1024]{1,0:T(8,128)(2,1)S(1)}, bf16[64,1024]{1,0:T(8,128)(2,1)S(1)}, u32[]{:S(2)}, u32[]{:S(2)}) collective-permute-start(bf16[64,1024]{1,0:T(8,128)(2,1)S(1)} %get-tuple-element.126), channel_id=1, source_target_pairs={{0,30},{1,3},{2,0},{3,5},{4,2},{5,7},{6,4},{7,9},{8,6},{9,11},{10,... | collective-permute-start | bytes 393224 | tf_op jit(solution)/shard_map/ppermute | solution.py:592
  37.5 5.0 %collective-permute-done.8.got = bf16[128,512]{1,0:T(8,128)(2,1)S(1)} collective-permute-done((bf16[128,512]{1,0:T(8,128)(2,1)S(1)}, bf16[128,512]{1,0:T(8,128)(2,1)S(1)}, u32[]{:S(2)}, u32[]{:S(2)}) %collective-permute-start.8) | collective-permute-done | bytes 131104 | tf_op jit(solution)/shard_map/ppermute | solution.py:592
  42.7 1.5 %near_back_b.1 = (bf16[256,128]{1,0:T(8,128)(2,1)S(1)}, f32[256,128]{1,0:T(8,128)S(1)}, f32[256,128]{1,0:T(8,128)S(1)}, bf16[2,192,128]{2,1,0:T(8,128)(2,1)S(1)}, bf16[2,192,128]{2,1,0:T(8,128)(2,1)S(1)}) custom-call(bf16[4,896,256]{2,1,0:T(8,128)(2,1)S(1)} %get-tuple-element.98.refs_0_, bf16[496,512]{1,0:T(8,128)(2,1)S(1)} %get-tuple-element.77.q_all.refs_1_, ...), custom_call_target="tpu_custom_call" | custom-call | flops 3000000000 | bytes 1048576 | tf_op jit(solution)/shard_map/near_back_b/pallas_call | solution.py:576
  44.2 2.7 %collective-permute-done.9.got = bf16[64,512]{1,0:T(8,128)(2,1)S(1)} collective-permute-done((bf16[64,512]{1,0:T(8,128)(2,1)S(1)}, bf16[64,512]{1,0:T(8,128)(2,1)S(1)}, u32[]{:S(2)}, u32[]{:S(2)}) %collective-permute-start.9) | collective-permute-done | bytes 65568 | tf_op jit(solution)/shard_map/ppermute | solution.py:592
  46.9 1.8 %collective-permute-start.10 = (bf16[32,512]{1,0:T(8,128)(2,1)S(1)}, bf16[32,512]{1,0:T(8,128)(2,1)S(1)}, u32[]{:S(2)}, u32[]{:S(2)}) collective-permute-start(bf16[32,512]{1,0:T(8,128)(2,1)S(1)} %get-tuple-element.124), channel_id=1, source_target_pairs={{0,24},{1,25},{2,26},{3,27},{4,28},{5,29},{6,30},{7,31},{8,16},{9,... | collective-permute-start | bytes 98312 | tf_op jit(solution)/shard_map/ppermute | solution.py:592
  48.8 1.4 %near_back_c.1 = (bf16[256,128]{1,0:T(8,128)(2,1)S(1)}, f32[256,128]{1,0:T(8,128)S(1)}, f32[256,128]{1,0:T(8,128)S(1)}, bf16[2,192,128]{2,1,0:T(8,128)(2,1)S(1)}, bf16[2,192,128]{2,1,0:T(8,128)(2,1)S(1)}) custom-call(bf16[4,896,256]{2,1,0:T(8,128)(2,1)S(1)} %get-tuple-element.98.refs_0_, bf16[496,512]{1,0:T(8,128)(2,1)S(1)} %get-tuple-element.77.q_all.refs_1_, ...), custom_call_target="tpu_custom_call" | custom-call | flops 3000000000 | bytes 1048576 | tf_op jit(solution)/shard_map/near_back_c/pallas_call | solution.py:576
  50.2 1.9 %collective-permute-done.10.got = bf16[32,512]{1,0:T(8,128)(2,1)S(1)} collective-permute-done((bf16[32,512]{1,0:T(8,128)(2,1)S(1)}, bf16[32,512]{1,0:T(8,128)(2,1)S(1)}, u32[]{:S(2)}, u32[]{:S(2)}) %collective-permute-start.10) | collective-permute-done | bytes 32800 | tf_op jit(solution)/shard_map/ppermute | solution.py:592
  52.3 2.2 %near_back_d.1 = (bf16[256,512]{1,0:T(8,128)(2,1)}, f32[256,128]{1,0:T(8,128)S(1)}, f32[256,128]{1,0:T(8,128)S(1)}, bf16[192,1024]{1,0:T(8,128)(2,1)S(1)}, bf16[192,1024]{1,0:T(8,128)(2,1)S(1)}) custom-call(bf16[4,896,256]{2,1,0:T(8,128)(2,1)S(1)} %get-tuple-element.98.refs_0_, bf16[496,512]{1,0:T(8,128)(2,1)S(1)} %get-tuple-element.77.q_all.refs_1_, ...), custom_call_target="tpu_custom_call" | custom-call | flops 3000000000 | bytes 1048576 | tf_op jit(solution)/shard_map/near_back_d/pallas_call | solution.py:576
  54.5 1.5 %collective-permute-done.13.got = bf16[16,512]{1,0:T(8,128)(2,1)S(1)} collective-permute-done((bf16[16,512]{1,0:T(8,128)(2,1)S(1)}, bf16[16,512]{1,0:T(8,128)(2,1)S(1)}, u32[]{:S(2)}, u32[]{:S(2)}) %collective-permute-start.13) | collective-permute-done | bytes 16416 | tf_op jit(solution)/shard_map/ppermute | solution.py:592
  56.5 0.7 copies.1
  57.2 8.6 %all-to-all-start = ((bf16[8,16,512]{2,1,0:T(8,128)(2,1)}), bf16[8,16,512]{2,1,0:T(8,128)(2,1)S(1)}, u32[]{:S(2)}, u32[]{:S(2)}) async-start(bf16[8,16,512]{2,1,0:T(8,128)(2,1)} %copies.1), calls=%async_computation | async-start | bytes 262144 | tf_op jit(solution)/shard_map/all_to_all | solution.py:770
  65.7 2.4 %collective-permute-start.16 = (bf16[16,1024]{1,0:T(8,128)(2,1)S(1)}, bf16[16,1024]{1,0:T(8,128)(2,1)S(1)}, u32[]{:S(2)}, u32[]{:S(2)}) collective-permute-start(bf16[16,1024]{1,0:T(8,128)(2,1)S(1)} %get-tuple-element.144), channel_id=1, source_target_pairs={{0,6},{1,7},{2,28},{3,29},{4,10},{5,11},{6,0},{7,1},{8,14},{9,15},... | collective-permute-start | bytes 98312 | tf_op jit(solution)/shard_map/ppermute | solution.py:592
  68.1 2.7 %collective-permute-done.16.refs_12_ = bf16[16,1024]{1,0:T(8,128)(2,1)S(1)} collective-permute-done((bf16[16,1024]{1,0:T(8,128)(2,1)S(1)}, bf16[16,1024]{1,0:T(8,128)(2,1)S(1)}, u32[]{:S(2)}, u32[]{:S(2)}) %collective-permute-start.16) | collective-permute-done | bytes 32800 | tf_op jit(solution)/shard_map/ppermute | solution.py:592
  70.9 1.1 %combine.1 = (bf16[256,512]{1,0:T(8,128)(2,1)}, bf16[256,512]{1,0:T(8,128)(2,1)}, f32[8,128]{1,0:T(8,128)S(1)}) custom-call(f32[256,128]{1,0:T(8,128)S(1)} %get-tuple-element.129.refs_0_, f32[256,128]{1,0:T(8,128)S(1)} %get-tuple-element.130.refs_1_, f32[256,128]{1,0:T(8,128)S(1)} %get-tuple-element.131.refs_2_, f32[256,128]{1,0:T(8,128)S(1)} %get-tuple-element.132.refs_3_, ...), custom_call_target="tpu_custom_call" | custom-call | flops 1000000000 | bytes 1048576 | tf_op jit(solution)/shard_map/combine/pallas_call | solution.py:576
  72.0 1.5 %all-to-all-done.parts = bf16[8,16,512]{2,1,0:T(8,128)(2,1)S(1)} async-done(((bf16[8,16,512]{2,1,0:T(8,128)(2,1)}), bf16[8,16,512]{2,1,0:T(8,128)(2,1)S(1)}, u32[]{:S(2)}, u32[]{:S(2)}) %all-to-all-start) | async-done | bytes 131104 | tf_op jit(solution)/shard_map/all_to_all | solution.py:770
  (37 shorter events, 2.0 us)
Async XLA Ops:
  0.6 1.0 %copy-start.1 = (bf16[1,256,512]{2,1,0:T(8,128)(2,1)S(1)}, bf16[1,256,512]{2,1,0:T(8,128)(2,1)}, u32[]{:S(2)}) copy-start(bf16[1,256,512]{2,1,0:T(8,128)(2,1)} %param.7) | copy-start | bytes 786436
  1.6 0.9 %copy-start.2 = (bf16[1,256,512]{2,1,0:T(8,128)(2,1)S(1)}, bf16[1,256,512]{2,1,0:T(8,128)(2,1)}, u32[]{:S(2)}) copy-start(bf16[1,256,512]{2,1,0:T(8,128)(2,1)} %param.8) | copy-start | bytes 786436
  2.5 0.7 copy-start.5
  3.9 15.0 %collective-permute-start = (bf16[192,1152]{1,0:T(8,128)(2,1)S(1)}, bf16[192,1152]{1,0:T(8,128)(2,1)S(1)}, u32[]{:S(2)}, u32[]{:S(2)}) collective-permute-start(bf16[192,1152]{1,0:T(8,128)(2,1)S(1)} %get-tuple-element.81), channel_id=1, source_target_pairs={{0,1},{1,2},{2,3},{3,4},{4,5},{5,6},{6,7},{7,8},{8,9},{9,10},{10,1... | collective-permute-start | bytes 1327112 | tf_op jit(solution)/shard_map/ppermute | solution.py:592
  4.0 15.0 %collective-permute-start.1 = (bf16[192,1152]{1,0:T(8,128)(2,1)S(1)}, bf16[192,1152]{1,0:T(8,128)(2,1)S(1)}, u32[]{:S(2)}, u32[]{:S(2)}) collective-permute-start(bf16[192,1152]{1,0:T(8,128)(2,1)S(1)} %get-tuple-element.82), channel_id=1, source_target_pairs={{0,31},{1,0},{2,1},{3,2},{4,3},{5,4},{6,5},{7,6},{8,7},{9,8},{10,9... | collective-permute-start | bytes 1327112 | tf_op jit(solution)/shard_map/ppermute | solution.py:592
  9.1 4.4 %copy-start = (bf16[512,512]{1,0:T(8,128)(2,1)S(1)}, bf16[512,512]{1,0:T(8,128)(2,1)}, u32[]{:S(2)}) copy-start(bf16[512,512]{1,0:T(8,128)(2,1)} %w_hbm.1) | copy-start | bytes 1572868
  9.1 4.4 %copy-start.3 = (bf16[1,256,512]{2,1,0:T(8,128)(2,1)S(1)}, bf16[1,256,512]{2,1,0:T(8,128)(2,1)}, u32[]{:S(2)}) copy-start(bf16[1,256,512]{2,1,0:T(8,128)(2,1)} %param.6) | copy-start | bytes 786436
  9.1 4.4 %copy-start.4 = (bf16[1,256,512]{2,1,0:T(8,128)(2,1)S(1)}, bf16[1,256,512]{2,1,0:T(8,128)(2,1)}, u32[]{:S(2)}) copy-start(bf16[1,256,512]{2,1,0:T(8,128)(2,1)} %param.11) | copy-start | bytes 786436
  9.1 1.3 %collective-permute-start.2 = (bf16[48,1152]{1,0:T(8,128)(2,1)S(1)}, bf16[48,1152]{1,0:T(8,128)(2,1)S(1)}, u32[]{:S(2)}, u32[]{:S(2)}) collective-permute-start(bf16[48,1152]{1,0:T(8,128)(2,1)S(1)} %get-tuple-element.83.far), channel_id=1, source_target_pairs={{0,1},{1,0},{2,3},{3,2},{4,5},{5,4},{6,7},{7,6},{8,9},{9,8},{10,11... | collective-permute-start | bytes 331784 | tf_op jit(solution)/shard_map/ppermute | solution.py:592
  10.4 8.5 %collective-permute-start.3 = (bf16[64,1152]{1,0:T(8,128)(2,1)S(1)}, bf16[64,1152]{1,0:T(8,128)(2,1)S(1)}, u32[]{:S(2)}, u32[]{:S(2)}) collective-permute-start(bf16[64,1152]{1,0:T(8,128)(2,1)S(1)} %get-tuple-element.84), channel_id=1, source_target_pairs={{0,2},{1,31},{2,4},{3,1},{4,6},{5,3},{6,8},{7,5},{8,10},{9,7},{10,... | collective-permute-start | bytes 442376 | tf_op jit(solution)/shard_map/ppermute | solution.py:592
  10.5 8.5 %collective-permute-start.5 = (bf16[16,1152]{1,0:T(8,128)(2,1)S(1)}, bf16[16,1152]{1,0:T(8,128)(2,1)S(1)}, u32[]{:S(2)}, u32[]{:S(2)}) collective-permute-start(bf16[16,1152]{1,0:T(8,128)(2,1)S(1)} %get-tuple-element.93), channel_id=1, source_target_pairs={{0,6},{1,7},{2,28},{3,29},{4,10},{5,11},{6,0},{7,1},{8,14},{9,15},... | collective-permute-start | bytes 110600 | tf_op jit(solution)/shard_map/ppermute | solution.py:592
  13.5 8.0 %collective-permute-start.4 = (bf16[32,1152]{1,0:T(8,128)(2,1)S(1)}, bf16[32,1152]{1,0:T(8,128)(2,1)S(1)}, u32[]{:S(2)}, u32[]{:S(2)}) collective-permute-start(bf16[32,1152]{1,0:T(8,128)(2,1)S(1)} %get-tuple-element.92), channel_id=1, source_target_pairs={{0,4},{1,29},{2,6},{3,31},{4,8},{5,1},{6,10},{7,3},{8,12},{9,5},{1... | collective-permute-start | bytes 221192 | tf_op jit(solution)/shard_map/ppermute | solution.py:592
  21.5 1.8 %collective-permute-start.6 = (bf16[112,1152]{1,0:T(8,128)(2,1)S(1)}, bf16[112,1152]{1,0:T(8,128)(2,1)S(1)}, u32[]{:S(2)}, u32[]{:S(2)}) collective-permute-start(bf16[112,1152]{1,0:T(8,128)(2,1)S(1)} %get-tuple-element.95), channel_id=1, source_target_pairs={{0,1},{1,0},{2,3},{3,2},{4,5},{5,4},{6,7},{7,6},{8,9},{9,8},{10,11... | collective-permute-start | bytes 774152 | tf_op jit(solution)/shard_map/ppermute | solution.py:592
  30.0 2.8 %collective-permute-start.7 = (bf16[480,512]{1,0:T(8,128)(2,1)S(1)}, bf16[480,512]{1,0:T(8,128)(2,1)S(1)}, u32[]{:S(2)}, u32[]{:S(2)}) collective-permute-start(bf16[480,512]{1,0:T(8,128)(2,1)S(1)} %get-tuple-element.112), channel_id=1, source_target_pairs={{0,1},{1,0},{2,3},{3,2},{4,5},{5,4},{6,7},{7,6},{8,9},{9,8},{10,11... | collective-permute-start | bytes 1474568 | tf_op jit(solution)/shard_map/ppermute | solution.py:592
  33.0 9.5 %collective-permute-start.8 = (bf16[128,512]{1,0:T(8,128)(2,1)S(1)}, bf16[128,512]{1,0:T(8,128)(2,1)S(1)}, u32[]{:S(2)}, u32[]{:S(2)}) collective-permute-start(bf16[128,512]{1,0:T(8,128)(2,1)S(1)} %get-tuple-element.114), channel_id=1, source_target_pairs={{0,6},{1,7},{2,4},{3,5},{4,2},{5,3},{6,0},{7,1},{8,14},{9,15},{10,... | collective-permute-start | bytes 393224 | tf_op jit(solution)/shard_map/ppermute | solution.py:592
  33.9 10.2 %collective-permute-start.12 = (bf16[32,1024]{1,0:T(8,128)(2,1)S(1)}, bf16[32,1024]{1,0:T(8,128)(2,1)S(1)}, u32[]{:S(2)}, u32[]{:S(2)}) collective-permute-start(bf16[32,1024]{1,0:T(8,128)(2,1)S(1)} %get-tuple-element.127), channel_id=1, source_target_pairs={{0,28},{1,5},{2,30},{3,7},{4,0},{5,9},{6,2},{7,11},{8,4},{9,13},{1... | collective-permute-start | bytes 196616 | tf_op jit(solution)/shard_map/ppermute | solution.py:592
  34.7 9.4 %collective-permute-start.11 = (bf16[64,1024]{1,0:T(8,128)(2,1)S(1)}, bf16[64,1024]{1,0:T(8,128)(2,1)S(1)}, u32[]{:S(2)}, u32[]{:S(2)}) collective-permute-start(bf16[64,1024]{1,0:T(8,128)(2,1)S(1)} %get-tuple-element.126), channel_id=1, source_target_pairs={{0,30},{1,3},{2,0},{3,5},{4,2},{5,7},{6,4},{7,9},{8,6},{9,11},{10,... | collective-permute-start | bytes 393224 | tf_op jit(solution)/shard_map/ppermute | solution.py:592
  42.6 4.4 %collective-permute-start.9 = (bf16[64,512]{1,0:T(8,128)(2,1)S(1)}, bf16[64,512]{1,0:T(8,128)(2,1)S(1)}, u32[]{:S(2)}, u32[]{:S(2)}) collective-permute-start(bf16[64,512]{1,0:T(8,128)(2,1)S(1)} %get-tuple-element.119), channel_id=1, source_target_pairs={{0,2},{1,3},{2,0},{3,1},{4,6},{5,7},{6,4},{7,5},{8,10},{9,11},{10,... | collective-permute-start | bytes 196616 | tf_op jit(solution)/shard_map/ppermute | solution.py:592
  46.9 5.2 %collective-permute-start.10 = (bf16[32,512]{1,0:T(8,128)(2,1)S(1)}, bf16[32,512]{1,0:T(8,128)(2,1)S(1)}, u32[]{:S(2)}, u32[]{:S(2)}) collective-permute-start(bf16[32,512]{1,0:T(8,128)(2,1)S(1)} %get-tuple-element.124), channel_id=1, source_target_pairs={{0,24},{1,25},{2,26},{3,27},{4,28},{5,29},{6,30},{7,31},{8,16},{9,... | collective-permute-start | bytes 98312 | tf_op jit(solution)/shard_map/ppermute | solution.py:592
  52.2 3.8 %collective-permute-start.13 = (bf16[16,512]{1,0:T(8,128)(2,1)S(1)}, bf16[16,512]{1,0:T(8,128)(2,1)S(1)}, u32[]{:S(2)}, u32[]{:S(2)}) collective-permute-start(bf16[16,512]{1,0:T(8,128)(2,1)S(1)} %get-tuple-element.139), channel_id=1, source_target_pairs={{0,8},{1,9},{2,10},{3,11},{4,12},{5,13},{6,14},{7,15},{8,0},{9,1},... | collective-permute-start | bytes 49160 | tf_op jit(solution)/shard_map/ppermute | solution.py:592
  56.0 14.9 %collective-permute-start.14 = (bf16[192,1024]{1,0:T(8,128)(2,1)S(1)}, bf16[192,1024]{1,0:T(8,128)(2,1)S(1)}, u32[]{:S(2)}, u32[]{:S(2)}) collective-permute-start(bf16[192,1024]{1,0:T(8,128)(2,1)S(1)} %get-tuple-element.140), channel_id=1, source_target_pairs={{0,31},{1,0},{2,1},{3,2},{4,3},{5,4},{6,5},{7,6},{8,7},{9,8},{10,9... | collective-permute-start | bytes 1179656 | tf_op jit(solution)/shard_map/ppermute | solution.py:592
  56.0 14.9 %collective-permute-start.15 = (bf16[192,1024]{1,0:T(8,128)(2,1)S(1)}, bf16[192,1024]{1,0:T(8,128)(2,1)S(1)}, u32[]{:S(2)}, u32[]{:S(2)}) collective-permute-start(bf16[192,1024]{1,0:T(8,128)(2,1)S(1)} %get-tuple-element.141), channel_id=1, source_target_pairs={{0,1},{1,2},{2,3},{3,4},{4,5},{5,6},{6,7},{7,8},{8,9},{9,10},{10,1... | collective-permute-start | bytes 1179656 | tf_op jit(solution)/shard_map/ppermute | solution.py:592
  57.2 16.4 %all-to-all-start = ((bf16[8,16,512]{2,1,0:T(8,128)(2,1)}), bf16[8,16,512]{2,1,0:T(8,128)(2,1)S(1)}, u32[]{:S(2)}, u32[]{:S(2)}) async-start(bf16[8,16,512]{2,1,0:T(8,128)(2,1)} %copies.1), calls=%async_computation | async-start | bytes 262144 | tf_op jit(solution)/shard_map/all_to_all | solution.py:770
  65.7 2.4 %collective-permute-start.17 = (bf16[48,1024]{1,0:T(8,128)(2,1)S(1)}, bf16[48,1024]{1,0:T(8,128)(2,1)S(1)}, u32[]{:S(2)}, u32[]{:S(2)}) collective-permute-start(bf16[48,1024]{1,0:T(8,128)(2,1)S(1)} %far_split.1.refs_19_), channel_id=1, source_target_pairs={{0,1},{1,0},{2,3},{3,2},{4,5},{5,4},{6,7},{7,6},{8,9},{9,8},{10,11... | collective-permute-start | bytes 294920 | tf_op jit(solution)/shard_map/ppermute | solution.py:592
  65.7 5.1 %collective-permute-start.16 = (bf16[16,1024]{1,0:T(8,128)(2,1)S(1)}, bf16[16,1024]{1,0:T(8,128)(2,1)S(1)}, u32[]{:S(2)}, u32[]{:S(2)}) collective-permute-start(bf16[16,1024]{1,0:T(8,128)(2,1)S(1)} %get-tuple-element.144), channel_id=1, source_target_pairs={{0,6},{1,7},{2,28},{3,29},{4,10},{5,11},{6,0},{7,1},{8,14},{9,15},... | collective-permute-start | bytes 98312 | tf_op jit(solution)/shard_map/ppermute | solution.py:592

commit v7 on v6

--- a/solution.py
+++ b/solution.py
@@ -146,27 +146,28 @@
     return copies
 
 
-def coarsen_kernel(
-    seg_hbm, k_hbm, v_hbm, up, down, far, third, own0, own1, qdoc, seg, k, v, sems
-):
-    copies = fetch((seg_hbm, k_hbm, v_hbm), (seg, k, v), sems)
-    copies[0].wait()
+def documents_kernel(seg_hbm, qdoc, seg, sem):
+    copy = pltpu.make_async_copy(seg_hbm, seg, sem)
+    copy.start()
+    copy.wait()
     marks = jnp.where(seg[...] == iota((LANES, ROWS), 0), 1.0, 0.0).T.astype(BF16)
-
-    def key_side(x):
-        doc = iota(x.shape, 1) < DOCS
-        return jnp.where(doc, (1.0 - x.astype(F32)) * BLOCKED, 0.0).astype(BF16)
-
-    copies[1].wait()
-    copies[2].wait()
-    levels = [(k[...], v[...], key_side(marks))]
     qdoc[0:ROWS] = marks
     for level in range(1, LEVELS + 1):
         marks_c = dot(last_table(level), marks).astype(BF16)
         qdoc[AT[level] : AT[level] + COUNT[level]] = marks_c
+
+
+def coarsen_kernel(qdoc, k_hbm, v_hbm, up, down, far, third, own0, own1, k, v, sems):
+    copies = fetch((k_hbm, v_hbm), (k, v), sems)
+    doc = iota((ALL_ROWS, LANES), 1) < DOCS
+    docs = jnp.where(doc, (1.0 - qdoc[...].astype(F32)) * BLOCKED, 0.0).astype(BF16)
+    copies[0].wait()
+    copies[1].wait()
+    levels = [(k[...], v[...], docs[0:ROWS])]
+    for level in range(1, LEVELS + 1):
         keys = dot(gather_table(level, 0.5**level), levels[0][0]).astype(BF16)
         values = dot(gather_table(level), levels[0][1]).astype(BF16)
-        levels.append((keys, values, key_side(marks_c)))
+        levels.append((keys, values, docs[AT[level] : AT[level] + COUNT[level]]))
 
     def put(ref, at, level, start, stop):
         for part, lanes in zip(
@@ -219,9 +220,38 @@
     peak = peak.astype(BF16).astype(F32)
     p = jnp.exp(scores - peak).astype(BF16)
     ones = jnp.ones(values.shape, BF16)
-    both = unstacked(dot(p, jnp.concatenate([values, ones], axis=1)), rows)
-    wide_peak = jnp.where(head_lanes(rows), peak[:rows], peak[rows:])
-    return p, jnp.concatenate([both, wide_peak], axis=1)
+    both = dot(p, jnp.concatenate([values, ones], axis=1))
+    return p, unstacked(both[:, :LANES], rows), both[:, LANES:], peak
+
+
+def with_stats(stats, pair, sums, peak):
+    rows = sums.shape[0] // 2
+    lane = iota((rows, LANES), 1)
+    result = []
+    for old, new in zip(stats, (sums, peak)):
+        old = jnp.where(lane == 2 * pair, new[:rows], old)
+        result.append(jnp.where(lane == 2 * pair + 1, new[rows:], old))
+    return result
+
+
+def no_stats(rows):
+    return [jnp.zeros((rows, LANES), F32)] * 2
+
+
+def head_spread(pair):
+    shape = (2 * LANES, LANES)
+    head = iota(shape, 0) % LANES
+    return jnp.where(head == 2 * pair + iota(shape, 1) // HEAD_DIM, 1.0, 0.0).astype(BF16)
+
+
+def head_sum(pair):
+    shape = (2 * LANES, LANES)
+    head = 2 * pair + iota(shape, 0) % LANES // HEAD_DIM
+    return jnp.where(head == iota(shape, 1), 1.0, 0.0).astype(BF16)
+
+
+def both_parts(x):
+    return jnp.concatenate(split(x), axis=1)
 
 
 def docs_of(index, qdoc):
@@ -232,24 +262,30 @@
     return jnp.concatenate([docs, docs], axis=0)
 
 
-def near_kernel(q_all, qdoc, own0, own1, low, high, p_out, fine, coarse):
+def near_kernel(q_all, qdoc, own0, own1, low, high, p_out, fine, fine_stats, coarse, coarse_stats):
     for index in NEAR:
         level, start, rows, keys = GROUPS[index]
         at = AT[level] + start
         query_docs = docs_of(index, qdoc)
         key_docs = near_window(index, own0, own1, low, high, DOC_LANES) + key_place(index)
+        stats = no_stats(rows)
         for pair in range(PAIRS):
             window = [
                 near_window(index, own0, own1, low, high, lanes_of(pair, part)) for part in (0, 1)
             ]
-            p, stats = attend(
+            p, numer, sums, peak = attend(
                 q_all[at : at + rows, lanes_of(pair)], query_docs, window[0], key_docs, window[1]
             )
+            stats = with_stats(stats, pair, sums, peak)
             p_out[pair, P_AT[index] : P_AT[index] + 2 * rows, 0:keys] = p
             if level == 0:
-                fine[pair, at : at + rows] = stats
+                fine[at : at + rows, lanes_of(pair)] = numer
             else:
-                coarse[pair, at - ROWS : at - ROWS + rows] = stats.astype(BF16)
+                coarse[at - ROWS : at - ROWS + rows, lanes_of(pair)] = numer.astype(BF16)
+        if level == 0:
+            fine_stats[at : at + rows] = jnp.concatenate(stats, axis=1)
+        else:
+            coarse_stats[at - ROWS : at - ROWS + rows] = jnp.concatenate(stats, axis=1).astype(BF16)
 
 
 def far_refs(refs):
@@ -265,77 +301,91 @@
     return 16 * (16 * core + 4 * y + x)
 
 
-def merge_kernel(q_all, qdoc, fine, coarse, grad_att, d_out, *refs):
+def merge_kernel(
+    q_all, qdoc, fine, fine_stats, coarse, coarse_stats, grad_att, d_out, *refs
+):
     far = far_refs(refs[:4])
     attended_out, keep, give, p_out, g_out, d_side, d_w = refs[4:]
-    docs = [(docs_of(index, qdoc), far_window(ref, DOC_LANES)) for index, ref in zip(FAR, far)]
-    shape = (LANES, LANES)
-    same_head = jnp.where(iota(shape, 0) // HEAD_DIM == iota(shape, 1) // HEAD_DIM, 1.0, 0.0)
-    same_head = same_head.astype(BF16)
     spreads = [None] + [spread_table(level) for level in range(1, LEVELS + 1)]
     gathers = [None] + [gather_table(level) for level in range(1, LEVELS + 1)]
-    for pair in range(PAIRS):
-        cols = lanes_of(pair)
-        packed = [None, coarse[pair, 0:128], coarse[pair, 128:192]]
-        for index, ref, (query_docs, key_docs) in zip(FAR, far, docs):
-            level, _, rows, keys = GROUPS[index]
-            p, stats = attend(
-                q_all[AT[level] : AT[level] + rows, cols],
+    numers, stats = [None, coarse[0:128], coarse[128:192]], [None, coarse_stats[0:128]]
+    stats.append(coarse_stats[128:192])
+    for index, ref in zip(FAR, far):
+        level, _, rows, keys = GROUPS[index]
+        query_docs, key_docs = docs_of(index, qdoc), far_window(ref, DOC_LANES)
+        own_stats, own_numers = no_stats(rows), []
+        for pair in range(PAIRS):
+            p, numer, sums, peak = attend(
+                q_all[AT[level] : AT[level] + rows, lanes_of(pair)],
                 query_docs,
                 far_window(ref, lanes_of(pair)),
                 key_docs,
                 far_window(ref, lanes_of(pair, 1)),
             )
+            own_stats = with_stats(own_stats, pair, sums, peak)
+            own_numers.append(numer.astype(BF16))
             p_out[pair, P_AT[index] : P_AT[index] + 2 * rows, 0:keys] = p
-            packed.append(stats.astype(BF16))
-        wide = [fine[pair]] + [
-            dot(spreads[level], packed[level]) for level in range(1, LEVELS + 1)
-        ]
-        levels = [[x[:, LANES * i : LANES * (i + 1)] for i in range(3)] for x in wide]
-        top = functools.reduce(jnp.maximum, [x[2] for x in levels])
-        weights = [jnp.exp(x[2] - top) for x in levels]
-        norm = functools.reduce(
-            jnp.add, [wt * x[1] * float(2**i) for i, (wt, x) in enumerate(zip(weights, levels))]
-        )
-        numer = functools.reduce(jnp.add, [wt * x[0] for wt, x in zip(weights, levels)])
-        inverse = 1.0 / norm
-        attended = (numer * inverse).astype(BF16)
+        numers.append(jnp.concatenate(own_numers, axis=1))
+        stats.append(jnp.concatenate(own_stats, axis=1).astype(BF16))
+    wide = [fine_stats[...]] + [
+        dot(spreads[level], stats[level]) for level in range(1, LEVELS + 1)
+    ]
+    sums, peaks = [x[:, :LANES] for x in wide], [x[:, LANES:] for x in wide]
+    top = functools.reduce(jnp.maximum, peaks)
+    weights = [jnp.exp(x - top) for x in peaks]
+    norm = functools.reduce(
+        jnp.add, [wt * x * float(2**i) for i, (wt, x) in enumerate(zip(weights, sums))]
+    )
+    inverse = 1.0 / jnp.where(iota(norm.shape, 1) < 2 * PAIRS, norm, 1.0)
+    shares = [wt * inverse for wt in weights]
+    share_parts = [both_parts(x) for x in shares]
+    delta = jnp.zeros((ROWS, LANES), F32)
+    for pair in range(PAIRS):
+        cols = lanes_of(pair)
+        to_lanes = head_spread(pair)
+        wide_shares = [dot(x, to_lanes) for x in share_parts]
+        numer = wide_shares[0] * fine[:, cols]
+        for level in range(1, LEVELS + 1):
+            numer = numer + wide_shares[level] * dot(spreads[level], numers[level][:, cols])
+        attended = numer.astype(BF16)
+        attended_out[:, cols] = attended
         grad_w = dot(attended, d_out[...], 0, 0)
         for block in range(8):
             at = block_at(8 * pair + block)
             d_w[at : at + 16] = grad_w[16 * block : 16 * (block + 1)]
-        attended_out[:, cols] = attended
         grad = grad_att[:, cols]
-        high_part, low_part = split(grad * attended.astype(F32))
-        delta = dot(high_part, same_head) + dot(low_part, same_head)
+        delta = delta + dot(both_parts(grad * attended.astype(F32)), head_sum(pair))
         for level in range(LEVELS + 1):
-            share = weights[level] * inverse
-            at, rows = AT[level], COUNT[level]
-            if level == 0:
-                grad_c, delta_c = share * grad, share * delta
-            else:
-                d_high, d_low = split(share * delta)
-                terms = jnp.concatenate([(share * grad).astype(BF16), d_high, d_low], axis=1)
-                summed = dot(gathers[level], terms)
-                grad_c = summed[:, :LANES]
-                delta_c = summed[:, LANES : 2 * LANES] + summed[:, 2 * LANES :]
-            g_out[at : at + rows, cols] = grad_c.astype(BF16)
-            d_high, d_low = split(delta_c * -float(2**level))
-            upper = iota((rows, LANES), 1) % HEAD_DIM < HALF
-            d_side[at : at + rows, cols] = jnp.where(
-                upper, d_high.astype(F32), d_low.astype(F32)
-            ).astype(BF16)
+            rows = (wide_shares[level] * grad).astype(BF16)
+            if level > 0:
+                rows = dot(gathers[level], rows).astype(BF16)
+            g_out[AT[level] : AT[level] + COUNT[level], cols] = rows
     core = core_index()
     keep[...] = d_w[pl.ds(pl.multiple_of(core * 256, 256), 256)]
     give[...] = d_w[pl.ds(pl.multiple_of((1 - core) * 256, 256), 256)].astype(BF16)
-
-
-def attend_back(p, queries, grad, side, keys, values):
+    shape = (2 * LANES, LANES)
+    part, head = iota(shape, 0) // LANES, iota(shape, 0) % LANES
+    place = jnp.where((head < 8) & (iota(shape, 1) == 8 * part + head), 1.0, 0.0).astype(BF16)
+    for level in range(LEVELS + 1):
+        delta_c = shares[level] * delta
+        if level > 0:
+            summed = dot(gathers[level], both_parts(delta_c))
+            delta_c = summed[:, :LANES] + summed[:, LANES:]
+        terms = dot(both_parts(delta_c * -float(2**level)), place)
+        d_side[AT[level] : AT[level] + COUNT[level]] = terms.astype(BF16)
+
+
+def attend_back(pair, p, queries, grad, side, keys, values):
     rows = queries.shape[0]
-    ones = jnp.where(iota(values.shape, 1) % HALF == 0, 1.0, 0.0).astype(BF16)
+    ones = jnp.where(iota(values.shape, 1) < 16, 1.0, 0.0).astype(BF16)
     grad = stacked(grad)
+    lane = iota(side.shape, 1)
+    sides = [
+        side * jnp.where((lane < 16) & (lane % 8 == 2 * pair + i), 1.0, 0.0).astype(BF16)
+        for i in (0, 1)
+    ]
     product = dot(
-        jnp.concatenate([grad, stacked(side)], axis=1),
+        jnp.concatenate([grad, jnp.concatenate(sides, axis=0)], axis=1),
         jnp.concatenate([values, ones], axis=1),
         1,
         1,
@@ -360,10 +410,11 @@
             level, _, rows, keys = GROUPS[index]
             at = AT[level]
             grad_q, grad_k, grad_v = attend_back(
+                pair,
                 p_in[pair, P_AT[index] : P_AT[index] + 2 * rows, 0:keys],
                 q_all[at : at + rows, cols],
                 g_in[at : at + rows, cols],
-                d_side[at : at + rows, cols],
+                d_side[at : at + rows],
                 far_window(ref, cols),
                 far_window(ref, lanes_of(pair, 1)),
             )
@@ -395,10 +446,11 @@
             at = AT[level] + start
             grads.append(
                 attend_back(
+                    pair,
                     p_in[pair, P_AT[index] : P_AT[index] + 2 * rows, 0:keys],
                     q_all[at : at + rows, cols],
                     g_in[at : at + rows, cols],
-                    d_side[at : at + rows, cols],
+                    d_side[at : at + rows],
                     near_window(index, own0, own1, low, high, cols),
                     near_window(index, own0, own1, low, high, lanes_of(pair, 1)),
                 )
@@ -619,14 +671,22 @@
 def body(queries, key_rows, value_rows, segment_ids, w_out, d_out):
     q, k, v, grad_out = queries[0], key_rows[0], value_rows[0], d_out[0]
     tokens, dma = (ROWS, WIDTH), pltpu.SemaphoreType.DMA
-    up, down, far, third_rows, own0, own1, qdoc = call(
+    qdoc = call(
+        documents_kernel,
+        "documents",
+        [((ALL_ROWS, LANES), BF16)],
+        [segment_ids],
+        [pltpu.VMEM((1, ROWS), jnp.int32), dma(())],
+        in_hbm=1,
+    )[0]
+    up, down, far, third_rows, own0, own1 = call(
         coarsen_kernel,
         "coarsen",
         [((192, PACK), BF16), ((192, PACK), BF16), ((48, PACK), BF16), ((16, PACK), BF16)]
-        + [((ROWS, PACK), BF16), ((128, PACK), BF16), ((ALL_ROWS, LANES), BF16)],
-        [segment_ids, k, v],
-        [pltpu.VMEM((1, ROWS), jnp.int32)] + [pltpu.VMEM(tokens, BF16)] * 2 + [dma((3,))],
-        in_hbm=3,
+        + [((ROWS, PACK), BF16), ((128, PACK), BF16)],
+        [qdoc, k, v],
+        [pltpu.VMEM(tokens, BF16)] * 2 + [dma((2,))],
+        in_hbm=2,
     )
     far_partner = moved(far, partner)
     far3, far4 = call(
@@ -654,14 +714,11 @@
     )
     far = (own3, got4, got_third, moved(passed, partner))
     near = (own0, own1, low, high)
-    p_near, fine, coarse = call(
+    p_near, *near_sums = call(
         near_kernel,
         "near",
-        [
-            ((PAIRS, P_NEAR, 256), BF16),
-            ((PAIRS, ROWS, 3 * LANES), F32),
-            ((PAIRS, 192, 3 * LANES), BF16),
-        ],
+        [((PAIRS, P_NEAR, 256), BF16), (tokens, F32), ((ROWS, 2 * LANES), F32)]
+        + [((192, WIDTH), BF16), ((192, 2 * LANES), BF16)],
         [q_all, qdoc, *near],
         microseconds=50,
     )
@@ -670,11 +727,12 @@
         "merge",
         [(tokens, BF16), ((256, WIDTH), F32), ((256, WIDTH), BF16)]
         + [((PAIRS, P_FAR, LANES), BF16)]
-        + [((ALL_ROWS, WIDTH), BF16)] * 2,
-        [q_all, qdoc, fine, coarse, grad_att, grad_rows, *far],
+        + [((ALL_ROWS, WIDTH), BF16), ((ALL_ROWS, LANES), BF16)],
+        [q_all, qdoc, *near_sums, grad_att, grad_rows, *far],
         [pltpu.VMEM((WIDTH, WIDTH), F32)],
         microseconds=6,
     )
+
     def halved(keep, got, divisor, route, *after):
         rows = keep.shape[0] // 2
         keep, give = call(

time: 75 us -> 72.6 us (0.968)
  local copies, waits for them, and re-layouts: 2.58 us -> 0.75 us
    unnamed x12, local copies, waits for them, and re-layouts: 2.58 us -> 0.75 us
    pallas_call x19 -> x20, Pallas kernels: 19.7 us -> 19.1 us  [call(): pl.pallas_call(kernel, name=name, out_shape=[jax.ShapeDtypeStruct(shape,...]
  transfers between devices with their start and end apart: 19 -> 19, of which waited for: 9 -> 9; matrix products, arithmetic and copies ran while one was open for 0% -> 0% of each run, Pallas kernels for 15% -> 16%
where the time goes in v7:
time: 72.6 us; the launch traced here: 71.8 us
  starting transfers between devices  27 us (37%)
  waiting for transfers between devices  24 us (33%)
  Pallas kernels  19.1 us (26%)
  between operations  0.9 us (1%)
  local copies, waits for them, and re-layouts  0.75 us (1%)
    ppermute x18, waiting for transfers between devices, moved(): return lax.ppermute(x, 'ctx', [(i, route(i) % count) for i in range(count)])  22.5 us
    pallas_call x20, Pallas kernels, call(): pl.pallas_call(kernel, name=name, out_shape=[jax.ShapeDtypeStruct(shape,...  19.1 us
    ppermute x18, starting transfers between devices, moved(): return lax.ppermute(x, 'ctx', [(i, route(i) % count) for i in range(count)])  18.4 us
    all_to_all x1, starting transfers between devices, body(): copies = lax.all_to_all(copies, 'dp', 0, 0, tiled=True)  8.57 us
    all_to_all x1, waiting for transfers between devices, body(): copies = lax.all_to_all(copies, 'dp', 0, 0, tiled=True)  1.52 us
  transfers between devices with their start and end apart: 19, of which 9 were waited for; matrix products, arithmetic and copies ran while one was open for 0% of the time, Pallas kernels for 16%

profile of v7, /device:TPU:32, one launch (start us, length us, event | category | flops | bytes accessed | tf_op | source)
XLA Modules:
  0.0 71.8 jit_solution(6529341237493695574)
XLA Ops:
  0.7 0.7 %copy-done.5 = s32[1,256]{1,0:T(1,128)S(1)} copy-done((s32[1,256]{1,0:T(1,128)S(1)}, s32[1,256]{1,0:T(1,128)}, u32[]{:S(2)}) %copy-start.5) | copy-done | bytes 1048
  1.7 0.6 coarsen.1
  2.4 5.1 %collective-permute-start.1 = (bf16[192,1152]{1,0:T(8,128)(2,1)S(1)}, bf16[192,1152]{1,0:T(8,128)(2,1)S(1)}, u32[]{:S(2)}, u32[]{:S(2)}) collective-permute-start(bf16[192,1152]{1,0:T(8,128)(2,1)S(1)} %get-tuple-element.82), channel_id=1, source_target_pairs={{0,31},{1,0},{2,1},{3,2},{4,3},{5,4},{6,5},{7,6},{8,7},{9,8},{10,9... | collective-permute-start | bytes 1327112 | tf_op jit(solution)/shard_map/ppermute | solution.py:644
  7.5 1.3 %collective-permute-done.2.far_partner = bf16[48,1152]{1,0:T(8,128)(2,1)S(1)} collective-permute-done((bf16[48,1152]{1,0:T(8,128)(2,1)S(1)}, bf16[48,1152]{1,0:T(8,128)(2,1)S(1)}, u32[]{:S(2)}, u32[]{:S(2)}) %collective-permute-start.2) | collective-permute-done | bytes 110624 | tf_op jit(solution)/shard_map/ppermute | solution.py:644
  8.9 2.9 %collective-permute-start.5 = (bf16[16,1152]{1,0:T(8,128)(2,1)S(1)}, bf16[16,1152]{1,0:T(8,128)(2,1)S(1)}, u32[]{:S(2)}, u32[]{:S(2)}) collective-permute-start(bf16[16,1152]{1,0:T(8,128)(2,1)S(1)} %get-tuple-element.95), channel_id=1, source_target_pairs={{0,6},{1,7},{2,28},{3,29},{4,10},{5,11},{6,0},{7,1},{8,14},{9,15},... | collective-permute-start | bytes 110600 | tf_op jit(solution)/shard_map/ppermute | solution.py:644
  11.9 0.7 %prepare.1 = (bf16[496,512]{1,0:T(8,128)(2,1)S(1)}, f32[256,512]{1,0:T(8,128)S(1)}, bf16[512,512]{1,0:T(8,128)(2,1)S(1)}, bf16[256,512]{1,0:T(8,128)(2,1)S(1)}) custom-call(bf16[256,512]{1,0:T(8,128)(2,1)S(1)} %bitcast.10, bf16[256,512]{1,0:T(8,128)(2,1)S(1)} %bitcast.11, bf16[512,512]{1,0:T(8,128)(2,1)S(1)} %copy-done), custom_call_target="tpu_custom_call" | custom-call | flops 1000000000 | bytes 1048576 | tf_op jit(solution)/shard_map/prepare/pallas_call | solution.py:628
  12.6 4.8 %collective-permute-done.3.got3 = bf16[64,1152]{1,0:T(8,128)(2,1)S(1)} collective-permute-done((bf16[64,1152]{1,0:T(8,128)(2,1)S(1)}, bf16[64,1152]{1,0:T(8,128)(2,1)S(1)}, u32[]{:S(2)}, u32[]{:S(2)}) %collective-permute-start.3) | collective-permute-done | bytes 147488 | tf_op jit(solution)/shard_map/ppermute | solution.py:644
  17.4 2.5 %collective-permute-done.4.got4.refs_1_ = bf16[32,1152]{1,0:T(8,128)(2,1)S(1)} collective-permute-done((bf16[32,1152]{1,0:T(8,128)(2,1)S(1)}, bf16[32,1152]{1,0:T(8,128)(2,1)S(1)}, u32[]{:S(2)}, u32[]{:S(2)}) %collective-permute-start.4) | collective-permute-done | bytes 73760 | tf_op jit(solution)/shard_map/ppermute | solution.py:644
  20.0 1.7 %near.1 = (bf16[4,896,256]{2,1,0:T(8,128)(2,1)S(1)}, f32[256,512]{1,0:T(8,128)S(1)}, f32[256,256]{1,0:T(8,128)S(1)}, bf16[192,512]{1,0:T(8,128)(2,1)S(1)}, bf16[192,256]{1,0:T(8,128)(2,1)S(1)}) custom-call(bf16[496,512]{1,0:T(8,128)(2,1)S(1)} %get-tuple-element.78.q_all.refs_1_, bf16[496,128]{1,0:T(8,128)(2,1)S(1)} %documents.1.qdoc, ...), custom_call_target="tpu_custom_call" | custom-call | flops 49999998976 | bytes 1048576 | tf_op jit(solution)/shard_map/near/pallas_call | solution.py:628
  21.7 4.8 %merge.1 = (bf16[256,512]{1,0:T(8,128)(2,1)S(1)}, f32[256,512]{1,0:T(8,128)S(1)}, bf16[256,512]{1,0:T(8,128)(2,1)S(1)}, bf16[4,96,128]{2,1,0:T(8,128)(2,1)S(1)},...) custom-call(bf16[496,512]{1,0:T(8,128)(2,1)S(1)} %get-tuple-element.78.q_all.refs_1_, ...), custom_call_target="tpu_custom_call" | custom-call | flops 6000000000 | bytes 1048576 | tf_op jit(solution)/shard_map/merge/pallas_call | solution.py:628
  26.5 1.1 %far_back.1 = (bf16[48,512]{1,0:T(8,128)(2,1)S(1)}, bf16[32,1024]{1,0:T(8,128)(2,1)S(1)}, bf16[32,1024]{1,0:T(8,128)(2,1)S(1)}, bf16[16,1024]{1,0:T(8,128)(2,1)S(1)}, bf16[480,512]{1,0:T(8,128)(2,1)S(1)}) custom-call(bf16[4,96,128]{2,1,0:T(8,128)(2,1)S(1)} %get-tuple-element.103.p_in, bf16[496,512]{1,0:T(8,128)(2,1)S(1)} %get-tuple-element.78.q_all.refs_1_, ...), custom_call_target="tpu_custom_call" | custom-call | flops 1000000000 | bytes 1048576 | tf_op jit(solution)/shard_map/far_back/pallas_call | solution.py:628
  27.6 0.8 %collective-permute-start.7 = (bf16[480,512]{1,0:T(8,128)(2,1)S(1)}, bf16[480,512]{1,0:T(8,128)(2,1)S(1)}, u32[]{:S(2)}, u32[]{:S(2)}) collective-permute-start(bf16[480,512]{1,0:T(8,128)(2,1)S(1)} %get-tuple-element.114), channel_id=1, source_target_pairs={{0,1},{1,0},{2,3},{3,2},{4,5},{5,4},{6,7},{7,6},{8,9},{9,8},{10,11... | collective-permute-start | bytes 1474568 | tf_op jit(solution)/shard_map/ppermute | solution.py:644
  28.4 2.0 %near_back_a.1 = (bf16[256,128]{1,0:T(8,128)(2,1)S(1)}, f32[256,128]{1,0:T(8,128)S(1)}, f32[256,128]{1,0:T(8,128)S(1)}, bf16[2,192,128]{2,1,0:T(8,128)(2,1)S(1)}...) custom-call(bf16[256,512]{1,0:T(8,128)(2,1)S(1)} %get-tuple-element.98.attended, ...), custom_call_target="tpu_custom_call" | custom-call | flops 3000000000 | bytes 1048576 | tf_op jit(solution)/shard_map/near_back_a/pallas_call | solution.py:628
  30.6 0.9 %collective-permute-start.8 = (bf16[128,512]{1,0:T(8,128)(2,1)S(1)}, bf16[128,512]{1,0:T(8,128)(2,1)S(1)}, u32[]{:S(2)}, u32[]{:S(2)}) collective-permute-start(bf16[128,512]{1,0:T(8,128)(2,1)S(1)} %get-tuple-element.116), channel_id=1, source_target_pairs={{0,6},{1,7},{2,4},{3,5},{4,2},{5,3},{6,0},{7,1},{8,14},{9,15},{10,... | collective-permute-start | bytes 393224 | tf_op jit(solution)/shard_map/ppermute | solution.py:644
  31.5 0.8 %collective-permute-start.12 = (bf16[32,1024]{1,0:T(8,128)(2,1)S(1)}, bf16[32,1024]{1,0:T(8,128)(2,1)S(1)}, u32[]{:S(2)}, u32[]{:S(2)}) collective-permute-start(bf16[32,1024]{1,0:T(8,128)(2,1)S(1)} %get-tuple-element.129), channel_id=1, source_target_pairs={{0,28},{1,5},{2,30},{3,7},{4,0},{5,9},{6,2},{7,11},{8,4},{9,13},{1... | collective-permute-start | bytes 196616 | tf_op jit(solution)/shard_map/ppermute | solution.py:644
  32.3 2.8 %collective-permute-start.11 = (bf16[64,1024]{1,0:T(8,128)(2,1)S(1)}, bf16[64,1024]{1,0:T(8,128)(2,1)S(1)}, u32[]{:S(2)}, u32[]{:S(2)}) collective-permute-start(bf16[64,1024]{1,0:T(8,128)(2,1)S(1)} %get-tuple-element.128), channel_id=1, source_target_pairs={{0,30},{1,3},{2,0},{3,5},{4,2},{5,7},{6,4},{7,9},{8,6},{9,11},{10,... | collective-permute-start | bytes 393224 | tf_op jit(solution)/shard_map/ppermute | solution.py:644
  35.1 5.0 %collective-permute-done.8.got = bf16[128,512]{1,0:T(8,128)(2,1)S(1)} collective-permute-done((bf16[128,512]{1,0:T(8,128)(2,1)S(1)}, bf16[128,512]{1,0:T(8,128)(2,1)S(1)}, u32[]{:S(2)}, u32[]{:S(2)}) %collective-permute-start.8) | collective-permute-done | bytes 131104 | tf_op jit(solution)/shard_map/ppermute | solution.py:644
  40.3 1.5 %near_back_b.1 = (bf16[256,128]{1,0:T(8,128)(2,1)S(1)}, f32[256,128]{1,0:T(8,128)S(1)}, f32[256,128]{1,0:T(8,128)S(1)}, bf16[2,192,128]{2,1,0:T(8,128)(2,1)S(1)}, bf16[2,192,128]{2,1,0:T(8,128)(2,1)S(1)}) custom-call(bf16[4,896,256]{2,1,0:T(8,128)(2,1)S(1)} %get-tuple-element.100.refs_0_, bf16[496,512]{1,0:T(8,128)(2,1)S(1)} %get-tuple-element.78.q_all.refs_1_, ...), custom_call_target="tpu_custom_call" | custom-call | flops 3000000000 | bytes 1048576 | tf_op jit(solution)/shard_map/near_back_b/pallas_call | solution.py:628
  41.8 2.7 %collective-permute-done.9.got = bf16[64,512]{1,0:T(8,128)(2,1)S(1)} collective-permute-done((bf16[64,512]{1,0:T(8,128)(2,1)S(1)}, bf16[64,512]{1,0:T(8,128)(2,1)S(1)}, u32[]{:S(2)}, u32[]{:S(2)}) %collective-permute-start.9) | collective-permute-done | bytes 65568 | tf_op jit(solution)/shard_map/ppermute | solution.py:644
  44.6 1.8 %collective-permute-start.10 = (bf16[32,512]{1,0:T(8,128)(2,1)S(1)}, bf16[32,512]{1,0:T(8,128)(2,1)S(1)}, u32[]{:S(2)}, u32[]{:S(2)}) collective-permute-start(bf16[32,512]{1,0:T(8,128)(2,1)S(1)} %get-tuple-element.126), channel_id=1, source_target_pairs={{0,24},{1,25},{2,26},{3,27},{4,28},{5,29},{6,30},{7,31},{8,16},{9,... | collective-permute-start | bytes 98312 | tf_op jit(solution)/shard_map/ppermute | solution.py:644
  46.4 1.4 %near_back_c.1 = (bf16[256,128]{1,0:T(8,128)(2,1)S(1)}, f32[256,128]{1,0:T(8,128)S(1)}, f32[256,128]{1,0:T(8,128)S(1)}, bf16[2,192,128]{2,1,0:T(8,128)(2,1)S(1)}, bf16[2,192,128]{2,1,0:T(8,128)(2,1)S(1)}) custom-call(bf16[4,896,256]{2,1,0:T(8,128)(2,1)S(1)} %get-tuple-element.100.refs_0_, bf16[496,512]{1,0:T(8,128)(2,1)S(1)} %get-tuple-element.78.q_all.refs_1_, ...), custom_call_target="tpu_custom_call" | custom-call | flops 3000000000 | bytes 1048576 | tf_op jit(solution)/shard_map/near_back_c/pallas_call | solution.py:628
  47.8 2.0 %collective-permute-done.10.got = bf16[32,512]{1,0:T(8,128)(2,1)S(1)} collective-permute-done((bf16[32,512]{1,0:T(8,128)(2,1)S(1)}, bf16[32,512]{1,0:T(8,128)(2,1)S(1)}, u32[]{:S(2)}, u32[]{:S(2)}) %collective-permute-start.10) | collective-permute-done | bytes 32800 | tf_op jit(solution)/shard_map/ppermute | solution.py:644
  49.9 2.2 %near_back_d.1 = (bf16[256,512]{1,0:T(8,128)(2,1)}, f32[256,128]{1,0:T(8,128)S(1)}, f32[256,128]{1,0:T(8,128)S(1)}, bf16[192,1024]{1,0:T(8,128)(2,1)S(1)}, bf16[192,1024]{1,0:T(8,128)(2,1)S(1)}) custom-call(bf16[4,896,256]{2,1,0:T(8,128)(2,1)S(1)} %get-tuple-element.100.refs_0_, bf16[496,512]{1,0:T(8,128)(2,1)S(1)} %get-tuple-element.78.q_all.refs_1_, ...), custom_call_target="tpu_custom_call" | custom-call | flops 3000000000 | bytes 1048576 | tf_op jit(solution)/shard_map/near_back_d/pallas_call | solution.py:628
  52.1 1.5 %collective-permute-done.13.got = bf16[16,512]{1,0:T(8,128)(2,1)S(1)} collective-permute-done((bf16[16,512]{1,0:T(8,128)(2,1)S(1)}, bf16[16,512]{1,0:T(8,128)(2,1)S(1)}, u32[]{:S(2)}, u32[]{:S(2)}) %collective-permute-start.13) | collective-permute-done | bytes 16416 | tf_op jit(solution)/shard_map/ppermute | solution.py:644
  53.6 0.5 collective-permute-start.15
  54.1 0.7 copies.1
  54.8 8.6 %all-to-all-start = ((bf16[8,16,512]{2,1,0:T(8,128)(2,1)}), bf16[8,16,512]{2,1,0:T(8,128)(2,1)S(1)}, u32[]{:S(2)}, u32[]{:S(2)}) async-start(bf16[8,16,512]{2,1,0:T(8,128)(2,1)} %copies.1), calls=%async_computation | async-start | bytes 262144 | tf_op jit(solution)/shard_map/all_to_all | solution.py:828
  63.4 2.4 %collective-permute-start.16 = (bf16[16,1024]{1,0:T(8,128)(2,1)S(1)}, bf16[16,1024]{1,0:T(8,128)(2,1)S(1)}, u32[]{:S(2)}, u32[]{:S(2)}) collective-permute-start(bf16[16,1024]{1,0:T(8,128)(2,1)S(1)} %get-tuple-element.146), channel_id=1, source_target_pairs={{0,6},{1,7},{2,28},{3,29},{4,10},{5,11},{6,0},{7,1},{8,14},{9,15},... | collective-permute-start | bytes 98312 | tf_op jit(solution)/shard_map/ppermute | solution.py:644
  65.8 2.7 %collective-permute-done.16.refs_12_ = bf16[16,1024]{1,0:T(8,128)(2,1)S(1)} collective-permute-done((bf16[16,1024]{1,0:T(8,128)(2,1)S(1)}, bf16[16,1024]{1,0:T(8,128)(2,1)S(1)}, u32[]{:S(2)}, u32[]{:S(2)}) %collective-permute-start.16) | collective-permute-done | bytes 32800 | tf_op jit(solution)/shard_map/ppermute | solution.py:644
  68.5 1.1 %combine.1 = (bf16[256,512]{1,0:T(8,128)(2,1)}, bf16[256,512]{1,0:T(8,128)(2,1)}, f32[8,128]{1,0:T(8,128)S(1)}) custom-call(f32[256,128]{1,0:T(8,128)S(1)} %get-tuple-element.131.refs_0_, f32[256,128]{1,0:T(8,128)S(1)} %get-tuple-element.132.refs_1_, f32[256,128]{1,0:T(8,128)S(1)} %get-tuple-element.133.refs_2_, f32[256,128]{1,0:T(8,128)S(1)} %get-tuple-element.134.refs_3_, ...), custom_call_target="tpu_custom_call" | custom-call | flops 1000000000 | bytes 1048576 | tf_op jit(solution)/shard_map/combine/pallas_call | solution.py:628
  69.6 1.5 %all-to-all-done.parts = bf16[8,16,512]{2,1,0:T(8,128)(2,1)S(1)} async-done(((bf16[8,16,512]{2,1,0:T(8,128)(2,1)}), bf16[8,16,512]{2,1,0:T(8,128)(2,1)S(1)}, u32[]{:S(2)}, u32[]{:S(2)}) %all-to-all-start) | async-done | bytes 131104 | tf_op jit(solution)/shard_map/all_to_all | solution.py:828
  71.1 0.6 last_sum.1
  (38 shorter events, 1.1 us)
Async XLA Ops:
  0.6 1.1 %copy-start.2 = (bf16[1,256,512]{2,1,0:T(8,128)(2,1)S(1)}, bf16[1,256,512]{2,1,0:T(8,128)(2,1)}, u32[]{:S(2)}) copy-start(bf16[1,256,512]{2,1,0:T(8,128)(2,1)} %param.8) | copy-start | bytes 786436
  0.6 1.1 %copy-start.1 = (bf16[1,256,512]{2,1,0:T(8,128)(2,1)S(1)}, bf16[1,256,512]{2,1,0:T(8,128)(2,1)}, u32[]{:S(2)}) copy-start(bf16[1,256,512]{2,1,0:T(8,128)(2,1)} %param.7) | copy-start | bytes 786436
  0.7 0.7 %copy-start.5 = (s32[1,256]{1,0:T(1,128)S(1)}, s32[1,256]{1,0:T(1,128)}, u32[]{:S(2)}) copy-start(s32[1,256]{1,0:T(1,128)} %seg_hbm.1) | copy-start | bytes 3076
  2.3 15.0 %collective-permute-start = (bf16[192,1152]{1,0:T(8,128)(2,1)S(1)}, bf16[192,1152]{1,0:T(8,128)(2,1)S(1)}, u32[]{:S(2)}, u32[]{:S(2)}) collective-permute-start(bf16[192,1152]{1,0:T(8,128)(2,1)S(1)} %get-tuple-element.81), channel_id=1, source_target_pairs={{0,1},{1,2},{2,3},{3,4},{4,5},{5,6},{6,7},{7,8},{8,9},{9,10},{10,1... | collective-permute-start | bytes 1327112 | tf_op jit(solution)/shard_map/ppermute | solution.py:644
  2.4 15.0 %collective-permute-start.1 = (bf16[192,1152]{1,0:T(8,128)(2,1)S(1)}, bf16[192,1152]{1,0:T(8,128)(2,1)S(1)}, u32[]{:S(2)}, u32[]{:S(2)}) collective-permute-start(bf16[192,1152]{1,0:T(8,128)(2,1)S(1)} %get-tuple-element.82), channel_id=1, source_target_pairs={{0,31},{1,0},{2,1},{3,2},{4,3},{5,4},{6,5},{7,6},{8,7},{9,8},{10,9... | collective-permute-start | bytes 1327112 | tf_op jit(solution)/shard_map/ppermute | solution.py:644
  7.5 4.4 %copy-start = (bf16[512,512]{1,0:T(8,128)(2,1)S(1)}, bf16[512,512]{1,0:T(8,128)(2,1)}, u32[]{:S(2)}) copy-start(bf16[512,512]{1,0:T(8,128)(2,1)} %w_hbm.1) | copy-start | bytes 1572868
  7.5 4.4 %copy-start.3 = (bf16[1,256,512]{2,1,0:T(8,128)(2,1)S(1)}, bf16[1,256,512]{2,1,0:T(8,128)(2,1)}, u32[]{:S(2)}) copy-start(bf16[1,256,512]{2,1,0:T(8,128)(2,1)} %param.6) | copy-start | bytes 786436
  7.5 4.4 %copy-start.4 = (bf16[1,256,512]{2,1,0:T(8,128)(2,1)S(1)}, bf16[1,256,512]{2,1,0:T(8,128)(2,1)}, u32[]{:S(2)}) copy-start(bf16[1,256,512]{2,1,0:T(8,128)(2,1)} %param.11) | copy-start | bytes 786436
  7.5 1.3 %collective-permute-start.2 = (bf16[48,1152]{1,0:T(8,128)(2,1)S(1)}, bf16[48,1152]{1,0:T(8,128)(2,1)S(1)}, u32[]{:S(2)}, u32[]{:S(2)}) collective-permute-start(bf16[48,1152]{1,0:T(8,128)(2,1)S(1)} %get-tuple-element.83.far), channel_id=1, source_target_pairs={{0,1},{1,0},{2,3},{3,2},{4,5},{5,4},{6,7},{7,6},{8,9},{9,8},{10,11... | collective-permute-start | bytes 331784 | tf_op jit(solution)/shard_map/ppermute | solution.py:644
  8.8 8.5 %collective-permute-start.3 = (bf16[64,1152]{1,0:T(8,128)(2,1)S(1)}, bf16[64,1152]{1,0:T(8,128)(2,1)S(1)}, u32[]{:S(2)}, u32[]{:S(2)}) collective-permute-start(bf16[64,1152]{1,0:T(8,128)(2,1)S(1)} %get-tuple-element.84), channel_id=1, source_target_pairs={{0,2},{1,31},{2,4},{3,1},{4,6},{5,3},{6,8},{7,5},{8,10},{9,7},{10,... | collective-permute-start | bytes 442376 | tf_op jit(solution)/shard_map/ppermute | solution.py:644
  8.9 8.5 %collective-permute-start.5 = (bf16[16,1152]{1,0:T(8,128)(2,1)S(1)}, bf16[16,1152]{1,0:T(8,128)(2,1)S(1)}, u32[]{:S(2)}, u32[]{:S(2)}) collective-permute-start(bf16[16,1152]{1,0:T(8,128)(2,1)S(1)} %get-tuple-element.95), channel_id=1, source_target_pairs={{0,6},{1,7},{2,28},{3,29},{4,10},{5,11},{6,0},{7,1},{8,14},{9,15},... | collective-permute-start | bytes 110600 | tf_op jit(solution)/shard_map/ppermute | solution.py:644
  11.9 8.0 %collective-permute-start.4 = (bf16[32,1152]{1,0:T(8,128)(2,1)S(1)}, bf16[32,1152]{1,0:T(8,128)(2,1)S(1)}, u32[]{:S(2)}, u32[]{:S(2)}) collective-permute-start(bf16[32,1152]{1,0:T(8,128)(2,1)S(1)} %get-tuple-element.94), channel_id=1, source_target_pairs={{0,4},{1,29},{2,6},{3,31},{4,8},{5,1},{6,10},{7,3},{8,12},{9,5},{1... | collective-permute-start | bytes 221192 | tf_op jit(solution)/shard_map/ppermute | solution.py:644
  19.9 1.8 %collective-permute-start.6 = (bf16[112,1152]{1,0:T(8,128)(2,1)S(1)}, bf16[112,1152]{1,0:T(8,128)(2,1)S(1)}, u32[]{:S(2)}, u32[]{:S(2)}) collective-permute-start(bf16[112,1152]{1,0:T(8,128)(2,1)S(1)} %get-tuple-element.97), channel_id=1, source_target_pairs={{0,1},{1,0},{2,3},{3,2},{4,5},{5,4},{6,7},{7,6},{8,9},{9,8},{10,11... | collective-permute-start | bytes 774152 | tf_op jit(solution)/shard_map/ppermute | solution.py:644
  27.6 2.8 %collective-permute-start.7 = (bf16[480,512]{1,0:T(8,128)(2,1)S(1)}, bf16[480,512]{1,0:T(8,128)(2,1)S(1)}, u32[]{:S(2)}, u32[]{:S(2)}) collective-permute-start(bf16[480,512]{1,0:T(8,128)(2,1)S(1)} %get-tuple-element.114), channel_id=1, source_target_pairs={{0,1},{1,0},{2,3},{3,2},{4,5},{5,4},{6,7},{7,6},{8,9},{9,8},{10,11... | collective-permute-start | bytes 1474568 | tf_op jit(solution)/shard_map/ppermute | solution.py:644
  30.6 9.5 %collective-permute-start.8 = (bf16[128,512]{1,0:T(8,128)(2,1)S(1)}, bf16[128,512]{1,0:T(8,128)(2,1)S(1)}, u32[]{:S(2)}, u32[]{:S(2)}) collective-permute-start(bf16[128,512]{1,0:T(8,128)(2,1)S(1)} %get-tuple-element.116), channel_id=1, source_target_pairs={{0,6},{1,7},{2,4},{3,5},{4,2},{5,3},{6,0},{7,1},{8,14},{9,15},{10,... | collective-permute-start | bytes 393224 | tf_op jit(solution)/shard_map/ppermute | solution.py:644
  31.5 10.2 %collective-permute-start.12 = (bf16[32,1024]{1,0:T(8,128)(2,1)S(1)}, bf16[32,1024]{1,0:T(8,128)(2,1)S(1)}, u32[]{:S(2)}, u32[]{:S(2)}) collective-permute-start(bf16[32,1024]{1,0:T(8,128)(2,1)S(1)} %get-tuple-element.129), channel_id=1, source_target_pairs={{0,28},{1,5},{2,30},{3,7},{4,0},{5,9},{6,2},{7,11},{8,4},{9,13},{1... | collective-permute-start | bytes 196616 | tf_op jit(solution)/shard_map/ppermute | solution.py:644
  32.3 9.4 %collective-permute-start.11 = (bf16[64,1024]{1,0:T(8,128)(2,1)S(1)}, bf16[64,1024]{1,0:T(8,128)(2,1)S(1)}, u32[]{:S(2)}, u32[]{:S(2)}) collective-permute-start(bf16[64,1024]{1,0:T(8,128)(2,1)S(1)} %get-tuple-element.128), channel_id=1, source_target_pairs={{0,30},{1,3},{2,0},{3,5},{4,2},{5,7},{6,4},{7,9},{8,6},{9,11},{10,... | collective-permute-start | bytes 393224 | tf_op jit(solution)/shard_map/ppermute | solution.py:644
  40.2 4.4 %collective-permute-start.9 = (bf16[64,512]{1,0:T(8,128)(2,1)S(1)}, bf16[64,512]{1,0:T(8,128)(2,1)S(1)}, u32[]{:S(2)}, u32[]{:S(2)}) collective-permute-start(bf16[64,512]{1,0:T(8,128)(2,1)S(1)} %get-tuple-element.121), channel_id=1, source_target_pairs={{0,2},{1,3},{2,0},{3,1},{4,6},{5,7},{6,4},{7,5},{8,10},{9,11},{10,... | collective-permute-start | bytes 196616 | tf_op jit(solution)/shard_map/ppermute | solution.py:644
  44.6 5.2 %collective-permute-start.10 = (bf16[32,512]{1,0:T(8,128)(2,1)S(1)}, bf16[32,512]{1,0:T(8,128)(2,1)S(1)}, u32[]{:S(2)}, u32[]{:S(2)}) collective-permute-start(bf16[32,512]{1,0:T(8,128)(2,1)S(1)} %get-tuple-element.126), channel_id=1, source_target_pairs={{0,24},{1,25},{2,26},{3,27},{4,28},{5,29},{6,30},{7,31},{8,16},{9,... | collective-permute-start | bytes 98312 | tf_op jit(solution)/shard_map/ppermute | solution.py:644
  49.8 3.8 %collective-permute-start.13 = (bf16[16,512]{1,0:T(8,128)(2,1)S(1)}, bf16[16,512]{1,0:T(8,128)(2,1)S(1)}, u32[]{:S(2)}, u32[]{:S(2)}) collective-permute-start(bf16[16,512]{1,0:T(8,128)(2,1)S(1)} %get-tuple-element.141), channel_id=1, source_target_pairs={{0,8},{1,9},{2,10},{3,11},{4,12},{5,13},{6,14},{7,15},{8,0},{9,1},... | collective-permute-start | bytes 49160 | tf_op jit(solution)/shard_map/ppermute | solution.py:644
  53.6 14.9 %collective-permute-start.14 = (bf16[192,1024]{1,0:T(8,128)(2,1)S(1)}, bf16[192,1024]{1,0:T(8,128)(2,1)S(1)}, u32[]{:S(2)}, u32[]{:S(2)}) collective-permute-start(bf16[192,1024]{1,0:T(8,128)(2,1)S(1)} %get-tuple-element.142), channel_id=1, source_target_pairs={{0,31},{1,0},{2,1},{3,2},{4,3},{5,4},{6,5},{7,6},{8,7},{9,8},{10,9... | collective-permute-start | bytes 1179656 | tf_op jit(solution)/shard_map/ppermute | solution.py:644
  53.6 14.9 %collective-permute-start.15 = (bf16[192,1024]{1,0:T(8,128)(2,1)S(1)}, bf16[192,1024]{1,0:T(8,128)(2,1)S(1)}, u32[]{:S(2)}, u32[]{:S(2)}) collective-permute-start(bf16[192,1024]{1,0:T(8,128)(2,1)S(1)} %get-tuple-element.143), channel_id=1, source_target_pairs={{0,1},{1,2},{2,3},{3,4},{4,5},{5,6},{6,7},{7,8},{8,9},{9,10},{10,1... | collective-permute-start | bytes 1179656 | tf_op jit(solution)/shard_map/ppermute | solution.py:644
  54.8 16.4 %all-to-all-start = ((bf16[8,16,512]{2,1,0:T(8,128)(2,1)}), bf16[8,16,512]{2,1,0:T(8,128)(2,1)S(1)}, u32[]{:S(2)}, u32[]{:S(2)}) async-start(bf16[8,16,512]{2,1,0:T(8,128)(2,1)} %copies.1), calls=%async_computation | async-start | bytes 262144 | tf_op jit(solution)/shard_map/all_to_all | solution.py:828
  63.4 2.4 %collective-permute-start.17 = (bf16[48,1024]{1,0:T(8,128)(2,1)S(1)}, bf16[48,1024]{1,0:T(8,128)(2,1)S(1)}, u32[]{:S(2)}, u32[]{:S(2)}) collective-permute-start(bf16[48,1024]{1,0:T(8,128)(2,1)S(1)} %far_split.1.refs_19_), channel_id=1, source_target_pairs={{0,1},{1,0},{2,3},{3,2},{4,5},{5,4},{6,7},{7,6},{8,9},{9,8},{10,11... | collective-permute-start | bytes 294920 | tf_op jit(solution)/shard_map/ppermute | solution.py:644
  63.4 5.1 %collective-permute-start.16 = (bf16[16,1024]{1,0:T(8,128)(2,1)S(1)}, bf16[16,1024]{1,0:T(8,128)(2,1)S(1)}, u32[]{:S(2)}, u32[]{:S(2)}) collective-permute-start(bf16[16,1024]{1,0:T(8,128)(2,1)S(1)} %get-tuple-element.146), channel_id=1, source_target_pairs={{0,6},{1,7},{2,28},{3,29},{4,10},{5,11},{6,0},{7,1},{8,14},{9,15},... | collective-permute-start | bytes 98312 | tf_op jit(solution)/shard_map/ppermute | solution.py:644

commit v8 on v7

--- a/solution.py
+++ b/solution.py
@@ -462,62 +462,37 @@
         for part, value in ((0, 0.5), (1, 1.0)):
             a, b, c, d = (x[1 + part] for x in grads)
             middle = jnp.concatenate([a[64:128], a[128:256] + b[0:128], b[128:192]], axis=0)
-            own.append(middle + dot(spread_table(1, value), c[64:192].astype(BF16)))
+            near = dot(spread_table(1, value), c[64:192].astype(BF16))
+            own.append((middle + near).astype(BF16))
             to_low.append(jnp.concatenate([a[:64], c[:64], d[:64]], axis=0).astype(BF16))
             to_high.append(jnp.concatenate([b[192:], c[192:], d[64:]], axis=0).astype(BF16))
         yield pair, d_q, own, to_low, to_high
 
 
-def near_back_first_kernel(pairs, attended, w, *refs):
-    inputs, outs = refs[:9], refs[9:]
-    layer_out = None
-    if attended is not None:
-        layer_out, result, sem = outs[-3:]
-        result[...] = dot(attended[...], w[...]).astype(BF16)
-        copy = pltpu.make_async_copy(result, layer_out, sem)
-        copy.start()
-    d_q, own_k, own_v, to_low, to_high = outs[:5]
+def near_back_kernel(pairs, *refs):
+    inputs, outs = refs[:9], refs[-5:]
+    d_q, own_k, own_v, to_low, to_high = outs
     for pair, dq, own, low, high in near_back(pairs, *inputs):
         at = slice((pair - pairs[0]) * LANES, (pair - pairs[0] + 1) * LANES)
         d_q[:, at], own_k[:, at], own_v[:, at] = dq, own[0], own[1]
         for part in range(2):
             to_low[part, :, at], to_high[part, :, at] = low[part], high[part]
-    if attended is not None:
-        copy.wait()
-
-
-def near_back_a_kernel(attended, w, *refs):
-    near_back_first_kernel(NEAR_PARTS[0], attended, w, *refs)
-
-
-def near_back_more_kernel(pairs, *refs):
-    near_back_first_kernel(pairs, None, None, *refs[:9], *refs[-5:])
 
 
 def near_back_last_kernel(*refs):
-    inputs, earlier = refs[:9], [refs[at : at + 3] for at in (9, 12, 15)]
-    d_q_hbm, own_k, own_v, to_low, to_high, d_q, sems = refs[-7:]
-    for pairs, (dq, low, high) in zip(NEAR_PARTS, earlier):
-        cols = slice(pairs[0] * LANES, (pairs[-1] + 1) * LANES)
-        d_q[:, cols] = dq[...]
+    inputs, earlier = refs[:9], [refs[at : at + 2] for at in (9, 11, 13)]
+    d_q, own_k, own_v, to_low, to_high = refs[-5:]
+    for pairs, (low, high) in zip(NEAR_PARTS, earlier):
         for part in range(2):
-            lanes = slice(part * WIDTH + cols.start, part * WIDTH + cols.stop)
+            lanes = slice(
+                part * WIDTH + pairs[0] * LANES, part * WIDTH + (pairs[-1] + 1) * LANES
+            )
             to_low[:, lanes], to_high[:, lanes] = low[part], high[part]
-    last = NEAR_PARTS[-1][0] * LANES
-    before = pltpu.make_async_copy(d_q.at[:, 0:last], d_q_hbm.at[:, 0:last], sems.at[0])
-    before.start()
     for pair, dq, own, low, high in near_back(NEAR_PARTS[-1], *inputs):
-        d_q[:, lanes_of(pair)] = dq
-        own_k[...], own_v[...] = own[0], own[1]
-        after = pltpu.make_async_copy(
-            d_q.at[:, lanes_of(pair)], d_q_hbm.at[:, lanes_of(pair)], sems.at[1]
-        )
-        after.start()
+        d_q[...], own_k[...], own_v[...] = dq, own[0], own[1]
         for part in range(2):
             to_low[:, lanes_of(pair, part)] = low[part]
             to_high[:, lanes_of(pair, part)] = high[part]
-    before.wait()
-    after.wait()
 
 
 def pass_on_kernel(got3, got4, third, own3, out):
@@ -582,16 +557,27 @@
     out[...] = total.astype(BF16)
 
 
+def project_kernel(attended, w, _, layer_hbm, finished, layer_out, sem):
+    finished[...] = jnp.zeros(finished.shape, F32)
+    layer_out[...] = dot(attended[...], w[...]).astype(BF16)
+    copy = pltpu.make_async_copy(layer_out, layer_hbm, sem)
+    copy.start()
+    copy.wait()
+
+
 def combine_kernel(*refs):
-    own, (low, high) = (refs[0:4], refs[4:8]), refs[8:10]
+    own, (low, high), grads_q = (refs[0:4], refs[4:8]), refs[8:10], refs[14:18]
     back3, back4, third, swapped = refs[10:14]
-    d_k_hbm, d_v_hbm, finished, d_k, d_v, sems = refs[14:]
+    d_k_hbm, d_v_hbm, d_q_hbm, finished, d_k, d_v, d_q, sems = refs[18:]
     finished[...] = jnp.zeros(finished.shape, F32)
+    for pair, ref in enumerate(grads_q):
+        d_q[:, lanes_of(pair)] = ref[...]
+    copies = [pltpu.make_async_copy(d_q, d_q_hbm, sems.at[2])]
+    copies[0].start()
     core = core_index()
     far3 = core_rows(back3, core, 32).astype(F32) + swapped[0:32].astype(F32)
     far4 = core_rows(back4, core, 16).astype(F32) + swapped[32:48].astype(F32)
     far4 = far4 + third[...].astype(F32)
-    copies = []
     for part, out, out_hbm in ((0, d_k, d_k_hbm), (1, d_v, d_v_hbm)):
         lanes = slice(part * WIDTH, (part + 1) * WIDTH)
         table = jnp.concatenate(
@@ -611,7 +597,8 @@
             ],
             axis=0,
         ).astype(BF16)
-        whole = jnp.concatenate([x[...] for x in own[part]], axis=1) + dot(table, coarse)
+        whole = jnp.concatenate([x[...] for x in own[part]], axis=1).astype(F32)
+        whole = whole + dot(table, coarse)
         out[0:64] = (whole[0:64] + rim(high, 0)).astype(BF16)
         out[64:192] = whole[64:192].astype(BF16)
         out[192:256] = (whole[192:256] + rim(low, 0)).astype(BF16)
@@ -756,19 +743,15 @@
 
     def part_outs(part):
         width = len(NEAR_PARTS[part]) * LANES
-        return [((ROWS, width), BF16), ((ROWS, width), F32), ((ROWS, width), F32)] + [
-            ((2, 192, width), BF16)
-        ] * 2
+        return [((ROWS, width), BF16)] * 3 + [((2, 192, width), BF16)] * 2
 
     args = [p_near, q_all, g, d_side, *near, d_far]
-    *part_a, layer_out = call(
-        near_back_a_kernel,
+    part_a = call(
+        functools.partial(near_back_kernel, NEAR_PARTS[0]),
         "near_back_a",
-        part_outs(0) + [(tokens, BF16)],
-        [attended, w, *args],
-        [pltpu.VMEM(tokens, BF16), dma(())],
+        part_outs(0),
+        args,
         microseconds=3,
-        to_hbm=(5,),
     )
     sum3, sum4, sum_third, keep, give = call(
         partner_sum_kernel,
@@ -782,9 +765,18 @@
     got_w = moved(give, lambda i: i ^ 6)
     back3 = moved(sum3, back_3)
     back4 = moved(sum4, back_4)
-    keep, got_w = halved(keep, got_w, 2, lambda i: i ^ 2)
+    layer_out, projected = call(
+        project_kernel,
+        "project",
+        [(tokens, BF16), ((8, LANES), F32)],
+        [attended, w, sum3],
+        [pltpu.VMEM(tokens, BF16), dma(())],
+        in_hbm=1,
+        to_hbm=(0,),
+    )
+    keep, got_w = halved(keep, got_w, 2, lambda i: i ^ 2, projected)
     part_b = call(
-        functools.partial(near_back_more_kernel, NEAR_PARTS[1]),
+        functools.partial(near_back_kernel, NEAR_PARTS[1]),
         "near_back_b",
         part_outs(1),
         [*args, part_a[0], keep],
@@ -793,7 +785,7 @@
     )
     keep, got_w = halved(keep, got_w, 16, lambda i: i ^ 24, part_b[0])
     part_c = call(
-        functools.partial(near_back_more_kernel, NEAR_PARTS[2]),
+        functools.partial(near_back_kernel, NEAR_PARTS[2]),
         "near_back_c",
         part_outs(2),
         [*args, part_b[0], keep],
@@ -806,14 +798,10 @@
     d_q, own_k, own_v, to_low, to_high = call(
         near_back_last_kernel,
         "near_back_d",
-        [(tokens, BF16), ((ROWS, LANES), F32), ((ROWS, LANES), F32)]
-        + [((192, 2 * WIDTH), BF16)] * 2,
-        [*args, *(x for part in (part_a, part_b, part_c) for x in (part[0], *part[3:]))]
-        + [keep, give],
-        [pltpu.VMEM(tokens, BF16), dma((2,))],
+        part_outs(3)[:3] + [((192, 2 * WIDTH), BF16)] * 2,
+        [*args, *part_a[3:], *part_b[3:], *part_c[3:], keep, give],
         in_hbm=2,
         microseconds=3,
-        to_hbm=(0,),
     )
     to_low, to_high, got_w = lax.optimization_barrier((to_low, to_high, got_w))
     low_back = moved(to_low, lambda i: i - 1)
@@ -827,14 +815,15 @@
     sum_third, copies = lax.optimization_barrier((sum_third, copies))
     copies = lax.all_to_all(copies, "dp", 0, 0, tiled=True)
     back_third = moved(sum_third, third)
-    d_k, d_v, finished = call(
+    d_k, d_v, d_q, finished = call(
         combine_kernel,
         "combine",
-        [(tokens, BF16)] * 2 + [((8, LANES), F32)],
+        [(tokens, BF16)] * 3 + [((8, LANES), F32)],
         [part_a[1], part_b[1], part_c[1], own_k, part_a[2], part_b[2], part_c[2], own_v]
-        + [low_back, high_back, back3, back4, back_third, swapped],
-        [pltpu.VMEM(tokens, BF16)] * 2 + [dma((2,))],
-        to_hbm=(0, 1),
+        + [low_back, high_back, back3, back4, back_third, swapped]
+        + [part_a[0], part_b[0], part_c[0], d_q],
+        [pltpu.VMEM(tokens, BF16)] * 3 + [dma((3,))],
+        to_hbm=(0, 1, 2),
     )
     d_w = call(last_sum_kernel, "last_sum", [((16, WIDTH), BF16)], [copies, finished], in_hbm=1)[0]
     return layer_out[None], d_q[None], d_k[None], d_v[None], d_w

time: 72.6 us -> 72.4 us (level)
    pallas_call x20 -> x21, Pallas kernels: 19.1 us -> 19 us  [call(): pl.pallas_call(kernel, name=name, out_shape=[jax.ShapeDtypeStruct(shape,...]
where the time goes in v8:
time: 72.4 us; the launch traced here: 71.6 us
  starting transfers between devices  26.4 us (36%)
  waiting for transfers between devices  24.6 us (34%)
  Pallas kernels  19 us (26%)
  between operations  0.89 us (1%)
  local copies, waits for them, and re-layouts  0.75 us (1%)
    ppermute x18, waiting for transfers between devices, moved(): return lax.ppermute(x, 'ctx', [(i, route(i) % count) for i in range(count)])  23.2 us
    pallas_call x21, Pallas kernels, call(): pl.pallas_call(kernel, name=name, out_shape=[jax.ShapeDtypeStruct(shape,...  19 us
    ppermute x18, starting transfers between devices, moved(): return lax.ppermute(x, 'ctx', [(i, route(i) % count) for i in range(count)])  17.8 us
    all_to_all x1, starting transfers between devices, body(): copies = lax.all_to_all(copies, 'dp', 0, 0, tiled=True)  8.57 us
  transfers between devices with their start and end apart: 19, of which 9 were waited for; matrix products, arithmetic and copies ran while one was open for 0% of the time, Pallas kernels for 16%

profile of v8, /device:TPU:32, one launch (start us, length us, event | category | flops | bytes accessed | tf_op | source)
XLA Modules:
  0.0 71.6 jit_solution(14658806949081177155)
XLA Ops:
  0.7 0.7 %copy-done.5 = s32[1,256]{1,0:T(1,128)S(1)} copy-done((s32[1,256]{1,0:T(1,128)S(1)}, s32[1,256]{1,0:T(1,128)}, u32[]{:S(2)}) %copy-start.5) | copy-done | bytes 1048
  1.7 0.6 coarsen.1
  2.4 5.1 %collective-permute-start.1 = (bf16[192,1152]{1,0:T(8,128)(2,1)S(1)}, bf16[192,1152]{1,0:T(8,128)(2,1)S(1)}, u32[]{:S(2)}, u32[]{:S(2)}) collective-permute-start(bf16[192,1152]{1,0:T(8,128)(2,1)S(1)} %get-tuple-element.84), channel_id=1, source_target_pairs={{0,31},{1,0},{2,1},{3,2},{4,3},{5,4},{6,5},{7,6},{8,7},{9,8},{10,9... | collective-permute-start | bytes 1327112 | tf_op jit(solution)/shard_map/ppermute | solution.py:631
  7.5 1.3 %collective-permute-done.2.far_partner = bf16[48,1152]{1,0:T(8,128)(2,1)S(1)} collective-permute-done((bf16[48,1152]{1,0:T(8,128)(2,1)S(1)}, bf16[48,1152]{1,0:T(8,128)(2,1)S(1)}, u32[]{:S(2)}, u32[]{:S(2)}) %collective-permute-start.2) | collective-permute-done | bytes 110624 | tf_op jit(solution)/shard_map/ppermute | solution.py:631
  8.9 2.9 %collective-permute-start.5 = (bf16[16,1152]{1,0:T(8,128)(2,1)S(1)}, bf16[16,1152]{1,0:T(8,128)(2,1)S(1)}, u32[]{:S(2)}, u32[]{:S(2)}) collective-permute-start(bf16[16,1152]{1,0:T(8,128)(2,1)S(1)} %get-tuple-element.97), channel_id=1, source_target_pairs={{0,6},{1,7},{2,28},{3,29},{4,10},{5,11},{6,0},{7,1},{8,14},{9,15},... | collective-permute-start | bytes 110600 | tf_op jit(solution)/shard_map/ppermute | solution.py:631
  11.9 0.7 %prepare.1 = (bf16[496,512]{1,0:T(8,128)(2,1)S(1)}, f32[256,512]{1,0:T(8,128)S(1)}, bf16[512,512]{1,0:T(8,128)(2,1)S(1)}, bf16[256,512]{1,0:T(8,128)(2,1)S(1)}) custom-call(bf16[256,512]{1,0:T(8,128)(2,1)S(1)} %bitcast.10, bf16[256,512]{1,0:T(8,128)(2,1)S(1)} %bitcast.11, bf16[512,512]{1,0:T(8,128)(2,1)S(1)} %copy-done), custom_call_target="tpu_custom_call" | custom-call | flops 1000000000 | bytes 1048576 | tf_op jit(solution)/shard_map/prepare/pallas_call | solution.py:615
  12.6 4.8 %collective-permute-done.3.got3 = bf16[64,1152]{1,0:T(8,128)(2,1)S(1)} collective-permute-done((bf16[64,1152]{1,0:T(8,128)(2,1)S(1)}, bf16[64,1152]{1,0:T(8,128)(2,1)S(1)}, u32[]{:S(2)}, u32[]{:S(2)}) %collective-permute-start.3) | collective-permute-done | bytes 147488 | tf_op jit(solution)/shard_map/ppermute | solution.py:631
  17.4 2.5 %collective-permute-done.4.got4.refs_1_ = bf16[32,1152]{1,0:T(8,128)(2,1)S(1)} collective-permute-done((bf16[32,1152]{1,0:T(8,128)(2,1)S(1)}, bf16[32,1152]{1,0:T(8,128)(2,1)S(1)}, u32[]{:S(2)}, u32[]{:S(2)}) %collective-permute-start.4) | collective-permute-done | bytes 73760 | tf_op jit(solution)/shard_map/ppermute | solution.py:631
  20.0 1.7 %near.1 = (bf16[4,896,256]{2,1,0:T(8,128)(2,1)S(1)}, f32[256,512]{1,0:T(8,128)S(1)}, f32[256,256]{1,0:T(8,128)S(1)}, bf16[192,512]{1,0:T(8,128)(2,1)S(1)}, bf16[192,256]{1,0:T(8,128)(2,1)S(1)}) custom-call(bf16[496,512]{1,0:T(8,128)(2,1)S(1)} %get-tuple-element.80.q_all.refs_1_, bf16[496,128]{1,0:T(8,128)(2,1)S(1)} %documents.1.qdoc, ...), custom_call_target="tpu_custom_call" | custom-call | flops 49999998976 | bytes 1048576 | tf_op jit(solution)/shard_map/near/pallas_call | solution.py:615
  21.7 4.8 %merge.1 = (bf16[256,512]{1,0:T(8,128)(2,1)S(1)}, f32[256,512]{1,0:T(8,128)S(1)}, bf16[256,512]{1,0:T(8,128)(2,1)S(1)}, bf16[4,96,128]{2,1,0:T(8,128)(2,1)S(1)},...) custom-call(bf16[496,512]{1,0:T(8,128)(2,1)S(1)} %get-tuple-element.80.q_all.refs_1_, ...), custom_call_target="tpu_custom_call" | custom-call | flops 6000000000 | bytes 1048576 | tf_op jit(solution)/shard_map/merge/pallas_call | solution.py:615
  26.5 1.1 %far_back.1 = (bf16[48,512]{1,0:T(8,128)(2,1)S(1)}, bf16[32,1024]{1,0:T(8,128)(2,1)S(1)}, bf16[32,1024]{1,0:T(8,128)(2,1)S(1)}, bf16[16,1024]{1,0:T(8,128)(2,1)S(1)}, bf16[480,512]{1,0:T(8,128)(2,1)S(1)}) custom-call(bf16[4,96,128]{2,1,0:T(8,128)(2,1)S(1)} %get-tuple-element.102.p_in, bf16[496,512]{1,0:T(8,128)(2,1)S(1)} %get-tuple-element.80.q_all.refs_1_, ...), custom_call_target="tpu_custom_call" | custom-call | flops 1000000000 | bytes 1048576 | tf_op jit(solution)/shard_map/far_back/pallas_call | solution.py:615
  27.6 0.8 %collective-permute-start.7 = (bf16[480,512]{1,0:T(8,128)(2,1)S(1)}, bf16[480,512]{1,0:T(8,128)(2,1)S(1)}, u32[]{:S(2)}, u32[]{:S(2)}) collective-permute-start(bf16[480,512]{1,0:T(8,128)(2,1)S(1)} %get-tuple-element.110), channel_id=1, source_target_pairs={{0,1},{1,0},{2,3},{3,2},{4,5},{5,4},{6,7},{7,6},{8,9},{9,8},{10,11... | collective-permute-start | bytes 1474568 | tf_op jit(solution)/shard_map/ppermute | solution.py:631
  28.4 1.4 %near_back_a.1 = (bf16[256,128]{1,0:T(8,128)(2,1)S(1)}, bf16[256,128]{1,0:T(8,128)(2,1)S(1)}, bf16[256,128]{1,0:T(8,128)(2,1)S(1)}, bf16[2,192,128]{2,1,0:T(8,128)(2,1)S(1)}, bf16[2,192,128]{2,1,0:T(8,128)(2,1)S(1)}) custom-call(bf16[4,896,256]{2,1,0:T(8,128)(2,1)S(1)} %get-tuple-element.111.refs_0_, bf16[496,512]{1,0:T(8,128)(2,1)S(1)} %get-tuple-element.80.q_all.refs_1_, ...), custom_call_target="tpu_custom_call" | custom-call | flops 3000000000 | bytes 1048576 | tf_op jit(solution)/shard_map/near_back_a/pallas_call | solution.py:615
  30.1 0.9 %collective-permute-start.8 = (bf16[128,512]{1,0:T(8,128)(2,1)S(1)}, bf16[128,512]{1,0:T(8,128)(2,1)S(1)}, u32[]{:S(2)}, u32[]{:S(2)}) collective-permute-start(bf16[128,512]{1,0:T(8,128)(2,1)S(1)} %get-tuple-element.118), channel_id=1, source_target_pairs={{0,6},{1,7},{2,4},{3,5},{4,2},{5,3},{6,0},{7,1},{8,14},{9,15},{10,... | collective-permute-start | bytes 393224 | tf_op jit(solution)/shard_map/ppermute | solution.py:631
  31.0 0.9 %collective-permute-start.12 = (bf16[32,1024]{1,0:T(8,128)(2,1)S(1)}, bf16[32,1024]{1,0:T(8,128)(2,1)S(1)}, u32[]{:S(2)}, u32[]{:S(2)}) collective-permute-start(bf16[32,1024]{1,0:T(8,128)(2,1)S(1)} %get-tuple-element.135), channel_id=1, source_target_pairs={{0,28},{1,5},{2,30},{3,7},{4,0},{5,9},{6,2},{7,11},{8,4},{9,13},{1... | collective-permute-start | bytes 196616 | tf_op jit(solution)/shard_map/ppermute | solution.py:631
  31.9 2.7 %collective-permute-start.11 = (bf16[64,1024]{1,0:T(8,128)(2,1)S(1)}, bf16[64,1024]{1,0:T(8,128)(2,1)S(1)}, u32[]{:S(2)}, u32[]{:S(2)}) collective-permute-start(bf16[64,1024]{1,0:T(8,128)(2,1)S(1)} %get-tuple-element.114._), channel_id=1, source_target_pairs={{0,30},{1,3},{2,0},{3,5},{4,2},{5,7},{6,4},{7,9},{8,6},{9,11},{10,... | collective-permute-start | bytes 393224 | tf_op jit(solution)/shard_map/ppermute | solution.py:631
  34.6 1.0 %project.1 = (bf16[256,512]{1,0:T(8,128)(2,1)}, f32[8,128]{1,0:T(8,128)S(1)}) custom-call(bf16[256,512]{1,0:T(8,128)(2,1)S(1)} %get-tuple-element.100.attended, bf16[512,512]{1,0:T(8,128)(2,1)S(1)} %get-tuple-element.101.w, bf16[64,1024]{1,0:T(8,128)(2,1)S(1)} %get-tuple-element.114._), custom_call_target="tpu_custom_call" | custom-call | flops 1000000000 | bytes 1048576 | tf_op jit(solution)/shard_map/project/pallas_call | solution.py:615
  35.6 4.3 %collective-permute-done.8.got = bf16[128,512]{1,0:T(8,128)(2,1)S(1)} collective-permute-done((bf16[128,512]{1,0:T(8,128)(2,1)S(1)}, bf16[128,512]{1,0:T(8,128)(2,1)S(1)}, u32[]{:S(2)}, u32[]{:S(2)}) %collective-permute-start.8) | collective-permute-done | bytes 131104 | tf_op jit(solution)/shard_map/ppermute | solution.py:631
  40.1 1.4 %near_back_b.1 = (bf16[256,128]{1,0:T(8,128)(2,1)S(1)}, bf16[256,128]{1,0:T(8,128)(2,1)S(1)}, bf16[256,128]{1,0:T(8,128)(2,1)S(1)}, bf16[2,192,128]{2,1,0:T(8,128)(2,1)S(1)}, bf16[2,192,128]{2,1,0:T(8,128)(2,1)S(1)}) custom-call(bf16[4,896,256]{2,1,0:T(8,128)(2,1)S(1)} %get-tuple-element.111.refs_0_, bf16[496,512]{1,0:T(8,128)(2,1)S(1)} %get-tuple-element.80.q_all.refs_1_, ...), custom_call_target="tpu_custom_call" | custom-call | flops 3000000000 | bytes 1048576 | tf_op jit(solution)/shard_map/near_back_b/pallas_call | solution.py:615
  41.6 2.8 %collective-permute-done.9.got = bf16[64,512]{1,0:T(8,128)(2,1)S(1)} collective-permute-done((bf16[64,512]{1,0:T(8,128)(2,1)S(1)}, bf16[64,512]{1,0:T(8,128)(2,1)S(1)}, u32[]{:S(2)}, u32[]{:S(2)}) %collective-permute-start.9) | collective-permute-done | bytes 65568 | tf_op jit(solution)/shard_map/ppermute | solution.py:631
  44.4 1.8 %collective-permute-start.10 = (bf16[32,512]{1,0:T(8,128)(2,1)S(1)}, bf16[32,512]{1,0:T(8,128)(2,1)S(1)}, u32[]{:S(2)}, u32[]{:S(2)}) collective-permute-start(bf16[32,512]{1,0:T(8,128)(2,1)S(1)} %get-tuple-element.132), channel_id=1, source_target_pairs={{0,24},{1,25},{2,26},{3,27},{4,28},{5,29},{6,30},{7,31},{8,16},{9,... | collective-permute-start | bytes 98312 | tf_op jit(solution)/shard_map/ppermute | solution.py:631
  46.2 1.4 %near_back_c.1 = (bf16[256,128]{1,0:T(8,128)(2,1)S(1)}, bf16[256,128]{1,0:T(8,128)(2,1)S(1)}, bf16[256,128]{1,0:T(8,128)(2,1)S(1)}, bf16[2,192,128]{2,1,0:T(8,128)(2,1)S(1)}, bf16[2,192,128]{2,1,0:T(8,128)(2,1)S(1)}) custom-call(bf16[4,896,256]{2,1,0:T(8,128)(2,1)S(1)} %get-tuple-element.111.refs_0_, bf16[496,512]{1,0:T(8,128)(2,1)S(1)} %get-tuple-element.80.q_all.refs_1_, ...), custom_call_target="tpu_custom_call" | custom-call | flops 3000000000 | bytes 1048576 | tf_op jit(solution)/shard_map/near_back_c/pallas_call | solution.py:615
  47.6 1.9 %collective-permute-done.10.got = bf16[32,512]{1,0:T(8,128)(2,1)S(1)} collective-permute-done((bf16[32,512]{1,0:T(8,128)(2,1)S(1)}, bf16[32,512]{1,0:T(8,128)(2,1)S(1)}, u32[]{:S(2)}, u32[]{:S(2)}) %collective-permute-start.10) | collective-permute-done | bytes 32800 | tf_op jit(solution)/shard_map/ppermute | solution.py:631
  49.7 1.5 %near_back_d.1 = (bf16[256,128]{1,0:T(8,128)(2,1)S(1)}, bf16[256,128]{1,0:T(8,128)(2,1)S(1)}, bf16[256,128]{1,0:T(8,128)(2,1)S(1)}, bf16[192,1024]{1,0:T(8,128)(2,1)S(1)}, bf16[192,1024]{1,0:T(8,128)(2,1)S(1)}) custom-call(bf16[4,896,256]{2,1,0:T(8,128)(2,1)S(1)} %get-tuple-element.111.refs_0_, bf16[496,512]{1,0:T(8,128)(2,1)S(1)} %get-tuple-element.80.q_all.refs_1_, ...), custom_call_target="tpu_custom_call" | custom-call | flops 3000000000 | bytes 1048576 | tf_op jit(solution)/shard_map/near_back_d/pallas_call | solution.py:615
  51.2 2.2 %collective-permute-done.13.got = bf16[16,512]{1,0:T(8,128)(2,1)S(1)} collective-permute-done((bf16[16,512]{1,0:T(8,128)(2,1)S(1)}, bf16[16,512]{1,0:T(8,128)(2,1)S(1)}, u32[]{:S(2)}, u32[]{:S(2)}) %collective-permute-start.13) | collective-permute-done | bytes 16416 | tf_op jit(solution)/shard_map/ppermute | solution.py:631
  54.0 0.7 copies.1
  54.6 8.6 %all-to-all-start = ((bf16[8,16,512]{2,1,0:T(8,128)(2,1)}), bf16[8,16,512]{2,1,0:T(8,128)(2,1)S(1)}, u32[]{:S(2)}, u32[]{:S(2)}) async-start(bf16[8,16,512]{2,1,0:T(8,128)(2,1)} %copies.1), calls=%async_computation | async-start | bytes 262144 | tf_op jit(solution)/shard_map/all_to_all | solution.py:816
  63.2 1.7 %collective-permute-start.16 = (bf16[16,1024]{1,0:T(8,128)(2,1)S(1)}, bf16[16,1024]{1,0:T(8,128)(2,1)S(1)}, u32[]{:S(2)}, u32[]{:S(2)}) collective-permute-start(bf16[16,1024]{1,0:T(8,128)(2,1)S(1)} %get-tuple-element.148), channel_id=1, source_target_pairs={{0,6},{1,7},{2,28},{3,29},{4,10},{5,11},{6,0},{7,1},{8,14},{9,15},... | collective-permute-start | bytes 98312 | tf_op jit(solution)/shard_map/ppermute | solution.py:631
  64.9 3.4 %collective-permute-done.16.refs_12_ = bf16[16,1024]{1,0:T(8,128)(2,1)S(1)} collective-permute-done((bf16[16,1024]{1,0:T(8,128)(2,1)S(1)}, bf16[16,1024]{1,0:T(8,128)(2,1)S(1)}, u32[]{:S(2)}, u32[]{:S(2)}) %collective-permute-start.16) | collective-permute-done | bytes 32800 | tf_op jit(solution)/shard_map/ppermute | solution.py:631
  68.3 1.3 %combine.1 = (bf16[256,512]{1,0:T(8,128)(2,1)}, bf16[256,512]{1,0:T(8,128)(2,1)}, bf16[256,512]{1,0:T(8,128)(2,1)}, f32[8,128]{1,0:T(8,128)S(1)}) custom-call(bf16[256,128]{1,0:T(8,128)(2,1)S(1)} %get-tuple-element.116.refs_0_, bf16[256,128]{1,0:T(8,128)(2,1)S(1)} %get-tuple-element.121.refs_1_, bf16[256,128]{1,0:T(8,128)(2,1)S(1)} %get-tuple-element.125.refs_2_, ...), custom_call_target="tpu_custom_call" | custom-call | flops 1000000000 | bytes 1048576 | tf_op jit(solution)/shard_map/combine/pallas_call | solution.py:615
  69.6 1.4 %all-to-all-done.parts = bf16[8,16,512]{2,1,0:T(8,128)(2,1)S(1)} async-done(((bf16[8,16,512]{2,1,0:T(8,128)(2,1)}), bf16[8,16,512]{2,1,0:T(8,128)(2,1)S(1)}, u32[]{:S(2)}, u32[]{:S(2)}) %all-to-all-start) | async-done | bytes 131104 | tf_op jit(solution)/shard_map/all_to_all | solution.py:816
  71.0 0.6 last_sum.1
  (39 shorter events, 1.7 us)
Async XLA Ops:
  0.6 1.1 %copy-start.2 = (bf16[1,256,512]{2,1,0:T(8,128)(2,1)S(1)}, bf16[1,256,512]{2,1,0:T(8,128)(2,1)}, u32[]{:S(2)}) copy-start(bf16[1,256,512]{2,1,0:T(8,128)(2,1)} %param.8) | copy-start | bytes 786436
  0.6 1.1 %copy-start.1 = (bf16[1,256,512]{2,1,0:T(8,128)(2,1)S(1)}, bf16[1,256,512]{2,1,0:T(8,128)(2,1)}, u32[]{:S(2)}) copy-start(bf16[1,256,512]{2,1,0:T(8,128)(2,1)} %param.7) | copy-start | bytes 786436
  0.7 0.7 %copy-start.5 = (s32[1,256]{1,0:T(1,128)S(1)}, s32[1,256]{1,0:T(1,128)}, u32[]{:S(2)}) copy-start(s32[1,256]{1,0:T(1,128)} %seg_hbm.1) | copy-start | bytes 3076
  2.3 15.0 %collective-permute-start = (bf16[192,1152]{1,0:T(8,128)(2,1)S(1)}, bf16[192,1152]{1,0:T(8,128)(2,1)S(1)}, u32[]{:S(2)}, u32[]{:S(2)}) collective-permute-start(bf16[192,1152]{1,0:T(8,128)(2,1)S(1)} %get-tuple-element.83), channel_id=1, source_target_pairs={{0,1},{1,2},{2,3},{3,4},{4,5},{5,6},{6,7},{7,8},{8,9},{9,10},{10,1... | collective-permute-start | bytes 1327112 | tf_op jit(solution)/shard_map/ppermute | solution.py:631
  2.4 15.0 %collective-permute-start.1 = (bf16[192,1152]{1,0:T(8,128)(2,1)S(1)}, bf16[192,1152]{1,0:T(8,128)(2,1)S(1)}, u32[]{:S(2)}, u32[]{:S(2)}) collective-permute-start(bf16[192,1152]{1,0:T(8,128)(2,1)S(1)} %get-tuple-element.84), channel_id=1, source_target_pairs={{0,31},{1,0},{2,1},{3,2},{4,3},{5,4},{6,5},{7,6},{8,7},{9,8},{10,9... | collective-permute-start | bytes 1327112 | tf_op jit(solution)/shard_map/ppermute | solution.py:631
  7.5 4.4 %copy-start = (bf16[512,512]{1,0:T(8,128)(2,1)S(1)}, bf16[512,512]{1,0:T(8,128)(2,1)}, u32[]{:S(2)}) copy-start(bf16[512,512]{1,0:T(8,128)(2,1)} %w_hbm.1) | copy-start | bytes 1572868
  7.5 4.4 %copy-start.3 = (bf16[1,256,512]{2,1,0:T(8,128)(2,1)S(1)}, bf16[1,256,512]{2,1,0:T(8,128)(2,1)}, u32[]{:S(2)}) copy-start(bf16[1,256,512]{2,1,0:T(8,128)(2,1)} %param.6) | copy-start | bytes 786436
  7.5 4.4 %copy-start.4 = (bf16[1,256,512]{2,1,0:T(8,128)(2,1)S(1)}, bf16[1,256,512]{2,1,0:T(8,128)(2,1)}, u32[]{:S(2)}) copy-start(bf16[1,256,512]{2,1,0:T(8,128)(2,1)} %param.11) | copy-start | bytes 786436
  7.5 1.3 %collective-permute-start.2 = (bf16[48,1152]{1,0:T(8,128)(2,1)S(1)}, bf16[48,1152]{1,0:T(8,128)(2,1)S(1)}, u32[]{:S(2)}, u32[]{:S(2)}) collective-permute-start(bf16[48,1152]{1,0:T(8,128)(2,1)S(1)} %get-tuple-element.85.far), channel_id=1, source_target_pairs={{0,1},{1,0},{2,3},{3,2},{4,5},{5,4},{6,7},{7,6},{8,9},{9,8},{10,11... | collective-permute-start | bytes 331784 | tf_op jit(solution)/shard_map/ppermute | solution.py:631
  8.8 8.5 %collective-permute-start.3 = (bf16[64,1152]{1,0:T(8,128)(2,1)S(1)}, bf16[64,1152]{1,0:T(8,128)(2,1)S(1)}, u32[]{:S(2)}, u32[]{:S(2)}) collective-permute-start(bf16[64,1152]{1,0:T(8,128)(2,1)S(1)} %get-tuple-element.86), channel_id=1, source_target_pairs={{0,2},{1,31},{2,4},{3,1},{4,6},{5,3},{6,8},{7,5},{8,10},{9,7},{10,... | collective-permute-start | bytes 442376 | tf_op jit(solution)/shard_map/ppermute | solution.py:631
  8.9 8.5 %collective-permute-start.5 = (bf16[16,1152]{1,0:T(8,128)(2,1)S(1)}, bf16[16,1152]{1,0:T(8,128)(2,1)S(1)}, u32[]{:S(2)}, u32[]{:S(2)}) collective-permute-start(bf16[16,1152]{1,0:T(8,128)(2,1)S(1)} %get-tuple-element.97), channel_id=1, source_target_pairs={{0,6},{1,7},{2,28},{3,29},{4,10},{5,11},{6,0},{7,1},{8,14},{9,15},... | collective-permute-start | bytes 110600 | tf_op jit(solution)/shard_map/ppermute | solution.py:631
  11.9 8.0 %collective-permute-start.4 = (bf16[32,1152]{1,0:T(8,128)(2,1)S(1)}, bf16[32,1152]{1,0:T(8,128)(2,1)S(1)}, u32[]{:S(2)}, u32[]{:S(2)}) collective-permute-start(bf16[32,1152]{1,0:T(8,128)(2,1)S(1)} %get-tuple-element.96), channel_id=1, source_target_pairs={{0,4},{1,29},{2,6},{3,31},{4,8},{5,1},{6,10},{7,3},{8,12},{9,5},{1... | collective-permute-start | bytes 221192 | tf_op jit(solution)/shard_map/ppermute | solution.py:631
  19.9 1.8 %collective-permute-start.6 = (bf16[112,1152]{1,0:T(8,128)(2,1)S(1)}, bf16[112,1152]{1,0:T(8,128)(2,1)S(1)}, u32[]{:S(2)}, u32[]{:S(2)}) collective-permute-start(bf16[112,1152]{1,0:T(8,128)(2,1)S(1)} %get-tuple-element.99), channel_id=1, source_target_pairs={{0,1},{1,0},{2,3},{3,2},{4,5},{5,4},{6,7},{7,6},{8,9},{9,8},{10,11... | collective-permute-start | bytes 774152 | tf_op jit(solution)/shard_map/ppermute | solution.py:631
  27.6 2.3 %collective-permute-start.7 = (bf16[480,512]{1,0:T(8,128)(2,1)S(1)}, bf16[480,512]{1,0:T(8,128)(2,1)S(1)}, u32[]{:S(2)}, u32[]{:S(2)}) collective-permute-start(bf16[480,512]{1,0:T(8,128)(2,1)S(1)} %get-tuple-element.110), channel_id=1, source_target_pairs={{0,1},{1,0},{2,3},{3,2},{4,5},{5,4},{6,7},{7,6},{8,9},{9,8},{10,11... | collective-permute-start | bytes 1474568 | tf_op jit(solution)/shard_map/ppermute | solution.py:631
  30.1 9.9 %collective-permute-start.8 = (bf16[128,512]{1,0:T(8,128)(2,1)S(1)}, bf16[128,512]{1,0:T(8,128)(2,1)S(1)}, u32[]{:S(2)}, u32[]{:S(2)}) collective-permute-start(bf16[128,512]{1,0:T(8,128)(2,1)S(1)} %get-tuple-element.118), channel_id=1, source_target_pairs={{0,6},{1,7},{2,4},{3,5},{4,2},{5,3},{6,0},{7,1},{8,14},{9,15},{10,... | collective-permute-start | bytes 393224 | tf_op jit(solution)/shard_map/ppermute | solution.py:631
  31.0 10.6 %collective-permute-start.12 = (bf16[32,1024]{1,0:T(8,128)(2,1)S(1)}, bf16[32,1024]{1,0:T(8,128)(2,1)S(1)}, u32[]{:S(2)}, u32[]{:S(2)}) collective-permute-start(bf16[32,1024]{1,0:T(8,128)(2,1)S(1)} %get-tuple-element.135), channel_id=1, source_target_pairs={{0,28},{1,5},{2,30},{3,7},{4,0},{5,9},{6,2},{7,11},{8,4},{9,13},{1... | collective-permute-start | bytes 196616 | tf_op jit(solution)/shard_map/ppermute | solution.py:631
  31.9 9.7 %collective-permute-start.11 = (bf16[64,1024]{1,0:T(8,128)(2,1)S(1)}, bf16[64,1024]{1,0:T(8,128)(2,1)S(1)}, u32[]{:S(2)}, u32[]{:S(2)}) collective-permute-start(bf16[64,1024]{1,0:T(8,128)(2,1)S(1)} %get-tuple-element.114._), channel_id=1, source_target_pairs={{0,30},{1,3},{2,0},{3,5},{4,2},{5,7},{6,4},{7,9},{8,6},{9,11},{10,... | collective-permute-start | bytes 393224 | tf_op jit(solution)/shard_map/ppermute | solution.py:631
  40.0 4.4 %collective-permute-start.9 = (bf16[64,512]{1,0:T(8,128)(2,1)S(1)}, bf16[64,512]{1,0:T(8,128)(2,1)S(1)}, u32[]{:S(2)}, u32[]{:S(2)}) collective-permute-start(bf16[64,512]{1,0:T(8,128)(2,1)S(1)} %get-tuple-element.123), channel_id=1, source_target_pairs={{0,2},{1,3},{2,0},{3,1},{4,6},{5,7},{6,4},{7,5},{8,10},{9,11},{10,... | collective-permute-start | bytes 196616 | tf_op jit(solution)/shard_map/ppermute | solution.py:631
  44.4 5.2 %collective-permute-start.10 = (bf16[32,512]{1,0:T(8,128)(2,1)S(1)}, bf16[32,512]{1,0:T(8,128)(2,1)S(1)}, u32[]{:S(2)}, u32[]{:S(2)}) collective-permute-start(bf16[32,512]{1,0:T(8,128)(2,1)S(1)} %get-tuple-element.132), channel_id=1, source_target_pairs={{0,24},{1,25},{2,26},{3,27},{4,28},{5,29},{6,30},{7,31},{8,16},{9,... | collective-permute-start | bytes 98312 | tf_op jit(solution)/shard_map/ppermute | solution.py:631
  49.6 3.8 %collective-permute-start.13 = (bf16[16,512]{1,0:T(8,128)(2,1)S(1)}, bf16[16,512]{1,0:T(8,128)(2,1)S(1)}, u32[]{:S(2)}, u32[]{:S(2)}) collective-permute-start(bf16[16,512]{1,0:T(8,128)(2,1)S(1)} %get-tuple-element.143), channel_id=1, source_target_pairs={{0,8},{1,9},{2,10},{3,11},{4,12},{5,13},{6,14},{7,15},{8,0},{9,1},... | collective-permute-start | bytes 49160 | tf_op jit(solution)/shard_map/ppermute | solution.py:631
  53.4 14.9 %collective-permute-start.14 = (bf16[192,1024]{1,0:T(8,128)(2,1)S(1)}, bf16[192,1024]{1,0:T(8,128)(2,1)S(1)}, u32[]{:S(2)}, u32[]{:S(2)}) collective-permute-start(bf16[192,1024]{1,0:T(8,128)(2,1)S(1)} %get-tuple-element.144), channel_id=1, source_target_pairs={{0,31},{1,0},{2,1},{3,2},{4,3},{5,4},{6,5},{7,6},{8,7},{9,8},{10,9... | collective-permute-start | bytes 1179656 | tf_op jit(solution)/shard_map/ppermute | solution.py:631
  53.4 14.9 %collective-permute-start.15 = (bf16[192,1024]{1,0:T(8,128)(2,1)S(1)}, bf16[192,1024]{1,0:T(8,128)(2,1)S(1)}, u32[]{:S(2)}, u32[]{:S(2)}) collective-permute-start(bf16[192,1024]{1,0:T(8,128)(2,1)S(1)} %get-tuple-element.145), channel_id=1, source_target_pairs={{0,1},{1,2},{2,3},{3,4},{4,5},{5,6},{6,7},{7,8},{8,9},{9,10},{10,1... | collective-permute-start | bytes 1179656 | tf_op jit(solution)/shard_map/ppermute | solution.py:631
  54.6 16.4 %all-to-all-start = ((bf16[8,16,512]{2,1,0:T(8,128)(2,1)}), bf16[8,16,512]{2,1,0:T(8,128)(2,1)S(1)}, u32[]{:S(2)}, u32[]{:S(2)}) async-start(bf16[8,16,512]{2,1,0:T(8,128)(2,1)} %copies.1), calls=%async_computation | async-start | bytes 262144 | tf_op jit(solution)/shard_map/all_to_all | solution.py:816
  63.2 1.7 %collective-permute-start.17 = (bf16[48,1024]{1,0:T(8,128)(2,1)S(1)}, bf16[48,1024]{1,0:T(8,128)(2,1)S(1)}, u32[]{:S(2)}, u32[]{:S(2)}) collective-permute-start(bf16[48,1024]{1,0:T(8,128)(2,1)S(1)} %far_split.1.refs_16_), channel_id=1, source_target_pairs={{0,1},{1,0},{2,3},{3,2},{4,5},{5,4},{6,7},{7,6},{8,9},{9,8},{10,11... | collective-permute-start | bytes 294920 | tf_op jit(solution)/shard_map/ppermute | solution.py:631
  63.2 5.1 %collective-permute-start.16 = (bf16[16,1024]{1,0:T(8,128)(2,1)S(1)}, bf16[16,1024]{1,0:T(8,128)(2,1)S(1)}, u32[]{:S(2)}, u32[]{:S(2)}) collective-permute-start(bf16[16,1024]{1,0:T(8,128)(2,1)S(1)} %get-tuple-element.148), channel_id=1, source_target_pairs={{0,6},{1,7},{2,28},{3,29},{4,10},{5,11},{6,0},{7,1},{8,14},{9,15},... | collective-permute-start | bytes 98312 | tf_op jit(solution)/shard_map/ppermute | solution.py:631

commit v9 on v8

--- a/solution.py
+++ b/solution.py
@@ -298,7 +298,7 @@
 
 def block_at(block):
     x, y, core = block // 8, block // 2 % 4, block % 2
-    return 16 * (16 * core + 4 * y + x)
+    return 16 * (16 * core + 4 * x + y)
 
 
 def merge_kernel(
@@ -518,7 +518,7 @@
         sum4[:, lanes] = (came(64, 96) + to_4[:, lanes].astype(F32)).astype(BF16)
         sum_third[:, lanes] = (came(96, 112) + to_third[:, lanes].astype(F32)).astype(BF16)
     total[...] = keep[...] + message[0:256].astype(F32)
-    halve(total, 4, keep_out, give_out)
+    halve(total, 16, keep_out, give_out)
 
 
 def halve(total, divisor, keep, give):
@@ -762,7 +762,7 @@
         [pltpu.VMEM((256, WIDTH), F32)],
         in_hbm=1,
     )
-    got_w = moved(give, lambda i: i ^ 6)
+    got_w = moved(give, lambda i: i ^ 24)
     back3 = moved(sum3, back_3)
     back4 = moved(sum4, back_4)
     layer_out, projected = call(
@@ -774,7 +774,7 @@
         in_hbm=1,
         to_hbm=(0,),
     )
-    keep, got_w = halved(keep, got_w, 2, lambda i: i ^ 2, projected)
+    keep, got_w = halved(keep, got_w, 8, lambda i: i ^ 8, projected)
     part_b = call(
         functools.partial(near_back_kernel, NEAR_PARTS[1]),
         "near_back_b",
@@ -783,7 +783,7 @@
         in_hbm=2,
         microseconds=3,
     )
-    keep, got_w = halved(keep, got_w, 16, lambda i: i ^ 24, part_b[0])
+    keep, got_w = halved(keep, got_w, 4, lambda i: i ^ 6, part_b[0])
     part_c = call(
         functools.partial(near_back_kernel, NEAR_PARTS[2]),
         "near_back_c",
@@ -792,7 +792,7 @@
         in_hbm=2,
         microseconds=3,
     )
-    keep, got_w = halved(keep, got_w, 8, lambda i: i ^ 8, part_c[0])
+    keep, got_w = halved(keep, got_w, 2, lambda i: i ^ 2, part_c[0])
     give = call(far_split_kernel, "far_split", [((48, 2 * WIDTH), BF16)], [back3, back4])[0]
     swapped = moved(give, partner)
     d_q, own_k, own_v, to_low, to_high = call(

time: 72.4 us -> 69.9 us (0.965)
  waiting for transfers between devices: 24.6 us -> 20.8 us
  starting transfers between devices: 26.4 us -> 27.3 us
    ppermute x18, waiting for transfers between devices: 23.2 us -> 19.5 us  [moved(): return lax.ppermute(x, 'ctx', [(i, route(i) % count) for i in range(count)])]
    ppermute x18, starting transfers between devices: 17.8 us -> 18.7 us  [moved(): return lax.ppermute(x, 'ctx', [(i, route(i) % count) for i in range(count)])]
where the time goes in v9:
time: 69.9 us; the launch traced here: 68.8 us
  starting transfers between devices  27.3 us (39%)
  waiting for transfers between devices  20.8 us (30%)
  Pallas kernels  19 us (27%)
  between operations  0.89 us (1%)
  local copies, waits for them, and re-layouts  0.75 us (1%)
    ppermute x18, waiting for transfers between devices, moved(): return lax.ppermute(x, 'ctx', [(i, route(i) % count) for i in range(count)])  19.5 us
    pallas_call x21, Pallas kernels, call(): pl.pallas_call(kernel, name=name, out_shape=[jax.ShapeDtypeStruct(shape,...  19 us
    ppermute x18, starting transfers between devices, moved(): return lax.ppermute(x, 'ctx', [(i, route(i) % count) for i in range(count)])  18.7 us
    all_to_all x1, starting transfers between devices, body(): copies = lax.all_to_all(copies, 'dp', 0, 0, tiled=True)  8.57 us
  transfers between devices with their start and end apart: 19, of which 9 were waited for; matrix products, arithmetic and copies ran while one was open for 0% of the time, Pallas kernels for 16%

profile of v9, /device:TPU:32, one launch (start us, length us, event | category | flops | bytes accessed | tf_op | source)
XLA Modules:
  0.0 68.8 jit_solution(6926436454274304971)
XLA Ops:
  0.7 0.7 %copy-done.5 = s32[1,256]{1,0:T(1,128)S(1)} copy-done((s32[1,256]{1,0:T(1,128)S(1)}, s32[1,256]{1,0:T(1,128)}, u32[]{:S(2)}) %copy-start.5) | copy-done | bytes 1048
  1.4 0.3 documents.1.qdoc
  1.7 0.6 coarsen.1
  2.4 5.1 %collective-permute-start.1 = (bf16[192,1152]{1,0:T(8,128)(2,1)S(1)}, bf16[192,1152]{1,0:T(8,128)(2,1)S(1)}, u32[]{:S(2)}, u32[]{:S(2)}) collective-permute-start(bf16[192,1152]{1,0:T(8,128)(2,1)S(1)} %get-tuple-element.84), channel_id=1, source_target_pairs={{0,31},{1,0},{2,1},{3,2},{4,3},{5,4},{6,5},{7,6},{8,7},{9,8},{10,9... | collective-permute-start | bytes 1327112 | tf_op jit(solution)/shard_map/ppermute | solution.py:631
  7.5 1.3 %collective-permute-done.2.far_partner = bf16[48,1152]{1,0:T(8,128)(2,1)S(1)} collective-permute-done((bf16[48,1152]{1,0:T(8,128)(2,1)S(1)}, bf16[48,1152]{1,0:T(8,128)(2,1)S(1)}, u32[]{:S(2)}, u32[]{:S(2)}) %collective-permute-start.2) | collective-permute-done | bytes 110624 | tf_op jit(solution)/shard_map/ppermute | solution.py:631
  8.9 2.9 %collective-permute-start.5 = (bf16[16,1152]{1,0:T(8,128)(2,1)S(1)}, bf16[16,1152]{1,0:T(8,128)(2,1)S(1)}, u32[]{:S(2)}, u32[]{:S(2)}) collective-permute-start(bf16[16,1152]{1,0:T(8,128)(2,1)S(1)} %get-tuple-element.97), channel_id=1, source_target_pairs={{0,6},{1,7},{2,28},{3,29},{4,10},{5,11},{6,0},{7,1},{8,14},{9,15},... | collective-permute-start | bytes 110600 | tf_op jit(solution)/shard_map/ppermute | solution.py:631
  11.9 0.7 %prepare.1 = (bf16[496,512]{1,0:T(8,128)(2,1)S(1)}, f32[256,512]{1,0:T(8,128)S(1)}, bf16[512,512]{1,0:T(8,128)(2,1)S(1)}, bf16[256,512]{1,0:T(8,128)(2,1)S(1)}) custom-call(bf16[256,512]{1,0:T(8,128)(2,1)S(1)} %bitcast.10, bf16[256,512]{1,0:T(8,128)(2,1)S(1)} %bitcast.11, bf16[512,512]{1,0:T(8,128)(2,1)S(1)} %copy-done), custom_call_target="tpu_custom_call" | custom-call | flops 1000000000 | bytes 1048576 | tf_op jit(solution)/shard_map/prepare/pallas_call | solution.py:615
  12.6 4.8 %collective-permute-done.3.got3 = bf16[64,1152]{1,0:T(8,128)(2,1)S(1)} collective-permute-done((bf16[64,1152]{1,0:T(8,128)(2,1)S(1)}, bf16[64,1152]{1,0:T(8,128)(2,1)S(1)}, u32[]{:S(2)}, u32[]{:S(2)}) %collective-permute-start.3) | collective-permute-done | bytes 147488 | tf_op jit(solution)/shard_map/ppermute | solution.py:631
  17.4 2.5 %collective-permute-done.4.got4.refs_1_ = bf16[32,1152]{1,0:T(8,128)(2,1)S(1)} collective-permute-done((bf16[32,1152]{1,0:T(8,128)(2,1)S(1)}, bf16[32,1152]{1,0:T(8,128)(2,1)S(1)}, u32[]{:S(2)}, u32[]{:S(2)}) %collective-permute-start.4) | collective-permute-done | bytes 73760 | tf_op jit(solution)/shard_map/ppermute | solution.py:631
  20.0 1.7 %near.1 = (bf16[4,896,256]{2,1,0:T(8,128)(2,1)S(1)}, f32[256,512]{1,0:T(8,128)S(1)}, f32[256,256]{1,0:T(8,128)S(1)}, bf16[192,512]{1,0:T(8,128)(2,1)S(1)}, bf16[192,256]{1,0:T(8,128)(2,1)S(1)}) custom-call(bf16[496,512]{1,0:T(8,128)(2,1)S(1)} %get-tuple-element.80.q_all.refs_1_, bf16[496,128]{1,0:T(8,128)(2,1)S(1)} %documents.1.qdoc, ...), custom_call_target="tpu_custom_call" | custom-call | flops 49999998976 | bytes 1048576 | tf_op jit(solution)/shard_map/near/pallas_call | solution.py:615
  21.7 4.8 %merge.1 = (bf16[256,512]{1,0:T(8,128)(2,1)S(1)}, f32[256,512]{1,0:T(8,128)S(1)}, bf16[256,512]{1,0:T(8,128)(2,1)S(1)}, bf16[4,96,128]{2,1,0:T(8,128)(2,1)S(1)},...) custom-call(bf16[496,512]{1,0:T(8,128)(2,1)S(1)} %get-tuple-element.80.q_all.refs_1_, ...), custom_call_target="tpu_custom_call" | custom-call | flops 6000000000 | bytes 1048576 | tf_op jit(solution)/shard_map/merge/pallas_call | solution.py:615
  26.5 1.1 %far_back.1 = (bf16[48,512]{1,0:T(8,128)(2,1)S(1)}, bf16[32,1024]{1,0:T(8,128)(2,1)S(1)}, bf16[32,1024]{1,0:T(8,128)(2,1)S(1)}, bf16[16,1024]{1,0:T(8,128)(2,1)S(1)}, bf16[480,512]{1,0:T(8,128)(2,1)S(1)}) custom-call(bf16[4,96,128]{2,1,0:T(8,128)(2,1)S(1)} %get-tuple-element.102.p_in, bf16[496,512]{1,0:T(8,128)(2,1)S(1)} %get-tuple-element.80.q_all.refs_1_, ...), custom_call_target="tpu_custom_call" | custom-call | flops 1000000000 | bytes 1048576 | tf_op jit(solution)/shard_map/far_back/pallas_call | solution.py:615
  27.6 0.8 %collective-permute-start.7 = (bf16[480,512]{1,0:T(8,128)(2,1)S(1)}, bf16[480,512]{1,0:T(8,128)(2,1)S(1)}, u32[]{:S(2)}, u32[]{:S(2)}) collective-permute-start(bf16[480,512]{1,0:T(8,128)(2,1)S(1)} %get-tuple-element.110), channel_id=1, source_target_pairs={{0,1},{1,0},{2,3},{3,2},{4,5},{5,4},{6,7},{7,6},{8,9},{9,8},{10,11... | collective-permute-start | bytes 1474568 | tf_op jit(solution)/shard_map/ppermute | solution.py:631
  28.4 1.4 %near_back_a.1 = (bf16[256,128]{1,0:T(8,128)(2,1)S(1)}, bf16[256,128]{1,0:T(8,128)(2,1)S(1)}, bf16[256,128]{1,0:T(8,128)(2,1)S(1)}, bf16[2,192,128]{2,1,0:T(8,128)(2,1)S(1)}, bf16[2,192,128]{2,1,0:T(8,128)(2,1)S(1)}) custom-call(bf16[4,896,256]{2,1,0:T(8,128)(2,1)S(1)} %get-tuple-element.111.refs_0_, bf16[496,512]{1,0:T(8,128)(2,1)S(1)} %get-tuple-element.80.q_all.refs_1_, ...), custom_call_target="tpu_custom_call" | custom-call | flops 3000000000 | bytes 1048576 | tf_op jit(solution)/shard_map/near_back_a/pallas_call | solution.py:615
  30.1 1.8 %collective-permute-start.8 = (bf16[128,512]{1,0:T(8,128)(2,1)S(1)}, bf16[128,512]{1,0:T(8,128)(2,1)S(1)}, u32[]{:S(2)}, u32[]{:S(2)}) collective-permute-start(bf16[128,512]{1,0:T(8,128)(2,1)S(1)} %get-tuple-element.118), channel_id=1, source_target_pairs={{0,24},{1,25},{2,26},{3,27},{4,28},{5,29},{6,30},{7,31},{8,16},{9,... | collective-permute-start | bytes 393224 | tf_op jit(solution)/shard_map/ppermute | solution.py:631
  31.9 4.0 %collective-permute-start.11 = (bf16[64,1024]{1,0:T(8,128)(2,1)S(1)}, bf16[64,1024]{1,0:T(8,128)(2,1)S(1)}, u32[]{:S(2)}, u32[]{:S(2)}) collective-permute-start(bf16[64,1024]{1,0:T(8,128)(2,1)S(1)} %get-tuple-element.114._), channel_id=1, source_target_pairs={{0,30},{1,3},{2,0},{3,5},{4,2},{5,7},{6,4},{7,9},{8,6},{9,11},{10,... | collective-permute-start | bytes 393224 | tf_op jit(solution)/shard_map/ppermute | solution.py:631
  35.9 1.0 %project.1 = (bf16[256,512]{1,0:T(8,128)(2,1)}, f32[8,128]{1,0:T(8,128)S(1)}) custom-call(bf16[256,512]{1,0:T(8,128)(2,1)S(1)} %get-tuple-element.100.attended, bf16[512,512]{1,0:T(8,128)(2,1)S(1)} %get-tuple-element.101.w, bf16[64,1024]{1,0:T(8,128)(2,1)S(1)} %get-tuple-element.114._), custom_call_target="tpu_custom_call" | custom-call | flops 1000000000 | bytes 1048576 | tf_op jit(solution)/shard_map/project/pallas_call | solution.py:615
  37.3 1.5 %near_back_b.1 = (bf16[256,128]{1,0:T(8,128)(2,1)S(1)}, bf16[256,128]{1,0:T(8,128)(2,1)S(1)}, bf16[256,128]{1,0:T(8,128)(2,1)S(1)}, bf16[2,192,128]{2,1,0:T(8,128)(2,1)S(1)}, bf16[2,192,128]{2,1,0:T(8,128)(2,1)S(1)}) custom-call(bf16[4,896,256]{2,1,0:T(8,128)(2,1)S(1)} %get-tuple-element.111.refs_0_, bf16[496,512]{1,0:T(8,128)(2,1)S(1)} %get-tuple-element.80.q_all.refs_1_, ...), custom_call_target="tpu_custom_call" | custom-call | flops 3000000000 | bytes 1048576 | tf_op jit(solution)/shard_map/near_back_b/pallas_call | solution.py:615
  38.8 2.7 %collective-permute-done.9.got = bf16[64,512]{1,0:T(8,128)(2,1)S(1)} collective-permute-done((bf16[64,512]{1,0:T(8,128)(2,1)S(1)}, bf16[64,512]{1,0:T(8,128)(2,1)S(1)}, u32[]{:S(2)}, u32[]{:S(2)}) %collective-permute-start.9) | collective-permute-done | bytes 65568 | tf_op jit(solution)/shard_map/ppermute | solution.py:631
  41.6 1.5 %collective-permute-start.10 = (bf16[32,512]{1,0:T(8,128)(2,1)S(1)}, bf16[32,512]{1,0:T(8,128)(2,1)S(1)}, u32[]{:S(2)}, u32[]{:S(2)}) collective-permute-start(bf16[32,512]{1,0:T(8,128)(2,1)S(1)} %get-tuple-element.132), channel_id=1, source_target_pairs={{0,6},{1,7},{2,4},{3,5},{4,2},{5,3},{6,0},{7,1},{8,14},{9,15},{10,... | collective-permute-start | bytes 98312 | tf_op jit(solution)/shard_map/ppermute | solution.py:631
  43.0 1.4 %near_back_c.1 = (bf16[256,128]{1,0:T(8,128)(2,1)S(1)}, bf16[256,128]{1,0:T(8,128)(2,1)S(1)}, bf16[256,128]{1,0:T(8,128)(2,1)S(1)}, bf16[2,192,128]{2,1,0:T(8,128)(2,1)S(1)}, bf16[2,192,128]{2,1,0:T(8,128)(2,1)S(1)}) custom-call(bf16[4,896,256]{2,1,0:T(8,128)(2,1)S(1)} %get-tuple-element.111.refs_0_, bf16[496,512]{1,0:T(8,128)(2,1)S(1)} %get-tuple-element.80.q_all.refs_1_, ...), custom_call_target="tpu_custom_call" | custom-call | flops 3000000000 | bytes 1048576 | tf_op jit(solution)/shard_map/near_back_c/pallas_call | solution.py:615
  44.5 2.3 %collective-permute-done.10.got = bf16[32,512]{1,0:T(8,128)(2,1)S(1)} collective-permute-done((bf16[32,512]{1,0:T(8,128)(2,1)S(1)}, bf16[32,512]{1,0:T(8,128)(2,1)S(1)}, u32[]{:S(2)}, u32[]{:S(2)}) %collective-permute-start.10) | collective-permute-done | bytes 32800 | tf_op jit(solution)/shard_map/ppermute | solution.py:631
  46.9 1.5 %near_back_d.1 = (bf16[256,128]{1,0:T(8,128)(2,1)S(1)}, bf16[256,128]{1,0:T(8,128)(2,1)S(1)}, bf16[256,128]{1,0:T(8,128)(2,1)S(1)}, bf16[192,1024]{1,0:T(8,128)(2,1)S(1)}, bf16[192,1024]{1,0:T(8,128)(2,1)S(1)}) custom-call(bf16[4,896,256]{2,1,0:T(8,128)(2,1)S(1)} %get-tuple-element.111.refs_0_, bf16[496,512]{1,0:T(8,128)(2,1)S(1)} %get-tuple-element.80.q_all.refs_1_, ...), custom_call_target="tpu_custom_call" | custom-call | flops 3000000000 | bytes 1048576 | tf_op jit(solution)/shard_map/near_back_d/pallas_call | solution.py:615
  48.4 2.2 %collective-permute-done.13.got = bf16[16,512]{1,0:T(8,128)(2,1)S(1)} collective-permute-done((bf16[16,512]{1,0:T(8,128)(2,1)S(1)}, bf16[16,512]{1,0:T(8,128)(2,1)S(1)}, u32[]{:S(2)}, u32[]{:S(2)}) %collective-permute-start.13) | collective-permute-done | bytes 16416 | tf_op jit(solution)/shard_map/ppermute | solution.py:631
  50.6 0.5 collective-permute-start.15
  51.1 0.7 copies.1
  51.8 8.6 %all-to-all-start = ((bf16[8,16,512]{2,1,0:T(8,128)(2,1)}), bf16[8,16,512]{2,1,0:T(8,128)(2,1)S(1)}, u32[]{:S(2)}, u32[]{:S(2)}) async-start(bf16[8,16,512]{2,1,0:T(8,128)(2,1)} %copies.1), calls=%async_computation | async-start | bytes 262144 | tf_op jit(solution)/shard_map/all_to_all | solution.py:816
  60.4 1.7 %collective-permute-start.16 = (bf16[16,1024]{1,0:T(8,128)(2,1)S(1)}, bf16[16,1024]{1,0:T(8,128)(2,1)S(1)}, u32[]{:S(2)}, u32[]{:S(2)}) collective-permute-start(bf16[16,1024]{1,0:T(8,128)(2,1)S(1)} %get-tuple-element.148), channel_id=1, source_target_pairs={{0,6},{1,7},{2,28},{3,29},{4,10},{5,11},{6,0},{7,1},{8,14},{9,15},... | collective-permute-start | bytes 98312 | tf_op jit(solution)/shard_map/ppermute | solution.py:631
  62.1 3.4 %collective-permute-done.16.refs_12_ = bf16[16,1024]{1,0:T(8,128)(2,1)S(1)} collective-permute-done((bf16[16,1024]{1,0:T(8,128)(2,1)S(1)}, bf16[16,1024]{1,0:T(8,128)(2,1)S(1)}, u32[]{:S(2)}, u32[]{:S(2)}) %collective-permute-start.16) | collective-permute-done | bytes 32800 | tf_op jit(solution)/shard_map/ppermute | solution.py:631
  65.5 1.3 %combine.1 = (bf16[256,512]{1,0:T(8,128)(2,1)}, bf16[256,512]{1,0:T(8,128)(2,1)}, bf16[256,512]{1,0:T(8,128)(2,1)}, f32[8,128]{1,0:T(8,128)S(1)}) custom-call(bf16[256,128]{1,0:T(8,128)(2,1)S(1)} %get-tuple-element.116.refs_0_, bf16[256,128]{1,0:T(8,128)(2,1)S(1)} %get-tuple-element.121.refs_1_, bf16[256,128]{1,0:T(8,128)(2,1)S(1)} %get-tuple-element.125.refs_2_, ...), custom_call_target="tpu_custom_call" | custom-call | flops 1000000000 | bytes 1048576 | tf_op jit(solution)/shard_map/combine/pallas_call | solution.py:615
  66.8 1.4 %all-to-all-done.parts = bf16[8,16,512]{2,1,0:T(8,128)(2,1)S(1)} async-done(((bf16[8,16,512]{2,1,0:T(8,128)(2,1)}), bf16[8,16,512]{2,1,0:T(8,128)(2,1)S(1)}, u32[]{:S(2)}, u32[]{:S(2)}) %all-to-all-start) | async-done | bytes 131104 | tf_op jit(solution)/shard_map/all_to_all | solution.py:816
  68.1 0.6 last_sum.1
  (39 shorter events, 1.1 us)
Async XLA Ops:
  0.6 1.1 %copy-start.2 = (bf16[1,256,512]{2,1,0:T(8,128)(2,1)S(1)}, bf16[1,256,512]{2,1,0:T(8,128)(2,1)}, u32[]{:S(2)}) copy-start(bf16[1,256,512]{2,1,0:T(8,128)(2,1)} %param.8) | copy-start | bytes 786436
  0.6 1.1 %copy-start.1 = (bf16[1,256,512]{2,1,0:T(8,128)(2,1)S(1)}, bf16[1,256,512]{2,1,0:T(8,128)(2,1)}, u32[]{:S(2)}) copy-start(bf16[1,256,512]{2,1,0:T(8,128)(2,1)} %param.7) | copy-start | bytes 786436
  0.7 0.7 %copy-start.5 = (s32[1,256]{1,0:T(1,128)S(1)}, s32[1,256]{1,0:T(1,128)}, u32[]{:S(2)}) copy-start(s32[1,256]{1,0:T(1,128)} %seg_hbm.1) | copy-start | bytes 3076
  2.3 15.0 %collective-permute-start = (bf16[192,1152]{1,0:T(8,128)(2,1)S(1)}, bf16[192,1152]{1,0:T(8,128)(2,1)S(1)}, u32[]{:S(2)}, u32[]{:S(2)}) collective-permute-start(bf16[192,1152]{1,0:T(8,128)(2,1)S(1)} %get-tuple-element.83), channel_id=1, source_target_pairs={{0,1},{1,2},{2,3},{3,4},{4,5},{5,6},{6,7},{7,8},{8,9},{9,10},{10,1... | collective-permute-start | bytes 1327112 | tf_op jit(solution)/shard_map/ppermute | solution.py:631
  2.4 15.0 %collective-permute-start.1 = (bf16[192,1152]{1,0:T(8,128)(2,1)S(1)}, bf16[192,1152]{1,0:T(8,128)(2,1)S(1)}, u32[]{:S(2)}, u32[]{:S(2)}) collective-permute-start(bf16[192,1152]{1,0:T(8,128)(2,1)S(1)} %get-tuple-element.84), channel_id=1, source_target_pairs={{0,31},{1,0},{2,1},{3,2},{4,3},{5,4},{6,5},{7,6},{8,7},{9,8},{10,9... | collective-permute-start | bytes 1327112 | tf_op jit(solution)/shard_map/ppermute | solution.py:631
  7.5 4.4 %copy-start = (bf16[512,512]{1,0:T(8,128)(2,1)S(1)}, bf16[512,512]{1,0:T(8,128)(2,1)}, u32[]{:S(2)}) copy-start(bf16[512,512]{1,0:T(8,128)(2,1)} %w_hbm.1) | copy-start | bytes 1572868
  7.5 4.4 %copy-start.3 = (bf16[1,256,512]{2,1,0:T(8,128)(2,1)S(1)}, bf16[1,256,512]{2,1,0:T(8,128)(2,1)}, u32[]{:S(2)}) copy-start(bf16[1,256,512]{2,1,0:T(8,128)(2,1)} %param.6) | copy-start | bytes 786436
  7.5 4.4 %copy-start.4 = (bf16[1,256,512]{2,1,0:T(8,128)(2,1)S(1)}, bf16[1,256,512]{2,1,0:T(8,128)(2,1)}, u32[]{:S(2)}) copy-start(bf16[1,256,512]{2,1,0:T(8,128)(2,1)} %param.11) | copy-start | bytes 786436
  7.5 1.3 %collective-permute-start.2 = (bf16[48,1152]{1,0:T(8,128)(2,1)S(1)}, bf16[48,1152]{1,0:T(8,128)(2,1)S(1)}, u32[]{:S(2)}, u32[]{:S(2)}) collective-permute-start(bf16[48,1152]{1,0:T(8,128)(2,1)S(1)} %get-tuple-element.85.far), channel_id=1, source_target_pairs={{0,1},{1,0},{2,3},{3,2},{4,5},{5,4},{6,7},{7,6},{8,9},{9,8},{10,11... | collective-permute-start | bytes 331784 | tf_op jit(solution)/shard_map/ppermute | solution.py:631
  8.8 8.5 %collective-permute-start.3 = (bf16[64,1152]{1,0:T(8,128)(2,1)S(1)}, bf16[64,1152]{1,0:T(8,128)(2,1)S(1)}, u32[]{:S(2)}, u32[]{:S(2)}) collective-permute-start(bf16[64,1152]{1,0:T(8,128)(2,1)S(1)} %get-tuple-element.86), channel_id=1, source_target_pairs={{0,2},{1,31},{2,4},{3,1},{4,6},{5,3},{6,8},{7,5},{8,10},{9,7},{10,... | collective-permute-start | bytes 442376 | tf_op jit(solution)/shard_map/ppermute | solution.py:631
  8.9 8.5 %collective-permute-start.5 = (bf16[16,1152]{1,0:T(8,128)(2,1)S(1)}, bf16[16,1152]{1,0:T(8,128)(2,1)S(1)}, u32[]{:S(2)}, u32[]{:S(2)}) collective-permute-start(bf16[16,1152]{1,0:T(8,128)(2,1)S(1)} %get-tuple-element.97), channel_id=1, source_target_pairs={{0,6},{1,7},{2,28},{3,29},{4,10},{5,11},{6,0},{7,1},{8,14},{9,15},... | collective-permute-start | bytes 110600 | tf_op jit(solution)/shard_map/ppermute | solution.py:631
  11.9 8.0 %collective-permute-start.4 = (bf16[32,1152]{1,0:T(8,128)(2,1)S(1)}, bf16[32,1152]{1,0:T(8,128)(2,1)S(1)}, u32[]{:S(2)}, u32[]{:S(2)}) collective-permute-start(bf16[32,1152]{1,0:T(8,128)(2,1)S(1)} %get-tuple-element.96), channel_id=1, source_target_pairs={{0,4},{1,29},{2,6},{3,31},{4,8},{5,1},{6,10},{7,3},{8,12},{9,5},{1... | collective-permute-start | bytes 221192 | tf_op jit(solution)/shard_map/ppermute | solution.py:631
  19.9 1.8 %collective-permute-start.6 = (bf16[112,1152]{1,0:T(8,128)(2,1)S(1)}, bf16[112,1152]{1,0:T(8,128)(2,1)S(1)}, u32[]{:S(2)}, u32[]{:S(2)}) collective-permute-start(bf16[112,1152]{1,0:T(8,128)(2,1)S(1)} %get-tuple-element.99), channel_id=1, source_target_pairs={{0,1},{1,0},{2,3},{3,2},{4,5},{5,4},{6,7},{7,6},{8,9},{9,8},{10,11... | collective-permute-start | bytes 774152 | tf_op jit(solution)/shard_map/ppermute | solution.py:631
  27.6 2.3 %collective-permute-start.7 = (bf16[480,512]{1,0:T(8,128)(2,1)S(1)}, bf16[480,512]{1,0:T(8,128)(2,1)S(1)}, u32[]{:S(2)}, u32[]{:S(2)}) collective-permute-start(bf16[480,512]{1,0:T(8,128)(2,1)S(1)} %get-tuple-element.110), channel_id=1, source_target_pairs={{0,1},{1,0},{2,3},{3,2},{4,5},{5,4},{6,7},{7,6},{8,9},{9,8},{10,11... | collective-permute-start | bytes 1474568 | tf_op jit(solution)/shard_map/ppermute | solution.py:631
  30.1 7.1 %collective-permute-start.8 = (bf16[128,512]{1,0:T(8,128)(2,1)S(1)}, bf16[128,512]{1,0:T(8,128)(2,1)S(1)}, u32[]{:S(2)}, u32[]{:S(2)}) collective-permute-start(bf16[128,512]{1,0:T(8,128)(2,1)S(1)} %get-tuple-element.118), channel_id=1, source_target_pairs={{0,24},{1,25},{2,26},{3,27},{4,28},{5,29},{6,30},{7,31},{8,16},{9,... | collective-permute-start | bytes 393224 | tf_op jit(solution)/shard_map/ppermute | solution.py:631
  31.9 6.8 %collective-permute-start.12 = (bf16[32,1024]{1,0:T(8,128)(2,1)S(1)}, bf16[32,1024]{1,0:T(8,128)(2,1)S(1)}, u32[]{:S(2)}, u32[]{:S(2)}) collective-permute-start(bf16[32,1024]{1,0:T(8,128)(2,1)S(1)} %get-tuple-element.135), channel_id=1, source_target_pairs={{0,28},{1,5},{2,30},{3,7},{4,0},{5,9},{6,2},{7,11},{8,4},{9,13},{1... | collective-permute-start | bytes 196616 | tf_op jit(solution)/shard_map/ppermute | solution.py:631
  31.9 6.9 %collective-permute-start.11 = (bf16[64,1024]{1,0:T(8,128)(2,1)S(1)}, bf16[64,1024]{1,0:T(8,128)(2,1)S(1)}, u32[]{:S(2)}, u32[]{:S(2)}) collective-permute-start(bf16[64,1024]{1,0:T(8,128)(2,1)S(1)} %get-tuple-element.114._), channel_id=1, source_target_pairs={{0,30},{1,3},{2,0},{3,5},{4,2},{5,7},{6,4},{7,9},{8,6},{9,11},{10,... | collective-permute-start | bytes 393224 | tf_op jit(solution)/shard_map/ppermute | solution.py:631
  37.2 4.4 %collective-permute-start.9 = (bf16[64,512]{1,0:T(8,128)(2,1)S(1)}, bf16[64,512]{1,0:T(8,128)(2,1)S(1)}, u32[]{:S(2)}, u32[]{:S(2)}) collective-permute-start(bf16[64,512]{1,0:T(8,128)(2,1)S(1)} %get-tuple-element.123), channel_id=1, source_target_pairs={{0,8},{1,9},{2,10},{3,11},{4,12},{5,13},{6,14},{7,15},{8,0},{9,1},... | collective-permute-start | bytes 196616 | tf_op jit(solution)/shard_map/ppermute | solution.py:631
  41.6 5.2 %collective-permute-start.10 = (bf16[32,512]{1,0:T(8,128)(2,1)S(1)}, bf16[32,512]{1,0:T(8,128)(2,1)S(1)}, u32[]{:S(2)}, u32[]{:S(2)}) collective-permute-start(bf16[32,512]{1,0:T(8,128)(2,1)S(1)} %get-tuple-element.132), channel_id=1, source_target_pairs={{0,6},{1,7},{2,4},{3,5},{4,2},{5,3},{6,0},{7,1},{8,14},{9,15},{10,... | collective-permute-start | bytes 98312 | tf_op jit(solution)/shard_map/ppermute | solution.py:631
  46.8 3.8 %collective-permute-start.13 = (bf16[16,512]{1,0:T(8,128)(2,1)S(1)}, bf16[16,512]{1,0:T(8,128)(2,1)S(1)}, u32[]{:S(2)}, u32[]{:S(2)}) collective-permute-start(bf16[16,512]{1,0:T(8,128)(2,1)S(1)} %get-tuple-element.143), channel_id=1, source_target_pairs={{0,2},{1,3},{2,0},{3,1},{4,6},{5,7},{6,4},{7,5},{8,10},{9,11},{10,... | collective-permute-start | bytes 49160 | tf_op jit(solution)/shard_map/ppermute | solution.py:631
  50.6 14.9 %collective-permute-start.14 = (bf16[192,1024]{1,0:T(8,128)(2,1)S(1)}, bf16[192,1024]{1,0:T(8,128)(2,1)S(1)}, u32[]{:S(2)}, u32[]{:S(2)}) collective-permute-start(bf16[192,1024]{1,0:T(8,128)(2,1)S(1)} %get-tuple-element.144), channel_id=1, source_target_pairs={{0,31},{1,0},{2,1},{3,2},{4,3},{5,4},{6,5},{7,6},{8,7},{9,8},{10,9... | collective-permute-start | bytes 1179656 | tf_op jit(solution)/shard_map/ppermute | solution.py:631
  50.6 14.9 %collective-permute-start.15 = (bf16[192,1024]{1,0:T(8,128)(2,1)S(1)}, bf16[192,1024]{1,0:T(8,128)(2,1)S(1)}, u32[]{:S(2)}, u32[]{:S(2)}) collective-permute-start(bf16[192,1024]{1,0:T(8,128)(2,1)S(1)} %get-tuple-element.145), channel_id=1, source_target_pairs={{0,1},{1,2},{2,3},{3,4},{4,5},{5,6},{6,7},{7,8},{8,9},{9,10},{10,1... | collective-permute-start | bytes 1179656 | tf_op jit(solution)/shard_map/ppermute | solution.py:631
  51.8 16.4 %all-to-all-start = ((bf16[8,16,512]{2,1,0:T(8,128)(2,1)}), bf16[8,16,512]{2,1,0:T(8,128)(2,1)S(1)}, u32[]{:S(2)}, u32[]{:S(2)}) async-start(bf16[8,16,512]{2,1,0:T(8,128)(2,1)} %copies.1), calls=%async_computation | async-start | bytes 262144 | tf_op jit(solution)/shard_map/all_to_all | solution.py:816
  60.4 1.7 %collective-permute-start.17 = (bf16[48,1024]{1,0:T(8,128)(2,1)S(1)}, bf16[48,1024]{1,0:T(8,128)(2,1)S(1)}, u32[]{:S(2)}, u32[]{:S(2)}) collective-permute-start(bf16[48,1024]{1,0:T(8,128)(2,1)S(1)} %far_split.1.refs_16_), channel_id=1, source_target_pairs={{0,1},{1,0},{2,3},{3,2},{4,5},{5,4},{6,7},{7,6},{8,9},{9,8},{10,11... | collective-permute-start | bytes 294920 | tf_op jit(solution)/shard_map/ppermute | solution.py:631
  60.4 5.1 %collective-permute-start.16 = (bf16[16,1024]{1,0:T(8,128)(2,1)S(1)}, bf16[16,1024]{1,0:T(8,128)(2,1)S(1)}, u32[]{:S(2)}, u32[]{:S(2)}) collective-permute-start(bf16[16,1024]{1,0:T(8,128)(2,1)S(1)} %get-tuple-element.148), channel_id=1, source_target_pairs={{0,6},{1,7},{2,28},{3,29},{4,10},{5,11},{6,0},{7,1},{8,14},{9,15},... | collective-permute-start | bytes 98312 | tf_op jit(solution)/shard_map/ppermute | solution.py:631

commit v10 on v9

--- a/solution.py
+++ b/solution.py
@@ -532,10 +532,8 @@
     return ref[pl.ds(pl.multiple_of(core * rows, rows), rows)]
 
 
-def far_split_kernel(back3, back4, give):
-    other = 1 - core_index()
-    give[0:32] = core_rows(back3, other, 32)
-    give[32:48] = core_rows(back4, other, 16)
+def far_split_kernel(back, give):
+    give[...] = core_rows(back, 1 - core_index(), give.shape[0])
 
 
 def halve_kernel(divisor, keep, got, *refs):
@@ -566,17 +564,17 @@
 
 
 def combine_kernel(*refs):
-    own, (low, high), grads_q = (refs[0:4], refs[4:8]), refs[8:10], refs[14:18]
-    back3, back4, third, swapped = refs[10:14]
-    d_k_hbm, d_v_hbm, d_q_hbm, finished, d_k, d_v, d_q, sems = refs[18:]
+    own, (low, high), grads_q = (refs[0:4], refs[4:8]), refs[8:10], refs[15:19]
+    back3, back4, third, swapped3, swapped4 = refs[10:15]
+    d_k_hbm, d_v_hbm, d_q_hbm, finished, d_k, d_v, d_q, sems = refs[19:]
     finished[...] = jnp.zeros(finished.shape, F32)
     for pair, ref in enumerate(grads_q):
         d_q[:, lanes_of(pair)] = ref[...]
     copies = [pltpu.make_async_copy(d_q, d_q_hbm, sems.at[2])]
     copies[0].start()
     core = core_index()
-    far3 = core_rows(back3, core, 32).astype(F32) + swapped[0:32].astype(F32)
-    far4 = core_rows(back4, core, 16).astype(F32) + swapped[32:48].astype(F32)
+    far3 = core_rows(back3, core, 32).astype(F32) + swapped3[...].astype(F32)
+    far4 = core_rows(back4, core, 16).astype(F32) + swapped4[...].astype(F32)
     far4 = far4 + third[...].astype(F32)
     for part, out, out_hbm in ((0, d_k, d_k_hbm), (1, d_v, d_v_hbm)):
         lanes = slice(part * WIDTH, (part + 1) * WIDTH)
@@ -764,7 +762,6 @@
     )
     got_w = moved(give, lambda i: i ^ 24)
     back3 = moved(sum3, back_3)
-    back4 = moved(sum4, back_4)
     layer_out, projected = call(
         project_kernel,
         "project",
@@ -793,8 +790,8 @@
         microseconds=3,
     )
     keep, got_w = halved(keep, got_w, 2, lambda i: i ^ 2, part_c[0])
-    give = call(far_split_kernel, "far_split", [((48, 2 * WIDTH), BF16)], [back3, back4])[0]
-    swapped = moved(give, partner)
+    give = call(far_split_kernel, "split_3", [((32, 2 * WIDTH), BF16)], [back3])[0]
+    swapped3 = moved(give, partner)
     d_q, own_k, own_v, to_low, to_high = call(
         near_back_last_kernel,
         "near_back_d",
@@ -812,15 +809,18 @@
         [((lax.axis_size("dp"), 16, WIDTH), BF16)],
         [keep, got_w],
     )[0]
-    sum_third, copies = lax.optimization_barrier((sum_third, copies))
+    sum4, sum_third, copies = lax.optimization_barrier((sum4, sum_third, copies))
     copies = lax.all_to_all(copies, "dp", 0, 0, tiled=True)
+    back4 = moved(sum4, back_4)
     back_third = moved(sum_third, third)
+    give = call(far_split_kernel, "split_4", [((16, 2 * WIDTH), BF16)], [back4])[0]
+    swapped4 = moved(give, partner)
     d_k, d_v, d_q, finished = call(
         combine_kernel,
         "combine",
         [(tokens, BF16)] * 3 + [((8, LANES), F32)],
         [part_a[1], part_b[1], part_c[1], own_k, part_a[2], part_b[2], part_c[2], own_v]
-        + [low_back, high_back, back3, back4, back_third, swapped]
+        + [low_back, high_back, back3, back4, back_third, swapped3, swapped4]
         + [part_a[0], part_b[0], part_c[0], d_q],
         [pltpu.VMEM(tokens, BF16)] * 3 + [dma((3,))],
         to_hbm=(0, 1, 2),

time: 69.9 us -> 72.7 us (1.040)
  waiting for transfers between devices: 20.8 us -> 24.5 us
  starting transfers between devices: 27.3 us -> 26.1 us
    ppermute x18 -> x19, waiting for transfers between devices: 19.5 us -> 23.4 us  [moved(): return lax.ppermute(x, 'ctx', [(i, route(i) % count) for i in range(count)])]
    ppermute x18 -> x19, starting transfers between devices: 18.7 us -> 17.5 us  [moved(): return lax.ppermute(x, 'ctx', [(i, route(i) % count) for i in range(count)])]
    pallas_call x21 -> x22, Pallas kernels: 19 us -> 19 us  [call(): pl.pallas_call(kernel, name=name, out_shape=[jax.ShapeDtypeStruct(shape,...]
  transfers between devices with their start and end apart: 19 -> 20, of which waited for: 9 -> 10; matrix products, arithmetic and copies ran while one was open for 0% -> 0% of each run, Pallas kernels for 16% -> 16%
where the time goes in v10:
time: 72.7 us; the launch traced here: 71.3 us
  starting transfers between devices  26.1 us (36%)
  waiting for transfers between devices  24.5 us (34%)
  Pallas kernels  19 us (26%)
  between operations  0.9 us (1%)
  local copies, waits for them, and re-layouts  0.75 us (1%)
    ppermute x19, waiting for transfers between devices, moved(): return lax.ppermute(x, 'ctx', [(i, route(i) % count) for i in range(count)])  23.4 us
    pallas_call x22, Pallas kernels, call(): pl.pallas_call(kernel, name=name, out_shape=[jax.ShapeDtypeStruct(shape,...  19 us
    ppermute x19, starting transfers between devices, moved(): return lax.ppermute(x, 'ctx', [(i, route(i) % count) for i in range(count)])  17.5 us
    all_to_all x1, starting transfers between devices, body(): copies = lax.all_to_all(copies, 'dp', 0, 0, tiled=True)  8.57 us
  transfers between devices with their start and end apart: 20, of which 10 were waited for; matrix products, arithmetic and copies ran while one was open for 0% of the time, Pallas kernels for 16%

profile of v10, /device:TPU:32, one launch (start us, length us, event | category | flops | bytes accessed | tf_op | source)
XLA Modules:
  0.0 71.3 jit_solution(8509417692930196520)
XLA Ops:
  0.7 0.7 %copy-done.5 = s32[1,256]{1,0:T(1,128)S(1)} copy-done((s32[1,256]{1,0:T(1,128)S(1)}, s32[1,256]{1,0:T(1,128)}, u32[]{:S(2)}) %copy-start.5) | copy-done | bytes 1048
  1.7 0.6 coarsen.1
  2.4 5.1 %collective-permute-start.1 = (bf16[192,1152]{1,0:T(8,128)(2,1)S(1)}, bf16[192,1152]{1,0:T(8,128)(2,1)S(1)}, u32[]{:S(2)}, u32[]{:S(2)}) collective-permute-start(bf16[192,1152]{1,0:T(8,128)(2,1)S(1)} %get-tuple-element.85), channel_id=1, source_target_pairs={{0,31},{1,0},{2,1},{3,2},{4,3},{5,4},{6,5},{7,6},{8,7},{9,8},{10,9... | collective-permute-start | bytes 1327112 | tf_op jit(solution)/shard_map/ppermute | solution.py:629
  7.5 1.3 %collective-permute-done.2.far_partner = bf16[48,1152]{1,0:T(8,128)(2,1)S(1)} collective-permute-done((bf16[48,1152]{1,0:T(8,128)(2,1)S(1)}, bf16[48,1152]{1,0:T(8,128)(2,1)S(1)}, u32[]{:S(2)}, u32[]{:S(2)}) %collective-permute-start.2) | collective-permute-done | bytes 110624 | tf_op jit(solution)/shard_map/ppermute | solution.py:629
  8.9 2.9 %collective-permute-start.5 = (bf16[16,1152]{1,0:T(8,128)(2,1)S(1)}, bf16[16,1152]{1,0:T(8,128)(2,1)S(1)}, u32[]{:S(2)}, u32[]{:S(2)}) collective-permute-start(bf16[16,1152]{1,0:T(8,128)(2,1)S(1)} %get-tuple-element.98), channel_id=1, source_target_pairs={{0,6},{1,7},{2,28},{3,29},{4,10},{5,11},{6,0},{7,1},{8,14},{9,15},... | collective-permute-start | bytes 110600 | tf_op jit(solution)/shard_map/ppermute | solution.py:629
  11.9 0.7 %prepare.1 = (bf16[496,512]{1,0:T(8,128)(2,1)S(1)}, f32[256,512]{1,0:T(8,128)S(1)}, bf16[512,512]{1,0:T(8,128)(2,1)S(1)}, bf16[256,512]{1,0:T(8,128)(2,1)S(1)}) custom-call(bf16[256,512]{1,0:T(8,128)(2,1)S(1)} %bitcast.10, bf16[256,512]{1,0:T(8,128)(2,1)S(1)} %bitcast.11, bf16[512,512]{1,0:T(8,128)(2,1)S(1)} %copy-done), custom_call_target="tpu_custom_call" | custom-call | flops 1000000000 | bytes 1048576 | tf_op jit(solution)/shard_map/prepare/pallas_call | solution.py:613
  12.6 4.8 %collective-permute-done.3.got3 = bf16[64,1152]{1,0:T(8,128)(2,1)S(1)} collective-permute-done((bf16[64,1152]{1,0:T(8,128)(2,1)S(1)}, bf16[64,1152]{1,0:T(8,128)(2,1)S(1)}, u32[]{:S(2)}, u32[]{:S(2)}) %collective-permute-start.3) | collective-permute-done | bytes 147488 | tf_op jit(solution)/shard_map/ppermute | solution.py:629
  17.4 2.5 %collective-permute-done.4.got4.refs_1_ = bf16[32,1152]{1,0:T(8,128)(2,1)S(1)} collective-permute-done((bf16[32,1152]{1,0:T(8,128)(2,1)S(1)}, bf16[32,1152]{1,0:T(8,128)(2,1)S(1)}, u32[]{:S(2)}, u32[]{:S(2)}) %collective-permute-start.4) | collective-permute-done | bytes 73760 | tf_op jit(solution)/shard_map/ppermute | solution.py:629
  20.0 1.7 %near.1 = (bf16[4,896,256]{2,1,0:T(8,128)(2,1)S(1)}, f32[256,512]{1,0:T(8,128)S(1)}, f32[256,256]{1,0:T(8,128)S(1)}, bf16[192,512]{1,0:T(8,128)(2,1)S(1)}, bf16[192,256]{1,0:T(8,128)(2,1)S(1)}) custom-call(bf16[496,512]{1,0:T(8,128)(2,1)S(1)} %get-tuple-element.81.q_all.refs_1_, bf16[496,128]{1,0:T(8,128)(2,1)S(1)} %documents.1.qdoc, ...), custom_call_target="tpu_custom_call" | custom-call | flops 49999998976 | bytes 1048576 | tf_op jit(solution)/shard_map/near/pallas_call | solution.py:613
  21.7 4.8 %merge.1 = (bf16[256,512]{1,0:T(8,128)(2,1)S(1)}, f32[256,512]{1,0:T(8,128)S(1)}, bf16[256,512]{1,0:T(8,128)(2,1)S(1)}, bf16[4,96,128]{2,1,0:T(8,128)(2,1)S(1)},...) custom-call(bf16[496,512]{1,0:T(8,128)(2,1)S(1)} %get-tuple-element.81.q_all.refs_1_, ...), custom_call_target="tpu_custom_call" | custom-call | flops 6000000000 | bytes 1048576 | tf_op jit(solution)/shard_map/merge/pallas_call | solution.py:613
  26.5 1.1 %far_back.1 = (bf16[48,512]{1,0:T(8,128)(2,1)S(1)}, bf16[32,1024]{1,0:T(8,128)(2,1)S(1)}, bf16[32,1024]{1,0:T(8,128)(2,1)S(1)}, bf16[16,1024]{1,0:T(8,128)(2,1)S(1)}, bf16[480,512]{1,0:T(8,128)(2,1)S(1)}) custom-call(bf16[4,96,128]{2,1,0:T(8,128)(2,1)S(1)} %get-tuple-element.103.p_in, bf16[496,512]{1,0:T(8,128)(2,1)S(1)} %get-tuple-element.81.q_all.refs_1_, ...), custom_call_target="tpu_custom_call" | custom-call | flops 1000000000 | bytes 1048576 | tf_op jit(solution)/shard_map/far_back/pallas_call | solution.py:613
  27.6 0.8 %collective-permute-start.7 = (bf16[480,512]{1,0:T(8,128)(2,1)S(1)}, bf16[480,512]{1,0:T(8,128)(2,1)S(1)}, u32[]{:S(2)}, u32[]{:S(2)}) collective-permute-start(bf16[480,512]{1,0:T(8,128)(2,1)S(1)} %get-tuple-element.111), channel_id=1, source_target_pairs={{0,1},{1,0},{2,3},{3,2},{4,5},{5,4},{6,7},{7,6},{8,9},{9,8},{10,11... | collective-permute-start | bytes 1474568 | tf_op jit(solution)/shard_map/ppermute | solution.py:629
  28.4 1.4 %near_back_a.1 = (bf16[256,128]{1,0:T(8,128)(2,1)S(1)}, bf16[256,128]{1,0:T(8,128)(2,1)S(1)}, bf16[256,128]{1,0:T(8,128)(2,1)S(1)}, bf16[2,192,128]{2,1,0:T(8,128)(2,1)S(1)}, bf16[2,192,128]{2,1,0:T(8,128)(2,1)S(1)}) custom-call(bf16[4,896,256]{2,1,0:T(8,128)(2,1)S(1)} %get-tuple-element.112.refs_0_, bf16[496,512]{1,0:T(8,128)(2,1)S(1)} %get-tuple-element.81.q_all.refs_1_, ...), custom_call_target="tpu_custom_call" | custom-call | flops 3000000000 | bytes 1048576 | tf_op jit(solution)/shard_map/near_back_a/pallas_call | solution.py:613
  30.1 1.8 %collective-permute-start.8 = (bf16[128,512]{1,0:T(8,128)(2,1)S(1)}, bf16[128,512]{1,0:T(8,128)(2,1)S(1)}, u32[]{:S(2)}, u32[]{:S(2)}) collective-permute-start(bf16[128,512]{1,0:T(8,128)(2,1)S(1)} %get-tuple-element.119), channel_id=1, source_target_pairs={{0,24},{1,25},{2,26},{3,27},{4,28},{5,29},{6,30},{7,31},{8,16},{9,... | collective-permute-start | bytes 393224 | tf_op jit(solution)/shard_map/ppermute | solution.py:629
  31.9 1.8 %collective-permute-start.11 = (bf16[64,1024]{1,0:T(8,128)(2,1)S(1)}, bf16[64,1024]{1,0:T(8,128)(2,1)S(1)}, u32[]{:S(2)}, u32[]{:S(2)}) collective-permute-start(bf16[64,1024]{1,0:T(8,128)(2,1)S(1)} %get-tuple-element.115._), channel_id=1, source_target_pairs={{0,30},{1,3},{2,0},{3,5},{4,2},{5,7},{6,4},{7,9},{8,6},{9,11},{10,... | collective-permute-start | bytes 393224 | tf_op jit(solution)/shard_map/ppermute | solution.py:629
  33.7 1.0 %project.1 = (bf16[256,512]{1,0:T(8,128)(2,1)}, f32[8,128]{1,0:T(8,128)S(1)}) custom-call(bf16[256,512]{1,0:T(8,128)(2,1)S(1)} %get-tuple-element.101.attended, bf16[512,512]{1,0:T(8,128)(2,1)S(1)} %get-tuple-element.102.w, bf16[64,1024]{1,0:T(8,128)(2,1)S(1)} %get-tuple-element.115._), custom_call_target="tpu_custom_call" | custom-call | flops 1000000000 | bytes 1048576 | tf_op jit(solution)/shard_map/project/pallas_call | solution.py:613
  34.7 2.4 %collective-permute-done.8.got = bf16[128,512]{1,0:T(8,128)(2,1)S(1)} collective-permute-done((bf16[128,512]{1,0:T(8,128)(2,1)S(1)}, bf16[128,512]{1,0:T(8,128)(2,1)S(1)}, u32[]{:S(2)}, u32[]{:S(2)}) %collective-permute-start.8) | collective-permute-done | bytes 131104 | tf_op jit(solution)/shard_map/ppermute | solution.py:629
  37.3 1.5 %near_back_b.1 = (bf16[256,128]{1,0:T(8,128)(2,1)S(1)}, bf16[256,128]{1,0:T(8,128)(2,1)S(1)}, bf16[256,128]{1,0:T(8,128)(2,1)S(1)}, bf16[2,192,128]{2,1,0:T(8,128)(2,1)S(1)}, bf16[2,192,128]{2,1,0:T(8,128)(2,1)S(1)}) custom-call(bf16[4,896,256]{2,1,0:T(8,128)(2,1)S(1)} %get-tuple-element.112.refs_0_, bf16[496,512]{1,0:T(8,128)(2,1)S(1)} %get-tuple-element.81.q_all.refs_1_, ...), custom_call_target="tpu_custom_call" | custom-call | flops 3000000000 | bytes 1048576 | tf_op jit(solution)/shard_map/near_back_b/pallas_call | solution.py:613
  38.8 2.8 %collective-permute-done.9.got = bf16[64,512]{1,0:T(8,128)(2,1)S(1)} collective-permute-done((bf16[64,512]{1,0:T(8,128)(2,1)S(1)}, bf16[64,512]{1,0:T(8,128)(2,1)S(1)}, u32[]{:S(2)}, u32[]{:S(2)}) %collective-permute-start.9) | collective-permute-done | bytes 65568 | tf_op jit(solution)/shard_map/ppermute | solution.py:629
  41.6 0.9 %collective-permute-start.10 = (bf16[32,512]{1,0:T(8,128)(2,1)S(1)}, bf16[32,512]{1,0:T(8,128)(2,1)S(1)}, u32[]{:S(2)}, u32[]{:S(2)}) collective-permute-start(bf16[32,512]{1,0:T(8,128)(2,1)S(1)} %get-tuple-element.133), channel_id=1, source_target_pairs={{0,6},{1,7},{2,4},{3,5},{4,2},{5,3},{6,0},{7,1},{8,14},{9,15},{10,... | collective-permute-start | bytes 98312 | tf_op jit(solution)/shard_map/ppermute | solution.py:629
  42.5 1.4 %near_back_c.1 = (bf16[256,128]{1,0:T(8,128)(2,1)S(1)}, bf16[256,128]{1,0:T(8,128)(2,1)S(1)}, bf16[256,128]{1,0:T(8,128)(2,1)S(1)}, bf16[2,192,128]{2,1,0:T(8,128)(2,1)S(1)}, bf16[2,192,128]{2,1,0:T(8,128)(2,1)S(1)}) custom-call(bf16[4,896,256]{2,1,0:T(8,128)(2,1)S(1)} %get-tuple-element.112.refs_0_, bf16[496,512]{1,0:T(8,128)(2,1)S(1)} %get-tuple-element.81.q_all.refs_1_, ...), custom_call_target="tpu_custom_call" | custom-call | flops 3000000000 | bytes 1048576 | tf_op jit(solution)/shard_map/near_back_c/pallas_call | solution.py:613
  43.9 2.8 %collective-permute-done.10.got = bf16[32,512]{1,0:T(8,128)(2,1)S(1)} collective-permute-done((bf16[32,512]{1,0:T(8,128)(2,1)S(1)}, bf16[32,512]{1,0:T(8,128)(2,1)S(1)}, u32[]{:S(2)}, u32[]{:S(2)}) %collective-permute-start.10) | collective-permute-done | bytes 32800 | tf_op jit(solution)/shard_map/ppermute | solution.py:629
  46.9 1.5 %near_back_d.1 = (bf16[256,128]{1,0:T(8,128)(2,1)S(1)}, bf16[256,128]{1,0:T(8,128)(2,1)S(1)}, bf16[256,128]{1,0:T(8,128)(2,1)S(1)}, bf16[192,1024]{1,0:T(8,128)(2,1)S(1)}, bf16[192,1024]{1,0:T(8,128)(2,1)S(1)}) custom-call(bf16[4,896,256]{2,1,0:T(8,128)(2,1)S(1)} %get-tuple-element.112.refs_0_, bf16[496,512]{1,0:T(8,128)(2,1)S(1)} %get-tuple-element.81.q_all.refs_1_, ...), custom_call_target="tpu_custom_call" | custom-call | flops 3000000000 | bytes 1048576 | tf_op jit(solution)/shard_map/near_back_d/pallas_call | solution.py:613
  48.4 2.2 %collective-permute-done.12.got = bf16[16,512]{1,0:T(8,128)(2,1)S(1)} collective-permute-done((bf16[16,512]{1,0:T(8,128)(2,1)S(1)}, bf16[16,512]{1,0:T(8,128)(2,1)S(1)}, u32[]{:S(2)}, u32[]{:S(2)}) %collective-permute-start.12) | collective-permute-done | bytes 16416 | tf_op jit(solution)/shard_map/ppermute | solution.py:629
  51.1 0.7 copies.1
  51.8 2.7 %collective-permute-start.15 = (bf16[32,1024]{1,0:T(8,128)(2,1)S(1)}, bf16[32,1024]{1,0:T(8,128)(2,1)S(1)}, u32[]{:S(2)}, u32[]{:S(2)}) collective-permute-start(bf16[32,1024]{1,0:T(8,128)(2,1)S(1)} %get-tuple-element.149), channel_id=1, source_target_pairs={{0,28},{1,5},{2,30},{3,7},{4,0},{5,9},{6,2},{7,11},{8,4},{9,13},{1... | collective-permute-start | bytes 196616 | tf_op jit(solution)/shard_map/ppermute | solution.py:629
  54.5 8.6 %all-to-all-start = ((bf16[8,16,512]{2,1,0:T(8,128)(2,1)}), bf16[8,16,512]{2,1,0:T(8,128)(2,1)S(1)}, u32[]{:S(2)}, u32[]{:S(2)}) async-start(bf16[8,16,512]{2,1,0:T(8,128)(2,1)} %copies.1), calls=%async_computation | async-start | bytes 262144 | tf_op jit(solution)/shard_map/all_to_all | solution.py:813
  63.6 0.6 collective-permute-done.17.refs_13_
  64.3 3.9 %collective-permute-done.16.refs_12_ = bf16[16,1024]{1,0:T(8,128)(2,1)S(1)} collective-permute-done((bf16[16,1024]{1,0:T(8,128)(2,1)S(1)}, bf16[16,1024]{1,0:T(8,128)(2,1)S(1)}, u32[]{:S(2)}, u32[]{:S(2)}) %collective-permute-start.16) | collective-permute-done | bytes 32800 | tf_op jit(solution)/shard_map/ppermute | solution.py:629
  68.2 1.3 %combine.1 = (bf16[256,512]{1,0:T(8,128)(2,1)}, bf16[256,512]{1,0:T(8,128)(2,1)}, bf16[256,512]{1,0:T(8,128)(2,1)}, f32[8,128]{1,0:T(8,128)S(1)}) custom-call(bf16[256,128]{1,0:T(8,128)(2,1)S(1)} %get-tuple-element.117.refs_0_, bf16[256,128]{1,0:T(8,128)(2,1)S(1)} %get-tuple-element.122.refs_1_, bf16[256,128]{1,0:T(8,128)(2,1)S(1)} %get-tuple-element.126.refs_2_, ...), custom_call_target="tpu_custom_call" | custom-call | flops 1000000000 | bytes 1048576 | tf_op jit(solution)/shard_map/combine/pallas_call | solution.py:613
  69.5 1.2 %all-to-all-done.parts = bf16[8,16,512]{2,1,0:T(8,128)(2,1)S(1)} async-done(((bf16[8,16,512]{2,1,0:T(8,128)(2,1)}), bf16[8,16,512]{2,1,0:T(8,128)(2,1)S(1)}, u32[]{:S(2)}, u32[]{:S(2)}) %all-to-all-start) | async-done | bytes 131104 | tf_op jit(solution)/shard_map/all_to_all | solution.py:813
  70.6 0.6 last_sum.1
  (42 shorter events, 2.3 us)
Async XLA Ops:
  0.6 1.1 %copy-start.2 = (bf16[1,256,512]{2,1,0:T(8,128)(2,1)S(1)}, bf16[1,256,512]{2,1,0:T(8,128)(2,1)}, u32[]{:S(2)}) copy-start(bf16[1,256,512]{2,1,0:T(8,128)(2,1)} %param.8) | copy-start | bytes 786436
  0.6 1.1 %copy-start.1 = (bf16[1,256,512]{2,1,0:T(8,128)(2,1)S(1)}, bf16[1,256,512]{2,1,0:T(8,128)(2,1)}, u32[]{:S(2)}) copy-start(bf16[1,256,512]{2,1,0:T(8,128)(2,1)} %param.7) | copy-start | bytes 786436
  0.7 0.7 %copy-start.5 = (s32[1,256]{1,0:T(1,128)S(1)}, s32[1,256]{1,0:T(1,128)}, u32[]{:S(2)}) copy-start(s32[1,256]{1,0:T(1,128)} %seg_hbm.1) | copy-start | bytes 3076
  2.3 15.0 %collective-permute-start = (bf16[192,1152]{1,0:T(8,128)(2,1)S(1)}, bf16[192,1152]{1,0:T(8,128)(2,1)S(1)}, u32[]{:S(2)}, u32[]{:S(2)}) collective-permute-start(bf16[192,1152]{1,0:T(8,128)(2,1)S(1)} %get-tuple-element.84), channel_id=1, source_target_pairs={{0,1},{1,2},{2,3},{3,4},{4,5},{5,6},{6,7},{7,8},{8,9},{9,10},{10,1... | collective-permute-start | bytes 1327112 | tf_op jit(solution)/shard_map/ppermute | solution.py:629
  2.4 15.0 %collective-permute-start.1 = (bf16[192,1152]{1,0:T(8,128)(2,1)S(1)}, bf16[192,1152]{1,0:T(8,128)(2,1)S(1)}, u32[]{:S(2)}, u32[]{:S(2)}) collective-permute-start(bf16[192,1152]{1,0:T(8,128)(2,1)S(1)} %get-tuple-element.85), channel_id=1, source_target_pairs={{0,31},{1,0},{2,1},{3,2},{4,3},{5,4},{6,5},{7,6},{8,7},{9,8},{10,9... | collective-permute-start | bytes 1327112 | tf_op jit(solution)/shard_map/ppermute | solution.py:629
  7.5 4.4 %copy-start = (bf16[512,512]{1,0:T(8,128)(2,1)S(1)}, bf16[512,512]{1,0:T(8,128)(2,1)}, u32[]{:S(2)}) copy-start(bf16[512,512]{1,0:T(8,128)(2,1)} %w_hbm.1) | copy-start | bytes 1572868
  7.5 4.4 %copy-start.3 = (bf16[1,256,512]{2,1,0:T(8,128)(2,1)S(1)}, bf16[1,256,512]{2,1,0:T(8,128)(2,1)}, u32[]{:S(2)}) copy-start(bf16[1,256,512]{2,1,0:T(8,128)(2,1)} %param.6) | copy-start | bytes 786436
  7.5 4.4 %copy-start.4 = (bf16[1,256,512]{2,1,0:T(8,128)(2,1)S(1)}, bf16[1,256,512]{2,1,0:T(8,128)(2,1)}, u32[]{:S(2)}) copy-start(bf16[1,256,512]{2,1,0:T(8,128)(2,1)} %param.11) | copy-start | bytes 786436
  7.5 1.3 %collective-permute-start.2 = (bf16[48,1152]{1,0:T(8,128)(2,1)S(1)}, bf16[48,1152]{1,0:T(8,128)(2,1)S(1)}, u32[]{:S(2)}, u32[]{:S(2)}) collective-permute-start(bf16[48,1152]{1,0:T(8,128)(2,1)S(1)} %get-tuple-element.86.far), channel_id=1, source_target_pairs={{0,1},{1,0},{2,3},{3,2},{4,5},{5,4},{6,7},{7,6},{8,9},{9,8},{10,11... | collective-permute-start | bytes 331784 | tf_op jit(solution)/shard_map/ppermute | solution.py:629
  8.8 8.5 %collective-permute-start.3 = (bf16[64,1152]{1,0:T(8,128)(2,1)S(1)}, bf16[64,1152]{1,0:T(8,128)(2,1)S(1)}, u32[]{:S(2)}, u32[]{:S(2)}) collective-permute-start(bf16[64,1152]{1,0:T(8,128)(2,1)S(1)} %get-tuple-element.87), channel_id=1, source_target_pairs={{0,2},{1,31},{2,4},{3,1},{4,6},{5,3},{6,8},{7,5},{8,10},{9,7},{10,... | collective-permute-start | bytes 442376 | tf_op jit(solution)/shard_map/ppermute | solution.py:629
  8.9 8.5 %collective-permute-start.5 = (bf16[16,1152]{1,0:T(8,128)(2,1)S(1)}, bf16[16,1152]{1,0:T(8,128)(2,1)S(1)}, u32[]{:S(2)}, u32[]{:S(2)}) collective-permute-start(bf16[16,1152]{1,0:T(8,128)(2,1)S(1)} %get-tuple-element.98), channel_id=1, source_target_pairs={{0,6},{1,7},{2,28},{3,29},{4,10},{5,11},{6,0},{7,1},{8,14},{9,15},... | collective-permute-start | bytes 110600 | tf_op jit(solution)/shard_map/ppermute | solution.py:629
  11.9 8.0 %collective-permute-start.4 = (bf16[32,1152]{1,0:T(8,128)(2,1)S(1)}, bf16[32,1152]{1,0:T(8,128)(2,1)S(1)}, u32[]{:S(2)}, u32[]{:S(2)}) collective-permute-start(bf16[32,1152]{1,0:T(8,128)(2,1)S(1)} %get-tuple-element.97), channel_id=1, source_target_pairs={{0,4},{1,29},{2,6},{3,31},{4,8},{5,1},{6,10},{7,3},{8,12},{9,5},{1... | collective-permute-start | bytes 221192 | tf_op jit(solution)/shard_map/ppermute | solution.py:629
  19.9 1.8 %collective-permute-start.6 = (bf16[112,1152]{1,0:T(8,128)(2,1)S(1)}, bf16[112,1152]{1,0:T(8,128)(2,1)S(1)}, u32[]{:S(2)}, u32[]{:S(2)}) collective-permute-start(bf16[112,1152]{1,0:T(8,128)(2,1)S(1)} %get-tuple-element.100), channel_id=1, source_target_pairs={{0,1},{1,0},{2,3},{3,2},{4,5},{5,4},{6,7},{7,6},{8,9},{9,8},{10,11... | collective-permute-start | bytes 774152 | tf_op jit(solution)/shard_map/ppermute | solution.py:629
  27.6 2.3 %collective-permute-start.7 = (bf16[480,512]{1,0:T(8,128)(2,1)S(1)}, bf16[480,512]{1,0:T(8,128)(2,1)S(1)}, u32[]{:S(2)}, u32[]{:S(2)}) collective-permute-start(bf16[480,512]{1,0:T(8,128)(2,1)S(1)} %get-tuple-element.111), channel_id=1, source_target_pairs={{0,1},{1,0},{2,3},{3,2},{4,5},{5,4},{6,7},{7,6},{8,9},{9,8},{10,11... | collective-permute-start | bytes 1474568 | tf_op jit(solution)/shard_map/ppermute | solution.py:629
  30.1 7.1 %collective-permute-start.8 = (bf16[128,512]{1,0:T(8,128)(2,1)S(1)}, bf16[128,512]{1,0:T(8,128)(2,1)S(1)}, u32[]{:S(2)}, u32[]{:S(2)}) collective-permute-start(bf16[128,512]{1,0:T(8,128)(2,1)S(1)} %get-tuple-element.119), channel_id=1, source_target_pairs={{0,24},{1,25},{2,26},{3,27},{4,28},{5,29},{6,30},{7,31},{8,16},{9,... | collective-permute-start | bytes 393224 | tf_op jit(solution)/shard_map/ppermute | solution.py:629
  31.9 6.8 %collective-permute-start.11 = (bf16[64,1024]{1,0:T(8,128)(2,1)S(1)}, bf16[64,1024]{1,0:T(8,128)(2,1)S(1)}, u32[]{:S(2)}, u32[]{:S(2)}) collective-permute-start(bf16[64,1024]{1,0:T(8,128)(2,1)S(1)} %get-tuple-element.115._), channel_id=1, source_target_pairs={{0,30},{1,3},{2,0},{3,5},{4,2},{5,7},{6,4},{7,9},{8,6},{9,11},{10,... | collective-permute-start | bytes 393224 | tf_op jit(solution)/shard_map/ppermute | solution.py:629
  37.2 4.4 %collective-permute-start.9 = (bf16[64,512]{1,0:T(8,128)(2,1)S(1)}, bf16[64,512]{1,0:T(8,128)(2,1)S(1)}, u32[]{:S(2)}, u32[]{:S(2)}) collective-permute-start(bf16[64,512]{1,0:T(8,128)(2,1)S(1)} %get-tuple-element.124), channel_id=1, source_target_pairs={{0,8},{1,9},{2,10},{3,11},{4,12},{5,13},{6,14},{7,15},{8,0},{9,1},... | collective-permute-start | bytes 196616 | tf_op jit(solution)/shard_map/ppermute | solution.py:629
  41.6 5.2 %collective-permute-start.10 = (bf16[32,512]{1,0:T(8,128)(2,1)S(1)}, bf16[32,512]{1,0:T(8,128)(2,1)S(1)}, u32[]{:S(2)}, u32[]{:S(2)}) collective-permute-start(bf16[32,512]{1,0:T(8,128)(2,1)S(1)} %get-tuple-element.133), channel_id=1, source_target_pairs={{0,6},{1,7},{2,4},{3,5},{4,2},{5,3},{6,0},{7,1},{8,14},{9,15},{10,... | collective-permute-start | bytes 98312 | tf_op jit(solution)/shard_map/ppermute | solution.py:629
  46.8 3.8 %collective-permute-start.12 = (bf16[16,512]{1,0:T(8,128)(2,1)S(1)}, bf16[16,512]{1,0:T(8,128)(2,1)S(1)}, u32[]{:S(2)}, u32[]{:S(2)}) collective-permute-start(bf16[16,512]{1,0:T(8,128)(2,1)S(1)} %get-tuple-element.143), channel_id=1, source_target_pairs={{0,2},{1,3},{2,0},{3,1},{4,6},{5,7},{6,4},{7,5},{8,10},{9,11},{10,... | collective-permute-start | bytes 49160 | tf_op jit(solution)/shard_map/ppermute | solution.py:629
  50.6 17.5 %collective-permute-start.13 = (bf16[192,1024]{1,0:T(8,128)(2,1)S(1)}, bf16[192,1024]{1,0:T(8,128)(2,1)S(1)}, u32[]{:S(2)}, u32[]{:S(2)}) collective-permute-start(bf16[192,1024]{1,0:T(8,128)(2,1)S(1)} %get-tuple-element.144), channel_id=1, source_target_pairs={{0,31},{1,0},{2,1},{3,2},{4,3},{5,4},{6,5},{7,6},{8,7},{9,8},{10,9... | collective-permute-start | bytes 1179656 | tf_op jit(solution)/shard_map/ppermute | solution.py:629
  50.6 17.5 %collective-permute-start.14 = (bf16[192,1024]{1,0:T(8,128)(2,1)S(1)}, bf16[192,1024]{1,0:T(8,128)(2,1)S(1)}, u32[]{:S(2)}, u32[]{:S(2)}) collective-permute-start(bf16[192,1024]{1,0:T(8,128)(2,1)S(1)} %get-tuple-element.145), channel_id=1, source_target_pairs={{0,1},{1,2},{2,3},{3,4},{4,5},{5,6},{6,7},{7,8},{8,9},{9,10},{10,1... | collective-permute-start | bytes 1179656 | tf_op jit(solution)/shard_map/ppermute | solution.py:629
  51.8 11.3 %collective-permute-start.15 = (bf16[32,1024]{1,0:T(8,128)(2,1)S(1)}, bf16[32,1024]{1,0:T(8,128)(2,1)S(1)}, u32[]{:S(2)}, u32[]{:S(2)}) collective-permute-start(bf16[32,1024]{1,0:T(8,128)(2,1)S(1)} %get-tuple-element.149), channel_id=1, source_target_pairs={{0,28},{1,5},{2,30},{3,7},{4,0},{5,9},{6,2},{7,11},{8,4},{9,13},{1... | collective-permute-start | bytes 196616 | tf_op jit(solution)/shard_map/ppermute | solution.py:629
  54.5 16.2 %all-to-all-start = ((bf16[8,16,512]{2,1,0:T(8,128)(2,1)}), bf16[8,16,512]{2,1,0:T(8,128)(2,1)S(1)}, u32[]{:S(2)}, u32[]{:S(2)}) async-start(bf16[8,16,512]{2,1,0:T(8,128)(2,1)} %copies.1), calls=%async_computation | async-start | bytes 262144 | tf_op jit(solution)/shard_map/all_to_all | solution.py:813
  63.0 1.3 %collective-permute-start.17 = (bf16[32,1024]{1,0:T(8,128)(2,1)S(1)}, bf16[32,1024]{1,0:T(8,128)(2,1)S(1)}, u32[]{:S(2)}, u32[]{:S(2)}) collective-permute-start(bf16[32,1024]{1,0:T(8,128)(2,1)S(1)} %split_3.1.refs_16_), channel_id=1, source_target_pairs={{0,1},{1,0},{2,3},{3,2},{4,5},{5,4},{6,7},{7,6},{8,9},{9,8},{10,11... | collective-permute-start | bytes 196616 | tf_op jit(solution)/shard_map/ppermute | solution.py:629
  63.0 5.1 %collective-permute-start.16 = (bf16[16,1024]{1,0:T(8,128)(2,1)S(1)}, bf16[16,1024]{1,0:T(8,128)(2,1)S(1)}, u32[]{:S(2)}, u32[]{:S(2)}) collective-permute-start(bf16[16,1024]{1,0:T(8,128)(2,1)S(1)} %get-tuple-element.150), channel_id=1, source_target_pairs={{0,6},{1,7},{2,28},{3,29},{4,10},{5,11},{6,0},{7,1},{8,14},{9,15},... | collective-permute-start | bytes 98312 | tf_op jit(solution)/shard_map/ppermute | solution.py:629
  63.1 5.1 %collective-permute-start.18 = (bf16[16,1024]{1,0:T(8,128)(2,1)S(1)}, bf16[16,1024]{1,0:T(8,128)(2,1)S(1)}, u32[]{:S(2)}, u32[]{:S(2)}) collective-permute-start(bf16[16,1024]{1,0:T(8,128)(2,1)S(1)} %split_4.1), channel_id=1, source_target_pairs={{0,1},{1,0},{2,3},{3,2},{4,5},{5,4},{6,7},{7,6},{8,9},{9,8},{10,11... | collective-permute-start | bytes 98312 | tf_op jit(solution)/shard_map/ppermute | solution.py:629

commit v11 on v9

--- a/solution.py
+++ b/solution.py
@@ -298,7 +298,7 @@
 
 def block_at(block):
     x, y, core = block // 8, block // 2 % 4, block % 2
-    return 16 * (16 * core + 4 * x + y)
+    return 16 * (16 * core + 4 * (0, 2, 3, 1)[x] + y)
 
 
 def merge_kernel(
@@ -518,11 +518,12 @@
         sum4[:, lanes] = (came(64, 96) + to_4[:, lanes].astype(F32)).astype(BF16)
         sum_third[:, lanes] = (came(96, 112) + to_third[:, lanes].astype(F32)).astype(BF16)
     total[...] = keep[...] + message[0:256].astype(F32)
-    halve(total, 16, keep_out, give_out)
-
-
-def halve(total, divisor, keep, give):
-    side = lax.axis_index("ctx") // divisor % 2
+    halve(total, (8, 16), keep_out, give_out)
+
+
+def halve(total, divisors, keep, give):
+    index = lax.axis_index("ctx")
+    side = sum(index // divisor for divisor in divisors) % 2
     half = total.shape[0] // 2
     keep[...] = total[pl.ds(pl.multiple_of(side * half, half), half)]
     give[...] = total[pl.ds(pl.multiple_of((1 - side) * half, half), half)].astype(BF16)
@@ -541,7 +542,7 @@
 def halve_kernel(divisor, keep, got, *refs):
     keep_out, give_out, total = refs[-3:]
     total[...] = keep[...] + got[...].astype(F32)
-    halve(total, divisor, keep_out, give_out)
+    halve(total, (divisor,), keep_out, give_out)
 
 
 def copies_kernel(keep, got, *refs):
@@ -762,7 +763,7 @@
         [pltpu.VMEM((256, WIDTH), F32)],
         in_hbm=1,
     )
-    got_w = moved(give, lambda i: i ^ 24)
+    got_w = moved(give, lambda i: i ^ 8)
     back3 = moved(sum3, back_3)
     back4 = moved(sum4, back_4)
     layer_out, projected = call(
@@ -774,7 +775,7 @@
         in_hbm=1,
         to_hbm=(0,),
     )
-    keep, got_w = halved(keep, got_w, 8, lambda i: i ^ 8, projected)
+    keep, got_w = halved(keep, got_w, 16, lambda i: i ^ 24, projected)
     part_b = call(
         functools.partial(near_back_kernel, NEAR_PARTS[1]),
         "near_back_b",

time: 69.9 us -> 70.4 us (level)
  the two profiles are of different devices: /device:TPU:32 before, /device:TPU:31 now
where the time goes in v11:
time: 70.4 us; the launch traced here: 70.1 us
  waiting for transfers between devices  27.3 us (39%)
  starting transfers between devices  22.2 us (32%)
  Pallas kernels  19 us (27%)
  between operations  0.87 us (1%)
  local copies, waits for them, and re-layouts  0.75 us (1%)
    ppermute x18, waiting for transfers between devices, moved(): return lax.ppermute(x, 'ctx', [(i, route(i) % count) for i in range(count)])  23 us
    pallas_call x21, Pallas kernels, call(): pl.pallas_call(kernel, name=name, out_shape=[jax.ShapeDtypeStruct(shape,...  19 us
    ppermute x18, starting transfers between devices, moved(): return lax.ppermute(x, 'ctx', [(i, route(i) % count) for i in range(count)])  14.6 us
    all_to_all x1, starting transfers between devices, body(): copies = lax.all_to_all(copies, 'dp', 0, 0, tiled=True)  7.63 us
    all_to_all x1, waiting for transfers between devices, body(): copies = lax.all_to_all(copies, 'dp', 0, 0, tiled=True)  4.24 us
  transfers between devices with their start and end apart: 19, of which 11 were waited for; matrix products, arithmetic and copies ran while one was open for 0% of the time, Pallas kernels for 16%

profile of v11, /device:TPU:31, one launch (start us, length us, event | category | flops | bytes accessed | tf_op | source)
XLA Modules:
  0.0 70.1 jit_solution(13728182736127090593)
XLA Ops:
  0.7 0.7 %copy-done.5 = s32[1,256]{1,0:T(1,128)S(1)} copy-done((s32[1,256]{1,0:T(1,128)S(1)}, s32[1,256]{1,0:T(1,128)}, u32[]{:S(2)}) %copy-start.5) | copy-done | bytes 1048
  1.7 0.6 coarsen.1
  2.3 2.2 %collective-permute-start = (bf16[192,1152]{1,0:T(8,128)(2,1)S(1)}, bf16[192,1152]{1,0:T(8,128)(2,1)S(1)}, u32[]{:S(2)}, u32[]{:S(2)}) collective-permute-start(bf16[192,1152]{1,0:T(8,128)(2,1)S(1)} %get-tuple-element.83), channel_id=1, source_target_pairs={{0,1},{1,2},{2,3},{3,4},{4,5},{5,6},{6,7},{7,8},{8,9},{9,10},{10,1... | collective-permute-start | bytes 1327112 | tf_op jit(solution)/shard_map/ppermute | solution.py:632
  4.8 1.3 %collective-permute-done.2.far_partner = bf16[48,1152]{1,0:T(8,128)(2,1)S(1)} collective-permute-done((bf16[48,1152]{1,0:T(8,128)(2,1)S(1)}, bf16[48,1152]{1,0:T(8,128)(2,1)S(1)}, u32[]{:S(2)}, u32[]{:S(2)}) %collective-permute-start.2) | collective-permute-done | bytes 110624 | tf_op jit(solution)/shard_map/ppermute | solution.py:632
  6.4 2.5 %collective-permute-start.5 = (bf16[16,1152]{1,0:T(8,128)(2,1)S(1)}, bf16[16,1152]{1,0:T(8,128)(2,1)S(1)}, u32[]{:S(2)}, u32[]{:S(2)}) collective-permute-start(bf16[16,1152]{1,0:T(8,128)(2,1)S(1)} %get-tuple-element.97), channel_id=1, source_target_pairs={{0,6},{1,7},{2,28},{3,29},{4,10},{5,11},{6,0},{7,1},{8,14},{9,15},... | collective-permute-start | bytes 110600 | tf_op jit(solution)/shard_map/ppermute | solution.py:632
  9.2 0.7 %prepare.1 = (bf16[496,512]{1,0:T(8,128)(2,1)S(1)}, f32[256,512]{1,0:T(8,128)S(1)}, bf16[512,512]{1,0:T(8,128)(2,1)S(1)}, bf16[256,512]{1,0:T(8,128)(2,1)S(1)}) custom-call(bf16[256,512]{1,0:T(8,128)(2,1)S(1)} %bitcast.10, bf16[256,512]{1,0:T(8,128)(2,1)S(1)} %bitcast.11, bf16[512,512]{1,0:T(8,128)(2,1)S(1)} %copy-done), custom_call_target="tpu_custom_call" | custom-call | flops 1000000000 | bytes 1048576 | tf_op jit(solution)/shard_map/prepare/pallas_call | solution.py:616
  9.9 5.5 %collective-permute-done.3.got3 = bf16[64,1152]{1,0:T(8,128)(2,1)S(1)} collective-permute-done((bf16[64,1152]{1,0:T(8,128)(2,1)S(1)}, bf16[64,1152]{1,0:T(8,128)(2,1)S(1)}, u32[]{:S(2)}, u32[]{:S(2)}) %collective-permute-start.3) | collective-permute-done | bytes 147488 | tf_op jit(solution)/shard_map/ppermute | solution.py:632
  15.4 3.4 %collective-permute-done.1.high.refs_7_ = bf16[192,1152]{1,0:T(8,128)(2,1)S(1)} collective-permute-done((bf16[192,1152]{1,0:T(8,128)(2,1)S(1)}, bf16[192,1152]{1,0:T(8,128)(2,1)S(1)}, u32[]{:S(2)}, u32[]{:S(2)}) %collective-permute-start.1) | collective-permute-done | bytes 442400 | tf_op jit(solution)/shard_map/ppermute | solution.py:632
  18.9 1.1 %collective-permute-start.6 = (bf16[112,1152]{1,0:T(8,128)(2,1)S(1)}, bf16[112,1152]{1,0:T(8,128)(2,1)S(1)}, u32[]{:S(2)}, u32[]{:S(2)}) collective-permute-start(bf16[112,1152]{1,0:T(8,128)(2,1)S(1)} %get-tuple-element.99), channel_id=1, source_target_pairs={{0,1},{1,0},{2,3},{3,2},{4,5},{5,4},{6,7},{7,6},{8,9},{9,8},{10,11... | collective-permute-start | bytes 774152 | tf_op jit(solution)/shard_map/ppermute | solution.py:632
  20.0 1.7 %near.1 = (bf16[4,896,256]{2,1,0:T(8,128)(2,1)S(1)}, f32[256,512]{1,0:T(8,128)S(1)}, f32[256,256]{1,0:T(8,128)S(1)}, bf16[192,512]{1,0:T(8,128)(2,1)S(1)}, bf16[192,256]{1,0:T(8,128)(2,1)S(1)}) custom-call(bf16[496,512]{1,0:T(8,128)(2,1)S(1)} %get-tuple-element.80.q_all.refs_1_, bf16[496,128]{1,0:T(8,128)(2,1)S(1)} %documents.1.qdoc, ...), custom_call_target="tpu_custom_call" | custom-call | flops 49999998976 | bytes 1048576 | tf_op jit(solution)/shard_map/near/pallas_call | solution.py:616
  21.7 4.8 %merge.1 = (bf16[256,512]{1,0:T(8,128)(2,1)S(1)}, f32[256,512]{1,0:T(8,128)S(1)}, bf16[256,512]{1,0:T(8,128)(2,1)S(1)}, bf16[4,96,128]{2,1,0:T(8,128)(2,1)S(1)},...) custom-call(bf16[496,512]{1,0:T(8,128)(2,1)S(1)} %get-tuple-element.80.q_all.refs_1_, ...), custom_call_target="tpu_custom_call" | custom-call | flops 6000000000 | bytes 1048576 | tf_op jit(solution)/shard_map/merge/pallas_call | solution.py:616
  26.5 1.1 %far_back.1 = (bf16[48,512]{1,0:T(8,128)(2,1)S(1)}, bf16[32,1024]{1,0:T(8,128)(2,1)S(1)}, bf16[32,1024]{1,0:T(8,128)(2,1)S(1)}, bf16[16,1024]{1,0:T(8,128)(2,1)S(1)}, bf16[480,512]{1,0:T(8,128)(2,1)S(1)}) custom-call(bf16[4,96,128]{2,1,0:T(8,128)(2,1)S(1)} %get-tuple-element.102.p_in, bf16[496,512]{1,0:T(8,128)(2,1)S(1)} %get-tuple-element.80.q_all.refs_1_, ...), custom_call_target="tpu_custom_call" | custom-call | flops 1000000000 | bytes 1048576 | tf_op jit(solution)/shard_map/far_back/pallas_call | solution.py:616
  27.9 1.4 %near_back_a.1 = (bf16[256,128]{1,0:T(8,128)(2,1)S(1)}, bf16[256,128]{1,0:T(8,128)(2,1)S(1)}, bf16[256,128]{1,0:T(8,128)(2,1)S(1)}, bf16[2,192,128]{2,1,0:T(8,128)(2,1)S(1)}, bf16[2,192,128]{2,1,0:T(8,128)(2,1)S(1)}) custom-call(bf16[4,896,256]{2,1,0:T(8,128)(2,1)S(1)} %get-tuple-element.111.refs_0_, bf16[496,512]{1,0:T(8,128)(2,1)S(1)} %get-tuple-element.80.q_all.refs_1_, ...), custom_call_target="tpu_custom_call" | custom-call | flops 3000000000 | bytes 1048576 | tf_op jit(solution)/shard_map/near_back_a/pallas_call | solution.py:616
  29.4 0.4 collective-permute-done.7.message
  30.0 0.9 %collective-permute-start.12 = (bf16[32,1024]{1,0:T(8,128)(2,1)S(1)}, bf16[32,1024]{1,0:T(8,128)(2,1)S(1)}, u32[]{:S(2)}, u32[]{:S(2)}) collective-permute-start(bf16[32,1024]{1,0:T(8,128)(2,1)S(1)} %get-tuple-element.135), channel_id=1, source_target_pairs={{0,28},{1,5},{2,30},{3,7},{4,0},{5,9},{6,2},{7,11},{8,4},{9,13},{1... | collective-permute-start | bytes 196616 | tf_op jit(solution)/shard_map/ppermute | solution.py:632
  31.0 1.0 %project.1 = (bf16[256,512]{1,0:T(8,128)(2,1)}, f32[8,128]{1,0:T(8,128)S(1)}) custom-call(bf16[256,512]{1,0:T(8,128)(2,1)S(1)} %get-tuple-element.100.attended, bf16[512,512]{1,0:T(8,128)(2,1)S(1)} %get-tuple-element.101.w, bf16[64,1024]{1,0:T(8,128)(2,1)S(1)} %get-tuple-element.114._), custom_call_target="tpu_custom_call" | custom-call | flops 1000000000 | bytes 1048576 | tf_op jit(solution)/shard_map/project/pallas_call | solution.py:616
  32.0 3.0 %collective-permute-done.8.got = bf16[128,512]{1,0:T(8,128)(2,1)S(1)} collective-permute-done((bf16[128,512]{1,0:T(8,128)(2,1)S(1)}, bf16[128,512]{1,0:T(8,128)(2,1)S(1)}, u32[]{:S(2)}, u32[]{:S(2)}) %collective-permute-start.8) | collective-permute-done | bytes 131104 | tf_op jit(solution)/shard_map/ppermute | solution.py:632
  35.1 1.4 %near_back_b.1 = (bf16[256,128]{1,0:T(8,128)(2,1)S(1)}, bf16[256,128]{1,0:T(8,128)(2,1)S(1)}, bf16[256,128]{1,0:T(8,128)(2,1)S(1)}, bf16[2,192,128]{2,1,0:T(8,128)(2,1)S(1)}, bf16[2,192,128]{2,1,0:T(8,128)(2,1)S(1)}) custom-call(bf16[4,896,256]{2,1,0:T(8,128)(2,1)S(1)} %get-tuple-element.111.refs_0_, bf16[496,512]{1,0:T(8,128)(2,1)S(1)} %get-tuple-element.80.q_all.refs_1_, ...), custom_call_target="tpu_custom_call" | custom-call | flops 3000000000 | bytes 1048576 | tf_op jit(solution)/shard_map/near_back_b/pallas_call | solution.py:616
  36.6 2.8 %collective-permute-done.9.got = bf16[64,512]{1,0:T(8,128)(2,1)S(1)} collective-permute-done((bf16[64,512]{1,0:T(8,128)(2,1)S(1)}, bf16[64,512]{1,0:T(8,128)(2,1)S(1)}, u32[]{:S(2)}, u32[]{:S(2)}) %collective-permute-start.9) | collective-permute-done | bytes 65568 | tf_op jit(solution)/shard_map/ppermute | solution.py:632
  39.5 1.4 %collective-permute-start.10 = (bf16[32,512]{1,0:T(8,128)(2,1)S(1)}, bf16[32,512]{1,0:T(8,128)(2,1)S(1)}, u32[]{:S(2)}, u32[]{:S(2)}) collective-permute-start(bf16[32,512]{1,0:T(8,128)(2,1)S(1)} %get-tuple-element.132), channel_id=1, source_target_pairs={{0,6},{1,7},{2,4},{3,5},{4,2},{5,3},{6,0},{7,1},{8,14},{9,15},{10,... | collective-permute-start | bytes 98312 | tf_op jit(solution)/shard_map/ppermute | solution.py:632
  40.9 1.4 %near_back_c.1 = (bf16[256,128]{1,0:T(8,128)(2,1)S(1)}, bf16[256,128]{1,0:T(8,128)(2,1)S(1)}, bf16[256,128]{1,0:T(8,128)(2,1)S(1)}, bf16[2,192,128]{2,1,0:T(8,128)(2,1)S(1)}, bf16[2,192,128]{2,1,0:T(8,128)(2,1)S(1)}) custom-call(bf16[4,896,256]{2,1,0:T(8,128)(2,1)S(1)} %get-tuple-element.111.refs_0_, bf16[496,512]{1,0:T(8,128)(2,1)S(1)} %get-tuple-element.80.q_all.refs_1_, ...), custom_call_target="tpu_custom_call" | custom-call | flops 3000000000 | bytes 1048576 | tf_op jit(solution)/shard_map/near_back_c/pallas_call | solution.py:616
  42.3 1.2 %collective-permute-done.10.got = bf16[32,512]{1,0:T(8,128)(2,1)S(1)} collective-permute-done((bf16[32,512]{1,0:T(8,128)(2,1)S(1)}, bf16[32,512]{1,0:T(8,128)(2,1)S(1)}, u32[]{:S(2)}, u32[]{:S(2)}) %collective-permute-start.10) | collective-permute-done | bytes 32800 | tf_op jit(solution)/shard_map/ppermute | solution.py:632
  43.7 1.5 %near_back_d.1 = (bf16[256,128]{1,0:T(8,128)(2,1)S(1)}, bf16[256,128]{1,0:T(8,128)(2,1)S(1)}, bf16[256,128]{1,0:T(8,128)(2,1)S(1)}, bf16[192,1024]{1,0:T(8,128)(2,1)S(1)}, bf16[192,1024]{1,0:T(8,128)(2,1)S(1)}) custom-call(bf16[4,896,256]{2,1,0:T(8,128)(2,1)S(1)} %get-tuple-element.111.refs_0_, bf16[496,512]{1,0:T(8,128)(2,1)S(1)} %get-tuple-element.80.q_all.refs_1_, ...), custom_call_target="tpu_custom_call" | custom-call | flops 3000000000 | bytes 1048576 | tf_op jit(solution)/shard_map/near_back_d/pallas_call | solution.py:616
  45.2 1.3 %collective-permute-done.13.got = bf16[16,512]{1,0:T(8,128)(2,1)S(1)} collective-permute-done((bf16[16,512]{1,0:T(8,128)(2,1)S(1)}, bf16[16,512]{1,0:T(8,128)(2,1)S(1)}, u32[]{:S(2)}, u32[]{:S(2)}) %collective-permute-start.13) | collective-permute-done | bytes 16416 | tf_op jit(solution)/shard_map/ppermute | solution.py:632
  46.5 4.7 %collective-permute-start.14 = (bf16[192,1024]{1,0:T(8,128)(2,1)S(1)}, bf16[192,1024]{1,0:T(8,128)(2,1)S(1)}, u32[]{:S(2)}, u32[]{:S(2)}) collective-permute-start(bf16[192,1024]{1,0:T(8,128)(2,1)S(1)} %get-tuple-element.144), channel_id=1, source_target_pairs={{0,31},{1,0},{2,1},{3,2},{4,3},{5,4},{6,5},{7,6},{8,7},{9,8},{10,9... | collective-permute-start | bytes 1179656 | tf_op jit(solution)/shard_map/ppermute | solution.py:632
  51.6 0.7 copies.1
  52.3 7.6 %all-to-all-start = ((bf16[8,16,512]{2,1,0:T(8,128)(2,1)}), bf16[8,16,512]{2,1,0:T(8,128)(2,1)S(1)}, u32[]{:S(2)}, u32[]{:S(2)}) async-start(bf16[8,16,512]{2,1,0:T(8,128)(2,1)} %copies.1), calls=%async_computation | async-start | bytes 262144 | tf_op jit(solution)/shard_map/all_to_all | solution.py:817
  60.0 1.2 %collective-permute-done.17.refs_13_ = bf16[48,1024]{1,0:T(8,128)(2,1)S(1)} collective-permute-done((bf16[48,1024]{1,0:T(8,128)(2,1)S(1)}, bf16[48,1024]{1,0:T(8,128)(2,1)S(1)}, u32[]{:S(2)}, u32[]{:S(2)}) %collective-permute-start.17) | collective-permute-done | bytes 98336 | tf_op jit(solution)/shard_map/ppermute | solution.py:632
  61.2 2.8 %collective-permute-done.16.refs_12_ = bf16[16,1024]{1,0:T(8,128)(2,1)S(1)} collective-permute-done((bf16[16,1024]{1,0:T(8,128)(2,1)S(1)}, bf16[16,1024]{1,0:T(8,128)(2,1)S(1)}, u32[]{:S(2)}, u32[]{:S(2)}) %collective-permute-start.16) | collective-permute-done | bytes 32800 | tf_op jit(solution)/shard_map/ppermute | solution.py:632
  64.0 1.3 %combine.1 = (bf16[256,512]{1,0:T(8,128)(2,1)}, bf16[256,512]{1,0:T(8,128)(2,1)}, bf16[256,512]{1,0:T(8,128)(2,1)}, f32[8,128]{1,0:T(8,128)S(1)}) custom-call(bf16[256,128]{1,0:T(8,128)(2,1)S(1)} %get-tuple-element.116.refs_0_, bf16[256,128]{1,0:T(8,128)(2,1)S(1)} %get-tuple-element.121.refs_1_, bf16[256,128]{1,0:T(8,128)(2,1)S(1)} %get-tuple-element.125.refs_2_, ...), custom_call_target="tpu_custom_call" | custom-call | flops 1000000000 | bytes 1048576 | tf_op jit(solution)/shard_map/combine/pallas_call | solution.py:616
  65.3 4.2 %all-to-all-done.parts = bf16[8,16,512]{2,1,0:T(8,128)(2,1)S(1)} async-done(((bf16[8,16,512]{2,1,0:T(8,128)(2,1)}), bf16[8,16,512]{2,1,0:T(8,128)(2,1)S(1)}, u32[]{:S(2)}, u32[]{:S(2)}) %all-to-all-start) | async-done | bytes 131104 | tf_op jit(solution)/shard_map/all_to_all | solution.py:817
  69.5 0.6 last_sum.1
  (39 shorter events, 2.5 us)
Async XLA Ops:
  0.6 1.0 %copy-start.2 = (bf16[1,256,512]{2,1,0:T(8,128)(2,1)S(1)}, bf16[1,256,512]{2,1,0:T(8,128)(2,1)}, u32[]{:S(2)}) copy-start(bf16[1,256,512]{2,1,0:T(8,128)(2,1)} %param.8) | copy-start | bytes 786436
  0.6 1.0 %copy-start.1 = (bf16[1,256,512]{2,1,0:T(8,128)(2,1)S(1)}, bf16[1,256,512]{2,1,0:T(8,128)(2,1)}, u32[]{:S(2)}) copy-start(bf16[1,256,512]{2,1,0:T(8,128)(2,1)} %param.7) | copy-start | bytes 786436
  0.7 0.7 %copy-start.5 = (s32[1,256]{1,0:T(1,128)S(1)}, s32[1,256]{1,0:T(1,128)}, u32[]{:S(2)}) copy-start(s32[1,256]{1,0:T(1,128)} %seg_hbm.1) | copy-start | bytes 3076
  2.3 13.1 %collective-permute-start = (bf16[192,1152]{1,0:T(8,128)(2,1)S(1)}, bf16[192,1152]{1,0:T(8,128)(2,1)S(1)}, u32[]{:S(2)}, u32[]{:S(2)}) collective-permute-start(bf16[192,1152]{1,0:T(8,128)(2,1)S(1)} %get-tuple-element.83), channel_id=1, source_target_pairs={{0,1},{1,2},{2,3},{3,4},{4,5},{5,6},{6,7},{7,8},{8,9},{9,10},{10,1... | collective-permute-start | bytes 1327112 | tf_op jit(solution)/shard_map/ppermute | solution.py:632
  4.6 14.3 %collective-permute-start.1 = (bf16[192,1152]{1,0:T(8,128)(2,1)S(1)}, bf16[192,1152]{1,0:T(8,128)(2,1)S(1)}, u32[]{:S(2)}, u32[]{:S(2)}) collective-permute-start(bf16[192,1152]{1,0:T(8,128)(2,1)S(1)} %get-tuple-element.84), channel_id=1, source_target_pairs={{0,31},{1,0},{2,1},{3,2},{4,3},{5,4},{6,5},{7,6},{8,7},{9,8},{10,9... | collective-permute-start | bytes 1327112 | tf_op jit(solution)/shard_map/ppermute | solution.py:632
  4.6 4.6 %copy-start = (bf16[512,512]{1,0:T(8,128)(2,1)S(1)}, bf16[512,512]{1,0:T(8,128)(2,1)}, u32[]{:S(2)}) copy-start(bf16[512,512]{1,0:T(8,128)(2,1)} %w_hbm.1) | copy-start | bytes 1572868
  4.6 4.6 %copy-start.3 = (bf16[1,256,512]{2,1,0:T(8,128)(2,1)S(1)}, bf16[1,256,512]{2,1,0:T(8,128)(2,1)}, u32[]{:S(2)}) copy-start(bf16[1,256,512]{2,1,0:T(8,128)(2,1)} %param.6) | copy-start | bytes 786436
  4.6 4.6 %copy-start.4 = (bf16[1,256,512]{2,1,0:T(8,128)(2,1)S(1)}, bf16[1,256,512]{2,1,0:T(8,128)(2,1)}, u32[]{:S(2)}) copy-start(bf16[1,256,512]{2,1,0:T(8,128)(2,1)} %param.11) | copy-start | bytes 786436
  4.6 1.6 %collective-permute-start.2 = (bf16[48,1152]{1,0:T(8,128)(2,1)S(1)}, bf16[48,1152]{1,0:T(8,128)(2,1)S(1)}, u32[]{:S(2)}, u32[]{:S(2)}) collective-permute-start(bf16[48,1152]{1,0:T(8,128)(2,1)S(1)} %get-tuple-element.85.far), channel_id=1, source_target_pairs={{0,1},{1,0},{2,3},{3,2},{4,5},{5,4},{6,7},{7,6},{8,9},{9,8},{10,11... | collective-permute-start | bytes 331784 | tf_op jit(solution)/shard_map/ppermute | solution.py:632
  6.2 9.3 %collective-permute-start.3 = (bf16[64,1152]{1,0:T(8,128)(2,1)S(1)}, bf16[64,1152]{1,0:T(8,128)(2,1)S(1)}, u32[]{:S(2)}, u32[]{:S(2)}) collective-permute-start(bf16[64,1152]{1,0:T(8,128)(2,1)S(1)} %get-tuple-element.86), channel_id=1, source_target_pairs={{0,2},{1,31},{2,4},{3,1},{4,6},{5,3},{6,8},{7,5},{8,10},{9,7},{10,... | collective-permute-start | bytes 442376 | tf_op jit(solution)/shard_map/ppermute | solution.py:632
  6.4 12.5 %collective-permute-start.5 = (bf16[16,1152]{1,0:T(8,128)(2,1)S(1)}, bf16[16,1152]{1,0:T(8,128)(2,1)S(1)}, u32[]{:S(2)}, u32[]{:S(2)}) collective-permute-start(bf16[16,1152]{1,0:T(8,128)(2,1)S(1)} %get-tuple-element.97), channel_id=1, source_target_pairs={{0,6},{1,7},{2,28},{3,29},{4,10},{5,11},{6,0},{7,1},{8,14},{9,15},... | collective-permute-start | bytes 110600 | tf_op jit(solution)/shard_map/ppermute | solution.py:632
  8.9 10.0 %collective-permute-start.4 = (bf16[32,1152]{1,0:T(8,128)(2,1)S(1)}, bf16[32,1152]{1,0:T(8,128)(2,1)S(1)}, u32[]{:S(2)}, u32[]{:S(2)}) collective-permute-start(bf16[32,1152]{1,0:T(8,128)(2,1)S(1)} %get-tuple-element.96), channel_id=1, source_target_pairs={{0,4},{1,29},{2,6},{3,31},{4,8},{5,1},{6,10},{7,3},{8,12},{9,5},{1... | collective-permute-start | bytes 221192 | tf_op jit(solution)/shard_map/ppermute | solution.py:632
  18.9 2.8 %collective-permute-start.6 = (bf16[112,1152]{1,0:T(8,128)(2,1)S(1)}, bf16[112,1152]{1,0:T(8,128)(2,1)S(1)}, u32[]{:S(2)}, u32[]{:S(2)}) collective-permute-start(bf16[112,1152]{1,0:T(8,128)(2,1)S(1)} %get-tuple-element.99), channel_id=1, source_target_pairs={{0,1},{1,0},{2,3},{3,2},{4,5},{5,4},{6,7},{7,6},{8,9},{9,8},{10,11... | collective-permute-start | bytes 774152 | tf_op jit(solution)/shard_map/ppermute | solution.py:632
  27.6 2.1 %collective-permute-start.7 = (bf16[480,512]{1,0:T(8,128)(2,1)S(1)}, bf16[480,512]{1,0:T(8,128)(2,1)S(1)}, u32[]{:S(2)}, u32[]{:S(2)}) collective-permute-start(bf16[480,512]{1,0:T(8,128)(2,1)S(1)} %get-tuple-element.110), channel_id=1, source_target_pairs={{0,1},{1,0},{2,3},{3,2},{4,5},{5,4},{6,7},{7,6},{8,9},{9,8},{10,11... | collective-permute-start | bytes 1474568 | tf_op jit(solution)/shard_map/ppermute | solution.py:632
  29.9 5.0 %collective-permute-start.8 = (bf16[128,512]{1,0:T(8,128)(2,1)S(1)}, bf16[128,512]{1,0:T(8,128)(2,1)S(1)}, u32[]{:S(2)}, u32[]{:S(2)}) collective-permute-start(bf16[128,512]{1,0:T(8,128)(2,1)S(1)} %get-tuple-element.118), channel_id=1, source_target_pairs={{0,8},{1,9},{2,10},{3,11},{4,12},{5,13},{6,14},{7,15},{8,0},{9,1},... | collective-permute-start | bytes 393224 | tf_op jit(solution)/shard_map/ppermute | solution.py:632
  30.0 6.5 %collective-permute-start.12 = (bf16[32,1024]{1,0:T(8,128)(2,1)S(1)}, bf16[32,1024]{1,0:T(8,128)(2,1)S(1)}, u32[]{:S(2)}, u32[]{:S(2)}) collective-permute-start(bf16[32,1024]{1,0:T(8,128)(2,1)S(1)} %get-tuple-element.135), channel_id=1, source_target_pairs={{0,28},{1,5},{2,30},{3,7},{4,0},{5,9},{6,2},{7,11},{8,4},{9,13},{1... | collective-permute-start | bytes 196616 | tf_op jit(solution)/shard_map/ppermute | solution.py:632
  31.0 5.6 %collective-permute-start.11 = (bf16[64,1024]{1,0:T(8,128)(2,1)S(1)}, bf16[64,1024]{1,0:T(8,128)(2,1)S(1)}, u32[]{:S(2)}, u32[]{:S(2)}) collective-permute-start(bf16[64,1024]{1,0:T(8,128)(2,1)S(1)} %get-tuple-element.114._), channel_id=1, source_target_pairs={{0,30},{1,3},{2,0},{3,5},{4,2},{5,7},{6,4},{7,9},{8,6},{9,11},{10,... | collective-permute-start | bytes 393224 | tf_op jit(solution)/shard_map/ppermute | solution.py:632
  35.0 4.4 %collective-permute-start.9 = (bf16[64,512]{1,0:T(8,128)(2,1)S(1)}, bf16[64,512]{1,0:T(8,128)(2,1)S(1)}, u32[]{:S(2)}, u32[]{:S(2)}) collective-permute-start(bf16[64,512]{1,0:T(8,128)(2,1)S(1)} %get-tuple-element.123), channel_id=1, source_target_pairs={{0,24},{1,25},{2,26},{3,27},{4,28},{5,29},{6,30},{7,31},{8,16},{9,... | collective-permute-start | bytes 196616 | tf_op jit(solution)/shard_map/ppermute | solution.py:632
  39.5 4.1 %collective-permute-start.10 = (bf16[32,512]{1,0:T(8,128)(2,1)S(1)}, bf16[32,512]{1,0:T(8,128)(2,1)S(1)}, u32[]{:S(2)}, u32[]{:S(2)}) collective-permute-start(bf16[32,512]{1,0:T(8,128)(2,1)S(1)} %get-tuple-element.132), channel_id=1, source_target_pairs={{0,6},{1,7},{2,4},{3,5},{4,2},{5,3},{6,0},{7,1},{8,14},{9,15},{10,... | collective-permute-start | bytes 98312 | tf_op jit(solution)/shard_map/ppermute | solution.py:632
  43.6 3.0 %collective-permute-start.13 = (bf16[16,512]{1,0:T(8,128)(2,1)S(1)}, bf16[16,512]{1,0:T(8,128)(2,1)S(1)}, u32[]{:S(2)}, u32[]{:S(2)}) collective-permute-start(bf16[16,512]{1,0:T(8,128)(2,1)S(1)} %get-tuple-element.143), channel_id=1, source_target_pairs={{0,2},{1,3},{2,0},{3,1},{4,6},{5,7},{6,4},{7,5},{8,10},{9,11},{10,... | collective-permute-start | bytes 49160 | tf_op jit(solution)/shard_map/ppermute | solution.py:632
  46.5 17.4 %collective-permute-start.14 = (bf16[192,1024]{1,0:T(8,128)(2,1)S(1)}, bf16[192,1024]{1,0:T(8,128)(2,1)S(1)}, u32[]{:S(2)}, u32[]{:S(2)}) collective-permute-start(bf16[192,1024]{1,0:T(8,128)(2,1)S(1)} %get-tuple-element.144), channel_id=1, source_target_pairs={{0,31},{1,0},{2,1},{3,2},{4,3},{5,4},{6,5},{7,6},{8,7},{9,8},{10,9... | collective-permute-start | bytes 1179656 | tf_op jit(solution)/shard_map/ppermute | solution.py:632
  51.2 12.8 %collective-permute-start.15 = (bf16[192,1024]{1,0:T(8,128)(2,1)S(1)}, bf16[192,1024]{1,0:T(8,128)(2,1)S(1)}, u32[]{:S(2)}, u32[]{:S(2)}) collective-permute-start(bf16[192,1024]{1,0:T(8,128)(2,1)S(1)} %get-tuple-element.145), channel_id=1, source_target_pairs={{0,1},{1,2},{2,3},{3,4},{4,5},{5,6},{6,7},{7,8},{8,9},{9,10},{10,1... | collective-permute-start | bytes 1179656 | tf_op jit(solution)/shard_map/ppermute | solution.py:632
  52.3 17.2 %all-to-all-start = ((bf16[8,16,512]{2,1,0:T(8,128)(2,1)}), bf16[8,16,512]{2,1,0:T(8,128)(2,1)S(1)}, u32[]{:S(2)}, u32[]{:S(2)}) async-start(bf16[8,16,512]{2,1,0:T(8,128)(2,1)} %copies.1), calls=%async_computation | async-start | bytes 262144 | tf_op jit(solution)/shard_map/all_to_all | solution.py:817
  59.9 1.3 %collective-permute-start.17 = (bf16[48,1024]{1,0:T(8,128)(2,1)S(1)}, bf16[48,1024]{1,0:T(8,128)(2,1)S(1)}, u32[]{:S(2)}, u32[]{:S(2)}) collective-permute-start(bf16[48,1024]{1,0:T(8,128)(2,1)S(1)} %far_split.1.refs_16_), channel_id=1, source_target_pairs={{0,1},{1,0},{2,3},{3,2},{4,5},{5,4},{6,7},{7,6},{8,9},{9,8},{10,11... | collective-permute-start | bytes 294920 | tf_op jit(solution)/shard_map/ppermute | solution.py:632
  59.9 4.1 %collective-permute-start.16 = (bf16[16,1024]{1,0:T(8,128)(2,1)S(1)}, bf16[16,1024]{1,0:T(8,128)(2,1)S(1)}, u32[]{:S(2)}, u32[]{:S(2)}) collective-permute-start(bf16[16,1024]{1,0:T(8,128)(2,1)S(1)} %get-tuple-element.148), channel_id=1, source_target_pairs={{0,6},{1,7},{2,28},{3,29},{4,10},{5,11},{6,0},{7,1},{8,14},{9,15},... | collective-permute-start | bytes 98312 | tf_op jit(solution)/shard_map/ppermute | solution.py:632

commit v12 on v11

--- a/solution.py
+++ b/solution.py
@@ -298,7 +298,7 @@
 
 def block_at(block):
     x, y, core = block // 8, block // 2 % 4, block % 2
-    return 16 * (16 * core + 4 * (0, 2, 3, 1)[x] + y)
+    return 16 * (16 * core + 4 * ((0, 2, 3, 1), (0, 1, 3, 2))[core][x] + y)
 
 
 def merge_kernel(
@@ -518,12 +518,13 @@
         sum4[:, lanes] = (came(64, 96) + to_4[:, lanes].astype(F32)).astype(BF16)
         sum_third[:, lanes] = (came(96, 112) + to_third[:, lanes].astype(F32)).astype(BF16)
     total[...] = keep[...] + message[0:256].astype(F32)
-    halve(total, (8, 16), keep_out, give_out)
+    halve(total, ((8, 16), (16,)), keep_out, give_out)
 
 
 def halve(total, divisors, keep, give):
     index = lax.axis_index("ctx")
-    side = sum(index // divisor for divisor in divisors) % 2
+    sides = [sum(index // divisor for divisor in chosen) % 2 for chosen in divisors]
+    side = sides[0] * (1 - index % 2) + sides[1] * (index % 2)
     half = total.shape[0] // 2
     keep[...] = total[pl.ds(pl.multiple_of(side * half, half), half)]
     give[...] = total[pl.ds(pl.multiple_of((1 - side) * half, half), half)].astype(BF16)
@@ -542,7 +543,7 @@
 def halve_kernel(divisor, keep, got, *refs):
     keep_out, give_out, total = refs[-3:]
     total[...] = keep[...] + got[...].astype(F32)
-    halve(total, (divisor,), keep_out, give_out)
+    halve(total, divisor, keep_out, give_out)
 
 
 def copies_kernel(keep, got, *refs):
@@ -763,7 +764,7 @@
         [pltpu.VMEM((256, WIDTH), F32)],
         in_hbm=1,
     )
-    got_w = moved(give, lambda i: i ^ 8)
+    got_w = moved(give, lambda i: i ^ (24 if i % 2 else 8))
     back3 = moved(sum3, back_3)
     back4 = moved(sum4, back_4)
     layer_out, projected = call(
@@ -775,7 +776,7 @@
         in_hbm=1,
         to_hbm=(0,),
     )
-    keep, got_w = halved(keep, got_w, 16, lambda i: i ^ 24, projected)
+    keep, got_w = halved(keep, got_w, ((16,), (8, 16)), lambda i: i ^ (8 if i % 2 else 24), projected)
     part_b = call(
         functools.partial(near_back_kernel, NEAR_PARTS[1]),
         "near_back_b",
@@ -784,7 +785,7 @@
         in_hbm=2,
         microseconds=3,
     )
-    keep, got_w = halved(keep, got_w, 4, lambda i: i ^ 6, part_b[0])
+    keep, got_w = halved(keep, got_w, ((4,), (4,)), lambda i: i ^ 6, part_b[0])
     part_c = call(
         functools.partial(near_back_kernel, NEAR_PARTS[2]),
         "near_back_c",
@@ -793,7 +794,7 @@
         in_hbm=2,
         microseconds=3,
     )
-    keep, got_w = halved(keep, got_w, 2, lambda i: i ^ 2, part_c[0])
+    keep, got_w = halved(keep, got_w, ((2,), (2,)), lambda i: i ^ 2, part_c[0])
     give = call(far_split_kernel, "far_split", [((48, 2 * WIDTH), BF16)], [back3, back4])[0]
     swapped = moved(give, partner)
     d_q, own_k, own_v, to_low, to_high = call(

time: 70.4 us -> 69.3 us (0.984)
  the two profiles are of different devices: /device:TPU:31 before, /device:TPU:32 now
where the time goes in v12:
time: 69.3 us; the launch traced here: 67.9 us
  starting transfers between devices  25.9 us (37%)
  waiting for transfers between devices  21.4 us (31%)
  Pallas kernels  19 us (27%)
  between operations  0.89 us (1%)
  local copies, waits for them, and re-layouts  0.75 us (1%)
    ppermute x18, waiting for transfers between devices, moved(): return lax.ppermute(x, 'ctx', [(i, route(i) % count) for i in range(count)])  20 us
    pallas_call x21, Pallas kernels, call(): pl.pallas_call(kernel, name=name, out_shape=[jax.ShapeDtypeStruct(shape,...  19 us
    ppermute x18, starting transfers between devices, moved(): return lax.ppermute(x, 'ctx', [(i, route(i) % count) for i in range(count)])  17.4 us
    all_to_all x1, starting transfers between devices, body(): copies = lax.all_to_all(copies, 'dp', 0, 0, tiled=True)  8.57 us
  transfers between devices with their start and end apart: 19, of which 9 were waited for; matrix products, arithmetic and copies ran while one was open for 0% of the time, Pallas kernels for 17%

profile of v12, /device:TPU:32, one launch (start us, length us, event | category | flops | bytes accessed | tf_op | source)
XLA Modules:
  0.0 67.9 jit_solution(7317150398620450970)
XLA Ops:
  0.7 0.7 %copy-done.5 = s32[1,256]{1,0:T(1,128)S(1)} copy-done((s32[1,256]{1,0:T(1,128)S(1)}, s32[1,256]{1,0:T(1,128)}, u32[]{:S(2)}) %copy-start.5) | copy-done | bytes 1048
  1.7 0.6 coarsen.1
  2.4 5.1 %collective-permute-start.1 = (bf16[192,1152]{1,0:T(8,128)(2,1)S(1)}, bf16[192,1152]{1,0:T(8,128)(2,1)S(1)}, u32[]{:S(2)}, u32[]{:S(2)}) collective-permute-start(bf16[192,1152]{1,0:T(8,128)(2,1)S(1)} %get-tuple-element.84), channel_id=1, source_target_pairs={{0,31},{1,0},{2,1},{3,2},{4,3},{5,4},{6,5},{7,6},{8,7},{9,8},{10,9... | collective-permute-start | bytes 1327112 | tf_op jit(solution)/shard_map/ppermute | solution.py:633
  7.5 1.3 %collective-permute-done.2.far_partner = bf16[48,1152]{1,0:T(8,128)(2,1)S(1)} collective-permute-done((bf16[48,1152]{1,0:T(8,128)(2,1)S(1)}, bf16[48,1152]{1,0:T(8,128)(2,1)S(1)}, u32[]{:S(2)}, u32[]{:S(2)}) %collective-permute-start.2) | collective-permute-done | bytes 110624 | tf_op jit(solution)/shard_map/ppermute | solution.py:633
  8.9 2.9 %collective-permute-start.5 = (bf16[16,1152]{1,0:T(8,128)(2,1)S(1)}, bf16[16,1152]{1,0:T(8,128)(2,1)S(1)}, u32[]{:S(2)}, u32[]{:S(2)}) collective-permute-start(bf16[16,1152]{1,0:T(8,128)(2,1)S(1)} %get-tuple-element.97), channel_id=1, source_target_pairs={{0,6},{1,7},{2,28},{3,29},{4,10},{5,11},{6,0},{7,1},{8,14},{9,15},... | collective-permute-start | bytes 110600 | tf_op jit(solution)/shard_map/ppermute | solution.py:633
  11.9 0.7 %prepare.1 = (bf16[496,512]{1,0:T(8,128)(2,1)S(1)}, f32[256,512]{1,0:T(8,128)S(1)}, bf16[512,512]{1,0:T(8,128)(2,1)S(1)}, bf16[256,512]{1,0:T(8,128)(2,1)S(1)}) custom-call(bf16[256,512]{1,0:T(8,128)(2,1)S(1)} %bitcast.10, bf16[256,512]{1,0:T(8,128)(2,1)S(1)} %bitcast.11, bf16[512,512]{1,0:T(8,128)(2,1)S(1)} %copy-done), custom_call_target="tpu_custom_call" | custom-call | flops 1000000000 | bytes 1048576 | tf_op jit(solution)/shard_map/prepare/pallas_call | solution.py:617
  12.6 4.8 %collective-permute-done.3.got3 = bf16[64,1152]{1,0:T(8,128)(2,1)S(1)} collective-permute-done((bf16[64,1152]{1,0:T(8,128)(2,1)S(1)}, bf16[64,1152]{1,0:T(8,128)(2,1)S(1)}, u32[]{:S(2)}, u32[]{:S(2)}) %collective-permute-start.3) | collective-permute-done | bytes 147488 | tf_op jit(solution)/shard_map/ppermute | solution.py:633
  17.4 2.5 %collective-permute-done.4.got4.refs_1_ = bf16[32,1152]{1,0:T(8,128)(2,1)S(1)} collective-permute-done((bf16[32,1152]{1,0:T(8,128)(2,1)S(1)}, bf16[32,1152]{1,0:T(8,128)(2,1)S(1)}, u32[]{:S(2)}, u32[]{:S(2)}) %collective-permute-start.4) | collective-permute-done | bytes 73760 | tf_op jit(solution)/shard_map/ppermute | solution.py:633
  20.0 1.7 %near.1 = (bf16[4,896,256]{2,1,0:T(8,128)(2,1)S(1)}, f32[256,512]{1,0:T(8,128)S(1)}, f32[256,256]{1,0:T(8,128)S(1)}, bf16[192,512]{1,0:T(8,128)(2,1)S(1)}, bf16[192,256]{1,0:T(8,128)(2,1)S(1)}) custom-call(bf16[496,512]{1,0:T(8,128)(2,1)S(1)} %get-tuple-element.80.q_all.refs_1_, bf16[496,128]{1,0:T(8,128)(2,1)S(1)} %documents.1.qdoc, ...), custom_call_target="tpu_custom_call" | custom-call | flops 49999998976 | bytes 1048576 | tf_op jit(solution)/shard_map/near/pallas_call | solution.py:617
  21.7 4.8 %merge.1 = (bf16[256,512]{1,0:T(8,128)(2,1)S(1)}, f32[256,512]{1,0:T(8,128)S(1)}, bf16[256,512]{1,0:T(8,128)(2,1)S(1)}, bf16[4,96,128]{2,1,0:T(8,128)(2,1)S(1)},...) custom-call(bf16[496,512]{1,0:T(8,128)(2,1)S(1)} %get-tuple-element.80.q_all.refs_1_, ...), custom_call_target="tpu_custom_call" | custom-call | flops 6000000000 | bytes 1048576 | tf_op jit(solution)/shard_map/merge/pallas_call | solution.py:617
  26.5 1.1 %far_back.1 = (bf16[48,512]{1,0:T(8,128)(2,1)S(1)}, bf16[32,1024]{1,0:T(8,128)(2,1)S(1)}, bf16[32,1024]{1,0:T(8,128)(2,1)S(1)}, bf16[16,1024]{1,0:T(8,128)(2,1)S(1)}, bf16[480,512]{1,0:T(8,128)(2,1)S(1)}) custom-call(bf16[4,96,128]{2,1,0:T(8,128)(2,1)S(1)} %get-tuple-element.102.p_in, bf16[496,512]{1,0:T(8,128)(2,1)S(1)} %get-tuple-element.80.q_all.refs_1_, ...), custom_call_target="tpu_custom_call" | custom-call | flops 1000000000 | bytes 1048576 | tf_op jit(solution)/shard_map/far_back/pallas_call | solution.py:617
  27.6 0.8 %collective-permute-start.7 = (bf16[480,512]{1,0:T(8,128)(2,1)S(1)}, bf16[480,512]{1,0:T(8,128)(2,1)S(1)}, u32[]{:S(2)}, u32[]{:S(2)}) collective-permute-start(bf16[480,512]{1,0:T(8,128)(2,1)S(1)} %get-tuple-element.110), channel_id=1, source_target_pairs={{0,1},{1,0},{2,3},{3,2},{4,5},{5,4},{6,7},{7,6},{8,9},{9,8},{10,11... | collective-permute-start | bytes 1474568 | tf_op jit(solution)/shard_map/ppermute | solution.py:633
  28.4 1.4 %near_back_a.1 = (bf16[256,128]{1,0:T(8,128)(2,1)S(1)}, bf16[256,128]{1,0:T(8,128)(2,1)S(1)}, bf16[256,128]{1,0:T(8,128)(2,1)S(1)}, bf16[2,192,128]{2,1,0:T(8,128)(2,1)S(1)}, bf16[2,192,128]{2,1,0:T(8,128)(2,1)S(1)}) custom-call(bf16[4,896,256]{2,1,0:T(8,128)(2,1)S(1)} %get-tuple-element.111.refs_0_, bf16[496,512]{1,0:T(8,128)(2,1)S(1)} %get-tuple-element.80.q_all.refs_1_, ...), custom_call_target="tpu_custom_call" | custom-call | flops 3000000000 | bytes 1048576 | tf_op jit(solution)/shard_map/near_back_a/pallas_call | solution.py:617
  30.4 1.5 %collective-permute-start.12 = (bf16[32,1024]{1,0:T(8,128)(2,1)S(1)}, bf16[32,1024]{1,0:T(8,128)(2,1)S(1)}, u32[]{:S(2)}, u32[]{:S(2)}) collective-permute-start(bf16[32,1024]{1,0:T(8,128)(2,1)S(1)} %get-tuple-element.135), channel_id=1, source_target_pairs={{0,28},{1,5},{2,30},{3,7},{4,0},{5,9},{6,2},{7,11},{8,4},{9,13},{1... | collective-permute-start | bytes 196616 | tf_op jit(solution)/shard_map/ppermute | solution.py:633
  31.8 1.8 %collective-permute-start.11 = (bf16[64,1024]{1,0:T(8,128)(2,1)S(1)}, bf16[64,1024]{1,0:T(8,128)(2,1)S(1)}, u32[]{:S(2)}, u32[]{:S(2)}) collective-permute-start(bf16[64,1024]{1,0:T(8,128)(2,1)S(1)} %get-tuple-element.114._), channel_id=1, source_target_pairs={{0,30},{1,3},{2,0},{3,5},{4,2},{5,7},{6,4},{7,9},{8,6},{9,11},{10,... | collective-permute-start | bytes 393224 | tf_op jit(solution)/shard_map/ppermute | solution.py:633
  33.7 1.0 %project.1 = (bf16[256,512]{1,0:T(8,128)(2,1)}, f32[8,128]{1,0:T(8,128)S(1)}) custom-call(bf16[256,512]{1,0:T(8,128)(2,1)S(1)} %get-tuple-element.100.attended, bf16[512,512]{1,0:T(8,128)(2,1)S(1)} %get-tuple-element.101.w, bf16[64,1024]{1,0:T(8,128)(2,1)S(1)} %get-tuple-element.114._), custom_call_target="tpu_custom_call" | custom-call | flops 1000000000 | bytes 1048576 | tf_op jit(solution)/shard_map/project/pallas_call | solution.py:617
  35.1 1.8 %collective-permute-start.9 = (bf16[64,512]{1,0:T(8,128)(2,1)S(1)}, bf16[64,512]{1,0:T(8,128)(2,1)S(1)}, u32[]{:S(2)}, u32[]{:S(2)}) collective-permute-start(bf16[64,512]{1,0:T(8,128)(2,1)S(1)} %get-tuple-element.123), channel_id=1, source_target_pairs={{0,24},{1,9},{2,26},{3,11},{4,28},{5,13},{6,30},{7,15},{8,16},{9,1... | collective-permute-start | bytes 196616 | tf_op jit(solution)/shard_map/ppermute | solution.py:633
  36.9 1.4 %near_back_b.1 = (bf16[256,128]{1,0:T(8,128)(2,1)S(1)}, bf16[256,128]{1,0:T(8,128)(2,1)S(1)}, bf16[256,128]{1,0:T(8,128)(2,1)S(1)}, bf16[2,192,128]{2,1,0:T(8,128)(2,1)S(1)}, bf16[2,192,128]{2,1,0:T(8,128)(2,1)S(1)}) custom-call(bf16[4,896,256]{2,1,0:T(8,128)(2,1)S(1)} %get-tuple-element.111.refs_0_, bf16[496,512]{1,0:T(8,128)(2,1)S(1)} %get-tuple-element.80.q_all.refs_1_, ...), custom_call_target="tpu_custom_call" | custom-call | flops 3000000000 | bytes 1048576 | tf_op jit(solution)/shard_map/near_back_b/pallas_call | solution.py:617
  38.4 2.2 %collective-permute-done.9.got = bf16[64,512]{1,0:T(8,128)(2,1)S(1)} collective-permute-done((bf16[64,512]{1,0:T(8,128)(2,1)S(1)}, bf16[64,512]{1,0:T(8,128)(2,1)S(1)}, u32[]{:S(2)}, u32[]{:S(2)}) %collective-permute-start.9) | collective-permute-done | bytes 65568 | tf_op jit(solution)/shard_map/ppermute | solution.py:633
  40.7 1.0 %collective-permute-start.10 = (bf16[32,512]{1,0:T(8,128)(2,1)S(1)}, bf16[32,512]{1,0:T(8,128)(2,1)S(1)}, u32[]{:S(2)}, u32[]{:S(2)}) collective-permute-start(bf16[32,512]{1,0:T(8,128)(2,1)S(1)} %get-tuple-element.132), channel_id=1, source_target_pairs={{0,6},{1,7},{2,4},{3,5},{4,2},{5,3},{6,0},{7,1},{8,14},{9,15},{10,... | collective-permute-start | bytes 98312 | tf_op jit(solution)/shard_map/ppermute | solution.py:633
  41.7 1.4 %near_back_c.1 = (bf16[256,128]{1,0:T(8,128)(2,1)S(1)}, bf16[256,128]{1,0:T(8,128)(2,1)S(1)}, bf16[256,128]{1,0:T(8,128)(2,1)S(1)}, bf16[2,192,128]{2,1,0:T(8,128)(2,1)S(1)}, bf16[2,192,128]{2,1,0:T(8,128)(2,1)S(1)}) custom-call(bf16[4,896,256]{2,1,0:T(8,128)(2,1)S(1)} %get-tuple-element.111.refs_0_, bf16[496,512]{1,0:T(8,128)(2,1)S(1)} %get-tuple-element.80.q_all.refs_1_, ...), custom_call_target="tpu_custom_call" | custom-call | flops 3000000000 | bytes 1048576 | tf_op jit(solution)/shard_map/near_back_c/pallas_call | solution.py:617
  43.1 2.8 %collective-permute-done.10.got = bf16[32,512]{1,0:T(8,128)(2,1)S(1)} collective-permute-done((bf16[32,512]{1,0:T(8,128)(2,1)S(1)}, bf16[32,512]{1,0:T(8,128)(2,1)S(1)}, u32[]{:S(2)}, u32[]{:S(2)}) %collective-permute-start.10) | collective-permute-done | bytes 32800 | tf_op jit(solution)/shard_map/ppermute | solution.py:633
  46.1 1.5 %near_back_d.1 = (bf16[256,128]{1,0:T(8,128)(2,1)S(1)}, bf16[256,128]{1,0:T(8,128)(2,1)S(1)}, bf16[256,128]{1,0:T(8,128)(2,1)S(1)}, bf16[192,1024]{1,0:T(8,128)(2,1)S(1)}, bf16[192,1024]{1,0:T(8,128)(2,1)S(1)}) custom-call(bf16[4,896,256]{2,1,0:T(8,128)(2,1)S(1)} %get-tuple-element.111.refs_0_, bf16[496,512]{1,0:T(8,128)(2,1)S(1)} %get-tuple-element.80.q_all.refs_1_, ...), custom_call_target="tpu_custom_call" | custom-call | flops 3000000000 | bytes 1048576 | tf_op jit(solution)/shard_map/near_back_d/pallas_call | solution.py:617
  47.6 2.2 %collective-permute-done.13.got = bf16[16,512]{1,0:T(8,128)(2,1)S(1)} collective-permute-done((bf16[16,512]{1,0:T(8,128)(2,1)S(1)}, bf16[16,512]{1,0:T(8,128)(2,1)S(1)}, u32[]{:S(2)}, u32[]{:S(2)}) %collective-permute-start.13) | collective-permute-done | bytes 16416 | tf_op jit(solution)/shard_map/ppermute | solution.py:633
  49.8 0.5 collective-permute-start.15
  50.3 0.7 copies.1
  51.0 8.6 %all-to-all-start = ((bf16[8,16,512]{2,1,0:T(8,128)(2,1)}), bf16[8,16,512]{2,1,0:T(8,128)(2,1)S(1)}, u32[]{:S(2)}, u32[]{:S(2)}) async-start(bf16[8,16,512]{2,1,0:T(8,128)(2,1)} %copies.1), calls=%async_computation | async-start | bytes 262144 | tf_op jit(solution)/shard_map/all_to_all | solution.py:818
  59.5 1.3 %collective-permute-start.16 = (bf16[16,1024]{1,0:T(8,128)(2,1)S(1)}, bf16[16,1024]{1,0:T(8,128)(2,1)S(1)}, u32[]{:S(2)}, u32[]{:S(2)}) collective-permute-start(bf16[16,1024]{1,0:T(8,128)(2,1)S(1)} %get-tuple-element.148), channel_id=1, source_target_pairs={{0,6},{1,7},{2,28},{3,29},{4,10},{5,11},{6,0},{7,1},{8,14},{9,15},... | collective-permute-start | bytes 98312 | tf_op jit(solution)/shard_map/ppermute | solution.py:633
  60.8 3.8 %collective-permute-done.16.refs_12_ = bf16[16,1024]{1,0:T(8,128)(2,1)S(1)} collective-permute-done((bf16[16,1024]{1,0:T(8,128)(2,1)S(1)}, bf16[16,1024]{1,0:T(8,128)(2,1)S(1)}, u32[]{:S(2)}, u32[]{:S(2)}) %collective-permute-start.16) | collective-permute-done | bytes 32800 | tf_op jit(solution)/shard_map/ppermute | solution.py:633
  64.7 1.3 %combine.1 = (bf16[256,512]{1,0:T(8,128)(2,1)}, bf16[256,512]{1,0:T(8,128)(2,1)}, bf16[256,512]{1,0:T(8,128)(2,1)}, f32[8,128]{1,0:T(8,128)S(1)}) custom-call(bf16[256,128]{1,0:T(8,128)(2,1)S(1)} %get-tuple-element.116.refs_0_, bf16[256,128]{1,0:T(8,128)(2,1)S(1)} %get-tuple-element.121.refs_1_, bf16[256,128]{1,0:T(8,128)(2,1)S(1)} %get-tuple-element.125.refs_2_, ...), custom_call_target="tpu_custom_call" | custom-call | flops 1000000000 | bytes 1048576 | tf_op jit(solution)/shard_map/combine/pallas_call | solution.py:617
  65.9 1.4 %all-to-all-done.parts = bf16[8,16,512]{2,1,0:T(8,128)(2,1)S(1)} async-done(((bf16[8,16,512]{2,1,0:T(8,128)(2,1)}), bf16[8,16,512]{2,1,0:T(8,128)(2,1)S(1)}, u32[]{:S(2)}, u32[]{:S(2)}) %all-to-all-start) | async-done | bytes 131104 | tf_op jit(solution)/shard_map/all_to_all | solution.py:818
  67.3 0.6 last_sum.1
  (39 shorter events, 1.8 us)
Async XLA Ops:
  0.6 1.1 %copy-start.2 = (bf16[1,256,512]{2,1,0:T(8,128)(2,1)S(1)}, bf16[1,256,512]{2,1,0:T(8,128)(2,1)}, u32[]{:S(2)}) copy-start(bf16[1,256,512]{2,1,0:T(8,128)(2,1)} %param.8) | copy-start | bytes 786436
  0.6 1.1 %copy-start.1 = (bf16[1,256,512]{2,1,0:T(8,128)(2,1)S(1)}, bf16[1,256,512]{2,1,0:T(8,128)(2,1)}, u32[]{:S(2)}) copy-start(bf16[1,256,512]{2,1,0:T(8,128)(2,1)} %param.7) | copy-start | bytes 786436
  0.7 0.7 %copy-start.5 = (s32[1,256]{1,0:T(1,128)S(1)}, s32[1,256]{1,0:T(1,128)}, u32[]{:S(2)}) copy-start(s32[1,256]{1,0:T(1,128)} %seg_hbm.1) | copy-start | bytes 3076
  2.3 15.0 %collective-permute-start = (bf16[192,1152]{1,0:T(8,128)(2,1)S(1)}, bf16[192,1152]{1,0:T(8,128)(2,1)S(1)}, u32[]{:S(2)}, u32[]{:S(2)}) collective-permute-start(bf16[192,1152]{1,0:T(8,128)(2,1)S(1)} %get-tuple-element.83), channel_id=1, source_target_pairs={{0,1},{1,2},{2,3},{3,4},{4,5},{5,6},{6,7},{7,8},{8,9},{9,10},{10,1... | collective-permute-start | bytes 1327112 | tf_op jit(solution)/shard_map/ppermute | solution.py:633
  2.4 15.0 %collective-permute-start.1 = (bf16[192,1152]{1,0:T(8,128)(2,1)S(1)}, bf16[192,1152]{1,0:T(8,128)(2,1)S(1)}, u32[]{:S(2)}, u32[]{:S(2)}) collective-permute-start(bf16[192,1152]{1,0:T(8,128)(2,1)S(1)} %get-tuple-element.84), channel_id=1, source_target_pairs={{0,31},{1,0},{2,1},{3,2},{4,3},{5,4},{6,5},{7,6},{8,7},{9,8},{10,9... | collective-permute-start | bytes 1327112 | tf_op jit(solution)/shard_map/ppermute | solution.py:633
  7.5 4.4 %copy-start = (bf16[512,512]{1,0:T(8,128)(2,1)S(1)}, bf16[512,512]{1,0:T(8,128)(2,1)}, u32[]{:S(2)}) copy-start(bf16[512,512]{1,0:T(8,128)(2,1)} %w_hbm.1) | copy-start | bytes 1572868
  7.5 4.4 %copy-start.3 = (bf16[1,256,512]{2,1,0:T(8,128)(2,1)S(1)}, bf16[1,256,512]{2,1,0:T(8,128)(2,1)}, u32[]{:S(2)}) copy-start(bf16[1,256,512]{2,1,0:T(8,128)(2,1)} %param.6) | copy-start | bytes 786436
  7.5 4.4 %copy-start.4 = (bf16[1,256,512]{2,1,0:T(8,128)(2,1)S(1)}, bf16[1,256,512]{2,1,0:T(8,128)(2,1)}, u32[]{:S(2)}) copy-start(bf16[1,256,512]{2,1,0:T(8,128)(2,1)} %param.11) | copy-start | bytes 786436
  7.5 1.3 %collective-permute-start.2 = (bf16[48,1152]{1,0:T(8,128)(2,1)S(1)}, bf16[48,1152]{1,0:T(8,128)(2,1)S(1)}, u32[]{:S(2)}, u32[]{:S(2)}) collective-permute-start(bf16[48,1152]{1,0:T(8,128)(2,1)S(1)} %get-tuple-element.85.far), channel_id=1, source_target_pairs={{0,1},{1,0},{2,3},{3,2},{4,5},{5,4},{6,7},{7,6},{8,9},{9,8},{10,11... | collective-permute-start | bytes 331784 | tf_op jit(solution)/shard_map/ppermute | solution.py:633
  8.8 8.5 %collective-permute-start.3 = (bf16[64,1152]{1,0:T(8,128)(2,1)S(1)}, bf16[64,1152]{1,0:T(8,128)(2,1)S(1)}, u32[]{:S(2)}, u32[]{:S(2)}) collective-permute-start(bf16[64,1152]{1,0:T(8,128)(2,1)S(1)} %get-tuple-element.86), channel_id=1, source_target_pairs={{0,2},{1,31},{2,4},{3,1},{4,6},{5,3},{6,8},{7,5},{8,10},{9,7},{10,... | collective-permute-start | bytes 442376 | tf_op jit(solution)/shard_map/ppermute | solution.py:633
  8.9 8.5 %collective-permute-start.5 = (bf16[16,1152]{1,0:T(8,128)(2,1)S(1)}, bf16[16,1152]{1,0:T(8,128)(2,1)S(1)}, u32[]{:S(2)}, u32[]{:S(2)}) collective-permute-start(bf16[16,1152]{1,0:T(8,128)(2,1)S(1)} %get-tuple-element.97), channel_id=1, source_target_pairs={{0,6},{1,7},{2,28},{3,29},{4,10},{5,11},{6,0},{7,1},{8,14},{9,15},... | collective-permute-start | bytes 110600 | tf_op jit(solution)/shard_map/ppermute | solution.py:633
  11.9 8.0 %collective-permute-start.4 = (bf16[32,1152]{1,0:T(8,128)(2,1)S(1)}, bf16[32,1152]{1,0:T(8,128)(2,1)S(1)}, u32[]{:S(2)}, u32[]{:S(2)}) collective-permute-start(bf16[32,1152]{1,0:T(8,128)(2,1)S(1)} %get-tuple-element.96), channel_id=1, source_target_pairs={{0,4},{1,29},{2,6},{3,31},{4,8},{5,1},{6,10},{7,3},{8,12},{9,5},{1... | collective-permute-start | bytes 221192 | tf_op jit(solution)/shard_map/ppermute | solution.py:633
  19.9 1.8 %collective-permute-start.6 = (bf16[112,1152]{1,0:T(8,128)(2,1)S(1)}, bf16[112,1152]{1,0:T(8,128)(2,1)S(1)}, u32[]{:S(2)}, u32[]{:S(2)}) collective-permute-start(bf16[112,1152]{1,0:T(8,128)(2,1)S(1)} %get-tuple-element.99), channel_id=1, source_target_pairs={{0,1},{1,0},{2,3},{3,2},{4,5},{5,4},{6,7},{7,6},{8,9},{9,8},{10,11... | collective-permute-start | bytes 774152 | tf_op jit(solution)/shard_map/ppermute | solution.py:633
  27.6 2.3 %collective-permute-start.7 = (bf16[480,512]{1,0:T(8,128)(2,1)S(1)}, bf16[480,512]{1,0:T(8,128)(2,1)S(1)}, u32[]{:S(2)}, u32[]{:S(2)}) collective-permute-start(bf16[480,512]{1,0:T(8,128)(2,1)S(1)} %get-tuple-element.110), channel_id=1, source_target_pairs={{0,1},{1,0},{2,3},{3,2},{4,5},{5,4},{6,7},{7,6},{8,9},{9,8},{10,11... | collective-permute-start | bytes 1474568 | tf_op jit(solution)/shard_map/ppermute | solution.py:633
  30.0 5.1 %collective-permute-start.8 = (bf16[128,512]{1,0:T(8,128)(2,1)S(1)}, bf16[128,512]{1,0:T(8,128)(2,1)S(1)}, u32[]{:S(2)}, u32[]{:S(2)}) collective-permute-start(bf16[128,512]{1,0:T(8,128)(2,1)S(1)} %get-tuple-element.118), channel_id=1, source_target_pairs={{0,8},{1,25},{2,10},{3,27},{4,12},{5,29},{6,14},{7,31},{8,0},{9,17... | collective-permute-start | bytes 393224 | tf_op jit(solution)/shard_map/ppermute | solution.py:633
  30.4 8.0 %collective-permute-start.12 = (bf16[32,1024]{1,0:T(8,128)(2,1)S(1)}, bf16[32,1024]{1,0:T(8,128)(2,1)S(1)}, u32[]{:S(2)}, u32[]{:S(2)}) collective-permute-start(bf16[32,1024]{1,0:T(8,128)(2,1)S(1)} %get-tuple-element.135), channel_id=1, source_target_pairs={{0,28},{1,5},{2,30},{3,7},{4,0},{5,9},{6,2},{7,11},{8,4},{9,13},{1... | collective-permute-start | bytes 196616 | tf_op jit(solution)/shard_map/ppermute | solution.py:633
  31.8 6.6 %collective-permute-start.11 = (bf16[64,1024]{1,0:T(8,128)(2,1)S(1)}, bf16[64,1024]{1,0:T(8,128)(2,1)S(1)}, u32[]{:S(2)}, u32[]{:S(2)}) collective-permute-start(bf16[64,1024]{1,0:T(8,128)(2,1)S(1)} %get-tuple-element.114._), channel_id=1, source_target_pairs={{0,30},{1,3},{2,0},{3,5},{4,2},{5,7},{6,4},{7,9},{8,6},{9,11},{10,... | collective-permute-start | bytes 393224 | tf_op jit(solution)/shard_map/ppermute | solution.py:633
  35.1 5.6 %collective-permute-start.9 = (bf16[64,512]{1,0:T(8,128)(2,1)S(1)}, bf16[64,512]{1,0:T(8,128)(2,1)S(1)}, u32[]{:S(2)}, u32[]{:S(2)}) collective-permute-start(bf16[64,512]{1,0:T(8,128)(2,1)S(1)} %get-tuple-element.123), channel_id=1, source_target_pairs={{0,24},{1,9},{2,26},{3,11},{4,28},{5,13},{6,30},{7,15},{8,16},{9,1... | collective-permute-start | bytes 196616 | tf_op jit(solution)/shard_map/ppermute | solution.py:633
  40.7 5.2 %collective-permute-start.10 = (bf16[32,512]{1,0:T(8,128)(2,1)S(1)}, bf16[32,512]{1,0:T(8,128)(2,1)S(1)}, u32[]{:S(2)}, u32[]{:S(2)}) collective-permute-start(bf16[32,512]{1,0:T(8,128)(2,1)S(1)} %get-tuple-element.132), channel_id=1, source_target_pairs={{0,6},{1,7},{2,4},{3,5},{4,2},{5,3},{6,0},{7,1},{8,14},{9,15},{10,... | collective-permute-start | bytes 98312 | tf_op jit(solution)/shard_map/ppermute | solution.py:633
  46.0 3.8 %collective-permute-start.13 = (bf16[16,512]{1,0:T(8,128)(2,1)S(1)}, bf16[16,512]{1,0:T(8,128)(2,1)S(1)}, u32[]{:S(2)}, u32[]{:S(2)}) collective-permute-start(bf16[16,512]{1,0:T(8,128)(2,1)S(1)} %get-tuple-element.143), channel_id=1, source_target_pairs={{0,2},{1,3},{2,0},{3,1},{4,6},{5,7},{6,4},{7,5},{8,10},{9,11},{10,... | collective-permute-start | bytes 49160 | tf_op jit(solution)/shard_map/ppermute | solution.py:633
  49.8 14.9 %collective-permute-start.14 = (bf16[192,1024]{1,0:T(8,128)(2,1)S(1)}, bf16[192,1024]{1,0:T(8,128)(2,1)S(1)}, u32[]{:S(2)}, u32[]{:S(2)}) collective-permute-start(bf16[192,1024]{1,0:T(8,128)(2,1)S(1)} %get-tuple-element.144), channel_id=1, source_target_pairs={{0,31},{1,0},{2,1},{3,2},{4,3},{5,4},{6,5},{7,6},{8,7},{9,8},{10,9... | collective-permute-start | bytes 1179656 | tf_op jit(solution)/shard_map/ppermute | solution.py:633
  49.8 14.9 %collective-permute-start.15 = (bf16[192,1024]{1,0:T(8,128)(2,1)S(1)}, bf16[192,1024]{1,0:T(8,128)(2,1)S(1)}, u32[]{:S(2)}, u32[]{:S(2)}) collective-permute-start(bf16[192,1024]{1,0:T(8,128)(2,1)S(1)} %get-tuple-element.145), channel_id=1, source_target_pairs={{0,1},{1,2},{2,3},{3,4},{4,5},{5,6},{6,7},{7,8},{8,9},{9,10},{10,1... | collective-permute-start | bytes 1179656 | tf_op jit(solution)/shard_map/ppermute | solution.py:633
  51.0 16.4 %all-to-all-start = ((bf16[8,16,512]{2,1,0:T(8,128)(2,1)}), bf16[8,16,512]{2,1,0:T(8,128)(2,1)S(1)}, u32[]{:S(2)}, u32[]{:S(2)}) async-start(bf16[8,16,512]{2,1,0:T(8,128)(2,1)} %copies.1), calls=%async_computation | async-start | bytes 262144 | tf_op jit(solution)/shard_map/all_to_all | solution.py:818
  59.5 1.3 %collective-permute-start.17 = (bf16[48,1024]{1,0:T(8,128)(2,1)S(1)}, bf16[48,1024]{1,0:T(8,128)(2,1)S(1)}, u32[]{:S(2)}, u32[]{:S(2)}) collective-permute-start(bf16[48,1024]{1,0:T(8,128)(2,1)S(1)} %far_split.1.refs_16_), channel_id=1, source_target_pairs={{0,1},{1,0},{2,3},{3,2},{4,5},{5,4},{6,7},{7,6},{8,9},{9,8},{10,11... | collective-permute-start | bytes 294920 | tf_op jit(solution)/shard_map/ppermute | solution.py:633
  59.5 5.1 %collective-permute-start.16 = (bf16[16,1024]{1,0:T(8,128)(2,1)S(1)}, bf16[16,1024]{1,0:T(8,128)(2,1)S(1)}, u32[]{:S(2)}, u32[]{:S(2)}) collective-permute-start(bf16[16,1024]{1,0:T(8,128)(2,1)S(1)} %get-tuple-element.148), channel_id=1, source_target_pairs={{0,6},{1,7},{2,28},{3,29},{4,10},{5,11},{6,0},{7,1},{8,14},{9,15},... | collective-permute-start | bytes 98312 | tf_op jit(solution)/shard_map/ppermute | solution.py:633
